TPU v7x, 256 devices: a whole 4x4x8 slice. The times are simulated.
256 devices in a mesh: prow: 16 (over y_lo, z), pcol: 16 (over x, y_hi, core).
Axes of the slice: x: 4, y: 4 (y_hi: 2, y_lo: 2; y = y_hi * 2 + y_lo), z: 8, core: 2. Of those that a mesh axis runs over, the one named last changes fastest.
Arguments:
- ancestor_inverse: bfloat16 [12288, 12288], P('pcol', 'prow'), may hold values from -0.0546875 to 0.0546875
- factor_panel: bfloat16 [3, 12288, 1024], P(None, 'prow', 'pcol'), may hold values from -1.5 to 1.5
- pattern: int32 [3, 96], replicated, may hold values 0 or 1
- diagonal_inverse: float32 [3, 1024, 1024], P(None, 'pcol', 'prow'), may hold values from -6 to 6
Outputs:
- offdiag_inverse: float32 [3, 12288, 1024], P(None, 'pcol', 'prow')
- diagonal_block: float32 [3, 1024, 1024], P(None, 'pcol', 'prow')
All inputs are finite; a program needn't handle non-finite values.
Results may differ from a plain program's by a relative error of at most 0.0003.
Values may be sent and summed in bfloat16 or wider, within the bound.
No kernel may reach another device: no remote copies, remote signals or barrier semaphores. Data moves between devices by JAX's collectives and lax.ppermute only.
A program may use at most 128 MiB of HBM per device.

v0:
```python
import jax
import jax.numpy as jnp
from jax import lax
from jax.sharding import PartitionSpec as P

BLK = 128


def spread_2(value, axis, source):
    kept = jnp.where(lax.axis_index(axis) == source, value, 0).astype(value.dtype)
    return lax.psum(kept, axis)


def local_mask(pattern, first, count, block):
    picked = lax.dynamic_slice_in_dim(pattern, first, count, 1)
    spread = jnp.broadcast_to(picked[:, :, None], (picked.shape[0], count, block))
    return spread.reshape(picked.shape[0], count * block)


def selected_step(ancestor_inverse, masked, mask_cols, diag_term):
    row_panel = lax.all_gather(masked, "pcol", axis=2, tiled=True)
    partial_value = jnp.einsum(
        "ij,kjn->kin", ancestor_inverse, row_panel, preferred_element_type=jnp.float32
    )
    group_ratio = lax.axis_size("prow") // lax.axis_size("pcol")
    col_index = lax.axis_index("pcol")
    pieces = spread_2(row_panel, "prow", col_index * group_ratio + 0)
    col_panel = pieces.astype(jnp.float32)
    reduced = lax.psum_scatter(partial_value, "prow", scatter_dimension=2, tiled=True)
    offdiag = -(reduced * mask_cols[:, :, None])
    square = jnp.einsum("kin,kim->knm", col_panel, offdiag, precision=lax.Precision.HIGHEST)
    diagonal = diag_term - lax.psum_scatter(square, "pcol", scatter_dimension=1, tiled=True)
    return (offdiag, diagonal)


def shards(ancestor_inverse, factor_panel, pattern, diagonal_inverse):
    per_prow = factor_panel.shape[1] // BLK
    per_pcol = ancestor_inverse.shape[0] // BLK
    mask_rows = local_mask(pattern, lax.axis_index("prow") * per_prow, per_prow, BLK).astype(
        jnp.bfloat16
    )
    mask_cols = local_mask(pattern, lax.axis_index("pcol") * per_pcol, per_pcol, BLK).astype(
        jnp.float32
    )
    masked = factor_panel * mask_rows[:, :, None]
    offdiag, diagonal = selected_step(ancestor_inverse, masked, mask_cols, diagonal_inverse)
    return (offdiag, diagonal)


def solution(mesh):
    in_specs = (P("pcol", "prow"), P(None, "prow", "pcol"), P(), P(None, "pcol", "prow"))
    out_specs = (P(None, "pcol", "prow"), P(None, "pcol", "prow"))
    return jax.shard_map(shards, mesh=mesh, in_specs=in_specs, out_specs=out_specs, check_vma=False)
```

profile of v0, /device:TPU:6, one launch (start us, length us, event | category | flops | bytes accessed | tf_op | source)
XLA Modules:
  0.0 442.0 jit_solution(10268001574837307801)
XLA Ops:
  7.2 0.0 copy-start
  7.2 0.0 all-gather.2.cloned.1.call-start
  7.2 0.9 dynamic-slice_convert_fusion
  8.1 0.1 broadcast_bitcast_fusion.1
  8.2 1.7 broadcast_multiply_fusion
  9.9 0.0 all-gather.2.cloned.1.call-update
  9.9 0.0 reduce-scatter.3.cloned.1.call-start
  10.0 67.1 %all-gather.2.cloned.1.call-done = bf16[3,768,1024]{1,2,0:T(8,128)(2,1)} async-done(((bf16[3,768,64]{1,2,0:T(8,128)(2,1)}), bf16[3,768,1024]{1,2,0:T(8,128)(2,1)}) %all-gather.2.cloned.1.call-update) | async-done | bytes 4718608 | tf_op jit(solution)/shard_map/all_gather | solution.py:21
  77.1 0.0 copy-done
  77.1 8.8 %convolution_bitcast_fusion = f32[3,768,1024]{1,2,0:T(8,128)} fusion(bf16[3,768,1024]{1,2,0:T(8,128)(2,1)} %all-gather.2.cloned.1.call-done, bf16[768,768]{1,0:T(8,128)(2,1)S(1)} %copy-done), kind=kOutput, calls=%fused_computation.1 | convolution fusion | flops 3623878656 | bytes 15335424 | tf_op jit(solution)/shard_map/ij,kjn->kin/dot_general | solution.py:22
  85.8 0.0 reduce-scatter.3.cloned.1.call-update
  85.9 0.0 all-reduce.2.cloned.1.call-start
  85.9 2.4 broadcast_select_fusion
  88.4 0.0 all-reduce.2.cloned.1.call-update
  88.4 0.0 reduce-scatter.5.cloned.1.call-start
  88.4 0.1 broadcast_bitcast_fusion
  88.5 108.4 %reduce-scatter.3.cloned.1.call-done = f32[3,768,64]{1,2,0:T(8,128)} async-done(((f32[3,768,1024]{1,2,0:T(8,128)}), f32[3,768,64]{1,2,0:T(8,128)}) %reduce-scatter.3.cloned.1.call-update) | async-done | bytes 589840 | tf_op jit(solution)/shard_map/reduce_scatter | solution.py:29
  196.9 0.0 copy-start.2
  196.9 1.1 multiply_negate_fusion
  198.0 0.0 copy-start.1
  198.0 155.0 %all-reduce.2.cloned.1.call-done = bf16[3,768,1024]{1,2,0:T(8,128)(2,1)} async-done(((bf16[3,768,1024]{1,2,0:T(8,128)(2,1)}), bf16[3,768,1024]{1,2,0:T(8,128)(2,1)}) %all-reduce.2.cloned.1.call-update) | async-done | bytes 4718608 | tf_op jit(solution)/shard_map/psum | solution.py:11
  353.0 7.3 %fusion.1 = f32[3,1024,64]{2,1,0:T(8,128)} fusion(bf16[3,768,1024]{1,2,0:T(8,128)(2,1)} %all-reduce.2.cloned.1.call-done, f32[3,768,64]{1,2,0:T(8,128)S(1)} %multiply_negate_fusion), kind=kOutput, calls=%fused_computation.11 | convolution fusion | flops 1811939328 | bytes 6094848 | tf_op jit(solution)/shard_map/kin,kim->knm/dot_general | solution.py:31
  360.3 0.0 reduce-scatter.5.cloned.1.call-update
  360.4 73.5 %reduce-scatter.5.cloned.1.call-done = f32[3,64,64]{2,1,0:T(8,128)} async-done(((f32[3,1024,64]{2,1,0:T(8,128)}), f32[3,64,64]{2,1,0:T(8,128)}) %reduce-scatter.5.cloned.1.call-update) | async-done | bytes 49168 | tf_op jit(solution)/shard_map/reduce_scatter | solution.py:32
  433.9 0.0 copy-done.2
  433.9 1.5 sub.3
  435.4 0.0 copy-done.1
  (2 shorter events, 0.0 us)
Async XLA Ops:
  7.2 69.9 %copy-start = (bf16[768,768]{1,0:T(8,128)(2,1)S(1)}, bf16[768,768]{1,0:T(8,128)(2,1)}, u32[]{:S(2)}) copy-start(bf16[768,768]{1,0:T(8,128)(2,1)} %param.4) | copy-start | bytes 3538948
  7.2 69.9 %all-gather.2.cloned.1.call-start = ((), (), s32[]{:S(2)}) async-start(), calls=%async_computation.2 | async-start | bytes 5013504 | tf_op jit(solution)/shard_map/all_gather | solution.py:21
  9.9 187.0 %reduce-scatter.3.cloned.1.call-start = ((), (), s32[]{:S(2)}) async-start(), calls=%async_computation.3 | async-start | bytes 10027008 | tf_op jit(solution)/shard_map/reduce_scatter | solution.py:29
  85.9 267.2 %all-reduce.2.cloned.1.call-start = ((), (), s32[]{:S(2)}) async-start(), calls=%async_computation.4 | async-start | bytes 9437184 | tf_op jit(solution)/shard_map/psum | solution.py:11
  88.4 345.5 %reduce-scatter.5.cloned.1.call-start = ((), (), s32[]{:S(2)}) async-start(), calls=%async_computation.5 | async-start | bytes 1671168 | tf_op jit(solution)/shard_map/reduce_scatter | solution.py:32
  196.9 237.0 %copy-start.2 = (f32[3,64,64]{2,1,0:T(8,128)S(1)}, f32[3,64,64]{2,1,0:T(8,128)}, u32[]{:S(2)}) copy-start(f32[3,64,64]{2,1,0:T(8,128)} %param.7) | copy-start | bytes 147460
  198.0 237.4 %copy-start.1 = (f32[3,768,64]{1,2,0:T(8,128)}, f32[3,768,64]{1,2,0:T(8,128)S(1)}, u32[]{:S(2)}) copy-start(f32[3,768,64]{1,2,0:T(8,128)S(1)} %multiply_negate_fusion) | copy-start | bytes 1769476
Sparse Core Ops, SparseCore 0:
  11.4 65.6 all-gather.1
  86.0 110.8 reduce-scatter.2
  199.6 153.4 all-reduce.1
  360.5 73.3 reduce-scatter.4
where the time goes:
time: 442 us
  waiting for transfers between devices  404 us (91%)
  matrix products  16.1 us (4%)
  between operations  13.8 us (3%)
  other arithmetic  7.69 us (2%)
    psum x1, waiting for transfers between devices, spread_2(): return lax.psum(kept, axis)  155 us
    reduce_scatter x1, waiting for transfers between devices, selected_step(): lax.psum_scatter(partial_value, 'prow', scatter_dimension=2, tiled=True)  108 us
    reduce_scatter x1, waiting for transfers between devices, selected_step(): lax.psum_scatter(square, 'pcol', scatter_dimension=1, tiled=True)  73.5 us
    all_gather x1, waiting for transfers between devices, selected_step(): row_panel = lax.all_gather(masked, 'pcol', axis=2, tiled=True)  67.1 us
  transfers between devices with their start and end apart: 4, of which 4 were waited for; matrix products, arithmetic and copies ran while one was open for 1% of the time, Pallas kernels for 0%

commit v1 on v0

v1 whole, which is shorter than its diff:
```python
import jax
import jax.numpy as jnp
import numpy as np
from jax import lax
from jax.sharding import Mesh, PartitionSpec as P

BLK = 128
AXES = ("yl", "z", "x", "yh", "core")
DIMS = (2, 8, 4, 2, 2)
GROUPS = ((0, 1, 2),)
NT = (((1,), (1,)), ((), ()))


def pairs(move):
    grid = np.arange(256).reshape(DIMS)
    return [(int(grid[at]), int(grid[move(*at)])) for at in np.ndindex(*DIMS)]


def send(value, move):
    return lax.ppermute(value, AXES, pairs(move))


def swap(yl, z, x, yh, c):
    return x // 2, z, yl * 2 + x % 2, yh, c


def swap_far(yl, z, x, yh, c):
    return x // 2, z, yl * 2 + x % 2, 1 - yh, c


def along_x(step):
    return lambda yl, z, x, yh, c: (yl, z, (x + step) % 4, yh, c)


def sibling(yl, z, x, yh, c):
    return yl, z, x, yh, 1 - c


def across(yl, z, x, yh, c):
    return 1 - yl, z, x, yh, c


def turned(yl, z, x, yh, c):
    row, col = yl * 8 + z, x * 4 + yh * 2 + c
    return col // 8, col % 8, row // 4, row // 2 % 2, row % 2


def homeward(yl, z, x, yh, c):
    slot = x * 4 + yh * 2 + c
    tile, other = slot // 2, slot % 2
    col = yl * 8 + tile
    return (yl + other) % 2, z, col // 4, col // 2 % 2, col % 2


def row_mask(pattern, block, per):
    picked = lax.dynamic_slice_in_dim(pattern, block * per, per, 1)
    return jnp.repeat(picked, BLK, axis=1)


def dot_nt(a, b):
    return lax.dot_general(a, b, NT, preferred_element_type=jnp.float32)


def ordered(first, near, far):
    return jnp.where(first, near, far), jnp.where(first, far, near)


def gather_panel(own):
    yl, x, yh, core = (lax.axis_index(name) for name in ("yl", "x", "yh", "core"))
    near, far = send(own, swap), send(own, swap_far)
    plane = jnp.stack(ordered(yh == 0, near, far))
    left, right, opposite = (send(plane, along_x(step)) for step in (1, 3, 2))
    own_rows = (x // 2) == yl
    here = ordered(own_rows, plane, opposite)
    back = (x + 3) % 4
    there = ordered((back // 2) == yl, left, right)
    halves = []
    for half in range(2):
        low, high = ordered(x % 2 == 0, here[half], there[half])
        halves.append(jnp.stack([low, high]))
    mine = jnp.stack(halves)
    theirs = send(mine, sibling)
    even, odd = ordered(core == 0, mine, theirs)
    return jnp.stack([even, odd], axis=3)


def shards(ancestor_inverse, factor_panel, pattern, diagonal_inverse):
    yl, z, x, yh, core = (lax.axis_index(name) for name in AXES)
    count, rows, cols = factor_panel.shape
    row, col = yl * 8 + z, x * 4 + yh * 2 + core
    per = rows // BLK
    keep_rows = row_mask(pattern, row, per).astype(jnp.bfloat16)
    keep_cols = row_mask(pattern, col, per).astype(jnp.float32)
    own = factor_panel.transpose(0, 2, 1) * keep_rows[:, None, :]
    beside = send(ancestor_inverse, across)
    facing = lax.all_gather(send(own, turned), "z", axis=0)
    offdiag, diagonal = [], []
    for group in GROUPS:
        size = len(group)
        span = slice(group[0], group[-1] + 1)
        panel = gather_panel(own[span]).reshape(2, 8 * size * cols, rows)
        partial = dot_nt(panel[0], ancestor_inverse) + dot_nt(panel[1], beside)
        reduced = lax.psum_scatter(partial, "z", scatter_dimension=0, tiled=True)
        reduced = reduced.reshape(size, cols, rows)
        offdiag.append(-(reduced * keep_cols[span, None, :]))
        both = jnp.stack([reduced, send(reduced, across)])
        high = lax.reduce_precision(both, 8, 7)
        tiles = 0
        for part in (high, both - high):
            tiles += jnp.einsum(
                "tknr,okmr->toknm",
                facing[:, span],
                part.astype(jnp.bfloat16),
                preferred_element_type=jnp.float32,
            )
        flat = tiles.reshape(16, size * cols * cols // 128, 128)
        summed = lax.all_to_all(flat, ("x", "yh", "core"), 0, 0, tiled=True).sum(0)
        diagonal.append(send(summed, homeward).reshape(size, cols, cols))
    offdiag = jnp.concatenate(offdiag).transpose(0, 2, 1)
    return offdiag, diagonal_inverse + jnp.concatenate(diagonal)


def solution(mesh):
    fine = Mesh(mesh.devices.reshape(DIMS), AXES)
    prow, pcol = ("yl", "z"), ("x", "yh", "core")
    in_specs = (P(pcol, prow), P(None, prow, pcol), P(), P(None, pcol, prow))
    out_specs = (P(None, pcol, prow), P(None, pcol, prow))
    return jax.shard_map(shards, mesh=fine, in_specs=in_specs, out_specs=out_specs, check_vma=False)
```

time: 442 us -> 254 us (0.57)
  waiting for transfers between devices: 404 us -> 181 us
  starting transfers between devices: 0.16 us -> 31.8 us
    psum x1 -> x0, waiting for transfers between devices: 155 us -> none  [spread_2(): return lax.psum(kept, axis)]
    reduce_scatter x2 -> x1, waiting for transfers between devices: 182 us -> 51.5 us  [shards(): reduced = lax.psum_scatter(partial, 'z', scatter_dimension=0, tiled=True)]
    ppermute x0 -> x10, waiting for transfers between devices: none -> 71.6 us  [send(): return lax.ppermute(value, AXES, pairs(move))]
    ppermute x0 -> x10, starting transfers between devices: none -> 24.4 us  [send(): return lax.ppermute(value, AXES, pairs(move))]
    all_gather x1, waiting for transfers between devices: 67.1 us -> 45.2 us  [shards(): facing = lax.all_gather(send(own, turned), 'z', axis=0)]
    all_to_all x0 -> x1, waiting for transfers between devices: none -> 12.9 us  [shards(): summed = lax.all_to_all(flat, ('x', 'yh', 'core'), 0, 0, tiled=True).sum(0)]
    all_to_all x0 -> x1, starting transfers between devices: none -> 7.36 us  [shards(): summed = lax.all_to_all(flat, ('x', 'yh', 'core'), 0, 0, tiled=True).sum(0)]
    another operation x0 -> x7, other arithmetic: none -> 4.58 us  [the longest x2 2.43 us: gather_panel(): return jnp.stack([even, odd], axis=3)]
  transfers between devices with their start and end apart: 4 -> 13, of which waited for: 4 -> 12; matrix products, arithmetic and copies ran while one was open for 1% -> 3% of each run, Pallas kernels for 0% -> 0%
where the time goes in v1:
time: 254 us; the launch traced here: 251 us
  waiting for transfers between devices  181 us (71%)
  starting transfers between devices  31.8 us (13%)
  between operations  14.2 us (6%)
  matrix products  13.4 us (5%)
  other arithmetic  7.97 us (3%)
  local copies, waits for them, and re-layouts  2.59 us (1%)
    ppermute x10, waiting for transfers between devices, send(): return lax.ppermute(value, AXES, pairs(move))  71.6 us
    reduce_scatter x1, waiting for transfers between devices, shards(): reduced = lax.psum_scatter(partial, 'z', scatter_dimension=0, tiled=True)  51.5 us
    all_gather x1, waiting for transfers between devices, shards(): facing = lax.all_gather(send(own, turned), 'z', axis=0)  45.2 us
    ppermute x10, starting transfers between devices, send(): return lax.ppermute(value, AXES, pairs(move))  24.4 us
    all_to_all x1, waiting for transfers between devices, shards(): summed = lax.all_to_all(flat, ('x', 'yh', 'core'), 0, 0, tiled=True).sum(0)  12.9 us
    dot_general x2, matrix products, dot_nt(): return lax.dot_general(a, b, NT, preferred_element_type=jnp.float32)  8.75 us
    all_to_all x1, starting transfers between devices, shards(): summed = lax.all_to_all(flat, ('x', 'yh', 'core'), 0, 0, tiled=True).sum(0)  7.36 us
  transfers between devices with their start and end apart: 13, of which 12 were waited for; matrix products, arithmetic and copies ran while one was open for 3% of the time, Pallas kernels for 0%

profile of v1, /device:TPU:6, one launch (start us, length us, event | category | flops | bytes accessed | tf_op | source)
XLA Modules:
  0.0 251.1 jit_solution(17405887968467050695)
XLA Ops:
  7.2 0.8 dynamic-slice_convert_fusion
  8.1 1.0 multiply_bitcast_fusion
  9.1 4.3 %collective-permute-start = (bf16[3,64,768]{2,1,0:T(8,128)(2,1)S(1)}, bf16[3,64,768]{2,1,0:T(8,128)(2,1)S(1)}, u32[]{:S(2)}, u32[]{:S(2)}) collective-permute-start(bf16[3,64,768]{2,1,0:T(8,128)(2,1)S(1)} %multiply_bitcast_fusion), channel_id=1, source_target_pairs={{0,0},{1,1},{2,2},{3,3},{4,4},{5,5},{6,6},{7,7},{8,128},{9,129},{1... | collective-permute-start | bytes 884744 | tf_op jit(solution)/shard_map/ppermute | solution.py:20
  13.5 3.8 %collective-permute-start.1 = (bf16[3,64,768]{2,1,0:T(8,128)(2,1)S(1)}, bf16[3,64,768]{2,1,0:T(8,128)(2,1)S(1)}, u32[]{:S(2)}, u32[]{:S(2)}) collective-permute-start(bf16[3,64,768]{2,1,0:T(8,128)(2,1)S(1)} %multiply_bitcast_fusion), channel_id=1, source_target_pairs={{0,2},{1,3},{2,0},{3,1},{4,6},{5,7},{6,4},{7,5},{8,130},{9,131},{1... | collective-permute-start | bytes 884744 | tf_op jit(solution)/shard_map/ppermute | solution.py:20
  17.3 6.1 %collective-permute-done = bf16[3,64,768]{2,1,0:T(8,128)(2,1)S(1)} collective-permute-done((bf16[3,64,768]{2,1,0:T(8,128)(2,1)S(1)}, bf16[3,64,768]{2,1,0:T(8,128)(2,1)S(1)}, u32[]{:S(2)}, u32[]{:S(2)}) %collective-permute-start) | collective-permute-done | bytes 294944 | tf_op jit(solution)/shard_map/ppermute | solution.py:20
  23.4 6.9 %collective-permute-done.1 = bf16[3,64,768]{2,1,0:T(8,128)(2,1)S(1)} collective-permute-done((bf16[3,64,768]{2,1,0:T(8,128)(2,1)S(1)}, bf16[3,64,768]{2,1,0:T(8,128)(2,1)S(1)}, u32[]{:S(2)}, u32[]{:S(2)}) %collective-permute-start.1) | collective-permute-done | bytes 294944 | tf_op jit(solution)/shard_map/ppermute | solution.py:20
  30.5 3.5 %collective-permute-start.3 = (bf16[2,3,64,768]{3,2,1,0:T(8,128)(2,1)S(1)}, bf16[2,3,64,768]{3,2,1,0:T(8,128)(2,1)S(1)}, u32[]{:S(2)}, u32[]{:S(2)}) collective-permute-start(bf16[2,3,64,768]{3,2,1,0:T(8,128)(2,1)S(1)} %pad_maximum_fusion.3), channel_id=1, source_target_pairs={{0,4},{1,5},{2,6},{3,7},{4,8},{5,9},{6,10},{7,11},{8,12},{9,13},{1... | collective-permute-start | bytes 1769480 | tf_op jit(solution)/shard_map/ppermute | solution.py:20
  34.0 14.3 %collective-permute-done.2 = bf16[2,3,64,768]{3,2,1,0:T(8,128)(2,1)S(1)} collective-permute-done((bf16[2,3,64,768]{3,2,1,0:T(8,128)(2,1)S(1)}, bf16[2,3,64,768]{3,2,1,0:T(8,128)(2,1)S(1)}, u32[]{:S(2)}, u32[]{:S(2)}) %collective-permute-start.2) | collective-permute-done | bytes 589856 | tf_op jit(solution)/shard_map/ppermute | solution.py:20
  48.3 8.1 %collective-permute-done.3 = bf16[2,3,64,768]{3,2,1,0:T(8,128)(2,1)S(1)} collective-permute-done((bf16[2,3,64,768]{3,2,1,0:T(8,128)(2,1)S(1)}, bf16[2,3,64,768]{3,2,1,0:T(8,128)(2,1)S(1)}, u32[]{:S(2)}, u32[]{:S(2)}) %collective-permute-start.3) | collective-permute-done | bytes 589856 | tf_op jit(solution)/shard_map/ppermute | solution.py:20
  56.4 2.4 collective-permute-done.4
  59.2 1.6 pad_maximum_fusion.1
  60.8 4.9 %collective-permute-done.5 = bf16[2,2,2,3,64,768]{5,4,3,2,1,0:T(8,128)(2,1)} collective-permute-done((bf16[2,2,2,3,64,768]{5,4,3,2,1,0:T(8,128)(2,1)}, bf16[2,2,2,3,64,768]{5,4,3,2,1,0:T(8,128)(2,1)}, u32[]{:S(2)}, u32[]{:S(2)}) %collective-permute-start.5) | collective-permute-done | bytes 2359328 | tf_op jit(solution)/shard_map/ppermute | solution.py:20
  65.7 2.0 select_bitcast_fusion
  67.7 0.5 pad_maximum_fusion
  68.1 3.3 %fusion.14 = f32[1536,768]{1,0:T(8,128)S(1)} fusion(bf16[1536,768]{1,0:T(8,128)(2,1)S(1)} %bitcast.72, bf16[768,768]{1,0:T(8,128)(2,1)} %param.4), kind=kOutput, calls=%fused_computation.42 | convolution fusion | flops 1811939328 | bytes 8257536 | tf_op jit(solution)/shard_map/dot_general | solution.py:61
  71.5 18.1 %collective-permute-done.6 = bf16[768,768]{1,0:T(8,128)(2,1)} collective-permute-done((bf16[768,768]{1,0:T(8,128)(2,1)}, bf16[768,768]{1,0:T(8,128)(2,1)}, u32[]{:S(2)}, u32[]{:S(2)}) %collective-permute-start.6) | collective-permute-done | bytes 1179680 | tf_op jit(solution)/shard_map/ppermute | solution.py:20
  89.5 5.4 %convolution_add_fusion = f32[1536,768]{1,0:T(8,128)} fusion(f32[1536,768]{1,0:T(8,128)S(1)} %fusion.14, bf16[1536,768]{1,0:T(8,128)(2,1)S(1)} %bitcast.71, bf16[768,768]{1,0:T(8,128)(2,1)} %collective-permute-done.6), kind=kOutput, calls=%fused_computation.2 | convolution fusion | flops 1813118976 | bytes 12976128 | tf_op jit(solution)/shard_map/dot_general | solution.py:61
  95.0 9.1 %collective-permute-start.8 = (bf16[3,64,768]{2,1,0:T(8,128)(2,1)S(1)}, bf16[3,64,768]{2,1,0:T(8,128)(2,1)S(1)}, u32[]{:S(2)}, u32[]{:S(2)}) collective-permute-start(bf16[3,64,768]{2,1,0:T(8,128)(2,1)S(1)} %multiply_bitcast_fusion), channel_id=1, source_target_pairs={{0,0},{1,16},{2,32},{3,48},{4,64},{5,80},{6,96},{7,112},{8,128},{9... | collective-permute-start | bytes 884744 | tf_op jit(solution)/shard_map/ppermute | solution.py:20
  104.2 8.6 %collective-permute-done.8 = bf16[3,64,768]{2,1,0:T(8,128)(2,1)S(1)} collective-permute-done((bf16[3,64,768]{2,1,0:T(8,128)(2,1)S(1)}, bf16[3,64,768]{2,1,0:T(8,128)(2,1)S(1)}, u32[]{:S(2)}, u32[]{:S(2)}) %collective-permute-start.8) | collective-permute-done | bytes 294944 | tf_op jit(solution)/shard_map/ppermute | solution.py:20
  112.8 0.7 copy-done.3
  113.6 51.5 %reduce-scatter.2.cloned.1.call-done = f32[192,768]{1,0:T(8,128)} async-done(((f32[1536,768]{1,0:T(8,128)}), f32[192,768]{1,0:T(8,128)}) %reduce-scatter.2.cloned.1.call-update) | async-done | bytes 589840 | tf_op jit(solution)/shard_map/reduce_scatter | solution.py:103
  165.1 45.2 %all-gather.3.cloned.1.call-done = bf16[24,64,768]{2,1,0:T(8,128)(2,1)} async-done(((bf16[3,64,768]{2,1,0:T(8,128)(2,1)}), bf16[24,64,768]{2,1,0:T(8,128)(2,1)}) %all-gather.3.cloned.1.call-update) | async-done | bytes 2359312 | tf_op jit(solution)/shard_map/all_gather | solution.py:96
  210.3 3.3 %fusion.1 = f32[3,2,64,8,64]{4,2,3,1,0:T(8,128)S(1)} fusion(bf16[8,3,64,768,1]{3,2,1,0,4:T(8,128)(2,1)} %bitcast.69, f32[1,3,64,768]{3,2,0,1:T(8,128)S(1)} %bitcast.73, f32[1,3,64,768]{3,2,0,1:T(8,128)} %bitcast.66), kind=kOutput, calls=%fused_computation.8 | convolution fusion | flops 303169536 | bytes 4325376 | tf_op jit(solution)/shard_map/tknr,okmr->toknm/dot_general | solution.py:110
  213.7 1.3 add_bitcast_fusion
  215.0 0.5 copy.16
  215.5 1.2 reshape.33
  216.6 7.4 %all-to-all-start = ((f32[16,96,128]{2,1,0:T(8,128)}), f32[16,96,128]{2,1,0:T(8,128)S(1)}, u32[]{:S(2)}, u32[]{:S(2)}) async-start(f32[16,96,128]{2,1,0:T(8,128)} %reshape.33), calls=%async_computation.1 | async-start | bytes 1572864 | tf_op jit(solution)/shard_map/all_to_all | solution.py:117
  224.1 12.9 %all-to-all-done = f32[16,96,128]{2,1,0:T(8,128)S(1)} async-done(((f32[16,96,128]{2,1,0:T(8,128)}), f32[16,96,128]{2,1,0:T(8,128)S(1)}, u32[]{:S(2)}, u32[]{:S(2)}) %all-to-all-start) | async-done | bytes 786464 | tf_op jit(solution)/shard_map/all_to_all | solution.py:117
  237.0 3.5 %collective-permute-start.9 = (f32[96,128]{1,0:T(8,128)S(1)}, f32[96,128]{1,0:T(8,128)S(1)}, u32[]{:S(2)}, u32[]{:S(2)}) collective-permute-start(f32[96,128]{1,0:T(8,128)S(1)} %reduce_sum.9), channel_id=1, source_target_pairs={{0,0},{1,128},{2,1},{3,129},{4,2},{5,130},{6,3},{7,131},{8,4},{9,1... | collective-permute-start | bytes 147464 | tf_op jit(solution)/shard_map/ppermute | solution.py:20
  240.4 0.9 negate_bitcast_fusion
  241.3 2.2 collective-permute-done.9
  243.6 0.7 add.53
  (29 shorter events, 1.0 us)
Async XLA Ops:
  7.2 157.9 %reduce-scatter.2.cloned.1.call-start = ((), (), s32[]{:S(2)}) async-start(), calls=%async_computation.2 | async-start | bytes 5308416 | tf_op jit(solution)/shard_map/reduce_scatter | solution.py:103
  9.1 14.2 %collective-permute-start = (bf16[3,64,768]{2,1,0:T(8,128)(2,1)S(1)}, bf16[3,64,768]{2,1,0:T(8,128)(2,1)S(1)}, u32[]{:S(2)}, u32[]{:S(2)}) collective-permute-start(bf16[3,64,768]{2,1,0:T(8,128)(2,1)S(1)} %multiply_bitcast_fusion), channel_id=1, source_target_pairs={{0,0},{1,1},{2,2},{3,3},{4,4},{5,5},{6,6},{7,7},{8,128},{9,129},{1... | collective-permute-start | bytes 884744 | tf_op jit(solution)/shard_map/ppermute | solution.py:20
  13.5 16.8 %collective-permute-start.1 = (bf16[3,64,768]{2,1,0:T(8,128)(2,1)S(1)}, bf16[3,64,768]{2,1,0:T(8,128)(2,1)S(1)}, u32[]{:S(2)}, u32[]{:S(2)}) collective-permute-start(bf16[3,64,768]{2,1,0:T(8,128)(2,1)S(1)} %multiply_bitcast_fusion), channel_id=1, source_target_pairs={{0,2},{1,3},{2,0},{3,1},{4,6},{5,7},{6,4},{7,5},{8,130},{9,131},{1... | collective-permute-start | bytes 884744 | tf_op jit(solution)/shard_map/ppermute | solution.py:20
  30.4 17.9 %collective-permute-start.2 = (bf16[2,3,64,768]{3,2,1,0:T(8,128)(2,1)S(1)}, bf16[2,3,64,768]{3,2,1,0:T(8,128)(2,1)S(1)}, u32[]{:S(2)}, u32[]{:S(2)}) collective-permute-start(bf16[2,3,64,768]{3,2,1,0:T(8,128)(2,1)S(1)} %pad_maximum_fusion.3), channel_id=1, source_target_pairs={{0,8},{1,9},{2,10},{3,11},{4,12},{5,13},{6,14},{7,15},{8,0},{9,1},... | collective-permute-start | bytes 1769480 | tf_op jit(solution)/shard_map/ppermute | solution.py:20
  30.5 25.9 %collective-permute-start.3 = (bf16[2,3,64,768]{3,2,1,0:T(8,128)(2,1)S(1)}, bf16[2,3,64,768]{3,2,1,0:T(8,128)(2,1)S(1)}, u32[]{:S(2)}, u32[]{:S(2)}) collective-permute-start(bf16[2,3,64,768]{3,2,1,0:T(8,128)(2,1)S(1)} %pad_maximum_fusion.3), channel_id=1, source_target_pairs={{0,4},{1,5},{2,6},{3,7},{4,8},{5,9},{6,10},{7,11},{8,12},{9,13},{1... | collective-permute-start | bytes 1769480 | tf_op jit(solution)/shard_map/ppermute | solution.py:20
  34.0 24.8 %collective-permute-start.4 = (bf16[2,3,64,768]{3,2,1,0:T(8,128)(2,1)S(1)}, bf16[2,3,64,768]{3,2,1,0:T(8,128)(2,1)S(1)}, u32[]{:S(2)}, u32[]{:S(2)}) collective-permute-start(bf16[2,3,64,768]{3,2,1,0:T(8,128)(2,1)S(1)} %pad_maximum_fusion.3), channel_id=1, source_target_pairs={{0,12},{1,13},{2,14},{3,15},{4,0},{5,1},{6,2},{7,3},{8,4},{9,5},{1... | collective-permute-start | bytes 1769480 | tf_op jit(solution)/shard_map/ppermute | solution.py:20
  60.8 4.9 %collective-permute-start.5 = (bf16[2,2,2,3,64,768]{5,4,3,2,1,0:T(8,128)(2,1)}, bf16[2,2,2,3,64,768]{5,4,3,2,1,0:T(8,128)(2,1)}, u32[]{:S(2)}, u32[]{:S(2)}) collective-permute-start(bf16[2,2,2,3,64,768]{5,4,3,2,1,0:T(8,128)(2,1)} %pad_maximum_fusion.1), channel_id=1, source_target_pairs={{0,1},{1,0},{2,3},{3,2},{4,5},{5,4},{6,7},{7,6},{8,9},{9,8},{10,11... | collective-permute-start | bytes 7077896 | tf_op jit(solution)/shard_map/ppermute | solution.py:20
  60.8 28.7 %collective-permute-start.6 = (bf16[768,768]{1,0:T(8,128)(2,1)}, bf16[768,768]{1,0:T(8,128)(2,1)}, u32[]{:S(2)}, u32[]{:S(2)}) collective-permute-start(bf16[768,768]{1,0:T(8,128)(2,1)} %param.4), channel_id=1, source_target_pairs={{0,128},{1,129},{2,130},{3,131},{4,132},{5,133},{6,134},{7,135},{8... | collective-permute-start | bytes 3538952 | tf_op jit(solution)/shard_map/ppermute | solution.py:20
  95.0 115.3 %all-gather.3.cloned.1.call-start = ((), (), s32[]{:S(2)}) async-start(), calls=%async_computation.3 | async-start | bytes 2654208 | tf_op jit(solution)/shard_map/all_gather | solution.py:96
  95.0 17.8 %collective-permute-start.8 = (bf16[3,64,768]{2,1,0:T(8,128)(2,1)S(1)}, bf16[3,64,768]{2,1,0:T(8,128)(2,1)S(1)}, u32[]{:S(2)}, u32[]{:S(2)}) collective-permute-start(bf16[3,64,768]{2,1,0:T(8,128)(2,1)S(1)} %multiply_bitcast_fusion), channel_id=1, source_target_pairs={{0,0},{1,16},{2,32},{3,48},{4,64},{5,80},{6,96},{7,112},{8,128},{9... | collective-permute-start | bytes 884744 | tf_op jit(solution)/shard_map/ppermute | solution.py:20
  112.8 0.7 copy-start.3
  165.1 45.2 %collective-permute-start.7 = (f32[3,64,768]{2,1,0:T(8,128)}, f32[3,64,768]{2,1,0:T(8,128)S(1)}, u32[]{:S(2)}, u32[]{:S(2)}) collective-permute-start(f32[3,64,768]{2,1,0:T(8,128)} %bitcast.65), channel_id=1, source_target_pairs={{0,128},{1,129},{2,130},{3,131},{4,132},{5,133},{6,134},{7,135},{8... | collective-permute-start | bytes 1769480 | tf_op jit(solution)/shard_map/ppermute | solution.py:20
  210.3 3.3 %copy-start = (f32[192,768]{1,0:T(8,128)S(1)}, f32[192,768]{1,0:T(8,128)}, u32[]{:S(2)}) copy-start(f32[192,768]{1,0:T(8,128)} %reduce-scatter.2.cloned.1.call-done) | copy-start | bytes 1769476
  210.3 3.3 %copy-start.2 = (bf16[24,64,768]{2,1,0:T(8,128)(2,1)S(1)}, bf16[24,64,768]{2,1,0:T(8,128)(2,1)}, u32[]{:S(2)}) copy-start(bf16[24,64,768]{2,1,0:T(8,128)(2,1)} %all-gather.3.cloned.1.call-done) | copy-start | bytes 7077892
  215.4 25.0 %copy-start.1 = (f32[192,768]{1,0:T(8,128)S(1)}, f32[192,768]{1,0:T(8,128)}, u32[]{:S(2)}) copy-start(f32[192,768]{1,0:T(8,128)} %reduce-scatter.2.cloned.1.call-done) | copy-start | bytes 1769476
  216.6 27.0 %copy-start.4 = (f32[3,64,64]{2,1,0:T(8,128)S(1)}, f32[3,64,64]{2,1,0:T(8,128)}, u32[]{:S(2)}) copy-start(f32[3,64,64]{2,1,0:T(8,128)} %param.7) | copy-start | bytes 147460
  216.6 20.3 %all-to-all-start = ((f32[16,96,128]{2,1,0:T(8,128)}), f32[16,96,128]{2,1,0:T(8,128)S(1)}, u32[]{:S(2)}, u32[]{:S(2)}) async-start(f32[16,96,128]{2,1,0:T(8,128)} %reshape.33), calls=%async_computation.1 | async-start | bytes 1572864 | tf_op jit(solution)/shard_map/all_to_all | solution.py:117
  237.0 6.6 %collective-permute-start.9 = (f32[96,128]{1,0:T(8,128)S(1)}, f32[96,128]{1,0:T(8,128)S(1)}, u32[]{:S(2)}, u32[]{:S(2)}) collective-permute-start(f32[96,128]{1,0:T(8,128)S(1)} %reduce_sum.9), channel_id=1, source_target_pairs={{0,0},{1,128},{2,1},{3,129},{4,2},{5,130},{6,3},{7,131},{8,4},{9,1... | collective-permute-start | bytes 147464 | tf_op jit(solution)/shard_map/ppermute | solution.py:20
Sparse Core Ops, SparseCore 0:
  95.1 69.9 reduce-scatter.1
  167.5 42.7 all-gather.2

commit v2 on v1

v2 whole, which is shorter than its diff:
```python
import jax
import jax.numpy as jnp
import numpy as np
from jax import lax
from jax.sharding import Mesh, PartitionSpec as P

BLK = 128
AXES = ("yl", "z", "x", "yh", "core")
DIMS = (2, 8, 4, 2, 2)
NT = (((1,), (1,)), ((), ()))


def pairs(move):
    grid = np.arange(256).reshape(DIMS)
    return [(int(grid[at]), int(grid[move(*at)])) for at in np.ndindex(*DIMS)]


def send(value, move):
    return lax.ppermute(value, AXES, pairs(move))


def swap(yl, z, x, yh, c):
    return x // 2, z, yl * 2 + x % 2, yh, c


def swap_far(yl, z, x, yh, c):
    return x // 2, z, yl * 2 + x % 2, 1 - yh, c


def along_x(step):
    return lambda yl, z, x, yh, c: (yl, z, (x + step) % 4, yh, c)


def sibling(yl, z, x, yh, c):
    return yl, z, x, yh, 1 - c


def across(yl, z, x, yh, c):
    return 1 - yl, z, x, yh, c


def turned(yl, z, x, yh, c):
    row, col = yl * 8 + z, x * 4 + yh * 2 + c
    return col // 8, col % 8, row // 4, row // 2 % 2, row % 2


def turned_across(yl, z, x, yh, c):
    return across(*turned(yl, z, x, yh, c))


def row_mask(pattern, block, per):
    picked = lax.dynamic_slice_in_dim(pattern, block * per, per, 1)
    return jnp.repeat(picked, BLK, axis=1)


def dot_nt(a, b):
    return lax.dot_general(a, b, NT, preferred_element_type=jnp.float32)


def ordered(first, near, far):
    return jnp.where(first, near, far), jnp.where(first, far, near)


def after(value, *others):
    return lax.optimization_barrier((value, *others))[0]


def spread_rows(place, near, far, partly=None):
    yl, x, yh = place
    if partly is not None:
        near, far = after(near, partly), after(far, partly)
    plane = jnp.stack(ordered(yh == 0, near, far))
    left, right, opposite = (send(plane, along_x(step)) for step in (1, 3, 2))
    here = ordered((x // 2) == yl, plane, opposite)
    there = ordered(((x + 3) % 4 // 2) == yl, left, right)
    halves = [jnp.stack(ordered(x % 2 == 0, here[half], there[half])) for half in range(2)]
    return jnp.stack(halves)


def spread_cores(core, mine):
    theirs = send(mine, sibling)
    return jnp.stack(ordered(core == 0, mine, theirs), axis=3)


def shards(ancestor_inverse, factor_panel, pattern, diagonal_inverse):
    yl, z, x, yh, core = (lax.axis_index(name) for name in AXES)
    count, rows, cols = factor_panel.shape
    row, col = yl * 8 + z, x * 4 + yh * 2 + core
    per = rows // BLK
    keep_rows = row_mask(pattern, row, per).astype(jnp.bfloat16)
    keep_cols = row_mask(pattern, col, per).astype(jnp.float32)
    own = factor_panel.transpose(0, 2, 1) * keep_rows[:, None, :]
    cut = rows // 3
    top = send(ancestor_inverse[:cut], across)
    bottom = send(ancestor_inverse[cut:], across)
    offdiag, tiles = [], []
    beside = None
    for k in range(count):
        near, far = send(own[k], swap), send(own[k], swap_far)
        mine = spread_rows((yl, x, yh), near, far, top if k == 0 else None)
        if k == 0:
            mine = after(mine, bottom)
            beside = jnp.concatenate([top, bottom])
        panel = spread_cores(core, mine).reshape(2, 8 * cols, rows)
        partial = dot_nt(panel[0], ancestor_inverse) + dot_nt(panel[1], beside)
        reduced = lax.psum_scatter(partial, "z", scatter_dimension=0, tiled=True)
        offdiag.append(-(reduced * keep_cols[k, None, :]))
        high = lax.reduce_precision(reduced, 8, 7)
        parts = jnp.concatenate([high, reduced - high]).astype(jnp.bfloat16)
        square = dot_nt(panel[0], send(parts, turned)) + dot_nt(panel[1], send(parts, turned_across))
        square = square.reshape(8, 2, cols // 2, 2 * cols)
        square = square[..., :cols] + square[..., cols:]
        tiles.append(jnp.concatenate([square[:, 0], square[:, 1]], axis=-1))
    tiles = jnp.concatenate(tiles, axis=1)
    summed = lax.all_to_all(tiles, "z", 0, 0, tiled=True).sum(0)
    summed = send(summed, turned).reshape(count, cols // 2, 2 * cols)
    diagonal = jnp.concatenate([summed[..., :cols], summed[..., cols:]], axis=1)
    return jnp.stack(offdiag).transpose(0, 2, 1), diagonal_inverse + diagonal


def solution(mesh):
    fine = Mesh(mesh.devices.reshape(DIMS), AXES)
    prow, pcol = ("yl", "z"), ("x", "yh", "core")
    in_specs = (P(pcol, prow), P(None, prow, pcol), P(), P(None, pcol, prow))
    out_specs = (P(None, pcol, prow), P(None, pcol, prow))
    return jax.shard_map(shards, mesh=fine, in_specs=in_specs, out_specs=out_specs, check_vma=False)
```

time: 254 us -> 289 us (1.14)
  starting transfers between devices: 31.8 us -> 68.7 us
  waiting for transfers between devices: 181 us -> 145 us
  blocking collectives: 0 us -> 28.9 us
  local copies, waits for them, and re-layouts: 2.59 us -> 7.1 us
  other arithmetic: 7.97 us -> 12.3 us
    all_gather x1 -> x0, waiting for transfers between devices: 45.2 us -> none  [shards(): facing = lax.all_gather(send(own, turned), 'z', axis=0)]
    ppermute x10 -> x27, starting transfers between devices: 24.4 us -> 68.6 us  [send(): return lax.ppermute(value, AXES, pairs(move))]
    all_to_all x0 -> x1, blocking collectives: none -> 28.9 us  [shards(): summed = lax.all_to_all(tiles, 'z', 0, 0, tiled=True).sum(0)]
    reduce_scatter x1 -> x3, waiting for transfers between devices: 51.5 us -> 72 us  [shards(): reduced = lax.psum_scatter(partial, 'z', scatter_dimension=0, tiled=True)]
    all_to_all x1 -> x0, waiting for transfers between devices: 12.9 us -> none  [shards(): summed = lax.all_to_all(flat, ('x', 'yh', 'core'), 0, 0, tiled=True).sum(0)]
    all_to_all x1 -> x0, starting transfers between devices: 7.36 us -> none  [shards(): summed = lax.all_to_all(flat, ('x', 'yh', 'core'), 0, 0, tiled=True).sum(0)]
    dot_general x2 -> x0, matrix products: 4.62 us -> none  [shards(): jnp.einsum('tknr,okmr->toknm', facing[:, span], part.astype(jnp.bfloat16)...]
    unnamed x14 -> x27, local copies, waits for them, and re-layouts: 0.89 us -> 4.09 us
  transfers between devices with their start and end apart: 13 -> 30, of which waited for: 12 -> 20; matrix products, arithmetic and copies ran while one was open for 3% -> 7% of each run, Pallas kernels for 0% -> 0%
where the time goes in v2:
time: 289 us; the launch traced here: 288 us
  waiting for transfers between devices  145 us (50%)
  starting transfers between devices  68.7 us (24%)
  blocking collectives  28.9 us (10%)
  between operations  14.4 us (5%)
  other arithmetic  12.3 us (4%)
  matrix products  11.5 us (4%)
  local copies, waits for them, and re-layouts  7.1 us (2%)
    ppermute x27, waiting for transfers between devices, send(): return lax.ppermute(value, AXES, pairs(move))  73.3 us
    reduce_scatter x3, waiting for transfers between devices, shards(): reduced = lax.psum_scatter(partial, 'z', scatter_dimension=0, tiled=True)  72 us
    ppermute x27, starting transfers between devices, send(): return lax.ppermute(value, AXES, pairs(move))  68.6 us
    all_to_all x1, blocking collectives, shards(): summed = lax.all_to_all(tiles, 'z', 0, 0, tiled=True).sum(0)  28.9 us
    dot_general x12, matrix products, dot_nt(): return lax.dot_general(a, b, NT, preferred_element_type=jnp.float32)  11.5 us
  transfers between devices with their start and end apart: 30, of which 20 were waited for; matrix products, arithmetic and copies ran while one was open for 7% of the time, Pallas kernels for 0%

profile of v2, /device:TPU:6, one launch (start us, length us, event | category | flops | bytes accessed | tf_op | source)
XLA Modules:
  0.0 288.3 jit_solution(1090814847509279554)
XLA Ops:
  9.3 4.3 %collective-permute-start.14 = (bf16[64,768]{1,0:T(8,128)(2,1)S(1)}, bf16[64,768]{1,0:T(8,128)(2,1)S(1)}, u32[]{:S(2)}, u32[]{:S(2)}) collective-permute-start(bf16[64,768]{1,0:T(8,128)(2,1)S(1)} %get-tuple-element.33), channel_id=1, source_target_pairs={{0,0},{1,1},{2,2},{3,3},{4,4},{5,5},{6,6},{7,7},{8,128},{9,129},{1... | collective-permute-start | bytes 294920 | tf_op jit(solution)/shard_map/ppermute | solution.py:19
  13.6 3.8 %collective-permute-start.15 = (bf16[64,768]{1,0:T(8,128)(2,1)S(1)}, bf16[64,768]{1,0:T(8,128)(2,1)S(1)}, u32[]{:S(2)}, u32[]{:S(2)}) collective-permute-start(bf16[64,768]{1,0:T(8,128)(2,1)S(1)} %get-tuple-element.33), channel_id=1, source_target_pairs={{0,2},{1,3},{2,0},{3,1},{4,6},{5,7},{6,4},{7,5},{8,130},{9,131},{1... | collective-permute-start | bytes 294920 | tf_op jit(solution)/shard_map/ppermute | solution.py:19
  17.4 3.4 %collective-permute-start.8 = (bf16[64,768]{1,0:T(8,128)(2,1)S(1)}, bf16[64,768]{1,0:T(8,128)(2,1)S(1)}, u32[]{:S(2)}, u32[]{:S(2)}) collective-permute-start(bf16[64,768]{1,0:T(8,128)(2,1)S(1)} %get-tuple-element.34), channel_id=1, source_target_pairs={{0,0},{1,1},{2,2},{3,3},{4,4},{5,5},{6,6},{7,7},{8,128},{9,129},{1... | collective-permute-start | bytes 294920 | tf_op jit(solution)/shard_map/ppermute | solution.py:19
  22.7 4.1 %collective-permute-done.8 = bf16[64,768]{1,0:T(8,128)(2,1)S(1)} collective-permute-done((bf16[64,768]{1,0:T(8,128)(2,1)S(1)}, bf16[64,768]{1,0:T(8,128)(2,1)S(1)}, u32[]{:S(2)}, u32[]{:S(2)}) %collective-permute-start.8) | collective-permute-done | bytes 98336 | tf_op jit(solution)/shard_map/ppermute | solution.py:19
  26.8 2.4 collective-permute-done.9
  29.3 2.6 collective-permute-start.11
  34.6 3.1 %collective-permute-done.10 = bf16[2,64,768]{2,1,0:T(8,128)(2,1)S(1)} collective-permute-done((bf16[2,64,768]{2,1,0:T(8,128)(2,1)S(1)}, bf16[2,64,768]{2,1,0:T(8,128)(2,1)S(1)}, u32[]{:S(2)}, u32[]{:S(2)}) %collective-permute-start.10) | collective-permute-done | bytes 196640 | tf_op jit(solution)/shard_map/ppermute | solution.py:19
  41.0 17.4 %collective-permute-done.1 = bf16[256,768]{1,0:T(8,128)(2,1)} collective-permute-done((bf16[256,768]{1,0:T(8,128)(2,1)S(1)}, bf16[256,768]{1,0:T(8,128)(2,1)}, u32[]{:S(2)}, u32[]{:S(2)}) %collective-permute-start.1) | collective-permute-done | bytes 393248 | tf_op jit(solution)/shard_map/ppermute | solution.py:19
  65.1 2.8 collective-permute-start.16
  69.9 2.6 collective-permute-done.16
  72.5 2.3 collective-permute-done.17
  76.0 2.3 collective-permute-done.19
  83.0 3.2 %collective-permute-start = (bf16[64,768]{1,0:T(8,128)(2,1)S(1)}, bf16[64,768]{1,0:T(8,128)(2,1)S(1)}, u32[]{:S(2)}, u32[]{:S(2)}) collective-permute-start(bf16[64,768]{1,0:T(8,128)(2,1)S(1)} %get-tuple-element.32), channel_id=1, source_target_pairs={{0,0},{1,1},{2,2},{3,3},{4,4},{5,5},{6,6},{7,7},{8,128},{9,129},{1... | collective-permute-start | bytes 294920 | tf_op jit(solution)/shard_map/ppermute | solution.py:19
  86.2 3.6 %collective-permute-start.2 = (bf16[64,768]{1,0:T(8,128)(2,1)S(1)}, bf16[64,768]{1,0:T(8,128)(2,1)S(1)}, u32[]{:S(2)}, u32[]{:S(2)}) collective-permute-start(bf16[64,768]{1,0:T(8,128)(2,1)S(1)} %get-tuple-element.32), channel_id=1, source_target_pairs={{0,2},{1,3},{2,0},{3,1},{4,6},{5,7},{6,4},{7,5},{8,130},{9,131},{1... | collective-permute-start | bytes 294920 | tf_op jit(solution)/shard_map/ppermute | solution.py:19
  89.8 3.2 %collective-permute-done = bf16[64,768]{1,0:T(8,128)(2,1)S(1)} collective-permute-done((bf16[64,768]{1,0:T(8,128)(2,1)S(1)}, bf16[64,768]{1,0:T(8,128)(2,1)S(1)}, u32[]{:S(2)}, u32[]{:S(2)}) %collective-permute-start) | collective-permute-done | bytes 98336 | tf_op jit(solution)/shard_map/ppermute | solution.py:19
  94.8 3.8 %collective-permute-start.4 = (bf16[2,64,768]{2,1,0:T(8,128)(2,1)S(1)}, bf16[2,64,768]{2,1,0:T(8,128)(2,1)S(1)}, u32[]{:S(2)}, u32[]{:S(2)}) collective-permute-start(bf16[2,64,768]{2,1,0:T(8,128)(2,1)S(1)} %pad_maximum_fusion.6), channel_id=1, source_target_pairs={{0,4},{1,5},{2,6},{3,7},{4,8},{5,9},{6,10},{7,11},{8,12},{9,13},{1... | collective-permute-start | bytes 589832 | tf_op jit(solution)/shard_map/ppermute | solution.py:19
  98.6 5.5 %collective-permute-done.3 = bf16[2,64,768]{2,1,0:T(8,128)(2,1)S(1)} collective-permute-done((bf16[2,64,768]{2,1,0:T(8,128)(2,1)S(1)}, bf16[2,64,768]{2,1,0:T(8,128)(2,1)S(1)}, u32[]{:S(2)}, u32[]{:S(2)}) %collective-permute-start.3) | collective-permute-done | bytes 196640 | tf_op jit(solution)/shard_map/ppermute | solution.py:19
  104.1 2.5 collective-permute-done.5
  116.1 6.9 %collective-permute-start.23 = (bf16[128,768]{1,0:T(8,128)(2,1)}, bf16[128,768]{1,0:T(8,128)(2,1)S(1)}, u32[]{:S(2)}, u32[]{:S(2)}) collective-permute-start(bf16[128,768]{1,0:T(8,128)(2,1)} %pad_maximum_fusion.10), channel_id=1, source_target_pairs={{0,128},{1,144},{2,160},{3,176},{4,192},{5,208},{6,224},{7,240},{8... | collective-permute-start | bytes 589832 | tf_op jit(solution)/shard_map/ppermute | solution.py:19
  123.0 3.1 %collective-permute-start.22 = (bf16[128,768]{1,0:T(8,128)(2,1)}, bf16[128,768]{1,0:T(8,128)(2,1)}, u32[]{:S(2)}, u32[]{:S(2)}) collective-permute-start(bf16[128,768]{1,0:T(8,128)(2,1)} %pad_maximum_fusion.10), channel_id=1, source_target_pairs={{0,0},{1,16},{2,32},{3,48},{4,64},{5,80},{6,96},{7,112},{8,128},{9... | collective-permute-start | bytes 589832 | tf_op jit(solution)/shard_map/ppermute | solution.py:19
  126.1 40.4 %reduce-scatter.8.cloned.1.call-done = f32[64,768]{1,0:T(8,128)} async-done(((f32[512,768]{1,0:T(8,128)}), f32[64,768]{1,0:T(8,128)}) %reduce-scatter.8.cloned.1.call-update) | async-done | bytes 196624 | tf_op jit(solution)/shard_map/reduce_scatter | solution.py:106
  168.2 3.4 %collective-permute-start.25 = (bf16[128,768]{1,0:T(8,128)(2,1)S(1)}, bf16[128,768]{1,0:T(8,128)(2,1)S(1)}, u32[]{:S(2)}, u32[]{:S(2)}) collective-permute-start(bf16[128,768]{1,0:T(8,128)(2,1)S(1)} %pad_maximum_fusion.11), channel_id=1, source_target_pairs={{0,128},{1,144},{2,160},{3,176},{4,192},{5,208},{6,224},{7,240},{8... | collective-permute-start | bytes 589832 | tf_op jit(solution)/shard_map/ppermute | solution.py:19
  171.6 8.7 %collective-permute-start.24 = (bf16[128,768]{1,0:T(8,128)(2,1)S(1)}, bf16[128,768]{1,0:T(8,128)(2,1)S(1)}, u32[]{:S(2)}, u32[]{:S(2)}) collective-permute-start(bf16[128,768]{1,0:T(8,128)(2,1)S(1)} %pad_maximum_fusion.11), channel_id=1, source_target_pairs={{0,0},{1,16},{2,32},{3,48},{4,64},{5,80},{6,96},{7,112},{8,128},{9... | collective-permute-start | bytes 589832 | tf_op jit(solution)/shard_map/ppermute | solution.py:19
  182.6 3.7 %collective-permute-done.24 = bf16[128,768]{1,0:T(8,128)(2,1)S(1)} collective-permute-done((bf16[128,768]{1,0:T(8,128)(2,1)S(1)}, bf16[128,768]{1,0:T(8,128)(2,1)S(1)}, u32[]{:S(2)}, u32[]{:S(2)}) %collective-permute-start.24) | collective-permute-done | bytes 196640 | tf_op jit(solution)/shard_map/ppermute | solution.py:19
  186.8 31.6 %reduce-scatter.4.cloned.1.call-done = f32[64,768]{1,0:T(8,128)} async-done(((f32[512,768]{1,0:T(8,128)}), f32[64,768]{1,0:T(8,128)}) %reduce-scatter.4.cloned.1.call-update) | async-done | bytes 196624 | tf_op jit(solution)/shard_map/reduce_scatter | solution.py:106
  219.4 4.4 %collective-permute-start.21 = (bf16[128,768]{1,0:T(8,128)(2,1)S(1)}, bf16[128,768]{1,0:T(8,128)(2,1)S(1)}, u32[]{:S(2)}, u32[]{:S(2)}) collective-permute-start(bf16[128,768]{1,0:T(8,128)(2,1)S(1)} %pad_maximum_fusion.9), channel_id=1, source_target_pairs={{0,128},{1,144},{2,160},{3,176},{4,192},{5,208},{6,224},{7,240},{8... | collective-permute-start | bytes 589832 | tf_op jit(solution)/shard_map/ppermute | solution.py:19
  223.8 5.1 %collective-permute-start.20 = (bf16[128,768]{1,0:T(8,128)(2,1)S(1)}, bf16[128,768]{1,0:T(8,128)(2,1)S(1)}, u32[]{:S(2)}, u32[]{:S(2)}) collective-permute-start(bf16[128,768]{1,0:T(8,128)(2,1)S(1)} %pad_maximum_fusion.9), channel_id=1, source_target_pairs={{0,0},{1,16},{2,32},{3,48},{4,64},{5,80},{6,96},{7,112},{8,128},{9... | collective-permute-start | bytes 589832 | tf_op jit(solution)/shard_map/ppermute | solution.py:19
  228.9 2.2 collective-permute-done.21
  231.5 6.9 %collective-permute-done.20 = bf16[128,768]{1,0:T(8,128)(2,1)S(1)} collective-permute-done((bf16[128,768]{1,0:T(8,128)(2,1)S(1)}, bf16[128,768]{1,0:T(8,128)(2,1)S(1)}, u32[]{:S(2)}, u32[]{:S(2)}) %collective-permute-start.20) | collective-permute-done | bytes 196640 | tf_op jit(solution)/shard_map/ppermute | solution.py:19
  239.2 28.9 %all_to_all.5 = f32[8,96,128]{2,1,0:T(8,128)S(1)} all-to-all(f32[8,96,128]{2,1,0:T(8,128)S(1)} %maximum_maximum_fusion), channel_id=1, replica_groups=mesh['yl'=2,'z'=8,'x'=4,'yh'=2,'core'=2] {'z'}, dimensions={0} | all-to-all | bytes 786432 | tf_op jit(solution)/shard_map/all_to_all | solution.py:115
  268.1 3.5 %collective-permute-start.26 = (f32[96,128]{1,0:T(8,128)S(1)}, f32[96,128]{1,0:T(8,128)S(1)}, u32[]{:S(2)}, u32[]{:S(2)}) collective-permute-start(f32[96,128]{1,0:T(8,128)S(1)} %reduce_sum.9), channel_id=1, source_target_pairs={{0,0},{1,16},{2,32},{3,48},{4,64},{5,80},{6,96},{7,112},{8,128},{9... | collective-permute-start | bytes 147464 | tf_op jit(solution)/shard_map/ppermute | solution.py:19
  272.5 8.5 %collective-permute-done.26 = f32[96,128]{1,0:T(8,128)S(1)} collective-permute-done((f32[96,128]{1,0:T(8,128)S(1)}, f32[96,128]{1,0:T(8,128)S(1)}, u32[]{:S(2)}, u32[]{:S(2)}) %collective-permute-start.26) | collective-permute-done | bytes 49184 | tf_op jit(solution)/shard_map/ppermute | solution.py:19
  (126 shorter events, 44.0 us)
Async XLA Ops:
  7.2 106.6 %reduce-scatter.6.cloned.1.call-start = ((), (), s32[]{:S(2)}) async-start(), calls=%async_computation.5 | async-start | bytes 1769472 | tf_op jit(solution)/shard_map/reduce_scatter | solution.py:106
  9.3 13.5 %collective-permute-start.14 = (bf16[64,768]{1,0:T(8,128)(2,1)S(1)}, bf16[64,768]{1,0:T(8,128)(2,1)S(1)}, u32[]{:S(2)}, u32[]{:S(2)}) collective-permute-start(bf16[64,768]{1,0:T(8,128)(2,1)S(1)} %get-tuple-element.33), channel_id=1, source_target_pairs={{0,0},{1,1},{2,2},{3,3},{4,4},{5,5},{6,6},{7,7},{8,128},{9,129},{1... | collective-permute-start | bytes 294920 | tf_op jit(solution)/shard_map/ppermute | solution.py:19
  13.6 9.1 %collective-permute-start.15 = (bf16[64,768]{1,0:T(8,128)(2,1)S(1)}, bf16[64,768]{1,0:T(8,128)(2,1)S(1)}, u32[]{:S(2)}, u32[]{:S(2)}) collective-permute-start(bf16[64,768]{1,0:T(8,128)(2,1)S(1)} %get-tuple-element.33), channel_id=1, source_target_pairs={{0,2},{1,3},{2,0},{3,1},{4,6},{5,7},{6,4},{7,5},{8,130},{9,131},{1... | collective-permute-start | bytes 294920 | tf_op jit(solution)/shard_map/ppermute | solution.py:19
  17.4 9.4 %collective-permute-start.8 = (bf16[64,768]{1,0:T(8,128)(2,1)S(1)}, bf16[64,768]{1,0:T(8,128)(2,1)S(1)}, u32[]{:S(2)}, u32[]{:S(2)}) collective-permute-start(bf16[64,768]{1,0:T(8,128)(2,1)S(1)} %get-tuple-element.34), channel_id=1, source_target_pairs={{0,0},{1,1},{2,2},{3,3},{4,4},{5,5},{6,6},{7,7},{8,128},{9,129},{1... | collective-permute-start | bytes 294920 | tf_op jit(solution)/shard_map/ppermute | solution.py:19
  20.9 8.3 %collective-permute-start.9 = (bf16[64,768]{1,0:T(8,128)(2,1)S(1)}, bf16[64,768]{1,0:T(8,128)(2,1)S(1)}, u32[]{:S(2)}, u32[]{:S(2)}) collective-permute-start(bf16[64,768]{1,0:T(8,128)(2,1)S(1)} %get-tuple-element.34), channel_id=1, source_target_pairs={{0,2},{1,3},{2,0},{3,1},{4,6},{5,7},{6,4},{7,5},{8,130},{9,131},{1... | collective-permute-start | bytes 294920 | tf_op jit(solution)/shard_map/ppermute | solution.py:19
  29.2 8.4 %collective-permute-start.10 = (bf16[2,64,768]{2,1,0:T(8,128)(2,1)S(1)}, bf16[2,64,768]{2,1,0:T(8,128)(2,1)S(1)}, u32[]{:S(2)}, u32[]{:S(2)}) collective-permute-start(bf16[2,64,768]{2,1,0:T(8,128)(2,1)S(1)} %pad_maximum_fusion.7), channel_id=1, source_target_pairs={{0,8},{1,9},{2,10},{3,11},{4,12},{5,13},{6,14},{7,15},{8,0},{9,1},... | collective-permute-start | bytes 589832 | tf_op jit(solution)/shard_map/ppermute | solution.py:19
  29.3 8.3 %collective-permute-start.11 = (bf16[2,64,768]{2,1,0:T(8,128)(2,1)S(1)}, bf16[2,64,768]{2,1,0:T(8,128)(2,1)S(1)}, u32[]{:S(2)}, u32[]{:S(2)}) collective-permute-start(bf16[2,64,768]{2,1,0:T(8,128)(2,1)S(1)} %pad_maximum_fusion.7), channel_id=1, source_target_pairs={{0,4},{1,5},{2,6},{3,7},{4,8},{5,9},{6,10},{7,11},{8,12},{9,13},{1... | collective-permute-start | bytes 589832 | tf_op jit(solution)/shard_map/ppermute | solution.py:19
  31.9 7.8 %collective-permute-start.12 = (bf16[2,64,768]{2,1,0:T(8,128)(2,1)S(1)}, bf16[2,64,768]{2,1,0:T(8,128)(2,1)S(1)}, u32[]{:S(2)}, u32[]{:S(2)}) collective-permute-start(bf16[2,64,768]{2,1,0:T(8,128)(2,1)S(1)} %pad_maximum_fusion.7), channel_id=1, source_target_pairs={{0,12},{1,13},{2,14},{3,15},{4,0},{5,1},{6,2},{7,3},{8,4},{9,5},{1... | collective-permute-start | bytes 589832 | tf_op jit(solution)/shard_map/ppermute | solution.py:19
  32.9 26.5 %collective-permute-start.6 = (bf16[512,768]{1,0:T(8,128)(2,1)}, bf16[512,768]{1,0:T(8,128)(2,1)}, u32[]{:S(2)}, u32[]{:S(2)}) collective-permute-start(bf16[512,768]{1,0:T(8,128)(2,1)} %slice.113), channel_id=1, source_target_pairs={{0,128},{1,129},{2,130},{3,131},{4,132},{5,133},{6,134},{7,135},{8... | collective-permute-start | bytes 2359304 | tf_op jit(solution)/shard_map/ppermute | solution.py:19
  40.8 19.8 %collective-permute-start.13 = (bf16[2,2,2,64,768]{4,3,2,1,0:T(8,128)(2,1)}, bf16[2,2,2,64,768]{4,3,2,1,0:T(8,128)(2,1)}, u32[]{:S(2)}, u32[]{:S(2)}) collective-permute-start(bf16[2,2,2,64,768]{4,3,2,1,0:T(8,128)(2,1)} %pad_maximum_fusion.4), channel_id=1, source_target_pairs={{0,1},{1,0},{2,3},{3,2},{4,5},{5,4},{6,7},{7,6},{8,9},{9,8},{10,11... | collective-permute-start | bytes 2359304 | tf_op jit(solution)/shard_map/ppermute | solution.py:19
  40.8 17.5 %collective-permute-start.1 = (bf16[256,768]{1,0:T(8,128)(2,1)S(1)}, bf16[256,768]{1,0:T(8,128)(2,1)}, u32[]{:S(2)}, u32[]{:S(2)}) collective-permute-start(bf16[256,768]{1,0:T(8,128)(2,1)S(1)} %slice.112), channel_id=1, source_target_pairs={{0,128},{1,129},{2,130},{3,131},{4,132},{5,133},{6,134},{7,135},{8... | collective-permute-start | bytes 1179656 | tf_op jit(solution)/shard_map/ppermute | solution.py:19
  65.0 101.5 %reduce-scatter.8.cloned.1.call-start = ((), (), s32[]{:S(2)}) async-start(), calls=%async_computation.6 | async-start | bytes 1769472 | tf_op jit(solution)/shard_map/reduce_scatter | solution.py:106
  65.1 7.4 %collective-permute-start.16 = (bf16[2,64,768]{2,1,0:T(8,128)(2,1)S(1)}, bf16[2,64,768]{2,1,0:T(8,128)(2,1)S(1)}, u32[]{:S(2)}, u32[]{:S(2)}) collective-permute-start(bf16[2,64,768]{2,1,0:T(8,128)(2,1)S(1)} %pad_maximum_fusion.8), channel_id=1, source_target_pairs={{0,8},{1,9},{2,10},{3,11},{4,12},{5,13},{6,14},{7,15},{8,0},{9,1},... | collective-permute-start | bytes 589832 | tf_op jit(solution)/shard_map/ppermute | solution.py:19
  67.8 6.9 %collective-permute-start.17 = (bf16[2,64,768]{2,1,0:T(8,128)(2,1)S(1)}, bf16[2,64,768]{2,1,0:T(8,128)(2,1)S(1)}, u32[]{:S(2)}, u32[]{:S(2)}) collective-permute-start(bf16[2,64,768]{2,1,0:T(8,128)(2,1)S(1)} %pad_maximum_fusion.8), channel_id=1, source_target_pairs={{0,4},{1,5},{2,6},{3,7},{4,8},{5,9},{6,10},{7,11},{8,12},{9,13},{1... | collective-permute-start | bytes 589832 | tf_op jit(solution)/shard_map/ppermute | solution.py:19
  68.7 6.9 %collective-permute-start.18 = (bf16[2,64,768]{2,1,0:T(8,128)(2,1)S(1)}, bf16[2,64,768]{2,1,0:T(8,128)(2,1)S(1)}, u32[]{:S(2)}, u32[]{:S(2)}) collective-permute-start(bf16[2,64,768]{2,1,0:T(8,128)(2,1)S(1)} %pad_maximum_fusion.8), channel_id=1, source_target_pairs={{0,12},{1,13},{2,14},{3,15},{4,0},{5,1},{6,2},{7,3},{8,4},{9,5},{1... | collective-permute-start | bytes 589832 | tf_op jit(solution)/shard_map/ppermute | solution.py:19
  75.9 2.4 collective-permute-start.19
  82.9 135.4 %reduce-scatter.4.cloned.1.call-start = ((), (), s32[]{:S(2)}) async-start(), calls=%async_computation.4 | async-start | bytes 1769472 | tf_op jit(solution)/shard_map/reduce_scatter | solution.py:106
  83.0 9.9 %collective-permute-start = (bf16[64,768]{1,0:T(8,128)(2,1)S(1)}, bf16[64,768]{1,0:T(8,128)(2,1)S(1)}, u32[]{:S(2)}, u32[]{:S(2)}) collective-permute-start(bf16[64,768]{1,0:T(8,128)(2,1)S(1)} %get-tuple-element.32), channel_id=1, source_target_pairs={{0,0},{1,1},{2,2},{3,3},{4,4},{5,5},{6,6},{7,7},{8,128},{9,129},{1... | collective-permute-start | bytes 294920 | tf_op jit(solution)/shard_map/ppermute | solution.py:19
  86.2 8.5 %collective-permute-start.2 = (bf16[64,768]{1,0:T(8,128)(2,1)S(1)}, bf16[64,768]{1,0:T(8,128)(2,1)S(1)}, u32[]{:S(2)}, u32[]{:S(2)}) collective-permute-start(bf16[64,768]{1,0:T(8,128)(2,1)S(1)} %get-tuple-element.32), channel_id=1, source_target_pairs={{0,2},{1,3},{2,0},{3,1},{4,6},{5,7},{6,4},{7,5},{8,130},{9,131},{1... | collective-permute-start | bytes 294920 | tf_op jit(solution)/shard_map/ppermute | solution.py:19
  94.7 9.3 %collective-permute-start.3 = (bf16[2,64,768]{2,1,0:T(8,128)(2,1)S(1)}, bf16[2,64,768]{2,1,0:T(8,128)(2,1)S(1)}, u32[]{:S(2)}, u32[]{:S(2)}) collective-permute-start(bf16[2,64,768]{2,1,0:T(8,128)(2,1)S(1)} %pad_maximum_fusion.6), channel_id=1, source_target_pairs={{0,8},{1,9},{2,10},{3,11},{4,12},{5,13},{6,14},{7,15},{8,0},{9,1},... | collective-permute-start | bytes 589832 | tf_op jit(solution)/shard_map/ppermute | solution.py:19
  94.8 9.2 %collective-permute-start.4 = (bf16[2,64,768]{2,1,0:T(8,128)(2,1)S(1)}, bf16[2,64,768]{2,1,0:T(8,128)(2,1)S(1)}, u32[]{:S(2)}, u32[]{:S(2)}) collective-permute-start(bf16[2,64,768]{2,1,0:T(8,128)(2,1)S(1)} %pad_maximum_fusion.6), channel_id=1, source_target_pairs={{0,4},{1,5},{2,6},{3,7},{4,8},{5,9},{6,10},{7,11},{8,12},{9,13},{1... | collective-permute-start | bytes 589832 | tf_op jit(solution)/shard_map/ppermute | solution.py:19
  98.6 8.0 %collective-permute-start.5 = (bf16[2,64,768]{2,1,0:T(8,128)(2,1)S(1)}, bf16[2,64,768]{2,1,0:T(8,128)(2,1)S(1)}, u32[]{:S(2)}, u32[]{:S(2)}) collective-permute-start(bf16[2,64,768]{2,1,0:T(8,128)(2,1)S(1)} %pad_maximum_fusion.6), channel_id=1, source_target_pairs={{0,12},{1,13},{2,14},{3,15},{4,0},{5,1},{6,2},{7,3},{8,4},{9,5},{1... | collective-permute-start | bytes 589832 | tf_op jit(solution)/shard_map/ppermute | solution.py:19
  106.8 2.4 collective-permute-start.7
  116.1 64.6 %copy-start.1 = (bf16[1,2,2,2,64,768]{5,4,3,2,1,0:T(8,128)(2,1)S(1)}, bf16[1,2,2,2,64,768]{5,4,3,2,1,0:T(8,128)(2,1)}, u32[]{:S(2)}) copy-start(bf16[1,2,2,2,64,768]{5,4,3,2,1,0:T(8,128)(2,1)} %copy-done) | copy-start | bytes 2359300
  116.1 64.2 %collective-permute-start.23 = (bf16[128,768]{1,0:T(8,128)(2,1)}, bf16[128,768]{1,0:T(8,128)(2,1)S(1)}, u32[]{:S(2)}, u32[]{:S(2)}) collective-permute-start(bf16[128,768]{1,0:T(8,128)(2,1)} %pad_maximum_fusion.10), channel_id=1, source_target_pairs={{0,128},{1,144},{2,160},{3,176},{4,192},{5,208},{6,224},{7,240},{8... | collective-permute-start | bytes 589832 | tf_op jit(solution)/shard_map/ppermute | solution.py:19
  123.0 57.7 %collective-permute-start.22 = (bf16[128,768]{1,0:T(8,128)(2,1)}, bf16[128,768]{1,0:T(8,128)(2,1)}, u32[]{:S(2)}, u32[]{:S(2)}) collective-permute-start(bf16[128,768]{1,0:T(8,128)(2,1)} %pad_maximum_fusion.10), channel_id=1, source_target_pairs={{0,0},{1,16},{2,32},{3,48},{4,64},{5,80},{6,96},{7,112},{8,128},{9... | collective-permute-start | bytes 589832 | tf_op jit(solution)/shard_map/ppermute | solution.py:19
  168.2 14.0 %collective-permute-start.25 = (bf16[128,768]{1,0:T(8,128)(2,1)S(1)}, bf16[128,768]{1,0:T(8,128)(2,1)S(1)}, u32[]{:S(2)}, u32[]{:S(2)}) collective-permute-start(bf16[128,768]{1,0:T(8,128)(2,1)S(1)} %pad_maximum_fusion.11), channel_id=1, source_target_pairs={{0,128},{1,144},{2,160},{3,176},{4,192},{5,208},{6,224},{7,240},{8... | collective-permute-start | bytes 589832 | tf_op jit(solution)/shard_map/ppermute | solution.py:19
  171.6 14.7 %collective-permute-start.24 = (bf16[128,768]{1,0:T(8,128)(2,1)S(1)}, bf16[128,768]{1,0:T(8,128)(2,1)S(1)}, u32[]{:S(2)}, u32[]{:S(2)}) collective-permute-start(bf16[128,768]{1,0:T(8,128)(2,1)S(1)} %pad_maximum_fusion.11), channel_id=1, source_target_pairs={{0,0},{1,16},{2,32},{3,48},{4,64},{5,80},{6,96},{7,112},{8,128},{9... | collective-permute-start | bytes 589832 | tf_op jit(solution)/shard_map/ppermute | solution.py:19
  219.4 11.7 %collective-permute-start.21 = (bf16[128,768]{1,0:T(8,128)(2,1)S(1)}, bf16[128,768]{1,0:T(8,128)(2,1)S(1)}, u32[]{:S(2)}, u32[]{:S(2)}) collective-permute-start(bf16[128,768]{1,0:T(8,128)(2,1)S(1)} %pad_maximum_fusion.9), channel_id=1, source_target_pairs={{0,128},{1,144},{2,160},{3,176},{4,192},{5,208},{6,224},{7,240},{8... | collective-permute-start | bytes 589832 | tf_op jit(solution)/shard_map/ppermute | solution.py:19
  223.8 14.6 %collective-permute-start.20 = (bf16[128,768]{1,0:T(8,128)(2,1)S(1)}, bf16[128,768]{1,0:T(8,128)(2,1)S(1)}, u32[]{:S(2)}, u32[]{:S(2)}) collective-permute-start(bf16[128,768]{1,0:T(8,128)(2,1)S(1)} %pad_maximum_fusion.9), channel_id=1, source_target_pairs={{0,0},{1,16},{2,32},{3,48},{4,64},{5,80},{6,96},{7,112},{8,128},{9... | collective-permute-start | bytes 589832 | tf_op jit(solution)/shard_map/ppermute | solution.py:19
  239.2 41.9 %copy-start.11 = (f32[3,64,64]{2,1,0:T(8,128)S(1)}, f32[3,64,64]{2,1,0:T(8,128)}, u32[]{:S(2)}) copy-start(f32[3,64,64]{2,1,0:T(8,128)} %param.7) | copy-start | bytes 147460
  268.1 12.9 %collective-permute-start.26 = (f32[96,128]{1,0:T(8,128)S(1)}, f32[96,128]{1,0:T(8,128)S(1)}, u32[]{:S(2)}, u32[]{:S(2)}) collective-permute-start(f32[96,128]{1,0:T(8,128)S(1)} %reduce_sum.9), channel_id=1, source_target_pairs={{0,0},{1,16},{2,32},{3,48},{4,64},{5,80},{6,96},{7,112},{8,128},{9... | collective-permute-start | bytes 147464 | tf_op jit(solution)/shard_map/ppermute | solution.py:19
  (10 other events, 120.8 us)
Sparse Core Ops, SparseCore 0:
  65.1 42.2 reduce-scatter.5
  110.0 56.4 reduce-scatter.7
  169.1 49.2 reduce-scatter.3

commit v3 on v2

v3 whole, which is shorter than its diff:
```python
import jax
import jax.numpy as jnp
import numpy as np
from jax import lax
from jax.sharding import Mesh, PartitionSpec as P

BLK = 128
AXES = ("yl", "z", "x", "yh", "core")
DIMS = (2, 8, 4, 2, 2)
NT = (((1,), (1,)), ((), ()))


def pairs(move):
    grid = np.arange(256).reshape(DIMS)
    return [(int(grid[at]), int(grid[move(*at)])) for at in np.ndindex(*DIMS)]


def send(value, move):
    return lax.ppermute(value, AXES, pairs(move))


def swap(yl, z, x, yh, c):
    return x // 2, z, yl * 2 + x % 2, yh, c


def swap_far(yl, z, x, yh, c):
    return x // 2, z, yl * 2 + x % 2, 1 - yh, c


def along_x(step):
    return lambda yl, z, x, yh, c: (yl, z, (x + step) % 4, yh, c)


def along_z(step):
    return lambda yl, z, x, yh, c: (yl, (z + step) % 8, x, yh, c)


def sibling(yl, z, x, yh, c):
    return yl, z, x, yh, 1 - c


def across(yl, z, x, yh, c):
    return 1 - yl, z, x, yh, c


def turned(yl, z, x, yh, c):
    row, col = yl * 8 + z, x * 4 + yh * 2 + c
    return col // 8, col % 8, row // 4, row // 2 % 2, row % 2


def turned_across(yl, z, x, yh, c):
    return across(*turned(yl, z, x, yh, c))


def homeward(step):
    return lambda yl, z, x, yh, c: turned(yl, (z + step) % 8, x, yh, c)


def row_mask(pattern, block, per):
    picked = lax.dynamic_slice_in_dim(pattern, block * per, per, 1)
    return jnp.repeat(picked, BLK, axis=1)


def dot_nt(a, b):
    return lax.dot_general(a, b, NT, preferred_element_type=jnp.float32)


def ordered(first, near, far):
    return jnp.where(first, near, far), jnp.where(first, far, near)


def dot_each(a, b):
    return jnp.einsum("knr,kmr->knm", a, b, preferred_element_type=jnp.float32)


def spread_rows(place, near, far):
    yl, x, yh = place
    plane = jnp.stack(ordered(yh == 0, near, far), axis=1)
    left, right, opposite = (send(plane, along_x(step)) for step in (1, 3, 2))
    here = ordered((x // 2) == yl, plane, opposite)
    there = ordered(((x + 3) % 4 // 2) == yl, left, right)
    halves = [jnp.stack(ordered(x % 2 == 0, here[h], there[h]), axis=1) for h in range(2)]
    return jnp.stack(halves)


def spread_cores(core, mine):
    theirs = send(mine, sibling)
    return jnp.stack(ordered(core == 0, mine, theirs), axis=4)


def sum_over_z(z, partial):
    def block(offset):
        return lax.dynamic_index_in_dim(partial, (z + offset) % 8, 1, keepdims=False)

    half = partial.shape[2] // 2
    down = send(block(4)[:, :half], along_z(-1))
    up = send(block(4)[:, half:], along_z(1))
    below, above = block(-3), block(3)
    down = jnp.concatenate([below[:, :half] + down, below[:, half:]], axis=1)
    up = jnp.concatenate([above[:, :half], above[:, half:] + up], axis=1)
    for offset in (2, 1, 0):
        down, up = send(down, along_z(-1)), send(up, along_z(1))
        if offset:
            down, up = block(-offset) + down, block(offset) + up
    return block(0) + down + up


def shards(ancestor_inverse, factor_panel, pattern, diagonal_inverse):
    yl, z, x, yh, core = (lax.axis_index(name) for name in AXES)
    count, rows, cols = factor_panel.shape
    row, col = yl * 8 + z, x * 4 + yh * 2 + core
    per = rows // BLK
    keep_rows = row_mask(pattern, row, per).astype(jnp.bfloat16)
    keep_cols = row_mask(pattern, col, per).astype(jnp.float32)
    own = factor_panel.transpose(0, 2, 1) * keep_rows[:, None, :]
    cut, wide = rows // 3, cols // 2
    top = send(ancestor_inverse[:cut], across)
    bottom = send(ancestor_inverse[cut:], across)
    offdiag, panels, parts_own, parts_beside = [], [], [], []
    for chunk in range(2):
        piece = own[:, chunk * wide : (chunk + 1) * wide]
        near, far = send(piece, swap), send(piece, swap_far)
        if chunk == 0:
            near, far, top = lax.optimization_barrier((near, far, top))
        mine = spread_rows((yl, x, yh), near, far)
        if chunk == 0:
            mine, bottom = lax.optimization_barrier((mine, bottom))
            beside = jnp.concatenate([top, bottom])
        panel = spread_cores(core, mine).reshape(2, count, 8 * wide, rows)
        panels.append(panel)
        flat = panel.reshape(2, count * 8 * wide, rows)
        partial = dot_nt(flat[0], ancestor_inverse) + dot_nt(flat[1], beside)
        reduced = sum_over_z(z, partial.reshape(count, 8, wide, rows))
        offdiag.append(-(reduced * keep_cols[:, None, :]))
        high = lax.reduce_precision(reduced, 8, 7)
        parts = jnp.stack([high, reduced - high], axis=1).astype(jnp.bfloat16)
        parts_own.append(send(parts, turned))
        parts_beside.append(send(parts, turned_across))
    parts_own = jnp.concatenate(parts_own, axis=2).reshape(count, 2 * cols, rows)
    parts_beside = jnp.concatenate(parts_beside, axis=2).reshape(count, 2 * cols, rows)
    squares = []
    for panel in panels:
        square = dot_each(panel[0], parts_own) + dot_each(panel[1], parts_beside)
        squares.append(square[..., :cols] + square[..., cols:])
    tiles = jnp.concatenate(squares, axis=-1).reshape(count, 8, wide, 2 * cols)
    total = 0
    for step in range(8):
        tile = lax.dynamic_index_in_dim(tiles, (z + step) % 8, 1, keepdims=False)
        total += send(tile, homeward(step))
    diagonal = jnp.concatenate([total[..., :cols], total[..., cols:]], axis=1)
    return jnp.concatenate(offdiag, axis=1).transpose(0, 2, 1), diagonal_inverse + diagonal


def solution(mesh):
    fine = Mesh(mesh.devices.reshape(DIMS), AXES)
    prow, pcol = ("yl", "z"), ("x", "yh", "core")
    in_specs = (P(pcol, prow), P(None, prow, pcol), P(), P(None, pcol, prow))
    out_specs = (P(None, pcol, prow), P(None, pcol, prow))
    return jax.shard_map(shards, mesh=fine, in_specs=in_specs, out_specs=out_specs, check_vma=False)
```

time: 289 us -> 280 us (0.969)
  starting transfers between devices: 68.7 us -> 158 us
  waiting for transfers between devices: 145 us -> 77.4 us
  blocking collectives: 28.9 us -> 0 us
  between operations: 14.4 us -> 1.35 us
  other arithmetic: 12.3 us -> 22.8 us
  matrix products: 11.5 us -> 6.67 us
  local copies, waits for them, and re-layouts: 7.1 us -> 11.5 us
    ppermute x27 -> x42, starting transfers between devices: 68.6 us -> 158 us  [send(): return lax.ppermute(value, AXES, pairs(move))]
    reduce_scatter x3 -> x0, waiting for transfers between devices: 72 us -> none  [shards(): reduced = lax.psum_scatter(partial, 'z', scatter_dimension=0, tiled=True)]
    all_to_all x1 -> x0, blocking collectives: 28.9 us -> none  [shards(): summed = lax.all_to_all(tiles, 'z', 0, 0, tiled=True).sum(0)]
    add x4 -> x12, other arithmetic: 0.87 us -> 8.13 us  [the longest x6 6.29 us: sum_over_z(): down, up = (block(-offset) + down, block(offset) + up)]
    dot_general x12 -> x4, matrix products: 11.5 us -> 4.53 us  [dot_nt(): return lax.dot_general(a, b, NT, preferred_element_type=jnp.float32)]
    ppermute x27 -> x42, waiting for transfers between devices: 73.3 us -> 77.4 us  [send(): return lax.ppermute(value, AXES, pairs(move))]
    another operation x17 -> x16, other arithmetic: 6.42 us -> 8.21 us  [the longest x4 3.66 us: spread_cores(): return jnp.stack(ordered(core == 0, mine, theirs), axis=4)]
  transfers between devices with their start and end apart: 30 -> 42, of which waited for: 20 -> 16; matrix products, arithmetic and copies ran while one was open for 7% -> 10% of each run, Pallas kernels for 0% -> 0%
where the time goes in v3:
time: 280 us; the launch traced here: 278 us
  starting transfers between devices  158 us (56%)
  waiting for transfers between devices  77.4 us (28%)
  other arithmetic  22.8 us (8%)
  local copies, waits for them, and re-layouts  11.5 us (4%)
  matrix products  6.67 us (2%)
    ppermute x42, starting transfers between devices, send(): return lax.ppermute(value, AXES, pairs(move))  158 us
    ppermute x42, waiting for transfers between devices, send(): return lax.ppermute(value, AXES, pairs(move))  77.4 us
    unnamed x27, local copies, waits for them, and re-layouts  6.88 us
    add x6, other arithmetic, sum_over_z(): down, up = (block(-offset) + down, block(offset) + up)  6.29 us
  transfers between devices with their start and end apart: 42, of which 16 were waited for; matrix products, arithmetic and copies ran while one was open for 10% of the time, Pallas kernels for 0%

profile of v3, /device:TPU:6, one launch (start us, length us, event | category | flops | bytes accessed | tf_op | source)
XLA Modules:
  0.0 278.0 jit_solution(8014851540668165306)
XLA Ops:
  2.6 4.3 %collective-permute-start.16 = (bf16[3,32,768]{2,1,0:T(8,128)(2,1)S(1)}, bf16[3,32,768]{2,1,0:T(8,128)(2,1)S(1)}, u32[]{:S(2)}, u32[]{:S(2)}) collective-permute-start(bf16[3,32,768]{2,1,0:T(8,128)(2,1)S(1)} %get-tuple-element.69), channel_id=1, source_target_pairs={{0,0},{1,1},{2,2},{3,3},{4,4},{5,5},{6,6},{7,7},{8,128},{9,129},{1... | collective-permute-start | bytes 442376 | tf_op jit(solution)/shard_map/ppermute | solution.py:19
  7.0 3.8 %collective-permute-start.17 = (bf16[3,32,768]{2,1,0:T(8,128)(2,1)S(1)}, bf16[3,32,768]{2,1,0:T(8,128)(2,1)S(1)}, u32[]{:S(2)}, u32[]{:S(2)}) collective-permute-start(bf16[3,32,768]{2,1,0:T(8,128)(2,1)S(1)} %get-tuple-element.69), channel_id=1, source_target_pairs={{0,2},{1,3},{2,0},{3,1},{4,6},{5,7},{6,4},{7,5},{8,130},{9,131},{1... | collective-permute-start | bytes 442376 | tf_op jit(solution)/shard_map/ppermute | solution.py:19
  10.8 3.4 %collective-permute-start = (bf16[3,32,768]{2,1,0:T(8,128)(2,1)S(1)}, bf16[3,32,768]{2,1,0:T(8,128)(2,1)S(1)}, u32[]{:S(2)}, u32[]{:S(2)}) collective-permute-start(bf16[3,32,768]{2,1,0:T(8,128)(2,1)S(1)} %get-tuple-element.68), channel_id=1, source_target_pairs={{0,0},{1,1},{2,2},{3,3},{4,4},{5,5},{6,6},{7,7},{8,128},{9,129},{1... | collective-permute-start | bytes 442376 | tf_op jit(solution)/shard_map/ppermute | solution.py:19
  14.4 4.2 %collective-permute-done.17 = bf16[3,32,768]{2,1,0:T(8,128)(2,1)S(1)} collective-permute-done((bf16[3,32,768]{2,1,0:T(8,128)(2,1)S(1)}, bf16[3,32,768]{2,1,0:T(8,128)(2,1)S(1)}, u32[]{:S(2)}, u32[]{:S(2)}) %collective-permute-start.17) | collective-permute-done | bytes 147488 | tf_op jit(solution)/shard_map/ppermute | solution.py:19
  18.7 3.5 %collective-permute-start.19 = (bf16[3,2,32,768]{3,2,1,0:T(8,128)(2,1)S(1)}, bf16[3,2,32,768]{3,2,1,0:T(8,128)(2,1)S(1)}, u32[]{:S(2)}, u32[]{:S(2)}) collective-permute-start(bf16[3,2,32,768]{3,2,1,0:T(8,128)(2,1)S(1)} %pad_maximum_fusion.10), channel_id=1, source_target_pairs={{0,4},{1,5},{2,6},{3,7},{4,8},{5,9},{6,10},{7,11},{8,12},{9,13},{1... | collective-permute-start | bytes 884744 | tf_op jit(solution)/shard_map/ppermute | solution.py:19
  23.9 12.5 %collective-permute-done.1 = bf16[3,32,768]{2,1,0:T(8,128)(2,1)S(1)} collective-permute-done((bf16[3,32,768]{2,1,0:T(8,128)(2,1)S(1)}, bf16[3,32,768]{2,1,0:T(8,128)(2,1)S(1)}, u32[]{:S(2)}, u32[]{:S(2)}) %collective-permute-start.1) | collective-permute-done | bytes 147488 | tf_op jit(solution)/shard_map/ppermute | solution.py:19
  38.5 3.5 %collective-permute-start.4 = (bf16[3,2,32,768]{3,2,0,1:T(8,128)(2,1)}, bf16[3,2,32,768]{3,2,0,1:T(8,128)(2,1)}, u32[]{:S(2)}, u32[]{:S(2)}) collective-permute-start(bf16[3,2,32,768]{3,2,0,1:T(8,128)(2,1)} %pad_maximum_fusion.7), channel_id=1, source_target_pairs={{0,4},{1,5},{2,6},{3,7},{4,8},{5,9},{6,10},{7,11},{8,12},{9,13},{1... | collective-permute-start | bytes 884744 | tf_op jit(solution)/shard_map/ppermute | solution.py:19
  44.7 5.5 %collective-permute-done.3 = bf16[3,2,32,768]{3,2,0,1:T(8,128)(2,1)} collective-permute-done((bf16[3,2,32,768]{3,2,0,1:T(8,128)(2,1)}, bf16[3,2,32,768]{3,2,0,1:T(8,128)(2,1)}, u32[]{:S(2)}, u32[]{:S(2)}) %collective-permute-start.3) | collective-permute-done | bytes 294944 | tf_op jit(solution)/shard_map/ppermute | solution.py:19
  50.2 3.6 %collective-permute-done.4 = bf16[3,2,32,768]{3,2,0,1:T(8,128)(2,1)} collective-permute-done((bf16[3,2,32,768]{3,2,0,1:T(8,128)(2,1)}, bf16[3,2,32,768]{3,2,0,1:T(8,128)(2,1)}, u32[]{:S(2)}, u32[]{:S(2)}) %collective-permute-start.4) | collective-permute-done | bytes 294944 | tf_op jit(solution)/shard_map/ppermute | solution.py:19
  57.7 5.1 %collective-permute-done.6 = bf16[512,768]{1,0:T(8,128)(2,1)} collective-permute-done((bf16[512,768]{1,0:T(8,128)(2,1)}, bf16[512,768]{1,0:T(8,128)(2,1)}, u32[]{:S(2)}, u32[]{:S(2)}) %collective-permute-start.6) | collective-permute-done | bytes 786464 | tf_op jit(solution)/shard_map/ppermute | solution.py:19
  71.9 5.9 %collective-permute-start.22 = (f32[3,16,768]{2,1,0:T(8,128)}, f32[3,16,768]{2,1,0:T(8,128)}, u32[]{:S(2)}, u32[]{:S(2)}) collective-permute-start(f32[3,16,768]{2,1,0:T(8,128)} %get-tuple-element.62), channel_id=1, source_target_pairs={{0,112},{1,113},{2,114},{3,115},{4,116},{5,117},{6,118},{7,119},{8... | collective-permute-start | bytes 442376 | tf_op jit(solution)/shard_map/ppermute | solution.py:19
  77.7 4.1 %collective-permute-done.22 = f32[3,16,768]{2,1,0:T(8,128)} collective-permute-done((f32[3,16,768]{2,1,0:T(8,128)}, f32[3,16,768]{2,1,0:T(8,128)}, u32[]{:S(2)}, u32[]{:S(2)}) %collective-permute-start.22) | collective-permute-done | bytes 147488 | tf_op jit(solution)/shard_map/ppermute | solution.py:19
  82.9 3.8 %collective-permute-start.23 = (f32[3,32,768]{2,1,0:T(8,128)S(1)}, f32[3,32,768]{2,1,0:T(8,128)S(1)}, u32[]{:S(2)}, u32[]{:S(2)}) collective-permute-start(f32[3,32,768]{2,1,0:T(8,128)S(1)} %pad_maximum_fusion.11), channel_id=1, source_target_pairs={{0,112},{1,113},{2,114},{3,115},{4,116},{5,117},{6,118},{7,119},{8... | collective-permute-start | bytes 884744 | tf_op jit(solution)/shard_map/ppermute | solution.py:19
  92.3 3.3 %collective-permute-start.8 = (f32[3,16,768]{2,1,0:T(8,128)S(1)}, f32[3,16,768]{2,1,0:T(8,128)S(1)}, u32[]{:S(2)}, u32[]{:S(2)}) collective-permute-start(f32[3,16,768]{2,1,0:T(8,128)S(1)} %get-tuple-element.56), channel_id=1, source_target_pairs={{0,112},{1,113},{2,114},{3,115},{4,116},{5,117},{6,118},{7,119},{8... | collective-permute-start | bytes 442376 | tf_op jit(solution)/shard_map/ppermute | solution.py:19
  96.6 3.3 %collective-permute-start.24 = (f32[3,32,768]{2,1,0:T(8,128)S(1)}, f32[3,32,768]{2,1,0:T(8,128)S(1)}, u32[]{:S(2)}, u32[]{:S(2)}) collective-permute-start(f32[3,32,768]{2,1,0:T(8,128)S(1)} %bitcast_add_fusion.2), channel_id=1, source_target_pairs={{0,112},{1,113},{2,114},{3,115},{4,116},{5,117},{6,118},{7,119},{8... | collective-permute-start | bytes 884744 | tf_op jit(solution)/shard_map/ppermute | solution.py:19
  102.1 5.2 %collective-permute-done.24 = f32[3,32,768]{2,1,0:T(8,128)S(1)} collective-permute-done((f32[3,32,768]{2,1,0:T(8,128)S(1)}, f32[3,32,768]{2,1,0:T(8,128)S(1)}, u32[]{:S(2)}, u32[]{:S(2)}) %collective-permute-start.24) | collective-permute-done | bytes 294944 | tf_op jit(solution)/shard_map/ppermute | solution.py:19
  111.3 3.8 %collective-permute-start.10 = (f32[3,32,768]{2,1,0:T(8,128)S(1)}, f32[3,32,768]{2,1,0:T(8,128)}, u32[]{:S(2)}, u32[]{:S(2)}) collective-permute-start(f32[3,32,768]{2,1,0:T(8,128)S(1)} %bitcast_add_fusion.7), channel_id=1, source_target_pairs={{0,112},{1,113},{2,114},{3,115},{4,116},{5,117},{6,118},{7,119},{8... | collective-permute-start | bytes 884744 | tf_op jit(solution)/shard_map/ppermute | solution.py:19
  115.2 4.9 %collective-permute-done.28 = f32[3,32,768]{2,1,0:T(8,128)S(1)} collective-permute-done((f32[3,32,768]{2,1,0:T(8,128)}, f32[3,32,768]{2,1,0:T(8,128)S(1)}, u32[]{:S(2)}, u32[]{:S(2)}) %collective-permute-start.28) | collective-permute-done | bytes 294944 | tf_op jit(solution)/shard_map/ppermute | solution.py:19
  121.2 5.3 %collective-permute-done.13 = f32[3,32,768]{2,1,0:T(8,128)} collective-permute-done((f32[3,32,768]{2,1,0:T(8,128)S(1)}, f32[3,32,768]{2,1,0:T(8,128)}, u32[]{:S(2)}, u32[]{:S(2)}) %collective-permute-start.13) | collective-permute-done | bytes 294944 | tf_op jit(solution)/shard_map/ppermute | solution.py:19
  129.5 3.2 %collective-permute-start.11 = (f32[3,32,768]{2,1,0:T(8,128)S(1)}, f32[3,32,768]{2,1,0:T(8,128)S(1)}, u32[]{:S(2)}, u32[]{:S(2)}) collective-permute-start(f32[3,32,768]{2,1,0:T(8,128)S(1)} %get-tuple-element.16), channel_id=1, source_target_pairs={{0,112},{1,113},{2,114},{3,115},{4,116},{5,117},{6,118},{7,119},{8... | collective-permute-start | bytes 884744 | tf_op jit(solution)/shard_map/ppermute | solution.py:19
  138.0 5.7 %collective-permute-start.33 = (bf16[3,2,32,768]{3,2,0,1:T(8,128)(2,1)S(1)}, bf16[3,2,32,768]{3,2,0,1:T(8,128)(2,1)}, u32[]{:S(2)}, u32[]{:S(2)}) collective-permute-start(bf16[3,2,32,768]{3,2,0,1:T(8,128)(2,1)S(1)} %pad_maximum_fusion.14), channel_id=1, source_target_pairs={{0,128},{1,144},{2,160},{3,176},{4,192},{5,208},{6,224},{7,240},{8... | collective-permute-start | bytes 884744 | tf_op jit(solution)/shard_map/ppermute | solution.py:19
  147.8 4.2 %collective-permute-start.32 = (bf16[3,2,32,768]{3,2,0,1:T(8,128)(2,1)S(1)}, bf16[3,2,32,768]{3,2,0,1:T(8,128)(2,1)}, u32[]{:S(2)}, u32[]{:S(2)}) collective-permute-start(bf16[3,2,32,768]{3,2,0,1:T(8,128)(2,1)S(1)} %pad_maximum_fusion.13), channel_id=1, source_target_pairs={{0,128},{1,144},{2,160},{3,176},{4,192},{5,208},{6,224},{7,240},{8... | collective-permute-start | bytes 884744 | tf_op jit(solution)/shard_map/ppermute | solution.py:19
  152.0 5.6 %collective-permute-start.31 = (bf16[3,2,32,768]{3,2,0,1:T(8,128)(2,1)S(1)}, bf16[3,2,32,768]{3,2,0,1:T(8,128)(2,1)}, u32[]{:S(2)}, u32[]{:S(2)}) collective-permute-start(bf16[3,2,32,768]{3,2,0,1:T(8,128)(2,1)S(1)} %pad_maximum_fusion.14), channel_id=1, source_target_pairs={{0,0},{1,16},{2,32},{3,48},{4,64},{5,80},{6,96},{7,112},{8,128},{9... | collective-permute-start | bytes 884744 | tf_op jit(solution)/shard_map/ppermute | solution.py:19
  157.5 7.2 %collective-permute-start.30 = (bf16[3,2,32,768]{3,2,0,1:T(8,128)(2,1)S(1)}, bf16[3,2,32,768]{3,2,0,1:T(8,128)(2,1)}, u32[]{:S(2)}, u32[]{:S(2)}) collective-permute-start(bf16[3,2,32,768]{3,2,0,1:T(8,128)(2,1)S(1)} %pad_maximum_fusion.13), channel_id=1, source_target_pairs={{0,0},{1,16},{2,32},{3,48},{4,64},{5,80},{6,96},{7,112},{8,128},{9... | collective-permute-start | bytes 884744 | tf_op jit(solution)/shard_map/ppermute | solution.py:19
  167.8 5.5 %collective-permute-done.30 = bf16[3,2,32,768]{3,2,0,1:T(8,128)(2,1)} collective-permute-done((bf16[3,2,32,768]{3,2,0,1:T(8,128)(2,1)S(1)}, bf16[3,2,32,768]{3,2,0,1:T(8,128)(2,1)}, u32[]{:S(2)}, u32[]{:S(2)}) %collective-permute-start.30) | collective-permute-done | bytes 294944 | tf_op jit(solution)/shard_map/ppermute | solution.py:19
  178.4 26.6 %collective-permute-start.41 = (f32[3,32,128]{2,1,0:T(8,128)S(1)}, f32[3,32,128]{2,1,0:T(8,128)S(1)}, u32[]{:S(2)}, u32[]{:S(2)}) collective-permute-start(f32[3,32,128]{2,1,0:T(8,128)S(1)} %get-tuple-element.43), channel_id=1, source_target_pairs={{0,7},{1,23},{2,39},{3,55},{4,71},{5,87},{6,103},{7,119},{8,135},{... | collective-permute-start | bytes 147464 | tf_op jit(solution)/shard_map/ppermute | solution.py:19
  205.0 15.3 %collective-permute-start.40 = (f32[3,32,128]{2,1,0:T(8,128)S(1)}, f32[3,32,128]{2,1,0:T(8,128)S(1)}, u32[]{:S(2)}, u32[]{:S(2)}) collective-permute-start(f32[3,32,128]{2,1,0:T(8,128)S(1)} %get-tuple-element.44), channel_id=1, source_target_pairs={{0,6},{1,22},{2,38},{3,54},{4,70},{5,86},{6,102},{7,118},{8,134},{... | collective-permute-start | bytes 147464 | tf_op jit(solution)/shard_map/ppermute | solution.py:19
  220.2 10.2 %collective-permute-start.39 = (f32[3,32,128]{2,1,0:T(8,128)S(1)}, f32[3,32,128]{2,1,0:T(8,128)S(1)}, u32[]{:S(2)}, u32[]{:S(2)}) collective-permute-start(f32[3,32,128]{2,1,0:T(8,128)S(1)} %get-tuple-element.45), channel_id=1, source_target_pairs={{0,5},{1,21},{2,37},{3,53},{4,69},{5,85},{6,101},{7,117},{8,133},{... | collective-permute-start | bytes 147464 | tf_op jit(solution)/shard_map/ppermute | solution.py:19
  230.5 11.8 %collective-permute-start.38 = (f32[3,32,128]{2,1,0:T(8,128)S(1)}, f32[3,32,128]{2,1,0:T(8,128)S(1)}, u32[]{:S(2)}, u32[]{:S(2)}) collective-permute-start(f32[3,32,128]{2,1,0:T(8,128)S(1)} %get-tuple-element.46), channel_id=1, source_target_pairs={{0,4},{1,20},{2,36},{3,52},{4,68},{5,84},{6,100},{7,116},{8,132},{... | collective-permute-start | bytes 147464 | tf_op jit(solution)/shard_map/ppermute | solution.py:19
  242.2 6.3 %collective-permute-start.37 = (f32[3,32,128]{2,1,0:T(8,128)S(1)}, f32[3,32,128]{2,1,0:T(8,128)S(1)}, u32[]{:S(2)}, u32[]{:S(2)}) collective-permute-start(f32[3,32,128]{2,1,0:T(8,128)S(1)} %get-tuple-element.47), channel_id=1, source_target_pairs={{0,3},{1,19},{2,35},{3,51},{4,67},{5,83},{6,99},{7,115},{8,131},{9... | collective-permute-start | bytes 147464 | tf_op jit(solution)/shard_map/ppermute | solution.py:19
  248.6 15.7 %collective-permute-start.36 = (f32[3,32,128]{2,1,0:T(8,128)S(1)}, f32[3,32,128]{2,1,0:T(8,128)S(1)}, u32[]{:S(2)}, u32[]{:S(2)}) collective-permute-start(f32[3,32,128]{2,1,0:T(8,128)S(1)} %get-tuple-element.48), channel_id=1, source_target_pairs={{0,2},{1,18},{2,34},{3,50},{4,66},{5,82},{6,98},{7,114},{8,130},{9... | collective-permute-start | bytes 147464 | tf_op jit(solution)/shard_map/ppermute | solution.py:19
  267.2 10.0 %collective-permute-done.34 = f32[3,32,128]{2,1,0:T(8,128)S(1)} collective-permute-done((f32[3,32,128]{2,1,0:T(8,128)S(1)}, f32[3,32,128]{2,1,0:T(8,128)S(1)}, u32[]{:S(2)}, u32[]{:S(2)}) %collective-permute-start.34) | collective-permute-done | bytes 49184 | tf_op jit(solution)/shard_map/ppermute | solution.py:19
  (147 shorter events, 60.4 us)
Async XLA Ops:
  2.6 11.7 %collective-permute-start.16 = (bf16[3,32,768]{2,1,0:T(8,128)(2,1)S(1)}, bf16[3,32,768]{2,1,0:T(8,128)(2,1)S(1)}, u32[]{:S(2)}, u32[]{:S(2)}) collective-permute-start(bf16[3,32,768]{2,1,0:T(8,128)(2,1)S(1)} %get-tuple-element.69), channel_id=1, source_target_pairs={{0,0},{1,1},{2,2},{3,3},{4,4},{5,5},{6,6},{7,7},{8,128},{9,129},{1... | collective-permute-start | bytes 442376 | tf_op jit(solution)/shard_map/ppermute | solution.py:19
  7.0 11.6 %collective-permute-start.17 = (bf16[3,32,768]{2,1,0:T(8,128)(2,1)S(1)}, bf16[3,32,768]{2,1,0:T(8,128)(2,1)S(1)}, u32[]{:S(2)}, u32[]{:S(2)}) collective-permute-start(bf16[3,32,768]{2,1,0:T(8,128)(2,1)S(1)} %get-tuple-element.69), channel_id=1, source_target_pairs={{0,2},{1,3},{2,0},{3,1},{4,6},{5,7},{6,4},{7,5},{8,130},{9,131},{1... | collective-permute-start | bytes 442376 | tf_op jit(solution)/shard_map/ppermute | solution.py:19
  10.8 11.5 %collective-permute-start = (bf16[3,32,768]{2,1,0:T(8,128)(2,1)S(1)}, bf16[3,32,768]{2,1,0:T(8,128)(2,1)S(1)}, u32[]{:S(2)}, u32[]{:S(2)}) collective-permute-start(bf16[3,32,768]{2,1,0:T(8,128)(2,1)S(1)} %get-tuple-element.68), channel_id=1, source_target_pairs={{0,0},{1,1},{2,2},{3,3},{4,4},{5,5},{6,6},{7,7},{8,128},{9,129},{1... | collective-permute-start | bytes 442376 | tf_op jit(solution)/shard_map/ppermute | solution.py:19
  14.3 22.1 %collective-permute-start.2 = (bf16[256,768]{1,0:T(8,128)(2,1)S(1)}, bf16[256,768]{1,0:T(8,128)(2,1)}, u32[]{:S(2)}, u32[]{:S(2)}) collective-permute-start(bf16[256,768]{1,0:T(8,128)(2,1)S(1)} %slice.91), channel_id=1, source_target_pairs={{0,128},{1,129},{2,130},{3,131},{4,132},{5,133},{6,134},{7,135},{8... | collective-permute-start | bytes 1179656 | tf_op jit(solution)/shard_map/ppermute | solution.py:19
  18.6 17.8 %collective-permute-start.18 = (bf16[3,2,32,768]{3,2,1,0:T(8,128)(2,1)S(1)}, bf16[3,2,32,768]{3,2,1,0:T(8,128)(2,1)S(1)}, u32[]{:S(2)}, u32[]{:S(2)}) collective-permute-start(bf16[3,2,32,768]{3,2,1,0:T(8,128)(2,1)S(1)} %pad_maximum_fusion.10), channel_id=1, source_target_pairs={{0,8},{1,9},{2,10},{3,11},{4,12},{5,13},{6,14},{7,15},{8,0},{9,1},... | collective-permute-start | bytes 884744 | tf_op jit(solution)/shard_map/ppermute | solution.py:19
  18.7 17.7 %collective-permute-start.19 = (bf16[3,2,32,768]{3,2,1,0:T(8,128)(2,1)S(1)}, bf16[3,2,32,768]{3,2,1,0:T(8,128)(2,1)S(1)}, u32[]{:S(2)}, u32[]{:S(2)}) collective-permute-start(bf16[3,2,32,768]{3,2,1,0:T(8,128)(2,1)S(1)} %pad_maximum_fusion.10), channel_id=1, source_target_pairs={{0,4},{1,5},{2,6},{3,7},{4,8},{5,9},{6,10},{7,11},{8,12},{9,13},{1... | collective-permute-start | bytes 884744 | tf_op jit(solution)/shard_map/ppermute | solution.py:19
  22.3 14.2 %collective-permute-start.20 = (bf16[3,2,32,768]{3,2,1,0:T(8,128)(2,1)S(1)}, bf16[3,2,32,768]{3,2,1,0:T(8,128)(2,1)S(1)}, u32[]{:S(2)}, u32[]{:S(2)}) collective-permute-start(bf16[3,2,32,768]{3,2,1,0:T(8,128)(2,1)S(1)} %pad_maximum_fusion.10), channel_id=1, source_target_pairs={{0,12},{1,13},{2,14},{3,15},{4,0},{5,1},{6,2},{7,3},{8,4},{9,5},{1... | collective-permute-start | bytes 884744 | tf_op jit(solution)/shard_map/ppermute | solution.py:19
  22.3 14.1 %collective-permute-start.1 = (bf16[3,32,768]{2,1,0:T(8,128)(2,1)S(1)}, bf16[3,32,768]{2,1,0:T(8,128)(2,1)S(1)}, u32[]{:S(2)}, u32[]{:S(2)}) collective-permute-start(bf16[3,32,768]{2,1,0:T(8,128)(2,1)S(1)} %get-tuple-element.68), channel_id=1, source_target_pairs={{0,2},{1,3},{2,0},{3,1},{4,6},{5,7},{6,4},{7,5},{8,130},{9,131},{1... | collective-permute-start | bytes 442376 | tf_op jit(solution)/shard_map/ppermute | solution.py:19
  37.8 26.2 %collective-permute-start.21 = (bf16[2,3,2,2,32,768]{5,4,3,2,1,0:T(8,128)(2,1)}, bf16[2,3,2,2,32,768]{5,4,3,2,1,0:T(8,128)(2,1)}, u32[]{:S(2)}, u32[]{:S(2)}) collective-permute-start(bf16[2,3,2,2,32,768]{5,4,3,2,1,0:T(8,128)(2,1)} %pad_maximum_fusion.3), channel_id=1, source_target_pairs={{0,1},{1,0},{2,3},{3,2},{4,5},{5,4},{6,7},{7,6},{8,9},{9,8},{10,11... | collective-permute-start | bytes 3538952 | tf_op jit(solution)/shard_map/ppermute | solution.py:19
  38.5 11.7 %collective-permute-start.3 = (bf16[3,2,32,768]{3,2,0,1:T(8,128)(2,1)}, bf16[3,2,32,768]{3,2,0,1:T(8,128)(2,1)}, u32[]{:S(2)}, u32[]{:S(2)}) collective-permute-start(bf16[3,2,32,768]{3,2,0,1:T(8,128)(2,1)} %pad_maximum_fusion.7), channel_id=1, source_target_pairs={{0,8},{1,9},{2,10},{3,11},{4,12},{5,13},{6,14},{7,15},{8,0},{9,1},... | collective-permute-start | bytes 884744 | tf_op jit(solution)/shard_map/ppermute | solution.py:19
  38.5 15.2 %collective-permute-start.4 = (bf16[3,2,32,768]{3,2,0,1:T(8,128)(2,1)}, bf16[3,2,32,768]{3,2,0,1:T(8,128)(2,1)}, u32[]{:S(2)}, u32[]{:S(2)}) collective-permute-start(bf16[3,2,32,768]{3,2,0,1:T(8,128)(2,1)} %pad_maximum_fusion.7), channel_id=1, source_target_pairs={{0,4},{1,5},{2,6},{3,7},{4,8},{5,9},{6,10},{7,11},{8,12},{9,13},{1... | collective-permute-start | bytes 884744 | tf_op jit(solution)/shard_map/ppermute | solution.py:19
  42.1 14.0 %collective-permute-start.5 = (bf16[3,2,32,768]{3,2,0,1:T(8,128)(2,1)}, bf16[3,2,32,768]{3,2,0,1:T(8,128)(2,1)}, u32[]{:S(2)}, u32[]{:S(2)}) collective-permute-start(bf16[3,2,32,768]{3,2,0,1:T(8,128)(2,1)} %pad_maximum_fusion.7), channel_id=1, source_target_pairs={{0,12},{1,13},{2,14},{3,15},{4,0},{5,1},{6,2},{7,3},{8,4},{9,5},{1... | collective-permute-start | bytes 884744 | tf_op jit(solution)/shard_map/ppermute | solution.py:19
  43.0 19.7 %collective-permute-start.6 = (bf16[512,768]{1,0:T(8,128)(2,1)}, bf16[512,768]{1,0:T(8,128)(2,1)}, u32[]{:S(2)}, u32[]{:S(2)}) collective-permute-start(bf16[512,768]{1,0:T(8,128)(2,1)} %slice.92), channel_id=1, source_target_pairs={{0,128},{1,129},{2,130},{3,131},{4,132},{5,133},{6,134},{7,135},{8... | collective-permute-start | bytes 2359304 | tf_op jit(solution)/shard_map/ppermute | solution.py:19
  62.7 24.1 %collective-permute-start.7 = (bf16[2,3,2,2,32,768]{5,4,3,2,1,0:T(8,128)(2,1)S(1)}, bf16[2,3,2,2,32,768]{5,4,3,2,1,0:T(8,128)(2,1)}, u32[]{:S(2)}, u32[]{:S(2)}) collective-permute-start(bf16[2,3,2,2,32,768]{5,4,3,2,1,0:T(8,128)(2,1)S(1)} %copy.41), channel_id=1, source_target_pairs={{0,1},{1,0},{2,3},{3,2},{4,5},{5,4},{6,7},{7,6},{8,9},{9,8},{10,11... | collective-permute-start | bytes 3538952 | tf_op jit(solution)/shard_map/ppermute | solution.py:19
  82.9 12.6 %collective-permute-start.23 = (f32[3,32,768]{2,1,0:T(8,128)S(1)}, f32[3,32,768]{2,1,0:T(8,128)S(1)}, u32[]{:S(2)}, u32[]{:S(2)}) collective-permute-start(f32[3,32,768]{2,1,0:T(8,128)S(1)} %pad_maximum_fusion.11), channel_id=1, source_target_pairs={{0,112},{1,113},{2,114},{3,115},{4,116},{5,117},{6,118},{7,119},{8... | collective-permute-start | bytes 884744 | tf_op jit(solution)/shard_map/ppermute | solution.py:19
  86.8 15.4 %collective-permute-start.27 = (f32[3,32,768]{2,1,0:T(8,128)S(1)}, f32[3,32,768]{2,1,0:T(8,128)S(1)}, u32[]{:S(2)}, u32[]{:S(2)}) collective-permute-start(f32[3,32,768]{2,1,0:T(8,128)S(1)} %pad_maximum_fusion.12), channel_id=1, source_target_pairs={{0,16},{1,17},{2,18},{3,19},{4,20},{5,21},{6,22},{7,23},{8,24},{9,... | collective-permute-start | bytes 884744 | tf_op jit(solution)/shard_map/ppermute | solution.py:19
  109.3 17.2 %collective-permute-start.13 = (f32[3,32,768]{2,1,0:T(8,128)S(1)}, f32[3,32,768]{2,1,0:T(8,128)}, u32[]{:S(2)}, u32[]{:S(2)}) collective-permute-start(f32[3,32,768]{2,1,0:T(8,128)S(1)} %pad_maximum_fusion.9), channel_id=1, source_target_pairs={{0,16},{1,17},{2,18},{3,19},{4,20},{5,21},{6,22},{7,23},{8,24},{9,... | collective-permute-start | bytes 884744 | tf_op jit(solution)/shard_map/ppermute | solution.py:19
  111.3 15.2 %collective-permute-start.10 = (f32[3,32,768]{2,1,0:T(8,128)S(1)}, f32[3,32,768]{2,1,0:T(8,128)}, u32[]{:S(2)}, u32[]{:S(2)}) collective-permute-start(f32[3,32,768]{2,1,0:T(8,128)S(1)} %bitcast_add_fusion.7), channel_id=1, source_target_pairs={{0,112},{1,113},{2,114},{3,115},{4,116},{5,117},{6,118},{7,119},{8... | collective-permute-start | bytes 884744 | tf_op jit(solution)/shard_map/ppermute | solution.py:19
  115.0 17.7 %collective-permute-start.25 = (f32[3,32,768]{2,1,0:T(8,128)}, f32[3,32,768]{2,1,0:T(8,128)}, u32[]{:S(2)}, u32[]{:S(2)}) collective-permute-start(f32[3,32,768]{2,1,0:T(8,128)} %get-tuple-element.25), channel_id=1, source_target_pairs={{0,112},{1,113},{2,114},{3,115},{4,116},{5,117},{6,118},{7,119},{8... | collective-permute-start | bytes 884744 | tf_op jit(solution)/shard_map/ppermute | solution.py:19
  121.1 11.7 %collective-permute-start.29 = (f32[3,32,768]{2,1,0:T(8,128)S(1)}, f32[3,32,768]{2,1,0:T(8,128)}, u32[]{:S(2)}, u32[]{:S(2)}) collective-permute-start(f32[3,32,768]{2,1,0:T(8,128)S(1)} %bitcast_add_fusion.1), channel_id=1, source_target_pairs={{0,16},{1,17},{2,18},{3,19},{4,20},{5,21},{6,22},{7,23},{8,24},{9,... | collective-permute-start | bytes 884744 | tf_op jit(solution)/shard_map/ppermute | solution.py:19
  129.5 14.1 %collective-permute-start.11 = (f32[3,32,768]{2,1,0:T(8,128)S(1)}, f32[3,32,768]{2,1,0:T(8,128)S(1)}, u32[]{:S(2)}, u32[]{:S(2)}) collective-permute-start(f32[3,32,768]{2,1,0:T(8,128)S(1)} %get-tuple-element.16), channel_id=1, source_target_pairs={{0,112},{1,113},{2,114},{3,115},{4,116},{5,117},{6,118},{7,119},{8... | collective-permute-start | bytes 884744 | tf_op jit(solution)/shard_map/ppermute | solution.py:19
  138.0 26.8 %collective-permute-start.33 = (bf16[3,2,32,768]{3,2,0,1:T(8,128)(2,1)S(1)}, bf16[3,2,32,768]{3,2,0,1:T(8,128)(2,1)}, u32[]{:S(2)}, u32[]{:S(2)}) collective-permute-start(bf16[3,2,32,768]{3,2,0,1:T(8,128)(2,1)S(1)} %pad_maximum_fusion.14), channel_id=1, source_target_pairs={{0,128},{1,144},{2,160},{3,176},{4,192},{5,208},{6,224},{7,240},{8... | collective-permute-start | bytes 884744 | tf_op jit(solution)/shard_map/ppermute | solution.py:19
  147.8 17.0 %collective-permute-start.32 = (bf16[3,2,32,768]{3,2,0,1:T(8,128)(2,1)S(1)}, bf16[3,2,32,768]{3,2,0,1:T(8,128)(2,1)}, u32[]{:S(2)}, u32[]{:S(2)}) collective-permute-start(bf16[3,2,32,768]{3,2,0,1:T(8,128)(2,1)S(1)} %pad_maximum_fusion.13), channel_id=1, source_target_pairs={{0,128},{1,144},{2,160},{3,176},{4,192},{5,208},{6,224},{7,240},{8... | collective-permute-start | bytes 884744 | tf_op jit(solution)/shard_map/ppermute | solution.py:19
  152.0 15.8 %collective-permute-start.31 = (bf16[3,2,32,768]{3,2,0,1:T(8,128)(2,1)S(1)}, bf16[3,2,32,768]{3,2,0,1:T(8,128)(2,1)}, u32[]{:S(2)}, u32[]{:S(2)}) collective-permute-start(bf16[3,2,32,768]{3,2,0,1:T(8,128)(2,1)S(1)} %pad_maximum_fusion.14), channel_id=1, source_target_pairs={{0,0},{1,16},{2,32},{3,48},{4,64},{5,80},{6,96},{7,112},{8,128},{9... | collective-permute-start | bytes 884744 | tf_op jit(solution)/shard_map/ppermute | solution.py:19
  157.5 15.8 %collective-permute-start.30 = (bf16[3,2,32,768]{3,2,0,1:T(8,128)(2,1)S(1)}, bf16[3,2,32,768]{3,2,0,1:T(8,128)(2,1)}, u32[]{:S(2)}, u32[]{:S(2)}) collective-permute-start(bf16[3,2,32,768]{3,2,0,1:T(8,128)(2,1)S(1)} %pad_maximum_fusion.13), channel_id=1, source_target_pairs={{0,0},{1,16},{2,32},{3,48},{4,64},{5,80},{6,96},{7,112},{8,128},{9... | collective-permute-start | bytes 884744 | tf_op jit(solution)/shard_map/ppermute | solution.py:19
  178.4 70.1 %collective-permute-start.41 = (f32[3,32,128]{2,1,0:T(8,128)S(1)}, f32[3,32,128]{2,1,0:T(8,128)S(1)}, u32[]{:S(2)}, u32[]{:S(2)}) collective-permute-start(f32[3,32,128]{2,1,0:T(8,128)S(1)} %get-tuple-element.43), channel_id=1, source_target_pairs={{0,7},{1,23},{2,39},{3,55},{4,71},{5,87},{6,103},{7,119},{8,135},{... | collective-permute-start | bytes 147464 | tf_op jit(solution)/shard_map/ppermute | solution.py:19
  205.0 59.3 %collective-permute-start.40 = (f32[3,32,128]{2,1,0:T(8,128)S(1)}, f32[3,32,128]{2,1,0:T(8,128)S(1)}, u32[]{:S(2)}, u32[]{:S(2)}) collective-permute-start(f32[3,32,128]{2,1,0:T(8,128)S(1)} %get-tuple-element.44), channel_id=1, source_target_pairs={{0,6},{1,22},{2,38},{3,54},{4,70},{5,86},{6,102},{7,118},{8,134},{... | collective-permute-start | bytes 147464 | tf_op jit(solution)/shard_map/ppermute | solution.py:19
  220.2 46.0 %collective-permute-start.39 = (f32[3,32,128]{2,1,0:T(8,128)S(1)}, f32[3,32,128]{2,1,0:T(8,128)S(1)}, u32[]{:S(2)}, u32[]{:S(2)}) collective-permute-start(f32[3,32,128]{2,1,0:T(8,128)S(1)} %get-tuple-element.45), channel_id=1, source_target_pairs={{0,5},{1,21},{2,37},{3,53},{4,69},{5,85},{6,101},{7,117},{8,133},{... | collective-permute-start | bytes 147464 | tf_op jit(solution)/shard_map/ppermute | solution.py:19
  230.5 36.8 %collective-permute-start.38 = (f32[3,32,128]{2,1,0:T(8,128)S(1)}, f32[3,32,128]{2,1,0:T(8,128)S(1)}, u32[]{:S(2)}, u32[]{:S(2)}) collective-permute-start(f32[3,32,128]{2,1,0:T(8,128)S(1)} %get-tuple-element.46), channel_id=1, source_target_pairs={{0,4},{1,20},{2,36},{3,52},{4,68},{5,84},{6,100},{7,116},{8,132},{... | collective-permute-start | bytes 147464 | tf_op jit(solution)/shard_map/ppermute | solution.py:19
  242.2 25.0 %collective-permute-start.37 = (f32[3,32,128]{2,1,0:T(8,128)S(1)}, f32[3,32,128]{2,1,0:T(8,128)S(1)}, u32[]{:S(2)}, u32[]{:S(2)}) collective-permute-start(f32[3,32,128]{2,1,0:T(8,128)S(1)} %get-tuple-element.47), channel_id=1, source_target_pairs={{0,3},{1,19},{2,35},{3,51},{4,67},{5,83},{6,99},{7,115},{8,131},{9... | collective-permute-start | bytes 147464 | tf_op jit(solution)/shard_map/ppermute | solution.py:19
  248.6 18.7 %collective-permute-start.36 = (f32[3,32,128]{2,1,0:T(8,128)S(1)}, f32[3,32,128]{2,1,0:T(8,128)S(1)}, u32[]{:S(2)}, u32[]{:S(2)}) collective-permute-start(f32[3,32,128]{2,1,0:T(8,128)S(1)} %get-tuple-element.48), channel_id=1, source_target_pairs={{0,2},{1,18},{2,34},{3,50},{4,66},{5,82},{6,98},{7,114},{8,130},{9... | collective-permute-start | bytes 147464 | tf_op jit(solution)/shard_map/ppermute | solution.py:19
  264.3 12.9 %collective-permute-start.34 = (f32[3,32,128]{2,1,0:T(8,128)S(1)}, f32[3,32,128]{2,1,0:T(8,128)S(1)}, u32[]{:S(2)}, u32[]{:S(2)}) collective-permute-start(f32[3,32,128]{2,1,0:T(8,128)S(1)} %get-tuple-element.49), channel_id=1, source_target_pairs={{0,0},{1,16},{2,32},{3,48},{4,64},{5,80},{6,96},{7,112},{8,128},{9... | collective-permute-start | bytes 147464 | tf_op jit(solution)/shard_map/ppermute | solution.py:19
  (21 other events, 248.1 us)

commit v4 on v3

--- a/solution.py
+++ b/solution.py
@@ -43,17 +43,25 @@
     return 1 - yl, z, x, yh, c
 
 
-def turned(yl, z, x, yh, c):
-    row, col = yl * 8 + z, x * 4 + yh * 2 + c
-    return col // 8, col % 8, row // 4, row // 2 % 2, row % 2
+def skewed(yl, z, x, yh, c):
+    return yl, z ^ (x % 2 * 4 + yh * 2 + c), x, yh, c
 
 
-def turned_across(yl, z, x, yh, c):
-    return across(*turned(yl, z, x, yh, c))
+def facing_place(yl, z, x, yh, c):
+    place = z ^ (x % 2 * 4 + yh * 2 + c)
+    return x // 2, z, yl * 2 + place // 4, place // 2 % 2, place % 2
 
 
-def homeward(step):
-    return lambda yl, z, x, yh, c: turned(yl, (z + step) % 8, x, yh, c)
+def beside_x(yl, z, x, yh, c):
+    return yl, z, x ^ 1, yh, c
+
+
+def over_y(yl, z, x, yh, c):
+    return yl, z, x, 1 - yh, c
+
+
+def homeward(flip):
+    return lambda yl, z, x, yh, c: (yl ^ (x // 2) ^ flip, z, yl * 2 + x % 2, yh, c)
 
 
 def row_mask(pattern, block, per):
@@ -113,42 +121,33 @@
     keep_rows = row_mask(pattern, row, per).astype(jnp.bfloat16)
     keep_cols = row_mask(pattern, col, per).astype(jnp.float32)
     own = factor_panel.transpose(0, 2, 1) * keep_rows[:, None, :]
-    cut, wide = rows // 3, cols // 2
-    top = send(ancestor_inverse[:cut], across)
-    bottom = send(ancestor_inverse[cut:], across)
-    offdiag, panels, parts_own, parts_beside = [], [], [], []
-    for chunk in range(2):
-        piece = own[:, chunk * wide : (chunk + 1) * wide]
-        near, far = send(piece, swap), send(piece, swap_far)
-        if chunk == 0:
-            near, far, top = lax.optimization_barrier((near, far, top))
-        mine = spread_rows((yl, x, yh), near, far)
-        if chunk == 0:
-            mine, bottom = lax.optimization_barrier((mine, bottom))
-            beside = jnp.concatenate([top, bottom])
-        panel = spread_cores(core, mine).reshape(2, count, 8 * wide, rows)
-        panels.append(panel)
-        flat = panel.reshape(2, count * 8 * wide, rows)
-        partial = dot_nt(flat[0], ancestor_inverse) + dot_nt(flat[1], beside)
-        reduced = sum_over_z(z, partial.reshape(count, 8, wide, rows))
-        offdiag.append(-(reduced * keep_cols[:, None, :]))
-        high = lax.reduce_precision(reduced, 8, 7)
-        parts = jnp.stack([high, reduced - high], axis=1).astype(jnp.bfloat16)
-        parts_own.append(send(parts, turned))
-        parts_beside.append(send(parts, turned_across))
-    parts_own = jnp.concatenate(parts_own, axis=2).reshape(count, 2 * cols, rows)
-    parts_beside = jnp.concatenate(parts_beside, axis=2).reshape(count, 2 * cols, rows)
-    squares = []
-    for panel in panels:
-        square = dot_each(panel[0], parts_own) + dot_each(panel[1], parts_beside)
-        squares.append(square[..., :cols] + square[..., cols:])
-    tiles = jnp.concatenate(squares, axis=-1).reshape(count, 8, wide, 2 * cols)
-    total = 0
-    for step in range(8):
-        tile = lax.dynamic_index_in_dim(tiles, (z + step) % 8, 1, keepdims=False)
-        total += send(tile, homeward(step))
-    diagonal = jnp.concatenate([total[..., :cols], total[..., cols:]], axis=1)
-    return jnp.concatenate(offdiag, axis=1).transpose(0, 2, 1), diagonal_inverse + diagonal
+    beside = send(ancestor_inverse, across)
+    near, far = send(own, swap), send(own, swap_far)
+    facing = lax.all_gather(send(send(own, skewed), facing_place), "z", axis=1)
+    mine = spread_rows((yl, x, yh), near, far)
+    mine, beside = lax.optimization_barrier((mine, beside))
+    panel = spread_cores(core, mine).reshape(2, count * 8 * cols, rows)
+    partial = dot_nt(panel[0], ancestor_inverse) + dot_nt(panel[1], beside)
+    partial = partial.reshape(count, 8, cols, rows)
+    wide = cols // 2
+    reduced = [sum_over_z(z, partial[:, :, at : at + wide]) for at in (0, wide)]
+    reduced = jnp.concatenate(reduced, axis=1)
+    offdiag = -(reduced * keep_cols[:, None, :])
+    high = lax.reduce_precision(reduced, 8, 7)
+    parts = jnp.stack([high, reduced - high], axis=1).astype(jnp.bfloat16)
+    parts = jnp.stack([parts, send(parts, across)], axis=2).reshape(count, 4 * cols, rows)
+    square = dot_each(facing.reshape(count, 8 * cols, rows), parts)
+    tiles = (square[..., : 2 * cols] + square[..., 2 * cols :]).reshape(count, 4, 2, cols, 2 * cols)
+    tiles = tiles[:, :, 0] + send(tiles[:, :, 1], sibling)
+    tiles = tiles[:, :2] + send(tiles[:, 2:], beside_x)
+    tiles = tiles[:, 0] + send(tiles[:, 1], over_y)
+    low, high = tiles[..., :cols], tiles[..., cols:]
+    diagonal = diagonal_inverse
+    for flip, picked in enumerate(ordered(x // 2 == 0, low, high)):
+        packed = jnp.concatenate([picked[:, :wide], picked[:, wide:]], axis=2)
+        packed = send(packed, homeward(flip))
+        diagonal += jnp.concatenate([packed[..., :cols], packed[..., cols:]], axis=1)
+    return offdiag.transpose(0, 2, 1), diagonal
 
 
 def solution(mesh):

time: 280 us -> 241 us (0.86)
  starting transfers between devices: 158 us -> 73.1 us
  waiting for transfers between devices: 77.4 us -> 124 us
  between operations: 1.35 us -> 14.5 us
  local copies, waits for them, and re-layouts: 11.5 us -> 2.24 us
  other arithmetic: 22.8 us -> 14.6 us
    ppermute x42 -> x31, starting transfers between devices: 158 us -> 73.1 us  [send(): return lax.ppermute(value, AXES, pairs(move))]
    ppermute x42 -> x31, waiting for transfers between devices: 77.4 us -> 124 us  [send(): return lax.ppermute(value, AXES, pairs(move))]
    unnamed x27 -> x11, local copies, waits for them, and re-layouts: 6.88 us -> 0.9 us
    dot_general x4 -> x2, matrix products: 4.53 us -> 6.65 us  [dot_nt(): return lax.dot_general(a, b, NT, preferred_element_type=jnp.float32)]
  transfers between devices with their start and end apart: 42 -> 32, of which waited for: 16 -> 24; matrix products, arithmetic and copies ran while one was open for 10% -> 8% of each run, Pallas kernels for 0% -> 0%
where the time goes in v4:
time: 241 us; the launch traced here: 238 us
  waiting for transfers between devices  124 us (51%)
  starting transfers between devices  73.1 us (30%)
  other arithmetic  14.6 us (6%)
  between operations  14.5 us (6%)
  matrix products  9.14 us (4%)
    ppermute x31, waiting for transfers between devices, send(): return lax.ppermute(value, AXES, pairs(move))  124 us
    ppermute x31, starting transfers between devices, send(): return lax.ppermute(value, AXES, pairs(move))  73.1 us
    dot_general x2, matrix products, dot_nt(): return lax.dot_general(a, b, NT, preferred_element_type=jnp.float32)  6.65 us
    add x6, other arithmetic, sum_over_z(): down, up = (block(-offset) + down, block(offset) + up)  4.96 us
  transfers between devices with their start and end apart: 32, of which 24 were waited for; matrix products, arithmetic and copies ran while one was open for 8% of the time, Pallas kernels for 0%

profile of v4, /device:TPU:6, one launch (start us, length us, event | category | flops | bytes accessed | tf_op | source)
XLA Modules:
  0.0 237.9 jit_solution(4966309936611171349)
XLA Ops:
  9.1 4.3 %collective-permute-start = (bf16[3,64,768]{2,1,0:T(8,128)(2,1)S(1)}, bf16[3,64,768]{2,1,0:T(8,128)(2,1)S(1)}, u32[]{:S(2)}, u32[]{:S(2)}) collective-permute-start(bf16[3,64,768]{2,1,0:T(8,128)(2,1)S(1)} %multiply_bitcast_fusion), channel_id=1, source_target_pairs={{0,0},{1,1},{2,2},{3,3},{4,4},{5,5},{6,6},{7,7},{8,128},{9,129},{1... | collective-permute-start | bytes 884744 | tf_op jit(solution)/shard_map/ppermute | solution.py:19
  13.5 3.8 %collective-permute-start.1 = (bf16[3,64,768]{2,1,0:T(8,128)(2,1)S(1)}, bf16[3,64,768]{2,1,0:T(8,128)(2,1)S(1)}, u32[]{:S(2)}, u32[]{:S(2)}) collective-permute-start(bf16[3,64,768]{2,1,0:T(8,128)(2,1)S(1)} %multiply_bitcast_fusion), channel_id=1, source_target_pairs={{0,2},{1,3},{2,0},{3,1},{4,6},{5,7},{6,4},{7,5},{8,130},{9,131},{1... | collective-permute-start | bytes 884744 | tf_op jit(solution)/shard_map/ppermute | solution.py:19
  17.3 6.1 %collective-permute-done = bf16[3,64,768]{2,1,0:T(8,128)(2,1)S(1)} collective-permute-done((bf16[3,64,768]{2,1,0:T(8,128)(2,1)S(1)}, bf16[3,64,768]{2,1,0:T(8,128)(2,1)S(1)}, u32[]{:S(2)}, u32[]{:S(2)}) %collective-permute-start) | collective-permute-done | bytes 294944 | tf_op jit(solution)/shard_map/ppermute | solution.py:19
  23.4 6.9 %collective-permute-done.1 = bf16[3,64,768]{2,1,0:T(8,128)(2,1)S(1)} collective-permute-done((bf16[3,64,768]{2,1,0:T(8,128)(2,1)S(1)}, bf16[3,64,768]{2,1,0:T(8,128)(2,1)S(1)}, u32[]{:S(2)}, u32[]{:S(2)}) %collective-permute-start.1) | collective-permute-done | bytes 294944 | tf_op jit(solution)/shard_map/ppermute | solution.py:19
  30.5 3.5 %collective-permute-start.3 = (bf16[3,2,64,768]{3,2,0,1:T(8,128)(2,1)S(1)}, bf16[3,2,64,768]{3,2,0,1:T(8,128)(2,1)S(1)}, u32[]{:S(2)}, u32[]{:S(2)}) collective-permute-start(bf16[3,2,64,768]{3,2,0,1:T(8,128)(2,1)S(1)} %pad_maximum_fusion.3), channel_id=1, source_target_pairs={{0,4},{1,5},{2,6},{3,7},{4,8},{5,9},{6,10},{7,11},{8,12},{9,13},{1... | collective-permute-start | bytes 1769480 | tf_op jit(solution)/shard_map/ppermute | solution.py:19
  34.6 13.7 %collective-permute-done.2 = bf16[3,2,64,768]{3,2,0,1:T(8,128)(2,1)S(1)} collective-permute-done((bf16[3,2,64,768]{3,2,0,1:T(8,128)(2,1)S(1)}, bf16[3,2,64,768]{3,2,0,1:T(8,128)(2,1)S(1)}, u32[]{:S(2)}, u32[]{:S(2)}) %collective-permute-start.2) | collective-permute-done | bytes 589856 | tf_op jit(solution)/shard_map/ppermute | solution.py:19
  48.3 8.1 %collective-permute-done.3 = bf16[3,2,64,768]{3,2,0,1:T(8,128)(2,1)S(1)} collective-permute-done((bf16[3,2,64,768]{3,2,0,1:T(8,128)(2,1)S(1)}, bf16[3,2,64,768]{3,2,0,1:T(8,128)(2,1)S(1)}, u32[]{:S(2)}, u32[]{:S(2)}) %collective-permute-start.3) | collective-permute-done | bytes 589856 | tf_op jit(solution)/shard_map/ppermute | solution.py:19
  60.5 9.1 %collective-permute-start.23 = (bf16[3,64,768]{2,1,0:T(8,128)(2,1)S(1)}, bf16[3,64,768]{2,1,0:T(8,128)(2,1)S(1)}, u32[]{:S(2)}, u32[]{:S(2)}) collective-permute-start(bf16[3,64,768]{2,1,0:T(8,128)(2,1)S(1)} %multiply_bitcast_fusion), channel_id=1, source_target_pairs={{0,0},{1,17},{2,34},{3,51},{4,68},{5,85},{6,102},{7,119},{8,8},{9,... | collective-permute-start | bytes 884744 | tf_op jit(solution)/shard_map/ppermute | solution.py:19
  69.6 6.3 %collective-permute-done.23 = bf16[3,64,768]{2,1,0:T(8,128)(2,1)S(1)} collective-permute-done((bf16[3,64,768]{2,1,0:T(8,128)(2,1)S(1)}, bf16[3,64,768]{2,1,0:T(8,128)(2,1)S(1)}, u32[]{:S(2)}, u32[]{:S(2)}) %collective-permute-start.23) | collective-permute-done | bytes 294944 | tf_op jit(solution)/shard_map/ppermute | solution.py:19
  75.9 3.4 %collective-permute-start.24 = (bf16[3,64,768]{2,1,0:T(8,128)(2,1)S(1)}, bf16[3,64,768]{2,1,0:T(8,128)(2,1)S(1)}, u32[]{:S(2)}, u32[]{:S(2)}) collective-permute-start(bf16[3,64,768]{2,1,0:T(8,128)(2,1)S(1)} %collective-permute-done.23), channel_id=1, source_target_pairs={{0,0},{1,1},{2,2},{3,3},{4,4},{5,5},{6,6},{7,7},{8,128},{9,129},{1... | collective-permute-start | bytes 884744 | tf_op jit(solution)/shard_map/ppermute | solution.py:19
  79.4 7.5 %collective-permute-done.24 = bf16[3,64,768]{2,1,0:T(8,128)(2,1)S(1)} collective-permute-done((bf16[3,64,768]{2,1,0:T(8,128)(2,1)S(1)}, bf16[3,64,768]{2,1,0:T(8,128)(2,1)S(1)}, u32[]{:S(2)}, u32[]{:S(2)}) %collective-permute-start.24) | collective-permute-done | bytes 294944 | tf_op jit(solution)/shard_map/ppermute | solution.py:19
  90.4 3.3 %fusion.21 = f32[1536,768]{1,0:T(8,128)S(1)} fusion(bf16[1536,768]{1,0:T(8,128)(2,1)S(1)} %bitcast.107, bf16[768,768]{1,0:T(8,128)(2,1)} %param.4), kind=kOutput, calls=%fused_computation.89 | convolution fusion | flops 1811939328 | bytes 8257536 | tf_op jit(solution)/shard_map/dot_general | solution.py:73
  93.9 3.3 %convolution_add_fusion = f32[1536,768]{1,0:T(8,128)S(1)} fusion(f32[1536,768]{1,0:T(8,128)S(1)} %fusion.21, bf16[1536,768]{1,0:T(8,128)(2,1)S(1)} %bitcast.106, bf16[768,768]{1,0:T(8,128)(2,1)} %collective-permute-done.5), kind=kOutput, calls=%fused_computation.2 | convolution fusion | flops 1813118976 | bytes 12976128 | tf_op jit(solution)/shard_map/dot_general | solution.py:73
  97.8 5.7 %collective-permute-start.11 = (f32[3,16,768]{2,1,0:T(8,128)S(1)}, f32[3,16,768]{2,1,0:T(8,128)S(1)}, u32[]{:S(2)}, u32[]{:S(2)}) collective-permute-start(f32[3,16,768]{2,1,0:T(8,128)S(1)} %get-tuple-element.35), channel_id=1, source_target_pairs={{0,16},{1,17},{2,18},{3,19},{4,20},{5,21},{6,22},{7,23},{8,24},{9,... | collective-permute-start | bytes 442376 | tf_op jit(solution)/shard_map/ppermute | solution.py:19
  103.7 5.0 %collective-permute-start.19 = (f32[3,16,768]{2,1,0:T(8,128)S(1)}, f32[3,16,768]{2,1,0:T(8,128)S(1)}, u32[]{:S(2)}, u32[]{:S(2)}) collective-permute-start(f32[3,16,768]{2,1,0:T(8,128)S(1)} %get-tuple-element.41), channel_id=1, source_target_pairs={{0,16},{1,17},{2,18},{3,19},{4,20},{5,21},{6,22},{7,23},{8,24},{9,... | collective-permute-start | bytes 442376 | tf_op jit(solution)/shard_map/ppermute | solution.py:19
  108.7 3.3 %collective-permute-start.15 = (f32[3,16,768]{2,1,0:T(8,128)S(1)}, f32[3,16,768]{2,1,0:T(8,128)S(1)}, u32[]{:S(2)}, u32[]{:S(2)}) collective-permute-start(f32[3,16,768]{2,1,0:T(8,128)S(1)} %get-tuple-element.40), channel_id=1, source_target_pairs={{0,112},{1,113},{2,114},{3,115},{4,116},{5,117},{6,118},{7,119},{8... | collective-permute-start | bytes 442376 | tf_op jit(solution)/shard_map/ppermute | solution.py:19
  112.0 3.8 %collective-permute-start.12 = (f32[3,32,768]{2,1,0:T(8,128)S(1)}, f32[3,32,768]{2,1,0:T(8,128)}, u32[]{:S(2)}, u32[]{:S(2)}) collective-permute-start(f32[3,32,768]{2,1,0:T(8,128)S(1)} %pad_maximum_fusion.7), channel_id=1, source_target_pairs={{0,16},{1,17},{2,18},{3,19},{4,20},{5,21},{6,22},{7,23},{8,24},{9,... | collective-permute-start | bytes 884744 | tf_op jit(solution)/shard_map/ppermute | solution.py:19
  116.0 3.4 %collective-permute-start.8 = (f32[3,32,768]{2,1,0:T(8,128)S(1)}, f32[3,32,768]{2,1,0:T(8,128)S(1)}, u32[]{:S(2)}, u32[]{:S(2)}) collective-permute-start(f32[3,32,768]{2,1,0:T(8,128)S(1)} %pad_maximum_fusion.6), channel_id=1, source_target_pairs={{0,112},{1,113},{2,114},{3,115},{4,116},{5,117},{6,118},{7,119},{8... | collective-permute-start | bytes 884744 | tf_op jit(solution)/shard_map/ppermute | solution.py:19
  119.5 2.8 %collective-permute-done.15 = f32[3,16,768]{2,1,0:T(8,128)S(1)} collective-permute-done((f32[3,16,768]{2,1,0:T(8,128)S(1)}, f32[3,16,768]{2,1,0:T(8,128)S(1)}, u32[]{:S(2)}, u32[]{:S(2)}) %collective-permute-start.15) | collective-permute-done | bytes 147488 | tf_op jit(solution)/shard_map/ppermute | solution.py:19
  122.4 2.8 %collective-permute-start.16 = (f32[3,32,768]{2,1,0:T(8,128)S(1)}, f32[3,32,768]{2,1,0:T(8,128)S(1)}, u32[]{:S(2)}, u32[]{:S(2)}) collective-permute-start(f32[3,32,768]{2,1,0:T(8,128)S(1)} %pad_maximum_fusion.8), channel_id=1, source_target_pairs={{0,112},{1,113},{2,114},{3,115},{4,116},{5,117},{6,118},{7,119},{8... | collective-permute-start | bytes 884744 | tf_op jit(solution)/shard_map/ppermute | solution.py:19
  125.2 9.8 %collective-permute-done.8 = f32[3,32,768]{2,1,0:T(8,128)S(1)} collective-permute-done((f32[3,32,768]{2,1,0:T(8,128)S(1)}, f32[3,32,768]{2,1,0:T(8,128)S(1)}, u32[]{:S(2)}, u32[]{:S(2)}) %collective-permute-start.8) | collective-permute-done | bytes 294944 | tf_op jit(solution)/shard_map/ppermute | solution.py:19
  135.0 2.8 %collective-permute-start.9 = (f32[3,32,768]{2,1,0:T(8,128)S(1)}, f32[3,32,768]{2,1,0:T(8,128)}, u32[]{:S(2)}, u32[]{:S(2)}) collective-permute-start(f32[3,32,768]{2,1,0:T(8,128)S(1)} %bitcast_add_fusion.7), channel_id=1, source_target_pairs={{0,112},{1,113},{2,114},{3,115},{4,116},{5,117},{6,118},{7,119},{8... | collective-permute-start | bytes 884744 | tf_op jit(solution)/shard_map/ppermute | solution.py:19
  137.9 9.7 %collective-permute-done.16 = f32[3,32,768]{2,1,0:T(8,128)S(1)} collective-permute-done((f32[3,32,768]{2,1,0:T(8,128)S(1)}, f32[3,32,768]{2,1,0:T(8,128)S(1)}, u32[]{:S(2)}, u32[]{:S(2)}) %collective-permute-start.16) | collective-permute-done | bytes 294944 | tf_op jit(solution)/shard_map/ppermute | solution.py:19
  150.0 4.5 %collective-permute-done.9 = f32[3,32,768]{2,1,0:T(8,128)} collective-permute-done((f32[3,32,768]{2,1,0:T(8,128)S(1)}, f32[3,32,768]{2,1,0:T(8,128)}, u32[]{:S(2)}, u32[]{:S(2)}) %collective-permute-start.9) | collective-permute-done | bytes 294944 | tf_op jit(solution)/shard_map/ppermute | solution.py:19
  168.1 3.0 %collective-permute-start.18 = (f32[3,32,768]{2,1,0:T(8,128)}, f32[3,32,768]{2,1,0:T(8,128)}, u32[]{:S(2)}, u32[]{:S(2)}) collective-permute-start(f32[3,32,768]{2,1,0:T(8,128)} %get-tuple-element.17), channel_id=1, source_target_pairs={{0,112},{1,113},{2,114},{3,115},{4,116},{5,117},{6,118},{7,119},{8... | collective-permute-start | bytes 884744 | tf_op jit(solution)/shard_map/ppermute | solution.py:19
  174.4 5.7 %collective-permute-done.14 = f32[3,32,768]{2,1,0:T(8,128)} collective-permute-done((f32[3,32,768]{2,1,0:T(8,128)S(1)}, f32[3,32,768]{2,1,0:T(8,128)}, u32[]{:S(2)}, u32[]{:S(2)}) %collective-permute-start.14) | collective-permute-done | bytes 294944 | tf_op jit(solution)/shard_map/ppermute | solution.py:19
  181.3 4.4 %collective-permute-done.22 = f32[3,32,768]{2,1,0:T(8,128)} collective-permute-done((f32[3,32,768]{2,1,0:T(8,128)S(1)}, f32[3,32,768]{2,1,0:T(8,128)}, u32[]{:S(2)}, u32[]{:S(2)}) %collective-permute-start.22) | collective-permute-done | bytes 294944 | tf_op jit(solution)/shard_map/ppermute | solution.py:19
  188.2 13.7 %collective-permute-done.25 = bf16[3,2,64,768]{3,2,0,1:T(8,128)(2,1)S(1)} collective-permute-done((bf16[3,2,64,768]{3,2,0,1:T(8,128)(2,1)S(1)}, bf16[3,2,64,768]{3,2,0,1:T(8,128)(2,1)S(1)}, u32[]{:S(2)}, u32[]{:S(2)}) %collective-permute-start.25) | collective-permute-done | bytes 589856 | tf_op jit(solution)/shard_map/ppermute | solution.py:19
  206.9 6.9 %collective-permute-done.27 = f32[3,2,64,128]{3,2,0,1:T(8,128)S(1)} collective-permute-done((f32[3,2,64,128]{3,2,0,1:T(8,128)S(1)}, f32[3,2,64,128]{3,2,0,1:T(8,128)S(1)}, u32[]{:S(2)}, u32[]{:S(2)}) %collective-permute-start.27) | collective-permute-done | bytes 196640 | tf_op jit(solution)/shard_map/ppermute | solution.py:19
  215.2 4.8 %collective-permute-done.28 = f32[3,64,128]{2,1,0:T(8,128)S(1)} collective-permute-done((f32[3,64,128]{2,1,0:T(8,128)S(1)}, f32[3,64,128]{2,1,0:T(8,128)S(1)}, u32[]{:S(2)}, u32[]{:S(2)}) %collective-permute-start.28) | collective-permute-done | bytes 98336 | tf_op jit(solution)/shard_map/ppermute | solution.py:19
  220.2 3.6 %collective-permute-start.30 = (f32[3,32,128]{2,1,0:T(8,128)S(1)}, f32[3,32,128]{2,1,0:T(8,128)S(1)}, u32[]{:S(2)}, u32[]{:S(2)}) collective-permute-start(f32[3,32,128]{2,1,0:T(8,128)S(1)} %pad_maximum_fusion.11), channel_id=1, source_target_pairs={{0,128},{1,129},{2,130},{3,131},{4,132},{5,133},{6,134},{7,135},{8... | collective-permute-start | bytes 147464 | tf_op jit(solution)/shard_map/ppermute | solution.py:19
  223.9 4.7 %collective-permute-start.29 = (f32[3,32,128]{2,1,0:T(8,128)S(1)}, f32[3,32,128]{2,1,0:T(8,128)S(1)}, u32[]{:S(2)}, u32[]{:S(2)}) collective-permute-start(f32[3,32,128]{2,1,0:T(8,128)S(1)} %pad_maximum_fusion.10), channel_id=1, source_target_pairs={{0,0},{1,1},{2,2},{3,3},{4,4},{5,5},{6,6},{7,7},{8,128},{9,129},{1... | collective-permute-start | bytes 147464 | tf_op jit(solution)/shard_map/ppermute | solution.py:19
  (99 shorter events, 43.6 us)
Async XLA Ops:
  7.2 195.0 %all-gather.3.cloned.1.call-start = ((), (), s32[]{:S(2)}) async-start(), calls=%async_computation | async-start | bytes 2654208 | tf_op jit(solution)/shard_map/all_gather | solution.py:126
  9.1 14.2 %collective-permute-start = (bf16[3,64,768]{2,1,0:T(8,128)(2,1)S(1)}, bf16[3,64,768]{2,1,0:T(8,128)(2,1)S(1)}, u32[]{:S(2)}, u32[]{:S(2)}) collective-permute-start(bf16[3,64,768]{2,1,0:T(8,128)(2,1)S(1)} %multiply_bitcast_fusion), channel_id=1, source_target_pairs={{0,0},{1,1},{2,2},{3,3},{4,4},{5,5},{6,6},{7,7},{8,128},{9,129},{1... | collective-permute-start | bytes 884744 | tf_op jit(solution)/shard_map/ppermute | solution.py:19
  13.5 16.8 %collective-permute-start.1 = (bf16[3,64,768]{2,1,0:T(8,128)(2,1)S(1)}, bf16[3,64,768]{2,1,0:T(8,128)(2,1)S(1)}, u32[]{:S(2)}, u32[]{:S(2)}) collective-permute-start(bf16[3,64,768]{2,1,0:T(8,128)(2,1)S(1)} %multiply_bitcast_fusion), channel_id=1, source_target_pairs={{0,2},{1,3},{2,0},{3,1},{4,6},{5,7},{6,4},{7,5},{8,130},{9,131},{1... | collective-permute-start | bytes 884744 | tf_op jit(solution)/shard_map/ppermute | solution.py:19
  30.4 17.9 %collective-permute-start.2 = (bf16[3,2,64,768]{3,2,0,1:T(8,128)(2,1)S(1)}, bf16[3,2,64,768]{3,2,0,1:T(8,128)(2,1)S(1)}, u32[]{:S(2)}, u32[]{:S(2)}) collective-permute-start(bf16[3,2,64,768]{3,2,0,1:T(8,128)(2,1)S(1)} %pad_maximum_fusion.3), channel_id=1, source_target_pairs={{0,8},{1,9},{2,10},{3,11},{4,12},{5,13},{6,14},{7,15},{8,0},{9,1},... | collective-permute-start | bytes 1769480 | tf_op jit(solution)/shard_map/ppermute | solution.py:19
  30.5 25.9 %collective-permute-start.3 = (bf16[3,2,64,768]{3,2,0,1:T(8,128)(2,1)S(1)}, bf16[3,2,64,768]{3,2,0,1:T(8,128)(2,1)S(1)}, u32[]{:S(2)}, u32[]{:S(2)}) collective-permute-start(bf16[3,2,64,768]{3,2,0,1:T(8,128)(2,1)S(1)} %pad_maximum_fusion.3), channel_id=1, source_target_pairs={{0,4},{1,5},{2,6},{3,7},{4,8},{5,9},{6,10},{7,11},{8,12},{9,13},{1... | collective-permute-start | bytes 1769480 | tf_op jit(solution)/shard_map/ppermute | solution.py:19
  34.0 24.8 %collective-permute-start.4 = (bf16[3,2,64,768]{3,2,0,1:T(8,128)(2,1)S(1)}, bf16[3,2,64,768]{3,2,0,1:T(8,128)(2,1)S(1)}, u32[]{:S(2)}, u32[]{:S(2)}) collective-permute-start(bf16[3,2,64,768]{3,2,0,1:T(8,128)(2,1)S(1)} %pad_maximum_fusion.3), channel_id=1, source_target_pairs={{0,12},{1,13},{2,14},{3,15},{4,0},{5,1},{6,2},{7,3},{8,4},{9,5},{1... | collective-permute-start | bytes 1769480 | tf_op jit(solution)/shard_map/ppermute | solution.py:19
  34.0 26.5 %collective-permute-start.5 = (bf16[768,768]{1,0:T(8,128)(2,1)}, bf16[768,768]{1,0:T(8,128)(2,1)}, u32[]{:S(2)}, u32[]{:S(2)}) collective-permute-start(bf16[768,768]{1,0:T(8,128)(2,1)} %param.4), channel_id=1, source_target_pairs={{0,128},{1,129},{2,130},{3,131},{4,132},{5,133},{6,134},{7,135},{8... | collective-permute-start | bytes 3538952 | tf_op jit(solution)/shard_map/ppermute | solution.py:19
  60.5 27.2 %collective-permute-start.6 = (bf16[2,3,2,2,64,768]{5,4,1,3,2,0:T(8,128)(2,1)S(1)}, bf16[2,3,2,2,64,768]{5,4,1,3,2,0:T(8,128)(2,1)}, u32[]{:S(2)}, u32[]{:S(2)}) collective-permute-start(bf16[2,3,2,2,64,768]{5,4,1,3,2,0:T(8,128)(2,1)S(1)} %pad_maximum_fusion.1), channel_id=1, source_target_pairs={{0,1},{1,0},{2,3},{3,2},{4,5},{5,4},{6,7},{7,6},{8,9},{9,8},{10,11... | collective-permute-start | bytes 7077896 | tf_op jit(solution)/shard_map/ppermute | solution.py:19
  60.5 15.4 %collective-permute-start.23 = (bf16[3,64,768]{2,1,0:T(8,128)(2,1)S(1)}, bf16[3,64,768]{2,1,0:T(8,128)(2,1)S(1)}, u32[]{:S(2)}, u32[]{:S(2)}) collective-permute-start(bf16[3,64,768]{2,1,0:T(8,128)(2,1)S(1)} %multiply_bitcast_fusion), channel_id=1, source_target_pairs={{0,0},{1,17},{2,34},{3,51},{4,68},{5,85},{6,102},{7,119},{8,8},{9,... | collective-permute-start | bytes 884744 | tf_op jit(solution)/shard_map/ppermute | solution.py:19
  75.9 11.0 %collective-permute-start.24 = (bf16[3,64,768]{2,1,0:T(8,128)(2,1)S(1)}, bf16[3,64,768]{2,1,0:T(8,128)(2,1)S(1)}, u32[]{:S(2)}, u32[]{:S(2)}) collective-permute-start(bf16[3,64,768]{2,1,0:T(8,128)(2,1)S(1)} %collective-permute-done.23), channel_id=1, source_target_pairs={{0,0},{1,1},{2,2},{3,3},{4,4},{5,5},{6,6},{7,7},{8,128},{9,129},{1... | collective-permute-start | bytes 884744 | tf_op jit(solution)/shard_map/ppermute | solution.py:19
  97.8 14.2 %collective-permute-start.11 = (f32[3,16,768]{2,1,0:T(8,128)S(1)}, f32[3,16,768]{2,1,0:T(8,128)S(1)}, u32[]{:S(2)}, u32[]{:S(2)}) collective-permute-start(f32[3,16,768]{2,1,0:T(8,128)S(1)} %get-tuple-element.35), channel_id=1, source_target_pairs={{0,16},{1,17},{2,18},{3,19},{4,20},{5,21},{6,22},{7,23},{8,24},{9,... | collective-permute-start | bytes 442376 | tf_op jit(solution)/shard_map/ppermute | solution.py:19
  103.5 12.5 %collective-permute-start.7 = (f32[3,16,768]{2,1,0:T(8,128)S(1)}, f32[3,16,768]{2,1,0:T(8,128)S(1)}, u32[]{:S(2)}, u32[]{:S(2)}) collective-permute-start(f32[3,16,768]{2,1,0:T(8,128)S(1)} %get-tuple-element.34), channel_id=1, source_target_pairs={{0,112},{1,113},{2,114},{3,115},{4,116},{5,117},{6,118},{7,119},{8... | collective-permute-start | bytes 442376 | tf_op jit(solution)/shard_map/ppermute | solution.py:19
  103.7 21.5 %collective-permute-start.19 = (f32[3,16,768]{2,1,0:T(8,128)S(1)}, f32[3,16,768]{2,1,0:T(8,128)S(1)}, u32[]{:S(2)}, u32[]{:S(2)}) collective-permute-start(f32[3,16,768]{2,1,0:T(8,128)S(1)} %get-tuple-element.41), channel_id=1, source_target_pairs={{0,16},{1,17},{2,18},{3,19},{4,20},{5,21},{6,22},{7,23},{8,24},{9,... | collective-permute-start | bytes 442376 | tf_op jit(solution)/shard_map/ppermute | solution.py:19
  108.7 13.6 %collective-permute-start.15 = (f32[3,16,768]{2,1,0:T(8,128)S(1)}, f32[3,16,768]{2,1,0:T(8,128)S(1)}, u32[]{:S(2)}, u32[]{:S(2)}) collective-permute-start(f32[3,16,768]{2,1,0:T(8,128)S(1)} %get-tuple-element.40), channel_id=1, source_target_pairs={{0,112},{1,113},{2,114},{3,115},{4,116},{5,117},{6,118},{7,119},{8... | collective-permute-start | bytes 442376 | tf_op jit(solution)/shard_map/ppermute | solution.py:19
  112.0 38.0 %collective-permute-start.12 = (f32[3,32,768]{2,1,0:T(8,128)S(1)}, f32[3,32,768]{2,1,0:T(8,128)}, u32[]{:S(2)}, u32[]{:S(2)}) collective-permute-start(f32[3,32,768]{2,1,0:T(8,128)S(1)} %pad_maximum_fusion.7), channel_id=1, source_target_pairs={{0,16},{1,17},{2,18},{3,19},{4,20},{5,21},{6,22},{7,23},{8,24},{9,... | collective-permute-start | bytes 884744 | tf_op jit(solution)/shard_map/ppermute | solution.py:19
  116.0 18.9 %collective-permute-start.8 = (f32[3,32,768]{2,1,0:T(8,128)S(1)}, f32[3,32,768]{2,1,0:T(8,128)S(1)}, u32[]{:S(2)}, u32[]{:S(2)}) collective-permute-start(f32[3,32,768]{2,1,0:T(8,128)S(1)} %pad_maximum_fusion.6), channel_id=1, source_target_pairs={{0,112},{1,113},{2,114},{3,115},{4,116},{5,117},{6,118},{7,119},{8... | collective-permute-start | bytes 884744 | tf_op jit(solution)/shard_map/ppermute | solution.py:19
  122.4 25.2 %collective-permute-start.16 = (f32[3,32,768]{2,1,0:T(8,128)S(1)}, f32[3,32,768]{2,1,0:T(8,128)S(1)}, u32[]{:S(2)}, u32[]{:S(2)}) collective-permute-start(f32[3,32,768]{2,1,0:T(8,128)S(1)} %pad_maximum_fusion.8), channel_id=1, source_target_pairs={{0,112},{1,113},{2,114},{3,115},{4,116},{5,117},{6,118},{7,119},{8... | collective-permute-start | bytes 884744 | tf_op jit(solution)/shard_map/ppermute | solution.py:19
  135.0 19.5 %collective-permute-start.9 = (f32[3,32,768]{2,1,0:T(8,128)S(1)}, f32[3,32,768]{2,1,0:T(8,128)}, u32[]{:S(2)}, u32[]{:S(2)}) collective-permute-start(f32[3,32,768]{2,1,0:T(8,128)S(1)} %bitcast_add_fusion.7), channel_id=1, source_target_pairs={{0,112},{1,113},{2,114},{3,115},{4,116},{5,117},{6,118},{7,119},{8... | collective-permute-start | bytes 884744 | tf_op jit(solution)/shard_map/ppermute | solution.py:19
  137.8 20.4 %collective-permute-start.20 = (f32[3,32,768]{2,1,0:T(8,128)S(1)}, f32[3,32,768]{2,1,0:T(8,128)}, u32[]{:S(2)}, u32[]{:S(2)}) collective-permute-start(f32[3,32,768]{2,1,0:T(8,128)S(1)} %pad_maximum_fusion.9), channel_id=1, source_target_pairs={{0,16},{1,17},{2,18},{3,19},{4,20},{5,21},{6,22},{7,23},{8,24},{9,... | collective-permute-start | bytes 884744 | tf_op jit(solution)/shard_map/ppermute | solution.py:19
  147.6 13.2 %collective-permute-start.17 = (f32[3,32,768]{2,1,0:T(8,128)S(1)}, f32[3,32,768]{2,1,0:T(8,128)}, u32[]{:S(2)}, u32[]{:S(2)}) collective-permute-start(f32[3,32,768]{2,1,0:T(8,128)S(1)} %bitcast_add_fusion.2), channel_id=1, source_target_pairs={{0,112},{1,113},{2,114},{3,115},{4,116},{5,117},{6,118},{7,119},{8... | collective-permute-start | bytes 884744 | tf_op jit(solution)/shard_map/ppermute | solution.py:19
  156.5 10.3 %collective-permute-start.13 = (f32[3,32,768]{2,1,0:T(8,128)S(1)}, f32[3,32,768]{2,1,0:T(8,128)S(1)}, u32[]{:S(2)}, u32[]{:S(2)}) collective-permute-start(f32[3,32,768]{2,1,0:T(8,128)S(1)} %get-tuple-element.13), channel_id=1, source_target_pairs={{0,16},{1,17},{2,18},{3,19},{4,20},{5,21},{6,22},{7,23},{8,24},{9,... | collective-permute-start | bytes 884744 | tf_op jit(solution)/shard_map/ppermute | solution.py:19
  162.6 11.1 %collective-permute-start.21 = (f32[3,32,768]{2,1,0:T(8,128)S(1)}, f32[3,32,768]{2,1,0:T(8,128)S(1)}, u32[]{:S(2)}, u32[]{:S(2)}) collective-permute-start(f32[3,32,768]{2,1,0:T(8,128)S(1)} %get-tuple-element.18), channel_id=1, source_target_pairs={{0,16},{1,17},{2,18},{3,19},{4,20},{5,21},{6,22},{7,23},{8,24},{9,... | collective-permute-start | bytes 884744 | tf_op jit(solution)/shard_map/ppermute | solution.py:19
  164.2 10.2 %collective-permute-start.10 = (f32[3,32,768]{2,1,0:T(8,128)}, f32[3,32,768]{2,1,0:T(8,128)}, u32[]{:S(2)}, u32[]{:S(2)}) collective-permute-start(f32[3,32,768]{2,1,0:T(8,128)} %get-tuple-element.12), channel_id=1, source_target_pairs={{0,112},{1,113},{2,114},{3,115},{4,116},{5,117},{6,118},{7,119},{8... | collective-permute-start | bytes 884744 | tf_op jit(solution)/shard_map/ppermute | solution.py:19
  167.8 12.3 %collective-permute-start.14 = (f32[3,32,768]{2,1,0:T(8,128)S(1)}, f32[3,32,768]{2,1,0:T(8,128)}, u32[]{:S(2)}, u32[]{:S(2)}) collective-permute-start(f32[3,32,768]{2,1,0:T(8,128)S(1)} %bitcast_add_fusion.6), channel_id=1, source_target_pairs={{0,16},{1,17},{2,18},{3,19},{4,20},{5,21},{6,22},{7,23},{8,24},{9,... | collective-permute-start | bytes 884744 | tf_op jit(solution)/shard_map/ppermute | solution.py:19
  168.1 13.2 %collective-permute-start.18 = (f32[3,32,768]{2,1,0:T(8,128)}, f32[3,32,768]{2,1,0:T(8,128)}, u32[]{:S(2)}, u32[]{:S(2)}) collective-permute-start(f32[3,32,768]{2,1,0:T(8,128)} %get-tuple-element.17), channel_id=1, source_target_pairs={{0,112},{1,113},{2,114},{3,115},{4,116},{5,117},{6,118},{7,119},{8... | collective-permute-start | bytes 884744 | tf_op jit(solution)/shard_map/ppermute | solution.py:19
  173.7 12.0 %collective-permute-start.22 = (f32[3,32,768]{2,1,0:T(8,128)S(1)}, f32[3,32,768]{2,1,0:T(8,128)}, u32[]{:S(2)}, u32[]{:S(2)}) collective-permute-start(f32[3,32,768]{2,1,0:T(8,128)S(1)} %bitcast_add_fusion.1), channel_id=1, source_target_pairs={{0,16},{1,17},{2,18},{3,19},{4,20},{5,21},{6,22},{7,23},{8,24},{9,... | collective-permute-start | bytes 884744 | tf_op jit(solution)/shard_map/ppermute | solution.py:19
  187.0 15.0 %collective-permute-start.25 = (bf16[3,2,64,768]{3,2,0,1:T(8,128)(2,1)S(1)}, bf16[3,2,64,768]{3,2,0,1:T(8,128)(2,1)S(1)}, u32[]{:S(2)}, u32[]{:S(2)}) collective-permute-start(bf16[3,2,64,768]{3,2,0,1:T(8,128)(2,1)S(1)} %pad_maximum_fusion.5), channel_id=1, source_target_pairs={{0,128},{1,129},{2,130},{3,131},{4,132},{5,133},{6,134},{7,135},{8... | collective-permute-start | bytes 1769480 | tf_op jit(solution)/shard_map/ppermute | solution.py:19
  204.9 1.8 collective-permute-start.26
  206.7 7.0 %collective-permute-start.27 = (f32[3,2,64,128]{3,2,0,1:T(8,128)S(1)}, f32[3,2,64,128]{3,2,0,1:T(8,128)S(1)}, u32[]{:S(2)}, u32[]{:S(2)}) collective-permute-start(f32[3,2,64,128]{3,2,0,1:T(8,128)S(1)} %slice.159), channel_id=1, source_target_pairs={{0,4},{1,5},{2,6},{3,7},{4,0},{5,1},{6,2},{7,3},{8,12},{9,13},{10,... | collective-permute-start | bytes 589832 | tf_op jit(solution)/shard_map/ppermute | solution.py:19
  213.8 6.2 %collective-permute-start.28 = (f32[3,64,128]{2,1,0:T(8,128)S(1)}, f32[3,64,128]{2,1,0:T(8,128)S(1)}, u32[]{:S(2)}, u32[]{:S(2)}) collective-permute-start(f32[3,64,128]{2,1,0:T(8,128)S(1)} %slice_bitcast_fusion), channel_id=1, source_target_pairs={{0,2},{1,3},{2,0},{3,1},{4,6},{5,7},{6,4},{7,5},{8,10},{9,11},{10,... | collective-permute-start | bytes 294920 | tf_op jit(solution)/shard_map/ppermute | solution.py:19
  220.2 8.4 %collective-permute-start.30 = (f32[3,32,128]{2,1,0:T(8,128)S(1)}, f32[3,32,128]{2,1,0:T(8,128)S(1)}, u32[]{:S(2)}, u32[]{:S(2)}) collective-permute-start(f32[3,32,128]{2,1,0:T(8,128)S(1)} %pad_maximum_fusion.11), channel_id=1, source_target_pairs={{0,128},{1,129},{2,130},{3,131},{4,132},{5,133},{6,134},{7,135},{8... | collective-permute-start | bytes 147464 | tf_op jit(solution)/shard_map/ppermute | solution.py:19
  223.9 6.4 %collective-permute-start.29 = (f32[3,32,128]{2,1,0:T(8,128)S(1)}, f32[3,32,128]{2,1,0:T(8,128)S(1)}, u32[]{:S(2)}, u32[]{:S(2)}) collective-permute-start(f32[3,32,128]{2,1,0:T(8,128)S(1)} %pad_maximum_fusion.10), channel_id=1, source_target_pairs={{0,0},{1,1},{2,2},{3,3},{4,4},{5,5},{6,6},{7,7},{8,128},{9,129},{1... | collective-permute-start | bytes 147464 | tf_op jit(solution)/shard_map/ppermute | solution.py:19
  (3 other events, 61.7 us)
Sparse Core Ops, SparseCore 0:
  87.8 61.5 all-gather.2

commit v5 on v4

--- a/solution.py
+++ b/solution.py
@@ -52,16 +52,12 @@
     return x // 2, z, yl * 2 + place // 4, place // 2 % 2, place % 2
 
 
-def beside_x(yl, z, x, yh, c):
-    return yl, z, x ^ 1, yh, c
-
-
 def over_y(yl, z, x, yh, c):
     return yl, z, x, 1 - yh, c
 
 
-def homeward(flip):
-    return lambda yl, z, x, yh, c: (yl ^ (x // 2) ^ flip, z, yl * 2 + x % 2, yh, c)
+def flip_x(bits):
+    return lambda yl, z, x, yh, c: (yl, z, x ^ bits, yh, c)
 
 
 def row_mask(pattern, block, per):
@@ -84,7 +80,9 @@
 def spread_rows(place, near, far):
     yl, x, yh = place
     plane = jnp.stack(ordered(yh == 0, near, far), axis=1)
-    left, right, opposite = (send(plane, along_x(step)) for step in (1, 3, 2))
+    left, right = send(plane, along_x(1)), send(plane, along_x(3))
+    opposite = [send(left[:, :1], along_x(1)), send(right[:, 1:], along_x(3))]
+    opposite = jnp.concatenate(opposite, axis=1)
     here = ordered((x // 2) == yl, plane, opposite)
     there = ordered(((x + 3) % 4 // 2) == yl, left, right)
     halves = [jnp.stack(ordered(x % 2 == 0, here[h], there[h]), axis=1) for h in range(2)]
@@ -123,9 +121,12 @@
     own = factor_panel.transpose(0, 2, 1) * keep_rows[:, None, :]
     beside = send(ancestor_inverse, across)
     near, far = send(own, swap), send(own, swap_far)
-    facing = lax.all_gather(send(send(own, skewed), facing_place), "z", axis=1)
+    near, far, turned = lax.optimization_barrier((near, far, send(own, skewed)))
     mine = spread_rows((yl, x, yh), near, far)
-    mine, beside = lax.optimization_barrier((mine, beside))
+    turned = send(turned, facing_place)
+    mine, beside, _ = lax.optimization_barrier((mine, beside, turned))
+    facing = lax.all_gather(turned, "z", axis=1)
+    facing = [facing, send(facing, across)]
     panel = spread_cores(core, mine).reshape(2, count * 8 * cols, rows)
     partial = dot_nt(panel[0], ancestor_inverse) + dot_nt(panel[1], beside)
     partial = partial.reshape(count, 8, cols, rows)
@@ -135,18 +136,20 @@
     offdiag = -(reduced * keep_cols[:, None, :])
     high = lax.reduce_precision(reduced, 8, 7)
     parts = jnp.stack([high, reduced - high], axis=1).astype(jnp.bfloat16)
-    parts = jnp.stack([parts, send(parts, across)], axis=2).reshape(count, 4 * cols, rows)
-    square = dot_each(facing.reshape(count, 8 * cols, rows), parts)
-    tiles = (square[..., : 2 * cols] + square[..., 2 * cols :]).reshape(count, 4, 2, cols, 2 * cols)
-    tiles = tiles[:, :, 0] + send(tiles[:, :, 1], sibling)
-    tiles = tiles[:, :2] + send(tiles[:, 2:], beside_x)
-    tiles = tiles[:, 0] + send(tiles[:, 1], over_y)
-    low, high = tiles[..., :cols], tiles[..., cols:]
-    diagonal = diagonal_inverse
-    for flip, picked in enumerate(ordered(x // 2 == 0, low, high)):
-        packed = jnp.concatenate([picked[:, :wide], picked[:, wide:]], axis=2)
-        packed = send(packed, homeward(flip))
-        diagonal += jnp.concatenate([packed[..., :cols], packed[..., cols:]], axis=1)
+    parts = parts.reshape(count, 2 * cols, rows)
+    tiles = []
+    for panel in facing:
+        square = dot_each(panel.reshape(count, 8 * cols, rows), parts)
+        tiles.append(square[..., :cols] + square[..., cols:])
+    tiles = jnp.concatenate(tiles, axis=2).reshape(count, 2, 2, 2, cols, 2 * cols)
+    tiles = tiles[:, :, :, 0] + send(tiles[:, :, :, 1], sibling)
+    tiles = tiles[:, :, 0] + send(tiles[:, :, 1], over_y)
+    kept, given = ordered((x // 2) == yl, tiles[..., :cols], tiles[..., cols:])
+    kept, given = (jnp.concatenate([t[:, :, :wide], t[:, :, wide:]], axis=3) for t in (kept, given))
+    packed = kept[:, 0] + send(kept[:, 1], flip_x(1))
+    packed += send(given[:, 0], flip_x(2)) + send(given[:, 1], flip_x(3))
+    diagonal = jnp.concatenate([packed[..., :cols], packed[..., cols:]], axis=1)
+    diagonal += diagonal_inverse
     return offdiag.transpose(0, 2, 1), diagonal
 
 

time: 241 us -> 229 us (0.950)
  waiting for transfers between devices: 124 us -> 116 us
    ppermute x31 -> x32, waiting for transfers between devices: 124 us -> 116 us  [send(): return lax.ppermute(value, AXES, pairs(move))]
    ppermute x31 -> x32, starting transfers between devices: 73.1 us -> 70.8 us  [send(): return lax.ppermute(value, AXES, pairs(move))]
  transfers between devices with their start and end apart: 32 -> 33, of which waited for: 24 -> 24; matrix products, arithmetic and copies ran while one was open for 8% -> 9% of each run, Pallas kernels for 0% -> 0%
where the time goes in v5:
time: 229 us; the launch traced here: 228 us
  waiting for transfers between devices  116 us (51%)
  starting transfers between devices  70.9 us (31%)
  other arithmetic  14.8 us (6%)
  between operations  14.5 us (6%)
  matrix products  10.1 us (4%)
    ppermute x32, waiting for transfers between devices, send(): return lax.ppermute(value, AXES, pairs(move))  116 us
    ppermute x32, starting transfers between devices, send(): return lax.ppermute(value, AXES, pairs(move))  70.8 us
    dot_general x2, matrix products, dot_nt(): return lax.dot_general(a, b, NT, preferred_element_type=jnp.float32)  6.72 us
    add x6, other arithmetic, sum_over_z(): down, up = (block(-offset) + down, block(offset) + up)  5.06 us
  transfers between devices with their start and end apart: 33, of which 24 were waited for; matrix products, arithmetic and copies ran while one was open for 9% of the time, Pallas kernels for 0%

profile of v5, /device:TPU:6, one launch (start us, length us, event | category | flops | bytes accessed | tf_op | source)
XLA Modules:
  0.0 228.1 jit_solution(14554320560577649435)
XLA Ops:
  9.1 4.3 %collective-permute-start = (bf16[3,64,768]{2,1,0:T(8,128)(2,1)S(1)}, bf16[3,64,768]{2,1,0:T(8,128)(2,1)S(1)}, u32[]{:S(2)}, u32[]{:S(2)}) collective-permute-start(bf16[3,64,768]{2,1,0:T(8,128)(2,1)S(1)} %multiply_bitcast_fusion), channel_id=1, source_target_pairs={{0,0},{1,1},{2,2},{3,3},{4,4},{5,5},{6,6},{7,7},{8,128},{9,129},{1... | collective-permute-start | bytes 884744 | tf_op jit(solution)/shard_map/ppermute | solution.py:19
  13.5 3.8 %collective-permute-start.1 = (bf16[3,64,768]{2,1,0:T(8,128)(2,1)S(1)}, bf16[3,64,768]{2,1,0:T(8,128)(2,1)S(1)}, u32[]{:S(2)}, u32[]{:S(2)}) collective-permute-start(bf16[3,64,768]{2,1,0:T(8,128)(2,1)S(1)} %multiply_bitcast_fusion), channel_id=1, source_target_pairs={{0,2},{1,3},{2,0},{3,1},{4,6},{5,7},{6,4},{7,5},{8,130},{9,131},{1... | collective-permute-start | bytes 884744 | tf_op jit(solution)/shard_map/ppermute | solution.py:19
  17.3 9.1 %collective-permute-start.2 = (bf16[3,64,768]{2,1,0:T(8,128)(2,1)S(1)}, bf16[3,64,768]{2,1,0:T(8,128)(2,1)S(1)}, u32[]{:S(2)}, u32[]{:S(2)}) collective-permute-start(bf16[3,64,768]{2,1,0:T(8,128)(2,1)S(1)} %multiply_bitcast_fusion), channel_id=1, source_target_pairs={{0,0},{1,17},{2,34},{3,51},{4,68},{5,85},{6,102},{7,119},{8,8},{9,... | collective-permute-start | bytes 884744 | tf_op jit(solution)/shard_map/ppermute | solution.py:19
  26.4 3.9 %collective-permute-done.1 = bf16[3,64,768]{2,1,0:T(8,128)(2,1)S(1)} collective-permute-done((bf16[3,64,768]{2,1,0:T(8,128)(2,1)S(1)}, bf16[3,64,768]{2,1,0:T(8,128)(2,1)S(1)}, u32[]{:S(2)}, u32[]{:S(2)}) %collective-permute-start.1) | collective-permute-done | bytes 294944 | tf_op jit(solution)/shard_map/ppermute | solution.py:19
  30.3 2.3 %collective-permute-done.2 = bf16[3,64,768]{2,1,0:T(8,128)(2,1)S(1)} collective-permute-done((bf16[3,64,768]{2,1,0:T(8,128)(2,1)S(1)}, bf16[3,64,768]{2,1,0:T(8,128)(2,1)S(1)}, u32[]{:S(2)}, u32[]{:S(2)}) %collective-permute-start.2) | collective-permute-done | bytes 294944 | tf_op jit(solution)/shard_map/ppermute | solution.py:19
  34.8 9.7 %collective-permute-done.3 = bf16[3,2,64,768]{3,2,0,1:T(8,128)(2,1)S(1)} collective-permute-done((bf16[3,2,64,768]{3,2,0,1:T(8,128)(2,1)S(1)}, bf16[3,2,64,768]{3,2,0,1:T(8,128)(2,1)S(1)}, u32[]{:S(2)}, u32[]{:S(2)}) %collective-permute-start.3) | collective-permute-done | bytes 589856 | tf_op jit(solution)/shard_map/ppermute | solution.py:19
  46.9 4.7 %collective-permute-start.8 = (bf16[3,64,768]{2,1,0:T(8,128)(2,1)S(1)}, bf16[3,64,768]{2,1,0:T(8,128)(2,1)S(1)}, u32[]{:S(2)}, u32[]{:S(2)}) collective-permute-start(bf16[3,64,768]{2,1,0:T(8,128)(2,1)S(1)} %collective-permute-done.2), channel_id=1, source_target_pairs={{0,0},{1,1},{2,2},{3,3},{4,4},{5,5},{6,6},{7,7},{8,128},{9,129},{1... | collective-permute-start | bytes 884744 | tf_op jit(solution)/shard_map/ppermute | solution.py:19
  52.2 2.8 %collective-permute-done.6 = bf16[3,1,64,768]{3,2,0,1:T(8,128)(2,1)S(1)} collective-permute-done((bf16[3,1,64,768]{3,2,0,1:T(8,128)(2,1)S(1)}, bf16[3,1,64,768]{3,2,0,1:T(8,128)(2,1)S(1)}, u32[]{:S(2)}, u32[]{:S(2)}) %collective-permute-start.6) | collective-permute-done | bytes 294944 | tf_op jit(solution)/shard_map/ppermute | solution.py:19
  55.6 5.5 %collective-permute-done.8 = bf16[3,64,768]{2,1,0:T(8,128)(2,1)S(1)} collective-permute-done((bf16[3,64,768]{2,1,0:T(8,128)(2,1)S(1)}, bf16[3,64,768]{2,1,0:T(8,128)(2,1)S(1)}, u32[]{:S(2)}, u32[]{:S(2)}) %collective-permute-start.8) | collective-permute-done | bytes 294944 | tf_op jit(solution)/shard_map/ppermute | solution.py:19
  61.1 16.1 %collective-permute-done.7 = bf16[768,768]{1,0:T(8,128)(2,1)} collective-permute-done((bf16[768,768]{1,0:T(8,128)(2,1)}, bf16[768,768]{1,0:T(8,128)(2,1)}, u32[]{:S(2)}, u32[]{:S(2)}) %collective-permute-start.7) | collective-permute-done | bytes 1179680 | tf_op jit(solution)/shard_map/ppermute | solution.py:19
  77.2 3.6 %collective-permute-start.9 = (bf16[2,3,2,2,64,768]{5,4,1,3,2,0:T(8,128)(2,1)S(1)}, bf16[2,3,2,2,64,768]{5,4,1,3,2,0:T(8,128)(2,1)}, u32[]{:S(2)}, u32[]{:S(2)}) collective-permute-start(bf16[2,3,2,2,64,768]{5,4,1,3,2,0:T(8,128)(2,1)S(1)} %pad_maximum_fusion.1), channel_id=1, source_target_pairs={{0,1},{1,0},{2,3},{3,2},{4,5},{5,4},{6,7},{7,6},{8,9},{9,8},{10,11... | collective-permute-start | bytes 7077896 | tf_op jit(solution)/shard_map/ppermute | solution.py:19
  80.9 4.3 %collective-permute-done.9 = bf16[2,3,2,2,64,768]{5,4,1,3,2,0:T(8,128)(2,1)} collective-permute-done((bf16[2,3,2,2,64,768]{5,4,1,3,2,0:T(8,128)(2,1)S(1)}, bf16[2,3,2,2,64,768]{5,4,1,3,2,0:T(8,128)(2,1)}, u32[]{:S(2)}, u32[]{:S(2)}) %collective-permute-start.9) | collective-permute-done | bytes 2359328 | tf_op jit(solution)/shard_map/ppermute | solution.py:19
  88.0 3.3 %fusion.26 = f32[1536,768]{1,0:T(8,128)S(1)} fusion(bf16[1536,768]{1,0:T(8,128)(2,1)S(1)} %bitcast.125, bf16[768,768]{1,0:T(8,128)(2,1)} %param.4), kind=kOutput, calls=%fused_computation.100 | convolution fusion | flops 1811939328 | bytes 8257536 | tf_op jit(solution)/shard_map/dot_general | solution.py:69
  91.4 3.4 %convolution_add_fusion = f32[1536,768]{1,0:T(8,128)S(1)} fusion(f32[1536,768]{1,0:T(8,128)S(1)} %fusion.26, bf16[1536,768]{1,0:T(8,128)(2,1)S(1)} %bitcast.126, bf16[768,768]{1,0:T(8,128)(2,1)} %collective-permute-done.7), kind=kOutput, calls=%fused_computation.2 | convolution fusion | flops 1813118976 | bytes 12976128 | tf_op jit(solution)/shard_map/dot_general | solution.py:69
  95.3 9.5 %collective-permute-start.14 = (f32[3,16,768]{2,1,0:T(8,128)S(1)}, f32[3,16,768]{2,1,0:T(8,128)S(1)}, u32[]{:S(2)}, u32[]{:S(2)}) collective-permute-start(f32[3,16,768]{2,1,0:T(8,128)S(1)} %get-tuple-element.39), channel_id=1, source_target_pairs={{0,16},{1,17},{2,18},{3,19},{4,20},{5,21},{6,22},{7,23},{8,24},{9,... | collective-permute-start | bytes 442376 | tf_op jit(solution)/shard_map/ppermute | solution.py:19
  108.9 2.7 %collective-permute-done.14 = f32[3,16,768]{2,1,0:T(8,128)S(1)} collective-permute-done((f32[3,16,768]{2,1,0:T(8,128)S(1)}, f32[3,16,768]{2,1,0:T(8,128)S(1)}, u32[]{:S(2)}, u32[]{:S(2)}) %collective-permute-start.14) | collective-permute-done | bytes 147488 | tf_op jit(solution)/shard_map/ppermute | solution.py:19
  111.6 2.6 %collective-permute-start.15 = (f32[3,32,768]{2,1,0:T(8,128)S(1)}, f32[3,32,768]{2,1,0:T(8,128)}, u32[]{:S(2)}, u32[]{:S(2)}) collective-permute-start(f32[3,32,768]{2,1,0:T(8,128)S(1)} %pad_maximum_fusion.7), channel_id=1, source_target_pairs={{0,16},{1,17},{2,18},{3,19},{4,20},{5,21},{6,22},{7,23},{8,24},{9,... | collective-permute-start | bytes 884744 | tf_op jit(solution)/shard_map/ppermute | solution.py:19
  116.2 3.0 %collective-permute-done.18 = f32[3,16,768]{2,1,0:T(8,128)S(1)} collective-permute-done((f32[3,16,768]{2,1,0:T(8,128)S(1)}, f32[3,16,768]{2,1,0:T(8,128)S(1)}, u32[]{:S(2)}, u32[]{:S(2)}) %collective-permute-start.18) | collective-permute-done | bytes 147488 | tf_op jit(solution)/shard_map/ppermute | solution.py:19
  119.3 2.5 %collective-permute-start.19 = (f32[3,32,768]{2,1,0:T(8,128)S(1)}, f32[3,32,768]{2,1,0:T(8,128)S(1)}, u32[]{:S(2)}, u32[]{:S(2)}) collective-permute-start(f32[3,32,768]{2,1,0:T(8,128)S(1)} %pad_maximum_fusion.8), channel_id=1, source_target_pairs={{0,112},{1,113},{2,114},{3,115},{4,116},{5,117},{6,118},{7,119},{8... | collective-permute-start | bytes 884744 | tf_op jit(solution)/shard_map/ppermute | solution.py:19
  121.8 10.0 %collective-permute-done.11 = f32[3,32,768]{2,1,0:T(8,128)S(1)} collective-permute-done((f32[3,32,768]{2,1,0:T(8,128)S(1)}, f32[3,32,768]{2,1,0:T(8,128)S(1)}, u32[]{:S(2)}, u32[]{:S(2)}) %collective-permute-start.11) | collective-permute-done | bytes 294944 | tf_op jit(solution)/shard_map/ppermute | solution.py:19
  131.8 2.5 %collective-permute-start.12 = (f32[3,32,768]{2,1,0:T(8,128)S(1)}, f32[3,32,768]{2,1,0:T(8,128)}, u32[]{:S(2)}, u32[]{:S(2)}) collective-permute-start(f32[3,32,768]{2,1,0:T(8,128)S(1)} %bitcast_add_fusion.7), channel_id=1, source_target_pairs={{0,112},{1,113},{2,114},{3,115},{4,116},{5,117},{6,118},{7,119},{8... | collective-permute-start | bytes 884744 | tf_op jit(solution)/shard_map/ppermute | solution.py:19
  134.5 8.4 %collective-permute-done.19 = f32[3,32,768]{2,1,0:T(8,128)S(1)} collective-permute-done((f32[3,32,768]{2,1,0:T(8,128)S(1)}, f32[3,32,768]{2,1,0:T(8,128)S(1)}, u32[]{:S(2)}, u32[]{:S(2)}) %collective-permute-start.19) | collective-permute-done | bytes 294944 | tf_op jit(solution)/shard_map/ppermute | solution.py:19
  143.0 3.5 %collective-permute-start.20 = (f32[3,32,768]{2,1,0:T(8,128)S(1)}, f32[3,32,768]{2,1,0:T(8,128)}, u32[]{:S(2)}, u32[]{:S(2)}) collective-permute-start(f32[3,32,768]{2,1,0:T(8,128)S(1)} %bitcast_add_fusion.2), channel_id=1, source_target_pairs={{0,112},{1,113},{2,114},{3,115},{4,116},{5,117},{6,118},{7,119},{8... | collective-permute-start | bytes 884744 | tf_op jit(solution)/shard_map/ppermute | solution.py:19
  146.5 2.9 %collective-permute-done.12 = f32[3,32,768]{2,1,0:T(8,128)} collective-permute-done((f32[3,32,768]{2,1,0:T(8,128)S(1)}, f32[3,32,768]{2,1,0:T(8,128)}, u32[]{:S(2)}, u32[]{:S(2)}) %collective-permute-start.12) | collective-permute-done | bytes 294944 | tf_op jit(solution)/shard_map/ppermute | solution.py:19
  151.5 2.1 collective-permute-start.16
  163.5 3.2 %collective-permute-start.21 = (f32[3,32,768]{2,1,0:T(8,128)}, f32[3,32,768]{2,1,0:T(8,128)}, u32[]{:S(2)}, u32[]{:S(2)}) collective-permute-start(f32[3,32,768]{2,1,0:T(8,128)} %get-tuple-element.23), channel_id=1, source_target_pairs={{0,112},{1,113},{2,114},{3,115},{4,116},{5,117},{6,118},{7,119},{8... | collective-permute-start | bytes 884744 | tf_op jit(solution)/shard_map/ppermute | solution.py:19
  169.4 5.6 %collective-permute-done.17 = f32[3,32,768]{2,1,0:T(8,128)} collective-permute-done((f32[3,32,768]{2,1,0:T(8,128)S(1)}, f32[3,32,768]{2,1,0:T(8,128)}, u32[]{:S(2)}, u32[]{:S(2)}) %collective-permute-start.17) | collective-permute-done | bytes 294944 | tf_op jit(solution)/shard_map/ppermute | solution.py:19
  176.3 4.7 %collective-permute-done.25 = f32[3,32,768]{2,1,0:T(8,128)} collective-permute-done((f32[3,32,768]{2,1,0:T(8,128)S(1)}, f32[3,32,768]{2,1,0:T(8,128)}, u32[]{:S(2)}, u32[]{:S(2)}) %collective-permute-start.25) | collective-permute-done | bytes 294944 | tf_op jit(solution)/shard_map/ppermute | solution.py:19
  183.2 16.0 %collective-permute-done.26 = bf16[3,8,64,768]{3,2,1,0:T(8,128)(2,1)} collective-permute-done((bf16[3,8,64,768]{3,2,1,0:T(8,128)(2,1)}, bf16[3,8,64,768]{3,2,1,0:T(8,128)(2,1)}, u32[]{:S(2)}, u32[]{:S(2)}) %collective-permute-start.26) | collective-permute-done | bytes 2359328 | tf_op jit(solution)/shard_map/ppermute | solution.py:19
  199.2 2.5 %fusion.28 = f32[3,512,128]{1,2,0:T(8,128)S(1)} fusion(bf16[3,512,768]{2,1,0:T(8,128)(2,1)} %bitcast.35, bf16[3,128,768]{2,1,0:T(8,128)(2,1)S(1)} %bitcast.118), kind=kOutput, calls=%fused_computation.102 | convolution fusion | flops 301989888 | bytes 3735552 | tf_op jit(solution)/shard_map/knr,kmr->knm/dot_general | solution.py:77
  204.8 7.8 %collective-permute-done.28 = f32[3,2,64,128]{3,2,1,0:T(8,128)S(1)} collective-permute-done((f32[3,2,64,128]{3,2,1,0:T(8,128)S(1)}, f32[3,2,64,128]{3,2,1,0:T(8,128)S(1)}, u32[]{:S(2)}, u32[]{:S(2)}) %collective-permute-start.28) | collective-permute-done | bytes 196640 | tf_op jit(solution)/shard_map/ppermute | solution.py:19
  213.0 3.1 %collective-permute-start.31 = (f32[3,32,128]{2,1,0:T(8,128)S(1)}, f32[3,32,128]{2,1,0:T(8,128)S(1)}, u32[]{:S(2)}, u32[]{:S(2)}) collective-permute-start(f32[3,32,128]{2,1,0:T(8,128)S(1)} %get-tuple-element.48), channel_id=1, source_target_pairs={{0,12},{1,13},{2,14},{3,15},{4,8},{5,9},{6,10},{7,11},{8,4},{9,5},... | collective-permute-start | bytes 147464 | tf_op jit(solution)/shard_map/ppermute | solution.py:19
  (108 shorter events, 44.1 us)
Async XLA Ops:
  7.2 139.3 %all-gather.3.cloned.1.call-start = ((), (), s32[]{:S(2)}) async-start(), calls=%async_computation | async-start | bytes 2654208 | tf_op jit(solution)/shard_map/all_gather | solution.py:128
  9.1 17.3 %collective-permute-start = (bf16[3,64,768]{2,1,0:T(8,128)(2,1)S(1)}, bf16[3,64,768]{2,1,0:T(8,128)(2,1)S(1)}, u32[]{:S(2)}, u32[]{:S(2)}) collective-permute-start(bf16[3,64,768]{2,1,0:T(8,128)(2,1)S(1)} %multiply_bitcast_fusion), channel_id=1, source_target_pairs={{0,0},{1,1},{2,2},{3,3},{4,4},{5,5},{6,6},{7,7},{8,128},{9,129},{1... | collective-permute-start | bytes 884744 | tf_op jit(solution)/shard_map/ppermute | solution.py:19
  13.5 16.8 %collective-permute-start.1 = (bf16[3,64,768]{2,1,0:T(8,128)(2,1)S(1)}, bf16[3,64,768]{2,1,0:T(8,128)(2,1)S(1)}, u32[]{:S(2)}, u32[]{:S(2)}) collective-permute-start(bf16[3,64,768]{2,1,0:T(8,128)(2,1)S(1)} %multiply_bitcast_fusion), channel_id=1, source_target_pairs={{0,2},{1,3},{2,0},{3,1},{4,6},{5,7},{6,4},{7,5},{8,130},{9,131},{1... | collective-permute-start | bytes 884744 | tf_op jit(solution)/shard_map/ppermute | solution.py:19
  17.3 15.3 %collective-permute-start.2 = (bf16[3,64,768]{2,1,0:T(8,128)(2,1)S(1)}, bf16[3,64,768]{2,1,0:T(8,128)(2,1)S(1)}, u32[]{:S(2)}, u32[]{:S(2)}) collective-permute-start(bf16[3,64,768]{2,1,0:T(8,128)(2,1)S(1)} %multiply_bitcast_fusion), channel_id=1, source_target_pairs={{0,0},{1,17},{2,34},{3,51},{4,68},{5,85},{6,102},{7,119},{8,8},{9,... | collective-permute-start | bytes 884744 | tf_op jit(solution)/shard_map/ppermute | solution.py:19
  32.7 11.8 %collective-permute-start.3 = (bf16[3,2,64,768]{3,2,0,1:T(8,128)(2,1)S(1)}, bf16[3,2,64,768]{3,2,0,1:T(8,128)(2,1)S(1)}, u32[]{:S(2)}, u32[]{:S(2)}) collective-permute-start(bf16[3,2,64,768]{3,2,0,1:T(8,128)(2,1)S(1)} %pad_maximum_fusion.3), channel_id=1, source_target_pairs={{0,4},{1,5},{2,6},{3,7},{4,8},{5,9},{6,10},{7,11},{8,12},{9,13},{1... | collective-permute-start | bytes 1769480 | tf_op jit(solution)/shard_map/ppermute | solution.py:19
  32.8 13.7 %collective-permute-start.5 = (bf16[3,2,64,768]{3,2,0,1:T(8,128)(2,1)S(1)}, bf16[3,2,64,768]{3,2,0,1:T(8,128)(2,1)S(1)}, u32[]{:S(2)}, u32[]{:S(2)}) collective-permute-start(bf16[3,2,64,768]{3,2,0,1:T(8,128)(2,1)S(1)} %pad_maximum_fusion.3), channel_id=1, source_target_pairs={{0,12},{1,13},{2,14},{3,15},{4,0},{5,1},{6,2},{7,3},{8,4},{9,5},{1... | collective-permute-start | bytes 1769480 | tf_op jit(solution)/shard_map/ppermute | solution.py:19
  44.5 7.7 %collective-permute-start.4 = (bf16[3,1,64,768]{3,2,0,1:T(8,128)(2,1)S(1)}, bf16[3,1,64,768]{3,2,0,1:T(8,128)(2,1)S(1)}, u32[]{:S(2)}, u32[]{:S(2)}) collective-permute-start(bf16[3,1,64,768]{3,2,0,1:T(8,128)(2,1)S(1)} %slice.154), channel_id=1, source_target_pairs={{0,4},{1,5},{2,6},{3,7},{4,8},{5,9},{6,10},{7,11},{8,12},{9,13},{1... | collective-permute-start | bytes 884744 | tf_op jit(solution)/shard_map/ppermute | solution.py:19
  45.5 31.7 %collective-permute-start.7 = (bf16[768,768]{1,0:T(8,128)(2,1)}, bf16[768,768]{1,0:T(8,128)(2,1)}, u32[]{:S(2)}, u32[]{:S(2)}) collective-permute-start(bf16[768,768]{1,0:T(8,128)(2,1)} %param.4), channel_id=1, source_target_pairs={{0,128},{1,129},{2,130},{3,131},{4,132},{5,133},{6,134},{7,135},{8... | collective-permute-start | bytes 3538952 | tf_op jit(solution)/shard_map/ppermute | solution.py:19
  46.6 8.4 %collective-permute-start.6 = (bf16[3,1,64,768]{3,2,0,1:T(8,128)(2,1)S(1)}, bf16[3,1,64,768]{3,2,0,1:T(8,128)(2,1)S(1)}, u32[]{:S(2)}, u32[]{:S(2)}) collective-permute-start(bf16[3,1,64,768]{3,2,0,1:T(8,128)(2,1)S(1)} %slice.155), channel_id=1, source_target_pairs={{0,12},{1,13},{2,14},{3,15},{4,0},{5,1},{6,2},{7,3},{8,4},{9,5},{1... | collective-permute-start | bytes 884744 | tf_op jit(solution)/shard_map/ppermute | solution.py:19
  46.9 14.2 %collective-permute-start.8 = (bf16[3,64,768]{2,1,0:T(8,128)(2,1)S(1)}, bf16[3,64,768]{2,1,0:T(8,128)(2,1)S(1)}, u32[]{:S(2)}, u32[]{:S(2)}) collective-permute-start(bf16[3,64,768]{2,1,0:T(8,128)(2,1)S(1)} %collective-permute-done.2), channel_id=1, source_target_pairs={{0,0},{1,1},{2,2},{3,3},{4,4},{5,5},{6,6},{7,7},{8,128},{9,129},{1... | collective-permute-start | bytes 884744 | tf_op jit(solution)/shard_map/ppermute | solution.py:19
  77.2 7.9 %collective-permute-start.9 = (bf16[2,3,2,2,64,768]{5,4,1,3,2,0:T(8,128)(2,1)S(1)}, bf16[2,3,2,2,64,768]{5,4,1,3,2,0:T(8,128)(2,1)}, u32[]{:S(2)}, u32[]{:S(2)}) collective-permute-start(bf16[2,3,2,2,64,768]{5,4,1,3,2,0:T(8,128)(2,1)S(1)} %pad_maximum_fusion.1), channel_id=1, source_target_pairs={{0,1},{1,0},{2,3},{3,2},{4,5},{5,4},{6,7},{7,6},{8,9},{9,8},{10,11... | collective-permute-start | bytes 7077896 | tf_op jit(solution)/shard_map/ppermute | solution.py:19
  95.3 16.2 %collective-permute-start.14 = (f32[3,16,768]{2,1,0:T(8,128)S(1)}, f32[3,16,768]{2,1,0:T(8,128)S(1)}, u32[]{:S(2)}, u32[]{:S(2)}) collective-permute-start(f32[3,16,768]{2,1,0:T(8,128)S(1)} %get-tuple-element.39), channel_id=1, source_target_pairs={{0,16},{1,17},{2,18},{3,19},{4,20},{5,21},{6,22},{7,23},{8,24},{9,... | collective-permute-start | bytes 442376 | tf_op jit(solution)/shard_map/ppermute | solution.py:19
  104.9 9.3 %collective-permute-start.10 = (f32[3,16,768]{2,1,0:T(8,128)S(1)}, f32[3,16,768]{2,1,0:T(8,128)S(1)}, u32[]{:S(2)}, u32[]{:S(2)}) collective-permute-start(f32[3,16,768]{2,1,0:T(8,128)S(1)} %get-tuple-element.38), channel_id=1, source_target_pairs={{0,112},{1,113},{2,114},{3,115},{4,116},{5,117},{6,118},{7,119},{8... | collective-permute-start | bytes 442376 | tf_op jit(solution)/shard_map/ppermute | solution.py:19
  105.0 16.7 %collective-permute-start.22 = (f32[3,16,768]{2,1,0:T(8,128)S(1)}, f32[3,16,768]{2,1,0:T(8,128)S(1)}, u32[]{:S(2)}, u32[]{:S(2)}) collective-permute-start(f32[3,16,768]{2,1,0:T(8,128)S(1)} %get-tuple-element.45), channel_id=1, source_target_pairs={{0,16},{1,17},{2,18},{3,19},{4,20},{5,21},{6,22},{7,23},{8,24},{9,... | collective-permute-start | bytes 442376 | tf_op jit(solution)/shard_map/ppermute | solution.py:19
  107.1 12.1 %collective-permute-start.18 = (f32[3,16,768]{2,1,0:T(8,128)S(1)}, f32[3,16,768]{2,1,0:T(8,128)S(1)}, u32[]{:S(2)}, u32[]{:S(2)}) collective-permute-start(f32[3,16,768]{2,1,0:T(8,128)S(1)} %get-tuple-element.44), channel_id=1, source_target_pairs={{0,112},{1,113},{2,114},{3,115},{4,116},{5,117},{6,118},{7,119},{8... | collective-permute-start | bytes 442376 | tf_op jit(solution)/shard_map/ppermute | solution.py:19
  111.6 34.9 %collective-permute-start.15 = (f32[3,32,768]{2,1,0:T(8,128)S(1)}, f32[3,32,768]{2,1,0:T(8,128)}, u32[]{:S(2)}, u32[]{:S(2)}) collective-permute-start(f32[3,32,768]{2,1,0:T(8,128)S(1)} %pad_maximum_fusion.7), channel_id=1, source_target_pairs={{0,16},{1,17},{2,18},{3,19},{4,20},{5,21},{6,22},{7,23},{8,24},{9,... | collective-permute-start | bytes 884744 | tf_op jit(solution)/shard_map/ppermute | solution.py:19
  114.2 17.6 %collective-permute-start.11 = (f32[3,32,768]{2,1,0:T(8,128)S(1)}, f32[3,32,768]{2,1,0:T(8,128)S(1)}, u32[]{:S(2)}, u32[]{:S(2)}) collective-permute-start(f32[3,32,768]{2,1,0:T(8,128)S(1)} %pad_maximum_fusion.6), channel_id=1, source_target_pairs={{0,112},{1,113},{2,114},{3,115},{4,116},{5,117},{6,118},{7,119},{8... | collective-permute-start | bytes 884744 | tf_op jit(solution)/shard_map/ppermute | solution.py:19
  119.3 23.6 %collective-permute-start.19 = (f32[3,32,768]{2,1,0:T(8,128)S(1)}, f32[3,32,768]{2,1,0:T(8,128)S(1)}, u32[]{:S(2)}, u32[]{:S(2)}) collective-permute-start(f32[3,32,768]{2,1,0:T(8,128)S(1)} %pad_maximum_fusion.8), channel_id=1, source_target_pairs={{0,112},{1,113},{2,114},{3,115},{4,116},{5,117},{6,118},{7,119},{8... | collective-permute-start | bytes 884744 | tf_op jit(solution)/shard_map/ppermute | solution.py:19
  131.8 17.5 %collective-permute-start.12 = (f32[3,32,768]{2,1,0:T(8,128)S(1)}, f32[3,32,768]{2,1,0:T(8,128)}, u32[]{:S(2)}, u32[]{:S(2)}) collective-permute-start(f32[3,32,768]{2,1,0:T(8,128)S(1)} %bitcast_add_fusion.7), channel_id=1, source_target_pairs={{0,112},{1,113},{2,114},{3,115},{4,116},{5,117},{6,118},{7,119},{8... | collective-permute-start | bytes 884744 | tf_op jit(solution)/shard_map/ppermute | solution.py:19
  134.4 19.2 %collective-permute-start.23 = (f32[3,32,768]{2,1,0:T(8,128)S(1)}, f32[3,32,768]{2,1,0:T(8,128)}, u32[]{:S(2)}, u32[]{:S(2)}) collective-permute-start(f32[3,32,768]{2,1,0:T(8,128)S(1)} %pad_maximum_fusion.9), channel_id=1, source_target_pairs={{0,16},{1,17},{2,18},{3,19},{4,20},{5,21},{6,22},{7,23},{8,24},{9,... | collective-permute-start | bytes 884744 | tf_op jit(solution)/shard_map/ppermute | solution.py:19
  143.0 12.3 %collective-permute-start.20 = (f32[3,32,768]{2,1,0:T(8,128)S(1)}, f32[3,32,768]{2,1,0:T(8,128)}, u32[]{:S(2)}, u32[]{:S(2)}) collective-permute-start(f32[3,32,768]{2,1,0:T(8,128)S(1)} %bitcast_add_fusion.2), channel_id=1, source_target_pairs={{0,112},{1,113},{2,114},{3,115},{4,116},{5,117},{6,118},{7,119},{8... | collective-permute-start | bytes 884744 | tf_op jit(solution)/shard_map/ppermute | solution.py:19
  146.5 52.7 %collective-permute-start.26 = (bf16[3,8,64,768]{3,2,1,0:T(8,128)(2,1)}, bf16[3,8,64,768]{3,2,1,0:T(8,128)(2,1)}, u32[]{:S(2)}, u32[]{:S(2)}) collective-permute-start(bf16[3,8,64,768]{3,2,1,0:T(8,128)(2,1)} %bitcast.124), channel_id=1, source_target_pairs={{0,128},{1,129},{2,130},{3,131},{4,132},{5,133},{6,134},{7,135},{8... | collective-permute-start | bytes 7077896 | tf_op jit(solution)/shard_map/ppermute | solution.py:19
  151.5 10.9 %collective-permute-start.16 = (f32[3,32,768]{2,1,0:T(8,128)}, f32[3,32,768]{2,1,0:T(8,128)S(1)}, u32[]{:S(2)}, u32[]{:S(2)}) collective-permute-start(f32[3,32,768]{2,1,0:T(8,128)} %get-tuple-element.19), channel_id=1, source_target_pairs={{0,16},{1,17},{2,18},{3,19},{4,20},{5,21},{6,22},{7,23},{8,24},{9,... | collective-permute-start | bytes 884744 | tf_op jit(solution)/shard_map/ppermute | solution.py:19
  157.1 11.6 %collective-permute-start.24 = (f32[3,32,768]{2,1,0:T(8,128)S(1)}, f32[3,32,768]{2,1,0:T(8,128)S(1)}, u32[]{:S(2)}, u32[]{:S(2)}) collective-permute-start(f32[3,32,768]{2,1,0:T(8,128)S(1)} %get-tuple-element.24), channel_id=1, source_target_pairs={{0,16},{1,17},{2,18},{3,19},{4,20},{5,21},{6,22},{7,23},{8,24},{9,... | collective-permute-start | bytes 884744 | tf_op jit(solution)/shard_map/ppermute | solution.py:19
  159.2 10.3 %collective-permute-start.13 = (f32[3,32,768]{2,1,0:T(8,128)}, f32[3,32,768]{2,1,0:T(8,128)}, u32[]{:S(2)}, u32[]{:S(2)}) collective-permute-start(f32[3,32,768]{2,1,0:T(8,128)} %get-tuple-element.18), channel_id=1, source_target_pairs={{0,112},{1,113},{2,114},{3,115},{4,116},{5,117},{6,118},{7,119},{8... | collective-permute-start | bytes 884744 | tf_op jit(solution)/shard_map/ppermute | solution.py:19
  163.3 11.7 %collective-permute-start.17 = (f32[3,32,768]{2,1,0:T(8,128)S(1)}, f32[3,32,768]{2,1,0:T(8,128)}, u32[]{:S(2)}, u32[]{:S(2)}) collective-permute-start(f32[3,32,768]{2,1,0:T(8,128)S(1)} %bitcast_add_fusion.6), channel_id=1, source_target_pairs={{0,16},{1,17},{2,18},{3,19},{4,20},{5,21},{6,22},{7,23},{8,24},{9,... | collective-permute-start | bytes 884744 | tf_op jit(solution)/shard_map/ppermute | solution.py:19
  163.5 12.8 %collective-permute-start.21 = (f32[3,32,768]{2,1,0:T(8,128)}, f32[3,32,768]{2,1,0:T(8,128)}, u32[]{:S(2)}, u32[]{:S(2)}) collective-permute-start(f32[3,32,768]{2,1,0:T(8,128)} %get-tuple-element.23), channel_id=1, source_target_pairs={{0,112},{1,113},{2,114},{3,115},{4,116},{5,117},{6,118},{7,119},{8... | collective-permute-start | bytes 884744 | tf_op jit(solution)/shard_map/ppermute | solution.py:19
  168.7 12.3 %collective-permute-start.25 = (f32[3,32,768]{2,1,0:T(8,128)S(1)}, f32[3,32,768]{2,1,0:T(8,128)}, u32[]{:S(2)}, u32[]{:S(2)}) collective-permute-start(f32[3,32,768]{2,1,0:T(8,128)S(1)} %bitcast_add_fusion.1), channel_id=1, source_target_pairs={{0,16},{1,17},{2,18},{3,19},{4,20},{5,21},{6,22},{7,23},{8,24},{9,... | collective-permute-start | bytes 884744 | tf_op jit(solution)/shard_map/ppermute | solution.py:19
  204.1 8.5 %collective-permute-start.28 = (f32[3,2,64,128]{3,2,1,0:T(8,128)S(1)}, f32[3,2,64,128]{3,2,1,0:T(8,128)S(1)}, u32[]{:S(2)}, u32[]{:S(2)}) collective-permute-start(f32[3,2,64,128]{3,2,1,0:T(8,128)S(1)} %slice_bitcast_fusion.2), channel_id=1, source_target_pairs={{0,2},{1,3},{2,0},{3,1},{4,6},{5,7},{6,4},{7,5},{8,10},{9,11},{10,... | collective-permute-start | bytes 589832 | tf_op jit(solution)/shard_map/ppermute | solution.py:19
  212.9 5.8 %collective-permute-start.30 = (f32[3,32,128]{2,1,0:T(8,128)S(1)}, f32[3,32,128]{2,1,0:T(8,128)S(1)}, u32[]{:S(2)}, u32[]{:S(2)}) collective-permute-start(f32[3,32,128]{2,1,0:T(8,128)S(1)} %get-tuple-element.49), channel_id=1, source_target_pairs={{0,8},{1,9},{2,10},{3,11},{4,12},{5,13},{6,14},{7,15},{8,0},{9,1},... | collective-permute-start | bytes 147464 | tf_op jit(solution)/shard_map/ppermute | solution.py:19
  213.0 5.9 %collective-permute-start.31 = (f32[3,32,128]{2,1,0:T(8,128)S(1)}, f32[3,32,128]{2,1,0:T(8,128)S(1)}, u32[]{:S(2)}, u32[]{:S(2)}) collective-permute-start(f32[3,32,128]{2,1,0:T(8,128)S(1)} %get-tuple-element.48), channel_id=1, source_target_pairs={{0,12},{1,13},{2,14},{3,15},{4,8},{5,9},{6,10},{7,11},{8,4},{9,5},... | collective-permute-start | bytes 147464 | tf_op jit(solution)/shard_map/ppermute | solution.py:19
  216.3 4.2 %collective-permute-start.29 = (f32[3,32,128]{2,1,0:T(8,128)S(1)}, f32[3,32,128]{2,1,0:T(8,128)S(1)}, u32[]{:S(2)}, u32[]{:S(2)}) collective-permute-start(f32[3,32,128]{2,1,0:T(8,128)S(1)} %fusion.15), channel_id=1, source_target_pairs={{0,4},{1,5},{2,6},{3,7},{4,0},{5,1},{6,2},{7,3},{8,12},{9,13},{10,... | collective-permute-start | bytes 147464 | tf_op jit(solution)/shard_map/ppermute | solution.py:19
  (5 other events, 72.1 us)
Sparse Core Ops, SparseCore 0:
  81.0 61.6 all-gather.2

commit v6 on v5

--- a/solution.py
+++ b/solution.py
@@ -73,15 +73,16 @@
     return jnp.where(first, near, far), jnp.where(first, far, near)
 
 
+def together(*values):
+    return lax.optimization_barrier(values)
+
+
 def dot_each(a, b):
     return jnp.einsum("knr,kmr->knm", a, b, preferred_element_type=jnp.float32)
 
 
-def spread_rows(place, near, far):
+def spread_rows(place, plane, left, right, opposite):
     yl, x, yh = place
-    plane = jnp.stack(ordered(yh == 0, near, far), axis=1)
-    left, right = send(plane, along_x(1)), send(plane, along_x(3))
-    opposite = [send(left[:, :1], along_x(1)), send(right[:, 1:], along_x(3))]
     opposite = jnp.concatenate(opposite, axis=1)
     here = ordered((x // 2) == yl, plane, opposite)
     there = ordered(((x + 3) % 4 // 2) == yl, left, right)
@@ -119,14 +120,20 @@
     keep_rows = row_mask(pattern, row, per).astype(jnp.bfloat16)
     keep_cols = row_mask(pattern, col, per).astype(jnp.float32)
     own = factor_panel.transpose(0, 2, 1) * keep_rows[:, None, :]
-    beside = send(ancestor_inverse, across)
+    cuts = rows // 3, rows * 5 // 6
+    beside = [send(piece, across) for piece in jnp.split(ancestor_inverse, cuts)]
     near, far = send(own, swap), send(own, swap_far)
-    near, far, turned = lax.optimization_barrier((near, far, send(own, skewed)))
-    mine = spread_rows((yl, x, yh), near, far)
+    near, far, turned, beside[0] = together(near, far, send(own, skewed), beside[0])
+    plane = jnp.stack(ordered(yh == 0, near, far), axis=1)
+    left, right = send(plane, along_x(1)), send(plane, along_x(3))
     turned = send(turned, facing_place)
-    mine, beside, _ = lax.optimization_barrier((mine, beside, turned))
+    left, right, turned, beside[1] = together(left, right, turned, beside[1])
     facing = lax.all_gather(turned, "z", axis=1)
     facing = [facing, send(facing, across)]
+    opposite = send(left[:, :1], along_x(1)), send(right[:, 1:], along_x(3))
+    *opposite, beside[2] = together(*opposite, beside[2])
+    beside = jnp.concatenate(beside)
+    mine = spread_rows((yl, x, yh), plane, left, right, opposite)
     panel = spread_cores(core, mine).reshape(2, count * 8 * cols, rows)
     partial = dot_nt(panel[0], ancestor_inverse) + dot_nt(panel[1], beside)
     partial = partial.reshape(count, 8, cols, rows)

time: 229 us -> 219 us (0.956); the launches traced: 228 us -> 216 us
  waiting for transfers between devices: 116 us -> 102 us
  local copies, waits for them, and re-layouts: 1.78 us -> 5.93 us
  starting transfers between devices: 70.9 us -> 67.6 us
    ppermute x32 -> x34, waiting for transfers between devices: 116 us -> 102 us  [send(): return lax.ppermute(value, AXES, pairs(move))]
    ppermute x32 -> x34, starting transfers between devices: 70.8 us -> 67.5 us  [send(): return lax.ppermute(value, AXES, pairs(move))]
    split x0 -> x3, local copies, waits for them, and re-layouts: none -> 2.83 us  [shards(): jnp.split(ancestor_inverse, cuts)]
  transfers between devices with their start and end apart: 33 -> 35, of which waited for: 24 -> 22; matrix products, arithmetic and copies ran while one was open for 9% -> 11% of each run, Pallas kernels for 0% -> 0%
where the time goes in v6:
time: 219 us; the launch traced here: 216 us
  waiting for transfers between devices  102 us (47%)
  starting transfers between devices  67.6 us (31%)
  other arithmetic  17 us (8%)
  between operations  14.5 us (7%)
  matrix products  8.68 us (4%)
  local copies, waits for them, and re-layouts  5.93 us (3%)
    ppermute x34, waiting for transfers between devices, send(): return lax.ppermute(value, AXES, pairs(move))  102 us
    ppermute x34, starting transfers between devices, send(): return lax.ppermute(value, AXES, pairs(move))  67.5 us
    dot_general x2, matrix products, dot_nt(): return lax.dot_general(a, b, NT, preferred_element_type=jnp.float32)  5.25 us
    add x6, other arithmetic, sum_over_z(): down, up = (block(-offset) + down, block(offset) + up)  5.05 us
  transfers between devices with their start and end apart: 35, of which 22 were waited for; matrix products, arithmetic and copies ran while one was open for 11% of the time, Pallas kernels for 0%

profile of v6, /device:TPU:6, one launch (start us, length us, event | category | flops | bytes accessed | tf_op | source)
XLA Modules:
  0.0 215.7 jit_solution(17323783643800428131)
XLA Ops:
  11.8 3.3 %collective-permute-start = (bf16[3,64,768]{2,1,0:T(8,128)(2,1)S(1)}, bf16[3,64,768]{2,1,0:T(8,128)(2,1)S(1)}, u32[]{:S(2)}, u32[]{:S(2)}) collective-permute-start(bf16[3,64,768]{2,1,0:T(8,128)(2,1)S(1)} %multiply_bitcast_fusion), channel_id=1, source_target_pairs={{0,0},{1,1},{2,2},{3,3},{4,4},{5,5},{6,6},{7,7},{8,128},{9,129},{1... | collective-permute-start | bytes 884744 | tf_op jit(solution)/shard_map/ppermute | solution.py:19
  15.2 4.7 %collective-permute-start.1 = (bf16[3,64,768]{2,1,0:T(8,128)(2,1)S(1)}, bf16[3,64,768]{2,1,0:T(8,128)(2,1)S(1)}, u32[]{:S(2)}, u32[]{:S(2)}) collective-permute-start(bf16[3,64,768]{2,1,0:T(8,128)(2,1)S(1)} %multiply_bitcast_fusion), channel_id=1, source_target_pairs={{0,2},{1,3},{2,0},{3,1},{4,6},{5,7},{6,4},{7,5},{8,130},{9,131},{1... | collective-permute-start | bytes 884744 | tf_op jit(solution)/shard_map/ppermute | solution.py:19
  19.8 9.1 %collective-permute-start.2 = (bf16[3,64,768]{2,1,0:T(8,128)(2,1)S(1)}, bf16[3,64,768]{2,1,0:T(8,128)(2,1)}, u32[]{:S(2)}, u32[]{:S(2)}) collective-permute-start(bf16[3,64,768]{2,1,0:T(8,128)(2,1)S(1)} %multiply_bitcast_fusion), channel_id=1, source_target_pairs={{0,0},{1,17},{2,34},{3,51},{4,68},{5,85},{6,102},{7,119},{8,8},{9,... | collective-permute-start | bytes 884744 | tf_op jit(solution)/shard_map/ppermute | solution.py:19
  30.1 2.4 %collective-permute-done.1 = bf16[3,64,768]{2,1,0:T(8,128)(2,1)S(1)} collective-permute-done((bf16[3,64,768]{2,1,0:T(8,128)(2,1)S(1)}, bf16[3,64,768]{2,1,0:T(8,128)(2,1)S(1)}, u32[]{:S(2)}, u32[]{:S(2)}) %collective-permute-start.1) | collective-permute-done | bytes 294944 | tf_op jit(solution)/shard_map/ppermute | solution.py:19
  32.5 2.7 %collective-permute-done.2 = bf16[3,64,768]{2,1,0:T(8,128)(2,1)} collective-permute-done((bf16[3,64,768]{2,1,0:T(8,128)(2,1)S(1)}, bf16[3,64,768]{2,1,0:T(8,128)(2,1)}, u32[]{:S(2)}, u32[]{:S(2)}) %collective-permute-start.2) | collective-permute-done | bytes 294944 | tf_op jit(solution)/shard_map/ppermute | solution.py:19
  38.2 2.9 %collective-permute-start.6 = (bf16[3,64,768]{2,1,0:T(8,128)(2,1)}, bf16[3,64,768]{2,1,0:T(8,128)(2,1)}, u32[]{:S(2)}, u32[]{:S(2)}) collective-permute-start(bf16[3,64,768]{2,1,0:T(8,128)(2,1)} %collective-permute-done.2), channel_id=1, source_target_pairs={{0,0},{1,1},{2,2},{3,3},{4,4},{5,5},{6,6},{7,7},{8,128},{9,129},{1... | collective-permute-start | bytes 884744 | tf_op jit(solution)/shard_map/ppermute | solution.py:19
  41.1 3.5 %collective-permute-done.7 = bf16[384,768]{1,0:T(8,128)(2,1)} collective-permute-done((bf16[384,768]{1,0:T(8,128)(2,1)S(1)}, bf16[384,768]{1,0:T(8,128)(2,1)}, u32[]{:S(2)}, u32[]{:S(2)}) %collective-permute-start.7) | collective-permute-done | bytes 589856 | tf_op jit(solution)/shard_map/ppermute | solution.py:19
  44.6 11.6 %collective-permute-done.6 = bf16[3,64,768]{2,1,0:T(8,128)(2,1)} collective-permute-done((bf16[3,64,768]{2,1,0:T(8,128)(2,1)}, bf16[3,64,768]{2,1,0:T(8,128)(2,1)}, u32[]{:S(2)}, u32[]{:S(2)}) %collective-permute-start.6) | collective-permute-done | bytes 294944 | tf_op jit(solution)/shard_map/ppermute | solution.py:19
  61.2 5.1 %collective-permute-done.10 = bf16[128,768]{1,0:T(8,128)(2,1)} collective-permute-done((bf16[128,768]{1,0:T(8,128)(2,1)}, bf16[128,768]{1,0:T(8,128)(2,1)}, u32[]{:S(2)}, u32[]{:S(2)}) %collective-permute-start.10) | collective-permute-done | bytes 196640 | tf_op jit(solution)/shard_map/ppermute | solution.py:19
  68.5 2.4 %collective-permute-start.11 = (bf16[2,3,2,2,64,768]{5,4,1,3,2,0:T(8,128)(2,1)}, bf16[2,3,2,2,64,768]{5,4,1,3,2,0:T(8,128)(2,1)}, u32[]{:S(2)}, u32[]{:S(2)}) collective-permute-start(bf16[2,3,2,2,64,768]{5,4,1,3,2,0:T(8,128)(2,1)} %pad_maximum_fusion.1), channel_id=1, source_target_pairs={{0,1},{1,0},{2,3},{3,2},{4,5},{5,4},{6,7},{7,6},{8,9},{9,8},{10,11... | collective-permute-start | bytes 7077896 | tf_op jit(solution)/shard_map/ppermute | solution.py:19
  70.9 4.5 %collective-permute-done.11 = bf16[2,3,2,2,64,768]{5,4,1,3,2,0:T(8,128)(2,1)} collective-permute-done((bf16[2,3,2,2,64,768]{5,4,1,3,2,0:T(8,128)(2,1)}, bf16[2,3,2,2,64,768]{5,4,1,3,2,0:T(8,128)(2,1)}, u32[]{:S(2)}, u32[]{:S(2)}) %collective-permute-start.11) | collective-permute-done | bytes 2359328 | tf_op jit(solution)/shard_map/ppermute | solution.py:19
  80.2 3.2 %convolution_add_fusion = f32[1536,768]{1,0:T(8,128)S(1)} fusion(f32[1536,768]{1,0:T(8,128)S(1)} %fusion.32, bf16[1536,768]{1,0:T(8,128)(2,1)S(1)} %bitcast.124, bf16[128,768]{1,0:T(8,128)(2,1)} %collective-permute-done.10, bf16[384,768]{1,0:T(8,128)(2,1)} %collective-permute-done.7, bf16[256,768]{1,0:T(8,128)(2,1)S(1)} %copy-done.5), kind=kOutput, calls=%fused_computation.2 | convolution fusion | flops 1816657920 | bytes 12976128 | tf_op jit(solution)/shard_map/dot_general | solution.py:69
  84.0 9.1 %collective-permute-start.16 = (f32[3,16,768]{2,1,0:T(8,128)S(1)}, f32[3,16,768]{2,1,0:T(8,128)S(1)}, u32[]{:S(2)}, u32[]{:S(2)}) collective-permute-start(f32[3,16,768]{2,1,0:T(8,128)S(1)} %get-tuple-element.51), channel_id=1, source_target_pairs={{0,16},{1,17},{2,18},{3,19},{4,20},{5,21},{6,22},{7,23},{8,24},{9,... | collective-permute-start | bytes 442376 | tf_op jit(solution)/shard_map/ppermute | solution.py:19
  93.2 2.1 collective-permute-start.24
  96.5 3.5 %collective-permute-done.16 = f32[3,16,768]{2,1,0:T(8,128)S(1)} collective-permute-done((f32[3,16,768]{2,1,0:T(8,128)S(1)}, f32[3,16,768]{2,1,0:T(8,128)S(1)}, u32[]{:S(2)}, u32[]{:S(2)}) %collective-permute-start.16) | collective-permute-done | bytes 147488 | tf_op jit(solution)/shard_map/ppermute | solution.py:19
  100.1 2.6 %collective-permute-start.17 = (f32[3,32,768]{2,1,0:T(8,128)S(1)}, f32[3,32,768]{2,1,0:T(8,128)}, u32[]{:S(2)}, u32[]{:S(2)}) collective-permute-start(f32[3,32,768]{2,1,0:T(8,128)S(1)} %pad_maximum_fusion.7), channel_id=1, source_target_pairs={{0,16},{1,17},{2,18},{3,19},{4,20},{5,21},{6,22},{7,23},{8,24},{9,... | collective-permute-start | bytes 884744 | tf_op jit(solution)/shard_map/ppermute | solution.py:19
  103.7 3.8 %collective-permute-done.20 = f32[3,16,768]{2,1,0:T(8,128)S(1)} collective-permute-done((f32[3,16,768]{2,1,0:T(8,128)S(1)}, f32[3,16,768]{2,1,0:T(8,128)S(1)}, u32[]{:S(2)}, u32[]{:S(2)}) %collective-permute-start.20) | collective-permute-done | bytes 147488 | tf_op jit(solution)/shard_map/ppermute | solution.py:19
  107.6 2.4 %collective-permute-start.21 = (f32[3,32,768]{2,1,0:T(8,128)S(1)}, f32[3,32,768]{2,1,0:T(8,128)S(1)}, u32[]{:S(2)}, u32[]{:S(2)}) collective-permute-start(f32[3,32,768]{2,1,0:T(8,128)S(1)} %pad_maximum_fusion.8), channel_id=1, source_target_pairs={{0,112},{1,113},{2,114},{3,115},{4,116},{5,117},{6,118},{7,119},{8... | collective-permute-start | bytes 884744 | tf_op jit(solution)/shard_map/ppermute | solution.py:19
  110.1 10.1 %collective-permute-done.13 = f32[3,32,768]{2,1,0:T(8,128)S(1)} collective-permute-done((f32[3,32,768]{2,1,0:T(8,128)S(1)}, f32[3,32,768]{2,1,0:T(8,128)S(1)}, u32[]{:S(2)}, u32[]{:S(2)}) %collective-permute-start.13) | collective-permute-done | bytes 294944 | tf_op jit(solution)/shard_map/ppermute | solution.py:19
  120.2 2.5 %collective-permute-start.14 = (f32[3,32,768]{2,1,0:T(8,128)S(1)}, f32[3,32,768]{2,1,0:T(8,128)}, u32[]{:S(2)}, u32[]{:S(2)}) collective-permute-start(f32[3,32,768]{2,1,0:T(8,128)S(1)} %bitcast_add_fusion.7), channel_id=1, source_target_pairs={{0,112},{1,113},{2,114},{3,115},{4,116},{5,117},{6,118},{7,119},{8... | collective-permute-start | bytes 884744 | tf_op jit(solution)/shard_map/ppermute | solution.py:19
  122.8 9.6 %collective-permute-done.21 = f32[3,32,768]{2,1,0:T(8,128)S(1)} collective-permute-done((f32[3,32,768]{2,1,0:T(8,128)S(1)}, f32[3,32,768]{2,1,0:T(8,128)S(1)}, u32[]{:S(2)}, u32[]{:S(2)}) %collective-permute-start.21) | collective-permute-done | bytes 294944 | tf_op jit(solution)/shard_map/ppermute | solution.py:19
  132.4 3.1 %collective-permute-start.22 = (f32[3,32,768]{2,1,0:T(8,128)S(1)}, f32[3,32,768]{2,1,0:T(8,128)}, u32[]{:S(2)}, u32[]{:S(2)}) collective-permute-start(f32[3,32,768]{2,1,0:T(8,128)S(1)} %bitcast_add_fusion.2), channel_id=1, source_target_pairs={{0,112},{1,113},{2,114},{3,115},{4,116},{5,117},{6,118},{7,119},{8... | collective-permute-start | bytes 884744 | tf_op jit(solution)/shard_map/ppermute | solution.py:19
  138.8 2.1 bitcast_add_fusion.8
  142.2 2.6 %collective-permute-done.22 = f32[3,32,768]{2,1,0:T(8,128)} collective-permute-done((f32[3,32,768]{2,1,0:T(8,128)S(1)}, f32[3,32,768]{2,1,0:T(8,128)}, u32[]{:S(2)}, u32[]{:S(2)}) %collective-permute-start.22) | collective-permute-done | bytes 294944 | tf_op jit(solution)/shard_map/ppermute | solution.py:19
  152.4 3.0 %collective-permute-start.23 = (f32[3,32,768]{2,1,0:T(8,128)}, f32[3,32,768]{2,1,0:T(8,128)}, u32[]{:S(2)}, u32[]{:S(2)}) collective-permute-start(f32[3,32,768]{2,1,0:T(8,128)} %get-tuple-element.35), channel_id=1, source_target_pairs={{0,112},{1,113},{2,114},{3,115},{4,116},{5,117},{6,118},{7,119},{8... | collective-permute-start | bytes 884744 | tf_op jit(solution)/shard_map/ppermute | solution.py:19
  155.4 2.3 %collective-permute-done.26 = f32[3,32,768]{2,1,0:T(8,128)S(1)} collective-permute-done((f32[3,32,768]{2,1,0:T(8,128)S(1)}, f32[3,32,768]{2,1,0:T(8,128)S(1)}, u32[]{:S(2)}, u32[]{:S(2)}) %collective-permute-start.26) | collective-permute-done | bytes 294944 | tf_op jit(solution)/shard_map/ppermute | solution.py:19
  158.2 6.0 %collective-permute-done.19 = f32[3,32,768]{2,1,0:T(8,128)} collective-permute-done((f32[3,32,768]{2,1,0:T(8,128)S(1)}, f32[3,32,768]{2,1,0:T(8,128)}, u32[]{:S(2)}, u32[]{:S(2)}) %collective-permute-start.19) | collective-permute-done | bytes 294944 | tf_op jit(solution)/shard_map/ppermute | solution.py:19
  165.4 4.4 %collective-permute-done.27 = f32[3,32,768]{2,1,0:T(8,128)} collective-permute-done((f32[3,32,768]{2,1,0:T(8,128)S(1)}, f32[3,32,768]{2,1,0:T(8,128)}, u32[]{:S(2)}, u32[]{:S(2)}) %collective-permute-start.27) | collective-permute-done | bytes 294944 | tf_op jit(solution)/shard_map/ppermute | solution.py:19
  172.0 16.3 %collective-permute-done.28 = bf16[3,8,64,768]{3,2,1,0:T(8,128)(2,1)} collective-permute-done((bf16[3,8,64,768]{3,2,1,0:T(8,128)(2,1)}, bf16[3,8,64,768]{3,2,1,0:T(8,128)(2,1)}, u32[]{:S(2)}, u32[]{:S(2)}) %collective-permute-start.28) | collective-permute-done | bytes 2359328 | tf_op jit(solution)/shard_map/ppermute | solution.py:19
  188.3 2.6 %fusion.34 = f32[3,512,128]{1,2,0:T(8,128)S(1)} fusion(bf16[3,512,768]{2,1,0:T(8,128)(2,1)} %bitcast.35, bf16[3,128,768]{2,1,0:T(8,128)(2,1)S(1)} %bitcast.117), kind=kOutput, calls=%fused_computation.108 | convolution fusion | flops 301989888 | bytes 3735552 | tf_op jit(solution)/shard_map/knr,kmr->knm/dot_general | solution.py:81
  194.0 7.7 %collective-permute-done.30 = f32[3,2,64,128]{3,2,1,0:T(8,128)S(1)} collective-permute-done((f32[3,2,64,128]{3,2,1,0:T(8,128)S(1)}, f32[3,2,64,128]{3,2,1,0:T(8,128)S(1)}, u32[]{:S(2)}, u32[]{:S(2)}) %collective-permute-start.30) | collective-permute-done | bytes 196640 | tf_op jit(solution)/shard_map/ppermute | solution.py:19
  203.2 2.6 %collective-permute-start.31 = (f32[3,32,128]{2,1,0:T(8,128)S(1)}, f32[3,32,128]{2,1,0:T(8,128)S(1)}, u32[]{:S(2)}, u32[]{:S(2)}) collective-permute-start(f32[3,32,128]{2,1,0:T(8,128)S(1)} %fusion.20), channel_id=1, source_target_pairs={{0,4},{1,5},{2,6},{3,7},{4,0},{5,1},{6,2},{7,3},{8,12},{9,13},{10,... | collective-permute-start | bytes 147464 | tf_op jit(solution)/shard_map/ppermute | solution.py:19
  (119 shorter events, 47.6 us)
Async XLA Ops:
  7.2 128.4 %all-gather.3.cloned.1.call-start = ((), (), s32[]{:S(2)}) async-start(), calls=%async_computation | async-start | bytes 2654208 | tf_op jit(solution)/shard_map/all_gather | solution.py:131
  8.2 27.0 %collective-permute-start.3 = (bf16[256,768]{1,0:T(8,128)(2,1)S(1)}, bf16[256,768]{1,0:T(8,128)(2,1)S(1)}, u32[]{:S(2)}, u32[]{:S(2)}) collective-permute-start(bf16[256,768]{1,0:T(8,128)(2,1)S(1)} %split.9), channel_id=1, source_target_pairs={{0,128},{1,129},{2,130},{3,131},{4,132},{5,133},{6,134},{7,135},{8... | collective-permute-start | bytes 1179656 | tf_op jit(solution)/shard_map/ppermute | solution.py:19
  11.8 18.3 %collective-permute-start = (bf16[3,64,768]{2,1,0:T(8,128)(2,1)S(1)}, bf16[3,64,768]{2,1,0:T(8,128)(2,1)S(1)}, u32[]{:S(2)}, u32[]{:S(2)}) collective-permute-start(bf16[3,64,768]{2,1,0:T(8,128)(2,1)S(1)} %multiply_bitcast_fusion), channel_id=1, source_target_pairs={{0,0},{1,1},{2,2},{3,3},{4,4},{5,5},{6,6},{7,7},{8,128},{9,129},{1... | collective-permute-start | bytes 884744 | tf_op jit(solution)/shard_map/ppermute | solution.py:19
  15.2 17.4 %collective-permute-start.1 = (bf16[3,64,768]{2,1,0:T(8,128)(2,1)S(1)}, bf16[3,64,768]{2,1,0:T(8,128)(2,1)S(1)}, u32[]{:S(2)}, u32[]{:S(2)}) collective-permute-start(bf16[3,64,768]{2,1,0:T(8,128)(2,1)S(1)} %multiply_bitcast_fusion), channel_id=1, source_target_pairs={{0,2},{1,3},{2,0},{3,1},{4,6},{5,7},{6,4},{7,5},{8,130},{9,131},{1... | collective-permute-start | bytes 884744 | tf_op jit(solution)/shard_map/ppermute | solution.py:19
  19.8 15.4 %collective-permute-start.2 = (bf16[3,64,768]{2,1,0:T(8,128)(2,1)S(1)}, bf16[3,64,768]{2,1,0:T(8,128)(2,1)}, u32[]{:S(2)}, u32[]{:S(2)}) collective-permute-start(bf16[3,64,768]{2,1,0:T(8,128)(2,1)S(1)} %multiply_bitcast_fusion), channel_id=1, source_target_pairs={{0,0},{1,17},{2,34},{3,51},{4,68},{5,85},{6,102},{7,119},{8,8},{9,... | collective-permute-start | bytes 884744 | tf_op jit(solution)/shard_map/ppermute | solution.py:19
  30.0 14.5 %collective-permute-start.7 = (bf16[384,768]{1,0:T(8,128)(2,1)S(1)}, bf16[384,768]{1,0:T(8,128)(2,1)}, u32[]{:S(2)}, u32[]{:S(2)}) collective-permute-start(bf16[384,768]{1,0:T(8,128)(2,1)S(1)} %split.10), channel_id=1, source_target_pairs={{0,128},{1,129},{2,130},{3,131},{4,132},{5,133},{6,134},{7,135},{8... | collective-permute-start | bytes 1769480 | tf_op jit(solution)/shard_map/ppermute | solution.py:19
  36.2 20.0 %collective-permute-start.4 = (bf16[3,2,64,768]{3,2,0,1:T(8,128)(2,1)}, bf16[3,2,64,768]{3,2,0,1:T(8,128)(2,1)S(1)}, u32[]{:S(2)}, u32[]{:S(2)}) collective-permute-start(bf16[3,2,64,768]{3,2,0,1:T(8,128)(2,1)} %pad_maximum_fusion.3), channel_id=1, source_target_pairs={{0,4},{1,5},{2,6},{3,7},{4,8},{5,9},{6,10},{7,11},{8,12},{9,13},{1... | collective-permute-start | bytes 1769480 | tf_op jit(solution)/shard_map/ppermute | solution.py:19
  36.8 19.3 %collective-permute-start.5 = (bf16[3,2,64,768]{3,2,0,1:T(8,128)(2,1)}, bf16[3,2,64,768]{3,2,0,1:T(8,128)(2,1)S(1)}, u32[]{:S(2)}, u32[]{:S(2)}) collective-permute-start(bf16[3,2,64,768]{3,2,0,1:T(8,128)(2,1)} %pad_maximum_fusion.3), channel_id=1, source_target_pairs={{0,12},{1,13},{2,14},{3,15},{4,0},{5,1},{6,2},{7,3},{8,4},{9,5},{1... | collective-permute-start | bytes 1769480 | tf_op jit(solution)/shard_map/ppermute | solution.py:19
  38.2 17.9 %collective-permute-start.6 = (bf16[3,64,768]{2,1,0:T(8,128)(2,1)}, bf16[3,64,768]{2,1,0:T(8,128)(2,1)}, u32[]{:S(2)}, u32[]{:S(2)}) collective-permute-start(bf16[3,64,768]{2,1,0:T(8,128)(2,1)} %collective-permute-done.2), channel_id=1, source_target_pairs={{0,0},{1,1},{2,2},{3,3},{4,4},{5,5},{6,6},{7,7},{8,128},{9,129},{1... | collective-permute-start | bytes 884744 | tf_op jit(solution)/shard_map/ppermute | solution.py:19
  56.9 9.5 %collective-permute-start.8 = (bf16[3,1,64,768]{3,2,0,1:T(8,128)(2,1)}, bf16[3,1,64,768]{3,2,0,1:T(8,128)(2,1)S(1)}, u32[]{:S(2)}, u32[]{:S(2)}) collective-permute-start(bf16[3,1,64,768]{3,2,0,1:T(8,128)(2,1)} %slice.116), channel_id=1, source_target_pairs={{0,4},{1,5},{2,6},{3,7},{4,8},{5,9},{6,10},{7,11},{8,12},{9,13},{1... | collective-permute-start | bytes 884744 | tf_op jit(solution)/shard_map/ppermute | solution.py:19
  57.6 8.7 %collective-permute-start.9 = (bf16[3,1,64,768]{3,2,0,1:T(8,128)(2,1)}, bf16[3,1,64,768]{3,2,0,1:T(8,128)(2,1)S(1)}, u32[]{:S(2)}, u32[]{:S(2)}) collective-permute-start(bf16[3,1,64,768]{3,2,0,1:T(8,128)(2,1)} %slice.117), channel_id=1, source_target_pairs={{0,12},{1,13},{2,14},{3,15},{4,0},{5,1},{6,2},{7,3},{8,4},{9,5},{1... | collective-permute-start | bytes 884744 | tf_op jit(solution)/shard_map/ppermute | solution.py:19
  60.4 6.0 %collective-permute-start.10 = (bf16[128,768]{1,0:T(8,128)(2,1)}, bf16[128,768]{1,0:T(8,128)(2,1)}, u32[]{:S(2)}, u32[]{:S(2)}) collective-permute-start(bf16[128,768]{1,0:T(8,128)(2,1)} %split.11), channel_id=1, source_target_pairs={{0,128},{1,129},{2,130},{3,131},{4,132},{5,133},{6,134},{7,135},{8... | collective-permute-start | bytes 589832 | tf_op jit(solution)/shard_map/ppermute | solution.py:19
  68.5 6.9 %collective-permute-start.11 = (bf16[2,3,2,2,64,768]{5,4,1,3,2,0:T(8,128)(2,1)}, bf16[2,3,2,2,64,768]{5,4,1,3,2,0:T(8,128)(2,1)}, u32[]{:S(2)}, u32[]{:S(2)}) collective-permute-start(bf16[2,3,2,2,64,768]{5,4,1,3,2,0:T(8,128)(2,1)} %pad_maximum_fusion.1), channel_id=1, source_target_pairs={{0,1},{1,0},{2,3},{3,2},{4,5},{5,4},{6,7},{7,6},{8,9},{9,8},{10,11... | collective-permute-start | bytes 7077896 | tf_op jit(solution)/shard_map/ppermute | solution.py:19
  84.0 16.0 %collective-permute-start.16 = (f32[3,16,768]{2,1,0:T(8,128)S(1)}, f32[3,16,768]{2,1,0:T(8,128)S(1)}, u32[]{:S(2)}, u32[]{:S(2)}) collective-permute-start(f32[3,16,768]{2,1,0:T(8,128)S(1)} %get-tuple-element.51), channel_id=1, source_target_pairs={{0,16},{1,17},{2,18},{3,19},{4,20},{5,21},{6,22},{7,23},{8,24},{9,... | collective-permute-start | bytes 442376 | tf_op jit(solution)/shard_map/ppermute | solution.py:19
  93.1 9.6 %collective-permute-start.12 = (f32[3,16,768]{2,1,0:T(8,128)S(1)}, f32[3,16,768]{2,1,0:T(8,128)S(1)}, u32[]{:S(2)}, u32[]{:S(2)}) collective-permute-start(f32[3,16,768]{2,1,0:T(8,128)S(1)} %get-tuple-element.50), channel_id=1, source_target_pairs={{0,112},{1,113},{2,114},{3,115},{4,116},{5,117},{6,118},{7,119},{8... | collective-permute-start | bytes 442376 | tf_op jit(solution)/shard_map/ppermute | solution.py:19
  93.2 16.9 %collective-permute-start.24 = (f32[3,16,768]{2,1,0:T(8,128)S(1)}, f32[3,16,768]{2,1,0:T(8,128)S(1)}, u32[]{:S(2)}, u32[]{:S(2)}) collective-permute-start(f32[3,16,768]{2,1,0:T(8,128)S(1)} %get-tuple-element.57), channel_id=1, source_target_pairs={{0,16},{1,17},{2,18},{3,19},{4,20},{5,21},{6,22},{7,23},{8,24},{9,... | collective-permute-start | bytes 442376 | tf_op jit(solution)/shard_map/ppermute | solution.py:19
  95.3 12.3 %collective-permute-start.20 = (f32[3,16,768]{2,1,0:T(8,128)S(1)}, f32[3,16,768]{2,1,0:T(8,128)S(1)}, u32[]{:S(2)}, u32[]{:S(2)}) collective-permute-start(f32[3,16,768]{2,1,0:T(8,128)S(1)} %get-tuple-element.56), channel_id=1, source_target_pairs={{0,112},{1,113},{2,114},{3,115},{4,116},{5,117},{6,118},{7,119},{8... | collective-permute-start | bytes 442376 | tf_op jit(solution)/shard_map/ppermute | solution.py:19
  100.1 37.4 %collective-permute-start.17 = (f32[3,32,768]{2,1,0:T(8,128)S(1)}, f32[3,32,768]{2,1,0:T(8,128)}, u32[]{:S(2)}, u32[]{:S(2)}) collective-permute-start(f32[3,32,768]{2,1,0:T(8,128)S(1)} %pad_maximum_fusion.7), channel_id=1, source_target_pairs={{0,16},{1,17},{2,18},{3,19},{4,20},{5,21},{6,22},{7,23},{8,24},{9,... | collective-permute-start | bytes 884744 | tf_op jit(solution)/shard_map/ppermute | solution.py:19
  102.7 17.4 %collective-permute-start.13 = (f32[3,32,768]{2,1,0:T(8,128)S(1)}, f32[3,32,768]{2,1,0:T(8,128)S(1)}, u32[]{:S(2)}, u32[]{:S(2)}) collective-permute-start(f32[3,32,768]{2,1,0:T(8,128)S(1)} %pad_maximum_fusion.6), channel_id=1, source_target_pairs={{0,112},{1,113},{2,114},{3,115},{4,116},{5,117},{6,118},{7,119},{8... | collective-permute-start | bytes 884744 | tf_op jit(solution)/shard_map/ppermute | solution.py:19
  107.6 24.8 %collective-permute-start.21 = (f32[3,32,768]{2,1,0:T(8,128)S(1)}, f32[3,32,768]{2,1,0:T(8,128)S(1)}, u32[]{:S(2)}, u32[]{:S(2)}) collective-permute-start(f32[3,32,768]{2,1,0:T(8,128)S(1)} %pad_maximum_fusion.8), channel_id=1, source_target_pairs={{0,112},{1,113},{2,114},{3,115},{4,116},{5,117},{6,118},{7,119},{8... | collective-permute-start | bytes 884744 | tf_op jit(solution)/shard_map/ppermute | solution.py:19
  120.2 18.6 %collective-permute-start.14 = (f32[3,32,768]{2,1,0:T(8,128)S(1)}, f32[3,32,768]{2,1,0:T(8,128)}, u32[]{:S(2)}, u32[]{:S(2)}) collective-permute-start(f32[3,32,768]{2,1,0:T(8,128)S(1)} %bitcast_add_fusion.7), channel_id=1, source_target_pairs={{0,112},{1,113},{2,114},{3,115},{4,116},{5,117},{6,118},{7,119},{8... | collective-permute-start | bytes 884744 | tf_op jit(solution)/shard_map/ppermute | solution.py:19
  122.7 19.5 %collective-permute-start.25 = (f32[3,32,768]{2,1,0:T(8,128)S(1)}, f32[3,32,768]{2,1,0:T(8,128)}, u32[]{:S(2)}, u32[]{:S(2)}) collective-permute-start(f32[3,32,768]{2,1,0:T(8,128)S(1)} %pad_maximum_fusion.9), channel_id=1, source_target_pairs={{0,16},{1,17},{2,18},{3,19},{4,20},{5,21},{6,22},{7,23},{8,24},{9,... | collective-permute-start | bytes 884744 | tf_op jit(solution)/shard_map/ppermute | solution.py:19
  132.4 12.4 %collective-permute-start.22 = (f32[3,32,768]{2,1,0:T(8,128)S(1)}, f32[3,32,768]{2,1,0:T(8,128)}, u32[]{:S(2)}, u32[]{:S(2)}) collective-permute-start(f32[3,32,768]{2,1,0:T(8,128)S(1)} %bitcast_add_fusion.2), channel_id=1, source_target_pairs={{0,112},{1,113},{2,114},{3,115},{4,116},{5,117},{6,118},{7,119},{8... | collective-permute-start | bytes 884744 | tf_op jit(solution)/shard_map/ppermute | solution.py:19
  135.5 52.8 %collective-permute-start.28 = (bf16[3,8,64,768]{3,2,1,0:T(8,128)(2,1)}, bf16[3,8,64,768]{3,2,1,0:T(8,128)(2,1)}, u32[]{:S(2)}, u32[]{:S(2)}) collective-permute-start(bf16[3,8,64,768]{3,2,1,0:T(8,128)(2,1)} %bitcast.123), channel_id=1, source_target_pairs={{0,128},{1,129},{2,130},{3,131},{4,132},{5,133},{6,134},{7,135},{8... | collective-permute-start | bytes 7077896 | tf_op jit(solution)/shard_map/ppermute | solution.py:19
  140.9 10.2 %collective-permute-start.18 = (f32[3,32,768]{2,1,0:T(8,128)}, f32[3,32,768]{2,1,0:T(8,128)S(1)}, u32[]{:S(2)}, u32[]{:S(2)}) collective-permute-start(f32[3,32,768]{2,1,0:T(8,128)} %get-tuple-element.31), channel_id=1, source_target_pairs={{0,16},{1,17},{2,18},{3,19},{4,20},{5,21},{6,22},{7,23},{8,24},{9,... | collective-permute-start | bytes 884744 | tf_op jit(solution)/shard_map/ppermute | solution.py:19
  146.6 11.1 %collective-permute-start.26 = (f32[3,32,768]{2,1,0:T(8,128)S(1)}, f32[3,32,768]{2,1,0:T(8,128)S(1)}, u32[]{:S(2)}, u32[]{:S(2)}) collective-permute-start(f32[3,32,768]{2,1,0:T(8,128)S(1)} %get-tuple-element.36), channel_id=1, source_target_pairs={{0,16},{1,17},{2,18},{3,19},{4,20},{5,21},{6,22},{7,23},{8,24},{9,... | collective-permute-start | bytes 884744 | tf_op jit(solution)/shard_map/ppermute | solution.py:19
  148.0 10.2 %collective-permute-start.15 = (f32[3,32,768]{2,1,0:T(8,128)}, f32[3,32,768]{2,1,0:T(8,128)}, u32[]{:S(2)}, u32[]{:S(2)}) collective-permute-start(f32[3,32,768]{2,1,0:T(8,128)} %get-tuple-element.30), channel_id=1, source_target_pairs={{0,112},{1,113},{2,114},{3,115},{4,116},{5,117},{6,118},{7,119},{8... | collective-permute-start | bytes 884744 | tf_op jit(solution)/shard_map/ppermute | solution.py:19
  152.1 12.0 %collective-permute-start.19 = (f32[3,32,768]{2,1,0:T(8,128)S(1)}, f32[3,32,768]{2,1,0:T(8,128)}, u32[]{:S(2)}, u32[]{:S(2)}) collective-permute-start(f32[3,32,768]{2,1,0:T(8,128)S(1)} %bitcast_add_fusion.6), channel_id=1, source_target_pairs={{0,16},{1,17},{2,18},{3,19},{4,20},{5,21},{6,22},{7,23},{8,24},{9,... | collective-permute-start | bytes 884744 | tf_op jit(solution)/shard_map/ppermute | solution.py:19
  152.4 12.9 %collective-permute-start.23 = (f32[3,32,768]{2,1,0:T(8,128)}, f32[3,32,768]{2,1,0:T(8,128)}, u32[]{:S(2)}, u32[]{:S(2)}) collective-permute-start(f32[3,32,768]{2,1,0:T(8,128)} %get-tuple-element.35), channel_id=1, source_target_pairs={{0,112},{1,113},{2,114},{3,115},{4,116},{5,117},{6,118},{7,119},{8... | collective-permute-start | bytes 884744 | tf_op jit(solution)/shard_map/ppermute | solution.py:19
  157.8 12.0 %collective-permute-start.27 = (f32[3,32,768]{2,1,0:T(8,128)S(1)}, f32[3,32,768]{2,1,0:T(8,128)}, u32[]{:S(2)}, u32[]{:S(2)}) collective-permute-start(f32[3,32,768]{2,1,0:T(8,128)S(1)} %bitcast_add_fusion.1), channel_id=1, source_target_pairs={{0,16},{1,17},{2,18},{3,19},{4,20},{5,21},{6,22},{7,23},{8,24},{9,... | collective-permute-start | bytes 884744 | tf_op jit(solution)/shard_map/ppermute | solution.py:19
  193.2 8.5 %collective-permute-start.30 = (f32[3,2,64,128]{3,2,1,0:T(8,128)S(1)}, f32[3,2,64,128]{3,2,1,0:T(8,128)S(1)}, u32[]{:S(2)}, u32[]{:S(2)}) collective-permute-start(f32[3,2,64,128]{3,2,1,0:T(8,128)S(1)} %slice_bitcast_fusion.2), channel_id=1, source_target_pairs={{0,2},{1,3},{2,0},{3,1},{4,6},{5,7},{6,4},{7,5},{8,10},{9,11},{10,... | collective-permute-start | bytes 589832 | tf_op jit(solution)/shard_map/ppermute | solution.py:19
  202.1 5.9 %collective-permute-start.33 = (f32[3,32,128]{2,1,0:T(8,128)S(1)}, f32[3,32,128]{2,1,0:T(8,128)S(1)}, u32[]{:S(2)}, u32[]{:S(2)}) collective-permute-start(f32[3,32,128]{2,1,0:T(8,128)S(1)} %get-tuple-element.60), channel_id=1, source_target_pairs={{0,12},{1,13},{2,14},{3,15},{4,8},{5,9},{6,10},{7,11},{8,4},{9,5},... | collective-permute-start | bytes 147464 | tf_op jit(solution)/shard_map/ppermute | solution.py:19
  (9 other events, 111.7 us)
Sparse Core Ops, SparseCore 0:
  71.0 61.7 all-gather.2

commit v7 on v6

--- a/solution.py
+++ b/solution.py
@@ -20,11 +20,11 @@
 
 
 def swap(yl, z, x, yh, c):
-    return x // 2, z, yl * 2 + x % 2, yh, c
+    return (yl, z, x, yh, c) if x // 2 == yl else (1 - yl, z, 3 - x, yh, c)
 
 
 def swap_far(yl, z, x, yh, c):
-    return x // 2, z, yl * 2 + x % 2, 1 - yh, c
+    return over_y(*swap(yl, z, x, yh, c))
 
 
 def along_x(step):
@@ -81,25 +81,14 @@
     return jnp.einsum("knr,kmr->knm", a, b, preferred_element_type=jnp.float32)
 
 
-def spread_rows(place, plane, left, right, opposite):
-    yl, x, yh = place
-    opposite = jnp.concatenate(opposite, axis=1)
-    here = ordered((x // 2) == yl, plane, opposite)
-    there = ordered(((x + 3) % 4 // 2) == yl, left, right)
-    halves = [jnp.stack(ordered(x % 2 == 0, here[h], there[h]), axis=1) for h in range(2)]
-    return jnp.stack(halves)
+def pair_rows(x, own_rows, plane, left, right, opposite):
+    mirror, other = ordered(x % 2 == 0, left, right)
+    here = ordered(own_rows, plane, mirror)
+    there = ordered(own_rows, other, jnp.concatenate(opposite, axis=1))
+    return jnp.stack([jnp.stack([here[h], there[h]], axis=1) for h in range(2)])
 
 
-def spread_cores(core, mine):
-    theirs = send(mine, sibling)
-    return jnp.stack(ordered(core == 0, mine, theirs), axis=4)
-
-
-def sum_over_z(z, partial):
-    def block(offset):
-        return lax.dynamic_index_in_dim(partial, (z + offset) % 8, 1, keepdims=False)
-
-    half = partial.shape[2] // 2
+def sum_over_z(block, half):
     down = send(block(4)[:, :half], along_z(-1))
     up = send(block(4)[:, half:], along_z(1))
     below, above = block(-3), block(3)
@@ -124,21 +113,39 @@
     beside = [send(piece, across) for piece in jnp.split(ancestor_inverse, cuts)]
     near, far = send(own, swap), send(own, swap_far)
     near, far, turned, beside[0] = together(near, far, send(own, skewed), beside[0])
-    plane = jnp.stack(ordered(yh == 0, near, far), axis=1)
+    plane = jnp.stack([near, far], axis=1)
     left, right = send(plane, along_x(1)), send(plane, along_x(3))
     turned = send(turned, facing_place)
     left, right, turned, beside[1] = together(left, right, turned, beside[1])
     facing = lax.all_gather(turned, "z", axis=1)
-    facing = [facing, send(facing, across)]
+    facing = [facing, None]
     opposite = send(left[:, :1], along_x(1)), send(right[:, 1:], along_x(3))
     *opposite, beside[2] = together(*opposite, beside[2])
     beside = jnp.concatenate(beside)
-    mine = spread_rows((yl, x, yh), plane, left, right, opposite)
-    panel = spread_cores(core, mine).reshape(2, count * 8 * cols, rows)
-    partial = dot_nt(panel[0], ancestor_inverse) + dot_nt(panel[1], beside)
-    partial = partial.reshape(count, 8, cols, rows)
+    own_rows = (x // 2) == yl
+    mine = pair_rows(x, own_rows, plane, left, right, opposite)
+
+    def product(panel):
+        panel = panel.reshape(2, count * 4 * cols, rows)
+        whole = dot_nt(panel[0], ancestor_inverse) + dot_nt(panel[1], beside)
+        return whole.reshape(count, 4, cols, rows)
+
+    theirs = send(mine, sibling)
+    near, far, facing[0] = together(product(mine), product(theirs), facing[0])
+    facing[1] = send(facing[0], across)
+    column = jnp.where(own_rows, x % 2, 1 - x % 2)
     wide = cols // 2
-    reduced = [sum_over_z(z, partial[:, :, at : at + wide]) for at in (0, wide)]
+
+    def block(first, offset):
+        place = (z + offset) % 8
+        at = (place // 4 ^ column) * 2 + (place // 2 % 2 ^ yh)
+        start, size = (0, at, first, 0), (count, 1, wide, rows)
+        picked = (lax.dynamic_slice(side, start, size) for side in (near, far))
+        return jnp.where(place % 2 == core, *picked).reshape(count, wide, rows)
+
+    reduced = [
+        sum_over_z(lambda offset, first=first: block(first, offset), wide // 2) for first in (0, wide)
+    ]
     reduced = jnp.concatenate(reduced, axis=1)
     offdiag = -(reduced * keep_cols[:, None, :])
     high = lax.reduce_precision(reduced, 8, 7)
@@ -150,11 +157,11 @@
         tiles.append(square[..., :cols] + square[..., cols:])
     tiles = jnp.concatenate(tiles, axis=2).reshape(count, 2, 2, 2, cols, 2 * cols)
     tiles = tiles[:, :, :, 0] + send(tiles[:, :, :, 1], sibling)
-    tiles = tiles[:, :, 0] + send(tiles[:, :, 1], over_y)
     kept, given = ordered((x // 2) == yl, tiles[..., :cols], tiles[..., cols:])
-    kept, given = (jnp.concatenate([t[:, :, :wide], t[:, :, wide:]], axis=3) for t in (kept, given))
+    kept, given = (jnp.concatenate([t[:, :, :, :wide], t[:, :, :, wide:]], axis=4) for t in (kept, given))
     packed = kept[:, 0] + send(kept[:, 1], flip_x(1))
     packed += send(given[:, 0], flip_x(2)) + send(given[:, 1], flip_x(3))
+    packed = packed[:, 0] + send(packed[:, 1], over_y)
     diagonal = jnp.concatenate([packed[..., :cols], packed[..., cols:]], axis=1)
     diagonal += diagonal_inverse
     return offdiag.transpose(0, 2, 1), diagonal

time: 219 us -> 216 us (0.986)
  starting transfers between devices: 67.6 us -> 56.8 us
  waiting for transfers between devices: 102 us -> 108 us
  local copies, waits for them, and re-layouts: 5.93 us -> 10.1 us
  other arithmetic: 17 us -> 13.4 us
  matrix products: 8.68 us -> 11.1 us
    all_gather x1, waiting for transfers between devices: 0.01 us -> 23.7 us  [shards(): facing = lax.all_gather(turned, 'z', axis=1)]
    ppermute x34, waiting for transfers between devices: 102 us -> 84.7 us  [send(): return lax.ppermute(value, AXES, pairs(move))]
    ppermute x34, starting transfers between devices: 67.5 us -> 56.7 us  [send(): return lax.ppermute(value, AXES, pairs(move))]
    add x6 -> x4, other arithmetic: 5.05 us -> 1.35 us  [sum_over_z(): down, up = (block(-offset) + down, block(offset) + up)]
    unnamed x17, local copies, waits for them, and re-layouts: 0.21 us -> 2.47 us
    another operation x8 -> x5, other arithmetic: 5.47 us -> 3.36 us  [the longest x3 3.23 us: pair_rows(): return jnp.stack([jnp.stack([here[h], there[h]], axis=1) for h in range(2)])]
    dot_general x2 -> x4, matrix products: 5.25 us -> 5.99 us  [dot_nt(): return lax.dot_general(a, b, NT, preferred_element_type=jnp.float32)]
  transfers between devices with their start and end apart: 35 -> 35, of which waited for: 22 -> 23; matrix products, arithmetic and copies ran while one was open for 11% -> 12% of each run, Pallas kernels for 0% -> 0%
where the time goes in v7:
time: 216 us; the launch traced here: 214 us
  waiting for transfers between devices  108 us (50%)
  starting transfers between devices  56.8 us (26%)
  between operations  14.5 us (7%)
  other arithmetic  13.4 us (6%)
  matrix products  11.1 us (5%)
  local copies, waits for them, and re-layouts  10.1 us (5%)
    ppermute x34, waiting for transfers between devices, send(): return lax.ppermute(value, AXES, pairs(move))  84.7 us
    ppermute x34, starting transfers between devices, send(): return lax.ppermute(value, AXES, pairs(move))  56.7 us
    all_gather x1, waiting for transfers between devices, shards(): facing = lax.all_gather(turned, 'z', axis=1)  23.7 us
    dot_general x4, matrix products, dot_nt(): return lax.dot_general(a, b, NT, preferred_element_type=jnp.float32)  5.99 us
    dot_general x2, matrix products, dot_each(): return jnp.einsum('knr,kmr->knm', a, b, preferred_element_type=jnp.float32)  5.1 us
  transfers between devices with their start and end apart: 35, of which 23 were waited for; matrix products, arithmetic and copies ran while one was open for 12% of the time, Pallas kernels for 0%

profile of v7, /device:TPU:6, one launch (start us, length us, event | category | flops | bytes accessed | tf_op | source)
XLA Modules:
  0.0 214.3 jit_solution(12431013556328336783)
XLA Ops:
  11.9 4.0 %collective-permute-start = (bf16[3,64,768]{2,1,0:T(8,128)(2,1)S(1)}, bf16[3,64,768]{2,1,0:T(8,128)(2,1)S(1)}, u32[]{:S(2)}, u32[]{:S(2)}) collective-permute-start(bf16[3,64,768]{2,1,0:T(8,128)(2,1)S(1)} %multiply_bitcast_fusion), channel_id=1, source_target_pairs={{0,0},{1,1},{2,2},{3,3},{4,4},{5,5},{6,6},{7,7},{8,132},{9,133},{1... | collective-permute-start | bytes 884744 | tf_op jit(solution)/shard_map/ppermute | solution.py:19
  15.9 3.6 %collective-permute-start.1 = (bf16[3,64,768]{2,1,0:T(8,128)(2,1)S(1)}, bf16[3,64,768]{2,1,0:T(8,128)(2,1)S(1)}, u32[]{:S(2)}, u32[]{:S(2)}) collective-permute-start(bf16[3,64,768]{2,1,0:T(8,128)(2,1)S(1)} %multiply_bitcast_fusion), channel_id=1, source_target_pairs={{0,2},{1,3},{2,0},{3,1},{4,6},{5,7},{6,4},{7,5},{8,134},{9,135},{1... | collective-permute-start | bytes 884744 | tf_op jit(solution)/shard_map/ppermute | solution.py:19
  19.5 9.1 %collective-permute-start.2 = (bf16[3,64,768]{2,1,0:T(8,128)(2,1)S(1)}, bf16[3,64,768]{2,1,0:T(8,128)(2,1)S(1)}, u32[]{:S(2)}, u32[]{:S(2)}) collective-permute-start(bf16[3,64,768]{2,1,0:T(8,128)(2,1)S(1)} %multiply_bitcast_fusion), channel_id=1, source_target_pairs={{0,0},{1,17},{2,34},{3,51},{4,68},{5,85},{6,102},{7,119},{8,8},{9,... | collective-permute-start | bytes 884744 | tf_op jit(solution)/shard_map/ppermute | solution.py:19
  29.8 2.4 %collective-permute-done.1 = bf16[3,64,768]{2,1,0:T(8,128)(2,1)S(1)} collective-permute-done((bf16[3,64,768]{2,1,0:T(8,128)(2,1)S(1)}, bf16[3,64,768]{2,1,0:T(8,128)(2,1)S(1)}, u32[]{:S(2)}, u32[]{:S(2)}) %collective-permute-start.1) | collective-permute-done | bytes 294944 | tf_op jit(solution)/shard_map/ppermute | solution.py:19
  32.2 2.6 %collective-permute-done.2 = bf16[3,64,768]{2,1,0:T(8,128)(2,1)S(1)} collective-permute-done((bf16[3,64,768]{2,1,0:T(8,128)(2,1)S(1)}, bf16[3,64,768]{2,1,0:T(8,128)(2,1)S(1)}, u32[]{:S(2)}, u32[]{:S(2)}) %collective-permute-start.2) | collective-permute-done | bytes 294944 | tf_op jit(solution)/shard_map/ppermute | solution.py:19
  37.0 3.1 %collective-permute-start.6 = (bf16[3,64,768]{2,1,0:T(8,128)(2,1)S(1)}, bf16[3,64,768]{2,1,0:T(8,128)(2,1)}, u32[]{:S(2)}, u32[]{:S(2)}) collective-permute-start(bf16[3,64,768]{2,1,0:T(8,128)(2,1)S(1)} %collective-permute-done.2), channel_id=1, source_target_pairs={{0,0},{1,1},{2,2},{3,3},{4,4},{5,5},{6,6},{7,7},{8,128},{9,129},{1... | collective-permute-start | bytes 884744 | tf_op jit(solution)/shard_map/ppermute | solution.py:19
  40.0 4.6 %collective-permute-done.7 = bf16[384,768]{1,0:T(8,128)(2,1)} collective-permute-done((bf16[384,768]{1,0:T(8,128)(2,1)S(1)}, bf16[384,768]{1,0:T(8,128)(2,1)}, u32[]{:S(2)}, u32[]{:S(2)}) %collective-permute-start.7) | collective-permute-done | bytes 589856 | tf_op jit(solution)/shard_map/ppermute | solution.py:19
  44.7 11.6 %collective-permute-done.6 = bf16[3,64,768]{2,1,0:T(8,128)(2,1)} collective-permute-done((bf16[3,64,768]{2,1,0:T(8,128)(2,1)S(1)}, bf16[3,64,768]{2,1,0:T(8,128)(2,1)}, u32[]{:S(2)}, u32[]{:S(2)}) %collective-permute-start.6) | collective-permute-done | bytes 294944 | tf_op jit(solution)/shard_map/ppermute | solution.py:19
  57.7 2.0 collective-permute-start.9
  60.5 7.2 %collective-permute-done.10 = bf16[128,768]{1,0:T(8,128)(2,1)} collective-permute-done((bf16[128,768]{1,0:T(8,128)(2,1)}, bf16[128,768]{1,0:T(8,128)(2,1)}, u32[]{:S(2)}, u32[]{:S(2)}) %collective-permute-start.10) | collective-permute-done | bytes 196640 | tf_op jit(solution)/shard_map/ppermute | solution.py:19
  80.6 2.6 %convolution_add_fusion = f32[768,768]{1,0:T(8,128)} fusion(f32[768,768]{1,0:T(8,128)S(1)} %fusion.28, bf16[768,768]{1,0:T(8,128)(2,1)S(1)} %bitcast.144, bf16[768,768]{1,0:T(8,128)(2,1)S(1)} %copy-done.2), kind=kOutput, calls=%fused_computation.1 | convolution fusion | flops 906559488 | bytes 7077888 | tf_op jit(solution)/shard_map/dot_general | solution.py:69
  83.2 23.7 %all-gather.3.cloned.1.call-done = bf16[3,512,768]{2,1,0:T(8,128)(2,1)} async-done(((bf16[3,64,768]{2,1,0:T(8,128)(2,1)}), bf16[3,512,768]{2,1,0:T(8,128)(2,1)}) %all-gather.3.cloned.1.call-update) | async-done | bytes 2359312 | tf_op jit(solution)/shard_map/all_gather | solution.py:120
  108.6 2.6 %collective-permute-start.12 = (f32[3,16,768]{2,1,0:T(8,128)S(1)}, f32[3,16,768]{2,1,0:T(8,128)S(1)}, u32[]{:S(2)}, u32[]{:S(2)}) collective-permute-start(f32[3,16,768]{2,1,0:T(8,128)S(1)} %get-tuple-element.68), channel_id=1, source_target_pairs={{0,112},{1,113},{2,114},{3,115},{4,116},{5,117},{6,118},{7,119},{8... | collective-permute-start | bytes 442376 | tf_op jit(solution)/shard_map/ppermute | solution.py:19
  113.3 2.2 %collective-permute-done.12 = f32[3,16,768]{2,1,0:T(8,128)S(1)} collective-permute-done((f32[3,16,768]{2,1,0:T(8,128)S(1)}, f32[3,16,768]{2,1,0:T(8,128)S(1)}, u32[]{:S(2)}, u32[]{:S(2)}) %collective-permute-start.12) | collective-permute-done | bytes 147488 | tf_op jit(solution)/shard_map/ppermute | solution.py:19
  115.6 2.9 %collective-permute-start.13 = (f32[3,32,768]{2,1,0:T(8,128)S(1)}, f32[3,32,768]{2,1,0:T(8,128)S(1)}, u32[]{:S(2)}, u32[]{:S(2)}) collective-permute-start(f32[3,32,768]{2,1,0:T(8,128)S(1)} %pad_maximum_fusion.7), channel_id=1, source_target_pairs={{0,112},{1,113},{2,114},{3,115},{4,116},{5,117},{6,118},{7,119},{8... | collective-permute-start | bytes 884744 | tf_op jit(solution)/shard_map/ppermute | solution.py:19
  118.5 2.3 %collective-permute-done.16 = f32[3,16,768]{2,1,0:T(8,128)S(1)} collective-permute-done((f32[3,16,768]{2,1,0:T(8,128)S(1)}, f32[3,16,768]{2,1,0:T(8,128)S(1)}, u32[]{:S(2)}, u32[]{:S(2)}) %collective-permute-start.16) | collective-permute-done | bytes 147488 | tf_op jit(solution)/shard_map/ppermute | solution.py:19
  123.2 3.7 %collective-permute-start.14 = (f32[3,32,768]{2,1,0:T(8,128)S(1)}, f32[3,32,768]{2,1,0:T(8,128)S(1)}, u32[]{:S(2)}, u32[]{:S(2)}) collective-permute-start(f32[3,32,768]{2,1,0:T(8,128)S(1)} %bitcast_add_fusion.7), channel_id=1, source_target_pairs={{0,112},{1,113},{2,114},{3,115},{4,116},{5,117},{6,118},{7,119},{8... | collective-permute-start | bytes 884744 | tf_op jit(solution)/shard_map/ppermute | solution.py:19
  128.8 5.5 %collective-permute-done.14 = f32[3,32,768]{2,1,0:T(8,128)S(1)} collective-permute-done((f32[3,32,768]{2,1,0:T(8,128)S(1)}, f32[3,32,768]{2,1,0:T(8,128)S(1)}, u32[]{:S(2)}, u32[]{:S(2)}) %collective-permute-start.14) | collective-permute-done | bytes 294944 | tf_op jit(solution)/shard_map/ppermute | solution.py:19
  134.9 3.6 %collective-permute-start.15 = (f32[3,32,768]{2,1,0:T(8,128)S(1)}, f32[3,32,768]{2,1,0:T(8,128)}, u32[]{:S(2)}, u32[]{:S(2)}) collective-permute-start(f32[3,32,768]{2,1,0:T(8,128)S(1)} %get-tuple-element.33), channel_id=1, source_target_pairs={{0,112},{1,113},{2,114},{3,115},{4,116},{5,117},{6,118},{7,119},{8... | collective-permute-start | bytes 884744 | tf_op jit(solution)/shard_map/ppermute | solution.py:19
  138.5 5.2 %collective-permute-done.18 = f32[3,32,768]{2,1,0:T(8,128)S(1)} collective-permute-done((f32[3,32,768]{2,1,0:T(8,128)S(1)}, f32[3,32,768]{2,1,0:T(8,128)S(1)}, u32[]{:S(2)}, u32[]{:S(2)}) %collective-permute-start.18) | collective-permute-done | bytes 294944 | tf_op jit(solution)/shard_map/ppermute | solution.py:19
  147.0 6.6 %collective-permute-done.19 = f32[3,32,768]{2,1,0:T(8,128)} collective-permute-done((f32[3,32,768]{2,1,0:T(8,128)S(1)}, f32[3,32,768]{2,1,0:T(8,128)}, u32[]{:S(2)}, u32[]{:S(2)}) %collective-permute-start.19) | collective-permute-done | bytes 294944 | tf_op jit(solution)/shard_map/ppermute | solution.py:19
  157.3 5.0 %collective-permute-done.22 = f32[3,32,768]{2,1,0:T(8,128)S(1)} collective-permute-done((f32[3,32,768]{2,1,0:T(8,128)S(1)}, f32[3,32,768]{2,1,0:T(8,128)S(1)}, u32[]{:S(2)}, u32[]{:S(2)}) %collective-permute-start.22) | collective-permute-done | bytes 294944 | tf_op jit(solution)/shard_map/ppermute | solution.py:19
  162.3 2.3 %collective-permute-done.26 = f32[3,32,768]{2,1,0:T(8,128)S(1)} collective-permute-done((f32[3,32,768]{2,1,0:T(8,128)S(1)}, f32[3,32,768]{2,1,0:T(8,128)S(1)}, u32[]{:S(2)}, u32[]{:S(2)}) %collective-permute-start.26) | collective-permute-done | bytes 294944 | tf_op jit(solution)/shard_map/ppermute | solution.py:19
  167.9 4.7 %collective-permute-done.23 = f32[3,32,768]{2,1,0:T(8,128)S(1)} collective-permute-done((f32[3,32,768]{2,1,0:T(8,128)S(1)}, f32[3,32,768]{2,1,0:T(8,128)S(1)}, u32[]{:S(2)}, u32[]{:S(2)}) %collective-permute-start.23) | collective-permute-done | bytes 294944 | tf_op jit(solution)/shard_map/ppermute | solution.py:19
  175.4 2.5 %fusion.29 = f32[3,512,128]{1,2,0:T(8,128)S(1)} fusion(bf16[3,512,768]{2,1,0:T(8,128)(2,1)} %bitcast.37, bf16[3,128,768]{2,1,0:T(8,128)(2,1)S(1)} %bitcast.141), kind=kOutput, calls=%fused_computation.98 | convolution fusion | flops 301989888 | bytes 3735552 | tf_op jit(solution)/shard_map/knr,kmr->knm/dot_general | solution.py:81
  178.0 9.1 %collective-permute-done.28 = bf16[3,8,64,768]{3,2,1,0:T(8,128)(2,1)} collective-permute-done((bf16[3,8,64,768]{3,2,1,0:T(8,128)(2,1)}, bf16[3,8,64,768]{3,2,1,0:T(8,128)(2,1)}, u32[]{:S(2)}, u32[]{:S(2)}) %collective-permute-start.28) | collective-permute-done | bytes 2359328 | tf_op jit(solution)/shard_map/ppermute | solution.py:19
  187.1 2.5 %fusion.30 = f32[3,512,128]{1,2,0:T(8,128)S(1)} fusion(bf16[3,512,768]{2,1,0:T(8,128)(2,1)} %bitcast.41, bf16[3,128,768]{2,1,0:T(8,128)(2,1)S(1)} %bitcast.142), kind=kOutput, calls=%fused_computation.99 | convolution fusion | flops 301989888 | bytes 3735552 | tf_op jit(solution)/shard_map/knr,kmr->knm/dot_general | solution.py:81
  192.3 1.8 collective-permute-start.31
  194.1 1.8 collective-permute-start.32
  196.3 2.5 %collective-permute-done.31 = f32[3,2,32,128]{3,2,1,0:T(8,128)S(1)} collective-permute-done((f32[3,2,32,128]{3,2,1,0:T(8,128)S(1)}, f32[3,2,32,128]{3,2,1,0:T(8,128)S(1)}, u32[]{:S(2)}, u32[]{:S(2)}) %collective-permute-start.31) | collective-permute-done | bytes 98336 | tf_op jit(solution)/shard_map/ppermute | solution.py:19
  198.9 2.0 collective-permute-done.32
  201.0 3.2 %collective-permute-start.33 = (f32[3,32,128]{2,1,0:T(8,128)S(1)}, f32[3,32,128]{2,1,0:T(8,128)S(1)}, u32[]{:S(2)}, u32[]{:S(2)}) collective-permute-start(f32[3,32,128]{2,1,0:T(8,128)S(1)} %slice_bitcast_fusion.2), channel_id=1, source_target_pairs={{0,2},{1,3},{2,0},{3,1},{4,6},{5,7},{6,4},{7,5},{8,10},{9,11},{10,... | collective-permute-start | bytes 147464 | tf_op jit(solution)/shard_map/ppermute | solution.py:19
  (114 shorter events, 51.0 us)
Async XLA Ops:
  7.2 99.8 %all-gather.3.cloned.1.call-start = ((), (), s32[]{:S(2)}) async-start(), calls=%async_computation | async-start | bytes 2654208 | tf_op jit(solution)/shard_map/all_gather | solution.py:120
  8.3 26.5 %collective-permute-start.3 = (bf16[256,768]{1,0:T(8,128)(2,1)S(1)}, bf16[256,768]{1,0:T(8,128)(2,1)}, u32[]{:S(2)}, u32[]{:S(2)}) collective-permute-start(bf16[256,768]{1,0:T(8,128)(2,1)S(1)} %split.9), channel_id=1, source_target_pairs={{0,128},{1,129},{2,130},{3,131},{4,132},{5,133},{6,134},{7,135},{8... | collective-permute-start | bytes 1179656 | tf_op jit(solution)/shard_map/ppermute | solution.py:19
  11.9 17.9 %collective-permute-start = (bf16[3,64,768]{2,1,0:T(8,128)(2,1)S(1)}, bf16[3,64,768]{2,1,0:T(8,128)(2,1)S(1)}, u32[]{:S(2)}, u32[]{:S(2)}) collective-permute-start(bf16[3,64,768]{2,1,0:T(8,128)(2,1)S(1)} %multiply_bitcast_fusion), channel_id=1, source_target_pairs={{0,0},{1,1},{2,2},{3,3},{4,4},{5,5},{6,6},{7,7},{8,132},{9,133},{1... | collective-permute-start | bytes 884744 | tf_op jit(solution)/shard_map/ppermute | solution.py:19
  15.9 16.3 %collective-permute-start.1 = (bf16[3,64,768]{2,1,0:T(8,128)(2,1)S(1)}, bf16[3,64,768]{2,1,0:T(8,128)(2,1)S(1)}, u32[]{:S(2)}, u32[]{:S(2)}) collective-permute-start(bf16[3,64,768]{2,1,0:T(8,128)(2,1)S(1)} %multiply_bitcast_fusion), channel_id=1, source_target_pairs={{0,2},{1,3},{2,0},{3,1},{4,6},{5,7},{6,4},{7,5},{8,134},{9,135},{1... | collective-permute-start | bytes 884744 | tf_op jit(solution)/shard_map/ppermute | solution.py:19
  19.5 15.3 %collective-permute-start.2 = (bf16[3,64,768]{2,1,0:T(8,128)(2,1)S(1)}, bf16[3,64,768]{2,1,0:T(8,128)(2,1)S(1)}, u32[]{:S(2)}, u32[]{:S(2)}) collective-permute-start(bf16[3,64,768]{2,1,0:T(8,128)(2,1)S(1)} %multiply_bitcast_fusion), channel_id=1, source_target_pairs={{0,0},{1,17},{2,34},{3,51},{4,68},{5,85},{6,102},{7,119},{8,8},{9,... | collective-permute-start | bytes 884744 | tf_op jit(solution)/shard_map/ppermute | solution.py:19
  29.7 15.0 %collective-permute-start.7 = (bf16[384,768]{1,0:T(8,128)(2,1)S(1)}, bf16[384,768]{1,0:T(8,128)(2,1)}, u32[]{:S(2)}, u32[]{:S(2)}) collective-permute-start(bf16[384,768]{1,0:T(8,128)(2,1)S(1)} %split.10), channel_id=1, source_target_pairs={{0,128},{1,129},{2,130},{3,131},{4,132},{5,133},{6,134},{7,135},{8... | collective-permute-start | bytes 1769480 | tf_op jit(solution)/shard_map/ppermute | solution.py:19
  34.9 21.4 %collective-permute-start.4 = (bf16[3,2,64,768]{3,2,1,0:T(8,128)(2,1)S(1)}, bf16[3,2,64,768]{3,2,1,0:T(8,128)(2,1)S(1)}, u32[]{:S(2)}, u32[]{:S(2)}) collective-permute-start(bf16[3,2,64,768]{3,2,1,0:T(8,128)(2,1)S(1)} %pad_maximum_fusion.4), channel_id=1, source_target_pairs={{0,4},{1,5},{2,6},{3,7},{4,8},{5,9},{6,10},{7,11},{8,12},{9,13},{1... | collective-permute-start | bytes 1769480 | tf_op jit(solution)/shard_map/ppermute | solution.py:19
  36.1 20.1 %collective-permute-start.5 = (bf16[3,2,64,768]{3,2,1,0:T(8,128)(2,1)S(1)}, bf16[3,2,64,768]{3,2,1,0:T(8,128)(2,1)S(1)}, u32[]{:S(2)}, u32[]{:S(2)}) collective-permute-start(bf16[3,2,64,768]{3,2,1,0:T(8,128)(2,1)S(1)} %pad_maximum_fusion.4), channel_id=1, source_target_pairs={{0,12},{1,13},{2,14},{3,15},{4,0},{5,1},{6,2},{7,3},{8,4},{9,5},{1... | collective-permute-start | bytes 1769480 | tf_op jit(solution)/shard_map/ppermute | solution.py:19
  37.0 19.3 %collective-permute-start.6 = (bf16[3,64,768]{2,1,0:T(8,128)(2,1)S(1)}, bf16[3,64,768]{2,1,0:T(8,128)(2,1)}, u32[]{:S(2)}, u32[]{:S(2)}) collective-permute-start(bf16[3,64,768]{2,1,0:T(8,128)(2,1)S(1)} %collective-permute-done.2), channel_id=1, source_target_pairs={{0,0},{1,1},{2,2},{3,3},{4,4},{5,5},{6,6},{7,7},{8,128},{9,129},{1... | collective-permute-start | bytes 884744 | tf_op jit(solution)/shard_map/ppermute | solution.py:19
  57.0 10.7 %collective-permute-start.8 = (bf16[3,1,64,768]{3,2,1,0:T(8,128)(2,1)}, bf16[3,1,64,768]{3,2,1,0:T(8,128)(2,1)S(1)}, u32[]{:S(2)}, u32[]{:S(2)}) collective-permute-start(bf16[3,1,64,768]{3,2,1,0:T(8,128)(2,1)} %slice.114), channel_id=1, source_target_pairs={{0,4},{1,5},{2,6},{3,7},{4,8},{5,9},{6,10},{7,11},{8,12},{9,13},{1... | collective-permute-start | bytes 884744 | tf_op jit(solution)/shard_map/ppermute | solution.py:19
  57.7 10.0 %collective-permute-start.9 = (bf16[3,1,64,768]{3,2,1,0:T(8,128)(2,1)}, bf16[3,1,64,768]{3,2,1,0:T(8,128)(2,1)S(1)}, u32[]{:S(2)}, u32[]{:S(2)}) collective-permute-start(bf16[3,1,64,768]{3,2,1,0:T(8,128)(2,1)} %slice.115), channel_id=1, source_target_pairs={{0,12},{1,13},{2,14},{3,15},{4,0},{5,1},{6,2},{7,3},{8,4},{9,5},{1... | collective-permute-start | bytes 884744 | tf_op jit(solution)/shard_map/ppermute | solution.py:19
  60.5 7.2 %collective-permute-start.10 = (bf16[128,768]{1,0:T(8,128)(2,1)}, bf16[128,768]{1,0:T(8,128)(2,1)}, u32[]{:S(2)}, u32[]{:S(2)}) collective-permute-start(bf16[128,768]{1,0:T(8,128)(2,1)} %split.11), channel_id=1, source_target_pairs={{0,128},{1,129},{2,130},{3,131},{4,132},{5,133},{6,134},{7,135},{8... | collective-permute-start | bytes 589832 | tf_op jit(solution)/shard_map/ppermute | solution.py:19
  71.0 6.5 %collective-permute-start.11 = (bf16[2,3,2,2,64,768]{5,4,3,2,1,0:T(8,128)(2,1)}, bf16[2,3,2,2,64,768]{5,4,3,2,1,0:T(8,128)(2,1)}, u32[]{:S(2)}, u32[]{:S(2)}) collective-permute-start(bf16[2,3,2,2,64,768]{5,4,3,2,1,0:T(8,128)(2,1)} %pad_maximum_fusion), channel_id=1, source_target_pairs={{0,1},{1,0},{2,3},{3,2},{4,5},{5,4},{6,7},{7,6},{8,9},{9,8},{10,11... | collective-permute-start | bytes 7077896 | tf_op jit(solution)/shard_map/ppermute | solution.py:19
  108.6 6.9 %collective-permute-start.12 = (f32[3,16,768]{2,1,0:T(8,128)S(1)}, f32[3,16,768]{2,1,0:T(8,128)S(1)}, u32[]{:S(2)}, u32[]{:S(2)}) collective-permute-start(f32[3,16,768]{2,1,0:T(8,128)S(1)} %get-tuple-element.68), channel_id=1, source_target_pairs={{0,112},{1,113},{2,114},{3,115},{4,116},{5,117},{6,118},{7,119},{8... | collective-permute-start | bytes 442376 | tf_op jit(solution)/shard_map/ppermute | solution.py:19
  111.2 15.7 %collective-permute-start.20 = (f32[3,16,768]{2,1,0:T(8,128)S(1)}, f32[3,16,768]{2,1,0:T(8,128)S(1)}, u32[]{:S(2)}, u32[]{:S(2)}) collective-permute-start(f32[3,16,768]{2,1,0:T(8,128)S(1)} %get-tuple-element.74), channel_id=1, source_target_pairs={{0,112},{1,113},{2,114},{3,115},{4,116},{5,117},{6,118},{7,119},{8... | collective-permute-start | bytes 442376 | tf_op jit(solution)/shard_map/ppermute | solution.py:19
  111.9 22.6 %collective-permute-start.24 = (f32[3,16,768]{2,1,0:T(8,128)S(1)}, f32[3,16,768]{2,1,0:T(8,128)S(1)}, u32[]{:S(2)}, u32[]{:S(2)}) collective-permute-start(f32[3,16,768]{2,1,0:T(8,128)S(1)} %get-tuple-element.75), channel_id=1, source_target_pairs={{0,16},{1,17},{2,18},{3,19},{4,20},{5,21},{6,22},{7,23},{8,24},{9,... | collective-permute-start | bytes 442376 | tf_op jit(solution)/shard_map/ppermute | solution.py:19
  113.3 7.4 %collective-permute-start.16 = (f32[3,16,768]{2,1,0:T(8,128)S(1)}, f32[3,16,768]{2,1,0:T(8,128)S(1)}, u32[]{:S(2)}, u32[]{:S(2)}) collective-permute-start(f32[3,16,768]{2,1,0:T(8,128)S(1)} %get-tuple-element.69), channel_id=1, source_target_pairs={{0,16},{1,17},{2,18},{3,19},{4,20},{5,21},{6,22},{7,23},{8,24},{9,... | collective-permute-start | bytes 442376 | tf_op jit(solution)/shard_map/ppermute | solution.py:19
  115.6 7.5 %collective-permute-start.13 = (f32[3,32,768]{2,1,0:T(8,128)S(1)}, f32[3,32,768]{2,1,0:T(8,128)S(1)}, u32[]{:S(2)}, u32[]{:S(2)}) collective-permute-start(f32[3,32,768]{2,1,0:T(8,128)S(1)} %pad_maximum_fusion.7), channel_id=1, source_target_pairs={{0,112},{1,113},{2,114},{3,115},{4,116},{5,117},{6,118},{7,119},{8... | collective-permute-start | bytes 884744 | tf_op jit(solution)/shard_map/ppermute | solution.py:19
  120.8 8.0 %collective-permute-start.17 = (f32[3,32,768]{2,1,0:T(8,128)S(1)}, f32[3,32,768]{2,1,0:T(8,128)S(1)}, u32[]{:S(2)}, u32[]{:S(2)}) collective-permute-start(f32[3,32,768]{2,1,0:T(8,128)S(1)} %pad_maximum_fusion.8), channel_id=1, source_target_pairs={{0,16},{1,17},{2,18},{3,19},{4,20},{5,21},{6,22},{7,23},{8,24},{9,... | collective-permute-start | bytes 884744 | tf_op jit(solution)/shard_map/ppermute | solution.py:19
  123.2 11.2 %collective-permute-start.14 = (f32[3,32,768]{2,1,0:T(8,128)S(1)}, f32[3,32,768]{2,1,0:T(8,128)S(1)}, u32[]{:S(2)}, u32[]{:S(2)}) collective-permute-start(f32[3,32,768]{2,1,0:T(8,128)S(1)} %bitcast_add_fusion.7), channel_id=1, source_target_pairs={{0,112},{1,113},{2,114},{3,115},{4,116},{5,117},{6,118},{7,119},{8... | collective-permute-start | bytes 884744 | tf_op jit(solution)/shard_map/ppermute | solution.py:19
  127.0 18.6 %collective-permute-start.21 = (f32[3,32,768]{2,1,0:T(8,128)S(1)}, f32[3,32,768]{2,1,0:T(8,128)}, u32[]{:S(2)}, u32[]{:S(2)}) collective-permute-start(f32[3,32,768]{2,1,0:T(8,128)S(1)} %pad_maximum_fusion.9), channel_id=1, source_target_pairs={{0,112},{1,113},{2,114},{3,115},{4,116},{5,117},{6,118},{7,119},{8... | collective-permute-start | bytes 884744 | tf_op jit(solution)/shard_map/ppermute | solution.py:19
  134.4 9.2 %collective-permute-start.18 = (f32[3,32,768]{2,1,0:T(8,128)S(1)}, f32[3,32,768]{2,1,0:T(8,128)S(1)}, u32[]{:S(2)}, u32[]{:S(2)}) collective-permute-start(f32[3,32,768]{2,1,0:T(8,128)S(1)} %get-tuple-element.34), channel_id=1, source_target_pairs={{0,16},{1,17},{2,18},{3,19},{4,20},{5,21},{6,22},{7,23},{8,24},{9,... | collective-permute-start | bytes 884744 | tf_op jit(solution)/shard_map/ppermute | solution.py:19
  134.6 12.3 %collective-permute-start.25 = (f32[3,32,768]{2,1,0:T(8,128)S(1)}, f32[3,32,768]{2,1,0:T(8,128)}, u32[]{:S(2)}, u32[]{:S(2)}) collective-permute-start(f32[3,32,768]{2,1,0:T(8,128)S(1)} %pad_maximum_fusion.10), channel_id=1, source_target_pairs={{0,16},{1,17},{2,18},{3,19},{4,20},{5,21},{6,22},{7,23},{8,24},{9,... | collective-permute-start | bytes 884744 | tf_op jit(solution)/shard_map/ppermute | solution.py:19
  134.9 12.1 %collective-permute-start.15 = (f32[3,32,768]{2,1,0:T(8,128)S(1)}, f32[3,32,768]{2,1,0:T(8,128)}, u32[]{:S(2)}, u32[]{:S(2)}) collective-permute-start(f32[3,32,768]{2,1,0:T(8,128)S(1)} %get-tuple-element.33), channel_id=1, source_target_pairs={{0,112},{1,113},{2,114},{3,115},{4,116},{5,117},{6,118},{7,119},{8... | collective-permute-start | bytes 884744 | tf_op jit(solution)/shard_map/ppermute | solution.py:19
  143.7 9.8 %collective-permute-start.19 = (f32[3,32,768]{2,1,0:T(8,128)S(1)}, f32[3,32,768]{2,1,0:T(8,128)}, u32[]{:S(2)}, u32[]{:S(2)}) collective-permute-start(f32[3,32,768]{2,1,0:T(8,128)S(1)} %bitcast_add_fusion.6), channel_id=1, source_target_pairs={{0,16},{1,17},{2,18},{3,19},{4,20},{5,21},{6,22},{7,23},{8,24},{9,... | collective-permute-start | bytes 884744 | tf_op jit(solution)/shard_map/ppermute | solution.py:19
  143.8 43.3 %collective-permute-start.28 = (bf16[3,8,64,768]{3,2,1,0:T(8,128)(2,1)}, bf16[3,8,64,768]{3,2,1,0:T(8,128)(2,1)}, u32[]{:S(2)}, u32[]{:S(2)}) collective-permute-start(bf16[3,8,64,768]{3,2,1,0:T(8,128)(2,1)} %bitcast.19), channel_id=1, source_target_pairs={{0,128},{1,129},{2,130},{3,131},{4,132},{5,133},{6,134},{7,135},{8... | collective-permute-start | bytes 7077896 | tf_op jit(solution)/shard_map/ppermute | solution.py:19
  155.2 7.1 %collective-permute-start.22 = (f32[3,32,768]{2,1,0:T(8,128)S(1)}, f32[3,32,768]{2,1,0:T(8,128)S(1)}, u32[]{:S(2)}, u32[]{:S(2)}) collective-permute-start(f32[3,32,768]{2,1,0:T(8,128)S(1)} %get-tuple-element.32), channel_id=1, source_target_pairs={{0,112},{1,113},{2,114},{3,115},{4,116},{5,117},{6,118},{7,119},{8... | collective-permute-start | bytes 884744 | tf_op jit(solution)/shard_map/ppermute | solution.py:19
  156.3 8.4 %collective-permute-start.26 = (f32[3,32,768]{2,1,0:T(8,128)S(1)}, f32[3,32,768]{2,1,0:T(8,128)S(1)}, u32[]{:S(2)}, u32[]{:S(2)}) collective-permute-start(f32[3,32,768]{2,1,0:T(8,128)S(1)} %get-tuple-element.31), channel_id=1, source_target_pairs={{0,16},{1,17},{2,18},{3,19},{4,20},{5,21},{6,22},{7,23},{8,24},{9,... | collective-permute-start | bytes 884744 | tf_op jit(solution)/shard_map/ppermute | solution.py:19
  165.8 6.8 %collective-permute-start.23 = (f32[3,32,768]{2,1,0:T(8,128)S(1)}, f32[3,32,768]{2,1,0:T(8,128)S(1)}, u32[]{:S(2)}, u32[]{:S(2)}) collective-permute-start(f32[3,32,768]{2,1,0:T(8,128)S(1)} %get-tuple-element.41), channel_id=1, source_target_pairs={{0,112},{1,113},{2,114},{3,115},{4,116},{5,117},{6,118},{7,119},{8... | collective-permute-start | bytes 884744 | tf_op jit(solution)/shard_map/ppermute | solution.py:19
  166.2 8.0 %collective-permute-start.27 = (f32[3,32,768]{2,1,0:T(8,128)S(1)}, f32[3,32,768]{2,1,0:T(8,128)S(1)}, u32[]{:S(2)}, u32[]{:S(2)}) collective-permute-start(f32[3,32,768]{2,1,0:T(8,128)S(1)} %get-tuple-element.42), channel_id=1, source_target_pairs={{0,16},{1,17},{2,18},{3,19},{4,20},{5,21},{6,22},{7,23},{8,24},{9,... | collective-permute-start | bytes 884744 | tf_op jit(solution)/shard_map/ppermute | solution.py:19
  192.3 6.5 %collective-permute-start.31 = (f32[3,2,32,128]{3,2,1,0:T(8,128)S(1)}, f32[3,2,32,128]{3,2,1,0:T(8,128)S(1)}, u32[]{:S(2)}, u32[]{:S(2)}) collective-permute-start(f32[3,2,32,128]{3,2,1,0:T(8,128)S(1)} %get-tuple-element.58), channel_id=1, source_target_pairs={{0,8},{1,9},{2,10},{3,11},{4,12},{5,13},{6,14},{7,15},{8,0},{9,1},... | collective-permute-start | bytes 294920 | tf_op jit(solution)/shard_map/ppermute | solution.py:19
  194.1 6.8 %collective-permute-start.32 = (f32[3,2,32,128]{3,2,1,0:T(8,128)S(1)}, f32[3,2,32,128]{3,2,1,0:T(8,128)S(1)}, u32[]{:S(2)}, u32[]{:S(2)}) collective-permute-start(f32[3,2,32,128]{3,2,1,0:T(8,128)S(1)} %get-tuple-element.57), channel_id=1, source_target_pairs={{0,12},{1,13},{2,14},{3,15},{4,8},{5,9},{6,10},{7,11},{8,4},{9,5},... | collective-permute-start | bytes 294920 | tf_op jit(solution)/shard_map/ppermute | solution.py:19
  (8 other events, 95.7 us)
Sparse Core Ops, SparseCore 0:
  60.6 46.2 all-gather.2

commit v8 on v7

--- a/solution.py
+++ b/solution.py
@@ -109,19 +109,16 @@
     keep_rows = row_mask(pattern, row, per).astype(jnp.bfloat16)
     keep_cols = row_mask(pattern, col, per).astype(jnp.float32)
     own = factor_panel.transpose(0, 2, 1) * keep_rows[:, None, :]
-    cuts = rows // 3, rows * 5 // 6
-    beside = [send(piece, across) for piece in jnp.split(ancestor_inverse, cuts)]
     near, far = send(own, swap), send(own, swap_far)
-    near, far, turned, beside[0] = together(near, far, send(own, skewed), beside[0])
+    near, far, turned, ancestor = together(near, far, send(own, skewed), ancestor_inverse)
+    beside = [send(piece, across) for piece in jnp.split(ancestor, (rows // 2, rows * 5 // 6))]
     plane = jnp.stack([near, far], axis=1)
     left, right = send(plane, along_x(1)), send(plane, along_x(3))
     turned = send(turned, facing_place)
-    left, right, turned, beside[1] = together(left, right, turned, beside[1])
-    facing = lax.all_gather(turned, "z", axis=1)
-    facing = [facing, None]
+    left, right, _, beside[0] = together(left, right, turned, beside[0])
+    facing = [lax.all_gather(turned, "z", axis=1), None]
     opposite = send(left[:, :1], along_x(1)), send(right[:, 1:], along_x(3))
-    *opposite, beside[2] = together(*opposite, beside[2])
-    beside = jnp.concatenate(beside)
+    *opposite, beside[1] = together(*opposite, beside[1])
     own_rows = (x // 2) == yl
     mine = pair_rows(x, own_rows, plane, left, right, opposite)
 
@@ -130,7 +127,8 @@
         whole = dot_nt(panel[0], ancestor_inverse) + dot_nt(panel[1], beside)
         return whole.reshape(count, 4, cols, rows)
 
-    theirs = send(mine, sibling)
+    theirs, beside[2] = together(send(mine, sibling), beside[2])
+    beside = jnp.concatenate(beside)
     near, far, facing[0] = together(product(mine), product(theirs), facing[0])
     facing[1] = send(facing[0], across)
     column = jnp.where(own_rows, x % 2, 1 - x % 2)

time: 216 us -> 214 us (level)
  waiting for transfers between devices: 108 us -> 101 us
  starting transfers between devices: 56.8 us -> 61.8 us
  local copies, waits for them, and re-layouts: 10.1 us -> 7.77 us
    all_gather x1, waiting for transfers between devices: 23.7 us -> 16.8 us  [shards(): facing = [lax.all_gather(turned, 'z', axis=1), None]]
    ppermute x34, starting transfers between devices: 56.7 us -> 61.8 us  [send(): return lax.ppermute(value, AXES, pairs(move))]
where the time goes in v8:
time: 214 us; the launch traced here: 213 us
  waiting for transfers between devices  101 us (47%)
  starting transfers between devices  61.8 us (29%)
  other arithmetic  15.1 us (7%)
  between operations  14.5 us (7%)
  matrix products  12.7 us (6%)
  local copies, waits for them, and re-layouts  7.77 us (4%)
    ppermute x34, waiting for transfers between devices, send(): return lax.ppermute(value, AXES, pairs(move))  83.8 us
    ppermute x34, starting transfers between devices, send(): return lax.ppermute(value, AXES, pairs(move))  61.8 us
    all_gather x1, waiting for transfers between devices, shards(): facing = [lax.all_gather(turned, 'z', axis=1), None]  16.8 us
    dot_general x4, matrix products, dot_nt(): return lax.dot_general(a, b, NT, preferred_element_type=jnp.float32)  7.66 us
    dot_general x2, matrix products, dot_each(): return jnp.einsum('knr,kmr->knm', a, b, preferred_element_type=jnp.float32)  5.09 us
  transfers between devices with their start and end apart: 35, of which 23 were waited for; matrix products, arithmetic and copies ran while one was open for 12% of the time, Pallas kernels for 0%

profile of v8, /device:TPU:6, one launch (start us, length us, event | category | flops | bytes accessed | tf_op | source)
XLA Modules:
  0.0 212.5 jit_solution(16958765146889103706)
XLA Ops:
  9.1 3.4 %collective-permute-start = (bf16[3,64,768]{2,1,0:T(8,128)(2,1)S(1)}, bf16[3,64,768]{2,1,0:T(8,128)(2,1)S(1)}, u32[]{:S(2)}, u32[]{:S(2)}) collective-permute-start(bf16[3,64,768]{2,1,0:T(8,128)(2,1)S(1)} %multiply_bitcast_fusion), channel_id=1, source_target_pairs={{0,0},{1,1},{2,2},{3,3},{4,4},{5,5},{6,6},{7,7},{8,132},{9,133},{1... | collective-permute-start | bytes 884744 | tf_op jit(solution)/shard_map/ppermute | solution.py:19
  12.5 4.5 %collective-permute-start.1 = (bf16[3,64,768]{2,1,0:T(8,128)(2,1)S(1)}, bf16[3,64,768]{2,1,0:T(8,128)(2,1)S(1)}, u32[]{:S(2)}, u32[]{:S(2)}) collective-permute-start(bf16[3,64,768]{2,1,0:T(8,128)(2,1)S(1)} %multiply_bitcast_fusion), channel_id=1, source_target_pairs={{0,2},{1,3},{2,0},{3,1},{4,6},{5,7},{6,4},{7,5},{8,134},{9,135},{1... | collective-permute-start | bytes 884744 | tf_op jit(solution)/shard_map/ppermute | solution.py:19
  17.0 9.1 %collective-permute-start.2 = (bf16[3,64,768]{2,1,0:T(8,128)(2,1)S(1)}, bf16[3,64,768]{2,1,0:T(8,128)(2,1)S(1)}, u32[]{:S(2)}, u32[]{:S(2)}) collective-permute-start(bf16[3,64,768]{2,1,0:T(8,128)(2,1)S(1)} %multiply_bitcast_fusion), channel_id=1, source_target_pairs={{0,0},{1,17},{2,34},{3,51},{4,68},{5,85},{6,102},{7,119},{8,8},{9,... | collective-permute-start | bytes 884744 | tf_op jit(solution)/shard_map/ppermute | solution.py:19
  26.1 3.9 %collective-permute-done.1 = bf16[3,64,768]{2,1,0:T(8,128)(2,1)S(1)} collective-permute-done((bf16[3,64,768]{2,1,0:T(8,128)(2,1)S(1)}, bf16[3,64,768]{2,1,0:T(8,128)(2,1)S(1)}, u32[]{:S(2)}, u32[]{:S(2)}) %collective-permute-start.1) | collective-permute-done | bytes 294944 | tf_op jit(solution)/shard_map/ppermute | solution.py:19
  30.0 2.3 %collective-permute-done.2 = bf16[3,64,768]{2,1,0:T(8,128)(2,1)S(1)} collective-permute-done((bf16[3,64,768]{2,1,0:T(8,128)(2,1)S(1)}, bf16[3,64,768]{2,1,0:T(8,128)(2,1)S(1)}, u32[]{:S(2)}, u32[]{:S(2)}) %collective-permute-start.2) | collective-permute-done | bytes 294944 | tf_op jit(solution)/shard_map/ppermute | solution.py:19
  32.5 2.0 collective-permute-start.4
  35.7 2.2 %collective-permute-start.5 = (bf16[3,64,768]{2,1,0:T(8,128)(2,1)S(1)}, bf16[3,64,768]{2,1,0:T(8,128)(2,1)}, u32[]{:S(2)}, u32[]{:S(2)}) collective-permute-start(bf16[3,64,768]{2,1,0:T(8,128)(2,1)S(1)} %collective-permute-done.2), channel_id=1, source_target_pairs={{0,0},{1,1},{2,2},{3,3},{4,4},{5,5},{6,6},{7,7},{8,128},{9,129},{1... | collective-permute-start | bytes 884744 | tf_op jit(solution)/shard_map/ppermute | solution.py:19
  40.8 10.3 %collective-permute-done.5 = bf16[3,64,768]{2,1,0:T(8,128)(2,1)} collective-permute-done((bf16[3,64,768]{2,1,0:T(8,128)(2,1)S(1)}, bf16[3,64,768]{2,1,0:T(8,128)(2,1)}, u32[]{:S(2)}, u32[]{:S(2)}) %collective-permute-start.5) | collective-permute-done | bytes 294944 | tf_op jit(solution)/shard_map/ppermute | solution.py:19
  51.3 2.1 collective-permute-start.8
  53.5 9.2 %collective-permute-done.9 = bf16[256,768]{1,0:T(8,128)(2,1)S(1)} collective-permute-done((bf16[256,768]{1,0:T(8,128)(2,1)}, bf16[256,768]{1,0:T(8,128)(2,1)S(1)}, u32[]{:S(2)}, u32[]{:S(2)}) %collective-permute-start.9) | collective-permute-done | bytes 393248 | tf_op jit(solution)/shard_map/ppermute | solution.py:19
  67.7 5.9 %collective-permute-start.10 = (bf16[2,3,2,2,64,768]{5,4,3,2,1,0:T(8,128)(2,1)}, bf16[2,3,2,2,64,768]{5,4,3,2,1,0:T(8,128)(2,1)S(1)}, u32[]{:S(2)}, u32[]{:S(2)}) collective-permute-start(bf16[2,3,2,2,64,768]{5,4,3,2,1,0:T(8,128)(2,1)} %pad_maximum_fusion), channel_id=1, source_target_pairs={{0,1},{1,0},{2,3},{3,2},{4,5},{5,4},{6,7},{7,6},{8,9},{9,8},{10,11... | collective-permute-start | bytes 7077896 | tf_op jit(solution)/shard_map/ppermute | solution.py:19
  76.7 2.8 %fusion.27 = f32[768,768]{1,0:T(8,128)S(1)} fusion(bf16[768,768]{1,0:T(8,128)(2,1)} %bitcast.149, bf16[768,768]{1,0:T(8,128)(2,1)} %param.4), kind=kOutput, calls=%fused_computation.96 | convolution fusion | flops 905969664 | bytes 4718592 | tf_op jit(solution)/shard_map/dot_general | solution.py:69
  85.0 2.6 %convolution_add_fusion.1 = f32[768,768]{1,0:T(8,128)} fusion(f32[768,768]{1,0:T(8,128)S(1)} %fusion.27, bf16[768,768]{1,0:T(8,128)(2,1)S(1)} %bitcast.143, bf16[768,768]{1,0:T(8,128)(2,1)S(1)} %constant_dynamic-update-slice_fusion.2), kind=kOutput, calls=%fused_computation.2 | convolution fusion | flops 906559488 | bytes 7077888 | tf_op jit(solution)/shard_map/dot_general | solution.py:69
  87.7 16.8 %all-gather.3.cloned.1.call-done = bf16[3,512,768]{2,1,0:T(8,128)(2,1)} async-done(((bf16[3,64,768]{2,1,0:T(8,128)(2,1)}), bf16[3,512,768]{2,1,0:T(8,128)(2,1)}) %all-gather.3.cloned.1.call-update) | async-done | bytes 2359312 | tf_op jit(solution)/shard_map/all_gather | solution.py:119
  106.2 2.6 %collective-permute-start.12 = (f32[3,16,768]{2,1,0:T(8,128)S(1)}, f32[3,16,768]{2,1,0:T(8,128)S(1)}, u32[]{:S(2)}, u32[]{:S(2)}) collective-permute-start(f32[3,16,768]{2,1,0:T(8,128)S(1)} %get-tuple-element.70), channel_id=1, source_target_pairs={{0,112},{1,113},{2,114},{3,115},{4,116},{5,117},{6,118},{7,119},{8... | collective-permute-start | bytes 442376 | tf_op jit(solution)/shard_map/ppermute | solution.py:19
  110.9 2.2 %collective-permute-done.12 = f32[3,16,768]{2,1,0:T(8,128)S(1)} collective-permute-done((f32[3,16,768]{2,1,0:T(8,128)S(1)}, f32[3,16,768]{2,1,0:T(8,128)S(1)}, u32[]{:S(2)}, u32[]{:S(2)}) %collective-permute-start.12) | collective-permute-done | bytes 147488 | tf_op jit(solution)/shard_map/ppermute | solution.py:19
  113.1 2.9 %collective-permute-start.13 = (f32[3,32,768]{2,1,0:T(8,128)S(1)}, f32[3,32,768]{2,1,0:T(8,128)S(1)}, u32[]{:S(2)}, u32[]{:S(2)}) collective-permute-start(f32[3,32,768]{2,1,0:T(8,128)S(1)} %pad_maximum_fusion.7), channel_id=1, source_target_pairs={{0,112},{1,113},{2,114},{3,115},{4,116},{5,117},{6,118},{7,119},{8... | collective-permute-start | bytes 884744 | tf_op jit(solution)/shard_map/ppermute | solution.py:19
  116.1 2.3 %collective-permute-done.16 = f32[3,16,768]{2,1,0:T(8,128)S(1)} collective-permute-done((f32[3,16,768]{2,1,0:T(8,128)S(1)}, f32[3,16,768]{2,1,0:T(8,128)S(1)}, u32[]{:S(2)}, u32[]{:S(2)}) %collective-permute-start.16) | collective-permute-done | bytes 147488 | tf_op jit(solution)/shard_map/ppermute | solution.py:19
  120.7 3.7 %collective-permute-start.14 = (f32[3,32,768]{2,1,0:T(8,128)S(1)}, f32[3,32,768]{2,1,0:T(8,128)S(1)}, u32[]{:S(2)}, u32[]{:S(2)}) collective-permute-start(f32[3,32,768]{2,1,0:T(8,128)S(1)} %bitcast_add_fusion.7), channel_id=1, source_target_pairs={{0,112},{1,113},{2,114},{3,115},{4,116},{5,117},{6,118},{7,119},{8... | collective-permute-start | bytes 884744 | tf_op jit(solution)/shard_map/ppermute | solution.py:19
  126.4 4.7 %collective-permute-done.14 = f32[3,32,768]{2,1,0:T(8,128)S(1)} collective-permute-done((f32[3,32,768]{2,1,0:T(8,128)S(1)}, f32[3,32,768]{2,1,0:T(8,128)S(1)}, u32[]{:S(2)}, u32[]{:S(2)}) %collective-permute-start.14) | collective-permute-done | bytes 294944 | tf_op jit(solution)/shard_map/ppermute | solution.py:19
  132.8 3.1 %collective-permute-start.15 = (f32[3,32,768]{2,1,0:T(8,128)}, f32[3,32,768]{2,1,0:T(8,128)}, u32[]{:S(2)}, u32[]{:S(2)}) collective-permute-start(f32[3,32,768]{2,1,0:T(8,128)} %get-tuple-element.35), channel_id=1, source_target_pairs={{0,112},{1,113},{2,114},{3,115},{4,116},{5,117},{6,118},{7,119},{8... | collective-permute-start | bytes 884744 | tf_op jit(solution)/shard_map/ppermute | solution.py:19
  135.9 6.0 %collective-permute-done.18 = f32[3,32,768]{2,1,0:T(8,128)S(1)} collective-permute-done((f32[3,32,768]{2,1,0:T(8,128)S(1)}, f32[3,32,768]{2,1,0:T(8,128)S(1)}, u32[]{:S(2)}, u32[]{:S(2)}) %collective-permute-start.18) | collective-permute-done | bytes 294944 | tf_op jit(solution)/shard_map/ppermute | solution.py:19
  145.0 7.2 %collective-permute-done.19 = f32[3,32,768]{2,1,0:T(8,128)} collective-permute-done((f32[3,32,768]{2,1,0:T(8,128)S(1)}, f32[3,32,768]{2,1,0:T(8,128)}, u32[]{:S(2)}, u32[]{:S(2)}) %collective-permute-start.19) | collective-permute-done | bytes 294944 | tf_op jit(solution)/shard_map/ppermute | solution.py:19
  155.9 5.9 %collective-permute-done.22 = f32[3,32,768]{2,1,0:T(8,128)S(1)} collective-permute-done((f32[3,32,768]{2,1,0:T(8,128)S(1)}, f32[3,32,768]{2,1,0:T(8,128)S(1)}, u32[]{:S(2)}, u32[]{:S(2)}) %collective-permute-start.22) | collective-permute-done | bytes 294944 | tf_op jit(solution)/shard_map/ppermute | solution.py:19
  166.9 4.7 %collective-permute-done.23 = f32[3,32,768]{2,1,0:T(8,128)S(1)} collective-permute-done((f32[3,32,768]{2,1,0:T(8,128)S(1)}, f32[3,32,768]{2,1,0:T(8,128)S(1)}, u32[]{:S(2)}, u32[]{:S(2)}) %collective-permute-start.23) | collective-permute-done | bytes 294944 | tf_op jit(solution)/shard_map/ppermute | solution.py:19
  174.4 2.5 %fusion.29 = f32[3,512,128]{1,2,0:T(8,128)S(1)} fusion(bf16[3,512,768]{2,1,0:T(8,128)(2,1)} %bitcast.37, bf16[3,128,768]{2,1,0:T(8,128)(2,1)S(1)} %bitcast.141), kind=kOutput, calls=%fused_computation.98 | convolution fusion | flops 301989888 | bytes 3735552 | tf_op jit(solution)/shard_map/knr,kmr->knm/dot_general | solution.py:81
  177.0 8.4 %collective-permute-done.28 = bf16[3,8,64,768]{3,2,1,0:T(8,128)(2,1)} collective-permute-done((bf16[3,8,64,768]{3,2,1,0:T(8,128)(2,1)}, bf16[3,8,64,768]{3,2,1,0:T(8,128)(2,1)}, u32[]{:S(2)}, u32[]{:S(2)}) %collective-permute-start.28) | collective-permute-done | bytes 2359328 | tf_op jit(solution)/shard_map/ppermute | solution.py:19
  185.3 2.5 %fusion.30 = f32[3,512,128]{1,2,0:T(8,128)S(1)} fusion(bf16[3,512,768]{2,1,0:T(8,128)(2,1)} %bitcast.41, bf16[3,128,768]{2,1,0:T(8,128)(2,1)S(1)} %bitcast.142), kind=kOutput, calls=%fused_computation.99 | convolution fusion | flops 301989888 | bytes 3735552 | tf_op jit(solution)/shard_map/knr,kmr->knm/dot_general | solution.py:81
  192.1 2.1 collective-permute-start.32
  194.6 2.5 %collective-permute-done.31 = f32[3,2,32,128]{3,2,1,0:T(8,128)S(1)} collective-permute-done((f32[3,2,32,128]{3,2,1,0:T(8,128)S(1)}, f32[3,2,32,128]{3,2,1,0:T(8,128)S(1)}, u32[]{:S(2)}, u32[]{:S(2)}) %collective-permute-start.31) | collective-permute-done | bytes 98336 | tf_op jit(solution)/shard_map/ppermute | solution.py:19
  197.1 2.0 collective-permute-done.32
  199.2 3.1 %collective-permute-start.33 = (f32[3,32,128]{2,1,0:T(8,128)S(1)}, f32[3,32,128]{2,1,0:T(8,128)S(1)}, u32[]{:S(2)}, u32[]{:S(2)}) collective-permute-start(f32[3,32,128]{2,1,0:T(8,128)S(1)} %slice_bitcast_fusion.2), channel_id=1, source_target_pairs={{0,2},{1,3},{2,0},{3,1},{4,6},{5,7},{6,4},{7,5},{8,10},{9,11},{10,... | collective-permute-start | bytes 147464 | tf_op jit(solution)/shard_map/ppermute | solution.py:19
  (120 shorter events, 52.4 us)
Async XLA Ops:
  7.2 97.3 %all-gather.3.cloned.1.call-start = ((), (), s32[]{:S(2)}) async-start(), calls=%async_computation | async-start | bytes 2654208 | tf_op jit(solution)/shard_map/all_gather | solution.py:119
  9.1 17.0 %collective-permute-start = (bf16[3,64,768]{2,1,0:T(8,128)(2,1)S(1)}, bf16[3,64,768]{2,1,0:T(8,128)(2,1)S(1)}, u32[]{:S(2)}, u32[]{:S(2)}) collective-permute-start(bf16[3,64,768]{2,1,0:T(8,128)(2,1)S(1)} %multiply_bitcast_fusion), channel_id=1, source_target_pairs={{0,0},{1,1},{2,2},{3,3},{4,4},{5,5},{6,6},{7,7},{8,132},{9,133},{1... | collective-permute-start | bytes 884744 | tf_op jit(solution)/shard_map/ppermute | solution.py:19
  12.5 17.4 %collective-permute-start.1 = (bf16[3,64,768]{2,1,0:T(8,128)(2,1)S(1)}, bf16[3,64,768]{2,1,0:T(8,128)(2,1)S(1)}, u32[]{:S(2)}, u32[]{:S(2)}) collective-permute-start(bf16[3,64,768]{2,1,0:T(8,128)(2,1)S(1)} %multiply_bitcast_fusion), channel_id=1, source_target_pairs={{0,2},{1,3},{2,0},{3,1},{4,6},{5,7},{6,4},{7,5},{8,134},{9,135},{1... | collective-permute-start | bytes 884744 | tf_op jit(solution)/shard_map/ppermute | solution.py:19
  17.0 15.3 %collective-permute-start.2 = (bf16[3,64,768]{2,1,0:T(8,128)(2,1)S(1)}, bf16[3,64,768]{2,1,0:T(8,128)(2,1)S(1)}, u32[]{:S(2)}, u32[]{:S(2)}) collective-permute-start(bf16[3,64,768]{2,1,0:T(8,128)(2,1)S(1)} %multiply_bitcast_fusion), channel_id=1, source_target_pairs={{0,0},{1,17},{2,34},{3,51},{4,68},{5,85},{6,102},{7,119},{8,8},{9,... | collective-permute-start | bytes 884744 | tf_op jit(solution)/shard_map/ppermute | solution.py:19
  32.4 18.8 %collective-permute-start.3 = (bf16[3,2,64,768]{3,2,1,0:T(8,128)(2,1)S(1)}, bf16[3,2,64,768]{3,2,1,0:T(8,128)(2,1)S(1)}, u32[]{:S(2)}, u32[]{:S(2)}) collective-permute-start(bf16[3,2,64,768]{3,2,1,0:T(8,128)(2,1)S(1)} %pad_maximum_fusion.4), channel_id=1, source_target_pairs={{0,4},{1,5},{2,6},{3,7},{4,8},{5,9},{6,10},{7,11},{8,12},{9,13},{1... | collective-permute-start | bytes 1769480 | tf_op jit(solution)/shard_map/ppermute | solution.py:19
  32.5 18.7 %collective-permute-start.4 = (bf16[3,2,64,768]{3,2,1,0:T(8,128)(2,1)S(1)}, bf16[3,2,64,768]{3,2,1,0:T(8,128)(2,1)S(1)}, u32[]{:S(2)}, u32[]{:S(2)}) collective-permute-start(bf16[3,2,64,768]{3,2,1,0:T(8,128)(2,1)S(1)} %pad_maximum_fusion.4), channel_id=1, source_target_pairs={{0,12},{1,13},{2,14},{3,15},{4,0},{5,1},{6,2},{7,3},{8,4},{9,5},{1... | collective-permute-start | bytes 1769480 | tf_op jit(solution)/shard_map/ppermute | solution.py:19
  35.6 15.6 %collective-permute-start.6 = (bf16[384,768]{1,0:T(8,128)(2,1)S(1)}, bf16[384,768]{1,0:T(8,128)(2,1)S(1)}, u32[]{:S(2)}, u32[]{:S(2)}) collective-permute-start(bf16[384,768]{1,0:T(8,128)(2,1)S(1)} %split.9), channel_id=1, source_target_pairs={{0,128},{1,129},{2,130},{3,131},{4,132},{5,133},{6,134},{7,135},{8... | collective-permute-start | bytes 1769480 | tf_op jit(solution)/shard_map/ppermute | solution.py:19
  35.7 15.5 %collective-permute-start.5 = (bf16[3,64,768]{2,1,0:T(8,128)(2,1)S(1)}, bf16[3,64,768]{2,1,0:T(8,128)(2,1)}, u32[]{:S(2)}, u32[]{:S(2)}) collective-permute-start(bf16[3,64,768]{2,1,0:T(8,128)(2,1)S(1)} %collective-permute-done.2), channel_id=1, source_target_pairs={{0,0},{1,1},{2,2},{3,3},{4,4},{5,5},{6,6},{7,7},{8,128},{9,129},{1... | collective-permute-start | bytes 884744 | tf_op jit(solution)/shard_map/ppermute | solution.py:19
  39.7 23.0 %collective-permute-start.9 = (bf16[256,768]{1,0:T(8,128)(2,1)}, bf16[256,768]{1,0:T(8,128)(2,1)S(1)}, u32[]{:S(2)}, u32[]{:S(2)}) collective-permute-start(bf16[256,768]{1,0:T(8,128)(2,1)} %split.10), channel_id=1, source_target_pairs={{0,128},{1,129},{2,130},{3,131},{4,132},{5,133},{6,134},{7,135},{8... | collective-permute-start | bytes 1179656 | tf_op jit(solution)/shard_map/ppermute | solution.py:19
  51.2 11.5 %collective-permute-start.7 = (bf16[3,1,64,768]{3,2,1,0:T(8,128)(2,1)S(1)}, bf16[3,1,64,768]{3,2,1,0:T(8,128)(2,1)S(1)}, u32[]{:S(2)}, u32[]{:S(2)}) collective-permute-start(bf16[3,1,64,768]{3,2,1,0:T(8,128)(2,1)S(1)} %slice.114), channel_id=1, source_target_pairs={{0,4},{1,5},{2,6},{3,7},{4,8},{5,9},{6,10},{7,11},{8,12},{9,13},{1... | collective-permute-start | bytes 884744 | tf_op jit(solution)/shard_map/ppermute | solution.py:19
  51.3 11.3 %collective-permute-start.8 = (bf16[3,1,64,768]{3,2,1,0:T(8,128)(2,1)S(1)}, bf16[3,1,64,768]{3,2,1,0:T(8,128)(2,1)S(1)}, u32[]{:S(2)}, u32[]{:S(2)}) collective-permute-start(bf16[3,1,64,768]{3,2,1,0:T(8,128)(2,1)S(1)} %slice.115), channel_id=1, source_target_pairs={{0,12},{1,13},{2,14},{3,15},{4,0},{5,1},{6,2},{7,3},{8,4},{9,5},{1... | collective-permute-start | bytes 884744 | tf_op jit(solution)/shard_map/ppermute | solution.py:19
  67.7 13.8 %collective-permute-start.10 = (bf16[2,3,2,2,64,768]{5,4,3,2,1,0:T(8,128)(2,1)}, bf16[2,3,2,2,64,768]{5,4,3,2,1,0:T(8,128)(2,1)S(1)}, u32[]{:S(2)}, u32[]{:S(2)}) collective-permute-start(bf16[2,3,2,2,64,768]{5,4,3,2,1,0:T(8,128)(2,1)} %pad_maximum_fusion), channel_id=1, source_target_pairs={{0,1},{1,0},{2,3},{3,2},{4,5},{5,4},{6,7},{7,6},{8,9},{9,8},{10,11... | collective-permute-start | bytes 7077896 | tf_op jit(solution)/shard_map/ppermute | solution.py:19
  74.6 6.9 %collective-permute-start.11 = (bf16[128,768]{1,0:T(8,128)(2,1)S(1)}, bf16[128,768]{1,0:T(8,128)(2,1)S(1)}, u32[]{:S(2)}, u32[]{:S(2)}) collective-permute-start(bf16[128,768]{1,0:T(8,128)(2,1)S(1)} %split.11), channel_id=1, source_target_pairs={{0,128},{1,129},{2,130},{3,131},{4,132},{5,133},{6,134},{7,135},{8... | collective-permute-start | bytes 589832 | tf_op jit(solution)/shard_map/ppermute | solution.py:19
  106.2 6.9 %collective-permute-start.12 = (f32[3,16,768]{2,1,0:T(8,128)S(1)}, f32[3,16,768]{2,1,0:T(8,128)S(1)}, u32[]{:S(2)}, u32[]{:S(2)}) collective-permute-start(f32[3,16,768]{2,1,0:T(8,128)S(1)} %get-tuple-element.70), channel_id=1, source_target_pairs={{0,112},{1,113},{2,114},{3,115},{4,116},{5,117},{6,118},{7,119},{8... | collective-permute-start | bytes 442376 | tf_op jit(solution)/shard_map/ppermute | solution.py:19
  108.8 15.7 %collective-permute-start.20 = (f32[3,16,768]{2,1,0:T(8,128)S(1)}, f32[3,16,768]{2,1,0:T(8,128)S(1)}, u32[]{:S(2)}, u32[]{:S(2)}) collective-permute-start(f32[3,16,768]{2,1,0:T(8,128)S(1)} %get-tuple-element.76), channel_id=1, source_target_pairs={{0,112},{1,113},{2,114},{3,115},{4,116},{5,117},{6,118},{7,119},{8... | collective-permute-start | bytes 442376 | tf_op jit(solution)/shard_map/ppermute | solution.py:19
  109.5 22.5 %collective-permute-start.24 = (f32[3,16,768]{2,1,0:T(8,128)S(1)}, f32[3,16,768]{2,1,0:T(8,128)S(1)}, u32[]{:S(2)}, u32[]{:S(2)}) collective-permute-start(f32[3,16,768]{2,1,0:T(8,128)S(1)} %get-tuple-element.77), channel_id=1, source_target_pairs={{0,16},{1,17},{2,18},{3,19},{4,20},{5,21},{6,22},{7,23},{8,24},{9,... | collective-permute-start | bytes 442376 | tf_op jit(solution)/shard_map/ppermute | solution.py:19
  110.9 7.5 %collective-permute-start.16 = (f32[3,16,768]{2,1,0:T(8,128)S(1)}, f32[3,16,768]{2,1,0:T(8,128)S(1)}, u32[]{:S(2)}, u32[]{:S(2)}) collective-permute-start(f32[3,16,768]{2,1,0:T(8,128)S(1)} %get-tuple-element.71), channel_id=1, source_target_pairs={{0,16},{1,17},{2,18},{3,19},{4,20},{5,21},{6,22},{7,23},{8,24},{9,... | collective-permute-start | bytes 442376 | tf_op jit(solution)/shard_map/ppermute | solution.py:19
  113.1 7.5 %collective-permute-start.13 = (f32[3,32,768]{2,1,0:T(8,128)S(1)}, f32[3,32,768]{2,1,0:T(8,128)S(1)}, u32[]{:S(2)}, u32[]{:S(2)}) collective-permute-start(f32[3,32,768]{2,1,0:T(8,128)S(1)} %pad_maximum_fusion.7), channel_id=1, source_target_pairs={{0,112},{1,113},{2,114},{3,115},{4,116},{5,117},{6,118},{7,119},{8... | collective-permute-start | bytes 884744 | tf_op jit(solution)/shard_map/ppermute | solution.py:19
  118.4 8.0 %collective-permute-start.17 = (f32[3,32,768]{2,1,0:T(8,128)S(1)}, f32[3,32,768]{2,1,0:T(8,128)S(1)}, u32[]{:S(2)}, u32[]{:S(2)}) collective-permute-start(f32[3,32,768]{2,1,0:T(8,128)S(1)} %pad_maximum_fusion.8), channel_id=1, source_target_pairs={{0,16},{1,17},{2,18},{3,19},{4,20},{5,21},{6,22},{7,23},{8,24},{9,... | collective-permute-start | bytes 884744 | tf_op jit(solution)/shard_map/ppermute | solution.py:19
  120.7 10.4 %collective-permute-start.14 = (f32[3,32,768]{2,1,0:T(8,128)S(1)}, f32[3,32,768]{2,1,0:T(8,128)S(1)}, u32[]{:S(2)}, u32[]{:S(2)}) collective-permute-start(f32[3,32,768]{2,1,0:T(8,128)S(1)} %bitcast_add_fusion.7), channel_id=1, source_target_pairs={{0,112},{1,113},{2,114},{3,115},{4,116},{5,117},{6,118},{7,119},{8... | collective-permute-start | bytes 884744 | tf_op jit(solution)/shard_map/ppermute | solution.py:19
  124.5 19.4 %collective-permute-start.21 = (f32[3,32,768]{2,1,0:T(8,128)S(1)}, f32[3,32,768]{2,1,0:T(8,128)}, u32[]{:S(2)}, u32[]{:S(2)}) collective-permute-start(f32[3,32,768]{2,1,0:T(8,128)S(1)} %pad_maximum_fusion.9), channel_id=1, source_target_pairs={{0,112},{1,113},{2,114},{3,115},{4,116},{5,117},{6,118},{7,119},{8... | collective-permute-start | bytes 884744 | tf_op jit(solution)/shard_map/ppermute | solution.py:19
  132.0 9.9 %collective-permute-start.18 = (f32[3,32,768]{2,1,0:T(8,128)S(1)}, f32[3,32,768]{2,1,0:T(8,128)S(1)}, u32[]{:S(2)}, u32[]{:S(2)}) collective-permute-start(f32[3,32,768]{2,1,0:T(8,128)S(1)} %get-tuple-element.36), channel_id=1, source_target_pairs={{0,16},{1,17},{2,18},{3,19},{4,20},{5,21},{6,22},{7,23},{8,24},{9,... | collective-permute-start | bytes 884744 | tf_op jit(solution)/shard_map/ppermute | solution.py:19
  132.0 13.0 %collective-permute-start.25 = (f32[3,32,768]{2,1,0:T(8,128)S(1)}, f32[3,32,768]{2,1,0:T(8,128)S(1)}, u32[]{:S(2)}, u32[]{:S(2)}) collective-permute-start(f32[3,32,768]{2,1,0:T(8,128)S(1)} %pad_maximum_fusion.10), channel_id=1, source_target_pairs={{0,16},{1,17},{2,18},{3,19},{4,20},{5,21},{6,22},{7,23},{8,24},{9,... | collective-permute-start | bytes 884744 | tf_op jit(solution)/shard_map/ppermute | solution.py:19
  132.8 12.3 %collective-permute-start.15 = (f32[3,32,768]{2,1,0:T(8,128)}, f32[3,32,768]{2,1,0:T(8,128)}, u32[]{:S(2)}, u32[]{:S(2)}) collective-permute-start(f32[3,32,768]{2,1,0:T(8,128)} %get-tuple-element.35), channel_id=1, source_target_pairs={{0,112},{1,113},{2,114},{3,115},{4,116},{5,117},{6,118},{7,119},{8... | collective-permute-start | bytes 884744 | tf_op jit(solution)/shard_map/ppermute | solution.py:19
  141.9 10.3 %collective-permute-start.19 = (f32[3,32,768]{2,1,0:T(8,128)S(1)}, f32[3,32,768]{2,1,0:T(8,128)}, u32[]{:S(2)}, u32[]{:S(2)}) collective-permute-start(f32[3,32,768]{2,1,0:T(8,128)S(1)} %bitcast_add_fusion.6), channel_id=1, source_target_pairs={{0,16},{1,17},{2,18},{3,19},{4,20},{5,21},{6,22},{7,23},{8,24},{9,... | collective-permute-start | bytes 884744 | tf_op jit(solution)/shard_map/ppermute | solution.py:19
  142.0 43.3 %collective-permute-start.28 = (bf16[3,8,64,768]{3,2,1,0:T(8,128)(2,1)}, bf16[3,8,64,768]{3,2,1,0:T(8,128)(2,1)}, u32[]{:S(2)}, u32[]{:S(2)}) collective-permute-start(bf16[3,8,64,768]{3,2,1,0:T(8,128)(2,1)} %bitcast.19), channel_id=1, source_target_pairs={{0,128},{1,129},{2,130},{3,131},{4,132},{5,133},{6,134},{7,135},{8... | collective-permute-start | bytes 7077896 | tf_op jit(solution)/shard_map/ppermute | solution.py:19
  153.8 8.0 %collective-permute-start.22 = (f32[3,32,768]{2,1,0:T(8,128)S(1)}, f32[3,32,768]{2,1,0:T(8,128)S(1)}, u32[]{:S(2)}, u32[]{:S(2)}) collective-permute-start(f32[3,32,768]{2,1,0:T(8,128)S(1)} %get-tuple-element.34), channel_id=1, source_target_pairs={{0,112},{1,113},{2,114},{3,115},{4,116},{5,117},{6,118},{7,119},{8... | collective-permute-start | bytes 884744 | tf_op jit(solution)/shard_map/ppermute | solution.py:19
  154.3 9.2 %collective-permute-start.26 = (f32[3,32,768]{2,1,0:T(8,128)S(1)}, f32[3,32,768]{2,1,0:T(8,128)S(1)}, u32[]{:S(2)}, u32[]{:S(2)}) collective-permute-start(f32[3,32,768]{2,1,0:T(8,128)S(1)} %get-tuple-element.33), channel_id=1, source_target_pairs={{0,16},{1,17},{2,18},{3,19},{4,20},{5,21},{6,22},{7,23},{8,24},{9,... | collective-permute-start | bytes 884744 | tf_op jit(solution)/shard_map/ppermute | solution.py:19
  164.6 7.0 %collective-permute-start.23 = (f32[3,32,768]{2,1,0:T(8,128)S(1)}, f32[3,32,768]{2,1,0:T(8,128)S(1)}, u32[]{:S(2)}, u32[]{:S(2)}) collective-permute-start(f32[3,32,768]{2,1,0:T(8,128)S(1)} %get-tuple-element.43), channel_id=1, source_target_pairs={{0,112},{1,113},{2,114},{3,115},{4,116},{5,117},{6,118},{7,119},{8... | collective-permute-start | bytes 884744 | tf_op jit(solution)/shard_map/ppermute | solution.py:19
  165.2 7.9 %collective-permute-start.27 = (f32[3,32,768]{2,1,0:T(8,128)S(1)}, f32[3,32,768]{2,1,0:T(8,128)S(1)}, u32[]{:S(2)}, u32[]{:S(2)}) collective-permute-start(f32[3,32,768]{2,1,0:T(8,128)S(1)} %get-tuple-element.44), channel_id=1, source_target_pairs={{0,16},{1,17},{2,18},{3,19},{4,20},{5,21},{6,22},{7,23},{8,24},{9,... | collective-permute-start | bytes 884744 | tf_op jit(solution)/shard_map/ppermute | solution.py:19
  190.5 6.5 %collective-permute-start.31 = (f32[3,2,32,128]{3,2,1,0:T(8,128)S(1)}, f32[3,2,32,128]{3,2,1,0:T(8,128)S(1)}, u32[]{:S(2)}, u32[]{:S(2)}) collective-permute-start(f32[3,2,32,128]{3,2,1,0:T(8,128)S(1)} %get-tuple-element.60), channel_id=1, source_target_pairs={{0,8},{1,9},{2,10},{3,11},{4,12},{5,13},{6,14},{7,15},{8,0},{9,1},... | collective-permute-start | bytes 294920 | tf_op jit(solution)/shard_map/ppermute | solution.py:19
  192.1 7.0 %collective-permute-start.32 = (f32[3,2,32,128]{3,2,1,0:T(8,128)S(1)}, f32[3,2,32,128]{3,2,1,0:T(8,128)S(1)}, u32[]{:S(2)}, u32[]{:S(2)}) collective-permute-start(f32[3,2,32,128]{3,2,1,0:T(8,128)S(1)} %get-tuple-element.59), channel_id=1, source_target_pairs={{0,12},{1,13},{2,14},{3,15},{4,8},{5,9},{6,10},{7,11},{8,4},{9,5},... | collective-permute-start | bytes 294920 | tf_op jit(solution)/shard_map/ppermute | solution.py:19
  (11 other events, 62.5 us)
Sparse Core Ops, SparseCore 0:
  53.6 50.8 all-gather.2

commit v9 on v8

--- a/solution.py
+++ b/solution.py
@@ -88,17 +88,31 @@
     return jnp.stack([jnp.stack([here[h], there[h]], axis=1) for h in range(2)])
 
 
-def sum_over_z(block, half):
-    down = send(block(4)[:, :half], along_z(-1))
-    up = send(block(4)[:, half:], along_z(1))
-    below, above = block(-3), block(3)
+def with_own(block, half, offset, down, up):
+    below, above = block(-offset), block(offset)
+    if offset < 3:
+        return below + down, above + up
     down = jnp.concatenate([below[:, :half] + down, below[:, half:]], axis=1)
     up = jnp.concatenate([above[:, :half], above[:, half:] + up], axis=1)
-    for offset in (2, 1, 0):
-        down, up = send(down, along_z(-1)), send(up, along_z(1))
-        if offset:
-            down, up = block(-offset) + down, block(offset) + up
-    return block(0) + down + up
+    return down, up
+
+
+def sum_over_z(first, second, half, extra):
+    def both_ways(pair):
+        return send(pair[0], along_z(-1)), send(pair[1], along_z(1))
+
+    def behind(pair, *others):
+        return together(*pair, *others)[:2]
+
+    one, two = ((block(4)[:, :half], block(4)[:, half:]) for block in (first, second))
+    for offset in (3, 2, 1):
+        got = both_ways(one)
+        if offset == 3:
+            *got, extra = together(*got, extra)
+        one = with_own(first, half, offset, *behind(got, *two))
+        two = with_own(second, half, offset, *behind(both_ways(two), *one))
+    one, two = both_ways(one), both_ways(two)
+    return first(0) + one[0] + one[1], second(0) + two[0] + two[1], extra
 
 
 def shards(ancestor_inverse, factor_panel, pattern, diagonal_inverse):
@@ -129,8 +143,7 @@
 
     theirs, beside[2] = together(send(mine, sibling), beside[2])
     beside = jnp.concatenate(beside)
-    near, far, facing[0] = together(product(mine), product(theirs), facing[0])
-    facing[1] = send(facing[0], across)
+    near, far = product(mine), product(theirs)
     column = jnp.where(own_rows, x % 2, 1 - x % 2)
     wide = cols // 2
 
@@ -141,9 +154,9 @@
         picked = (lax.dynamic_slice(side, start, size) for side in (near, far))
         return jnp.where(place % 2 == core, *picked).reshape(count, wide, rows)
 
-    reduced = [
-        sum_over_z(lambda offset, first=first: block(first, offset), wide // 2) for first in (0, wide)
-    ]
+    chunks = [lambda offset, first=first: block(first, offset) for first in (0, wide)]
+    *reduced, facing[0] = sum_over_z(*chunks, wide // 2, facing[0])
+    facing[1] = send(facing[0], across)
     reduced = jnp.concatenate(reduced, axis=1)
     offdiag = -(reduced * keep_cols[:, None, :])
     high = lax.reduce_precision(reduced, 8, 7)

time: 214 us -> 217 us (1.014)
  waiting for transfers between devices: 101 us -> 94.2 us
  other arithmetic: 15.1 us -> 20.3 us
  starting transfers between devices: 61.8 us -> 65.9 us
  local copies, waits for them, and re-layouts: 7.77 us -> 11.5 us
  matrix products: 12.7 us -> 9.24 us
    ppermute x34, waiting for transfers between devices: 83.8 us -> 76.9 us  [send(): return lax.ppermute(value, AXES, pairs(move))]
    add x8 -> x7, other arithmetic: 4.73 us -> 9.69 us  [the longest x3 5.18 us: with_own(): return (below + down, above + up)]
    ppermute x34, starting transfers between devices: 61.8 us -> 65.8 us  [send(): return lax.ppermute(value, AXES, pairs(move))]
    unnamed x23 -> x25, local copies, waits for them, and re-layouts: 3.17 us -> 5.85 us
where the time goes in v9:
time: 217 us; the launch traced here: 216 us
  waiting for transfers between devices  94.2 us (43%)
  starting transfers between devices  65.9 us (30%)
  other arithmetic  20.3 us (9%)
  between operations  14.9 us (7%)
  local copies, waits for them, and re-layouts  11.5 us (5%)
  matrix products  9.24 us (4%)
    ppermute x34, waiting for transfers between devices, send(): return lax.ppermute(value, AXES, pairs(move))  76.9 us
    ppermute x34, starting transfers between devices, send(): return lax.ppermute(value, AXES, pairs(move))  65.8 us
    all_gather x1, waiting for transfers between devices, shards(): facing = [lax.all_gather(turned, 'z', axis=1), None]  17.2 us
    unnamed x25, local copies, waits for them, and re-layouts  5.85 us
    dot_general x4, matrix products, dot_nt(): return lax.dot_general(a, b, NT, preferred_element_type=jnp.float32)  5.82 us
    add x3, other arithmetic, with_own(): return (below + down, above + up)  5.18 us
  transfers between devices with their start and end apart: 35, of which 23 were waited for; matrix products, arithmetic and copies ran while one was open for 12% of the time, Pallas kernels for 0%

profile of v9, /device:TPU:6, one launch (start us, length us, event | category | flops | bytes accessed | tf_op | source)
XLA Modules:
  0.0 215.9 jit_solution(18053635780097187575)
XLA Ops:
  9.2 3.4 %collective-permute-start = (bf16[3,64,768]{2,1,0:T(8,128)(2,1)S(1)}, bf16[3,64,768]{2,1,0:T(8,128)(2,1)S(1)}, u32[]{:S(2)}, u32[]{:S(2)}) collective-permute-start(bf16[3,64,768]{2,1,0:T(8,128)(2,1)S(1)} %multiply_bitcast_fusion), channel_id=1, source_target_pairs={{0,0},{1,1},{2,2},{3,3},{4,4},{5,5},{6,6},{7,7},{8,132},{9,133},{1... | collective-permute-start | bytes 884744 | tf_op jit(solution)/shard_map/ppermute | solution.py:19
  12.6 4.5 %collective-permute-start.1 = (bf16[3,64,768]{2,1,0:T(8,128)(2,1)S(1)}, bf16[3,64,768]{2,1,0:T(8,128)(2,1)S(1)}, u32[]{:S(2)}, u32[]{:S(2)}) collective-permute-start(bf16[3,64,768]{2,1,0:T(8,128)(2,1)S(1)} %multiply_bitcast_fusion), channel_id=1, source_target_pairs={{0,2},{1,3},{2,0},{3,1},{4,6},{5,7},{6,4},{7,5},{8,134},{9,135},{1... | collective-permute-start | bytes 884744 | tf_op jit(solution)/shard_map/ppermute | solution.py:19
  17.0 9.1 %collective-permute-start.2 = (bf16[3,64,768]{2,1,0:T(8,128)(2,1)S(1)}, bf16[3,64,768]{2,1,0:T(8,128)(2,1)S(1)}, u32[]{:S(2)}, u32[]{:S(2)}) collective-permute-start(bf16[3,64,768]{2,1,0:T(8,128)(2,1)S(1)} %multiply_bitcast_fusion), channel_id=1, source_target_pairs={{0,0},{1,17},{2,34},{3,51},{4,68},{5,85},{6,102},{7,119},{8,8},{9,... | collective-permute-start | bytes 884744 | tf_op jit(solution)/shard_map/ppermute | solution.py:19
  26.1 3.9 %collective-permute-done.1 = bf16[3,64,768]{2,1,0:T(8,128)(2,1)S(1)} collective-permute-done((bf16[3,64,768]{2,1,0:T(8,128)(2,1)S(1)}, bf16[3,64,768]{2,1,0:T(8,128)(2,1)S(1)}, u32[]{:S(2)}, u32[]{:S(2)}) %collective-permute-start.1) | collective-permute-done | bytes 294944 | tf_op jit(solution)/shard_map/ppermute | solution.py:19
  30.0 2.3 %collective-permute-done.2 = bf16[3,64,768]{2,1,0:T(8,128)(2,1)S(1)} collective-permute-done((bf16[3,64,768]{2,1,0:T(8,128)(2,1)S(1)}, bf16[3,64,768]{2,1,0:T(8,128)(2,1)S(1)}, u32[]{:S(2)}, u32[]{:S(2)}) %collective-permute-start.2) | collective-permute-done | bytes 294944 | tf_op jit(solution)/shard_map/ppermute | solution.py:19
  33.2 2.0 collective-permute-start.4
  36.1 2.2 %collective-permute-start.5 = (bf16[3,64,768]{2,1,0:T(8,128)(2,1)S(1)}, bf16[3,64,768]{2,1,0:T(8,128)(2,1)}, u32[]{:S(2)}, u32[]{:S(2)}) collective-permute-start(bf16[3,64,768]{2,1,0:T(8,128)(2,1)S(1)} %collective-permute-done.2), channel_id=1, source_target_pairs={{0,0},{1,1},{2,2},{3,3},{4,4},{5,5},{6,6},{7,7},{8,128},{9,129},{1... | collective-permute-start | bytes 884744 | tf_op jit(solution)/shard_map/ppermute | solution.py:19
  40.3 11.8 %collective-permute-done.5 = bf16[3,64,768]{2,1,0:T(8,128)(2,1)} collective-permute-done((bf16[3,64,768]{2,1,0:T(8,128)(2,1)S(1)}, bf16[3,64,768]{2,1,0:T(8,128)(2,1)}, u32[]{:S(2)}, u32[]{:S(2)}) %collective-permute-start.5) | collective-permute-done | bytes 294944 | tf_op jit(solution)/shard_map/ppermute | solution.py:19
  53.7 2.0 collective-permute-start.8
  55.7 7.6 %collective-permute-done.9 = bf16[256,768]{1,0:T(8,128)(2,1)S(1)} collective-permute-done((bf16[256,768]{1,0:T(8,128)(2,1)}, bf16[256,768]{1,0:T(8,128)(2,1)S(1)}, u32[]{:S(2)}, u32[]{:S(2)}) %collective-permute-start.9) | collective-permute-done | bytes 393248 | tf_op jit(solution)/shard_map/ppermute | solution.py:19
  67.3 7.3 %collective-permute-start.10 = (bf16[2,3,2,2,64,768]{5,4,3,2,1,0:T(8,128)(2,1)}, bf16[2,3,2,2,64,768]{5,4,3,2,1,0:T(8,128)(2,1)S(1)}, u32[]{:S(2)}, u32[]{:S(2)}) collective-permute-start(bf16[2,3,2,2,64,768]{5,4,3,2,1,0:T(8,128)(2,1)} %pad_maximum_fusion), channel_id=1, source_target_pairs={{0,1},{1,0},{2,3},{3,2},{4,5},{5,4},{6,7},{7,6},{8,9},{9,8},{10,11... | collective-permute-start | bytes 7077896 | tf_op jit(solution)/shard_map/ppermute | solution.py:19
  78.5 2.4 %fusion.53 = f32[768,768]{1,0:T(8,128)S(1)} fusion(bf16[768,768]{1,0:T(8,128)(2,1)S(1)} %bitcast.288, bf16[768,768]{1,0:T(8,128)(2,1)} %param.4), kind=kOutput, calls=%fused_computation.122 | convolution fusion | flops 905969664 | bytes 4718592 | tf_op jit(solution)/shard_map/dot_general | solution.py:69
  81.0 2.0 collective-permute-done.11
  89.2 3.9 %collective-permute-start.12 = (f32[3,16,768]{2,1,0:T(8,128)S(1)}, f32[3,16,768]{2,1,0:T(8,128)}, u32[]{:S(2)}, u32[]{:S(2)}) collective-permute-start(f32[3,16,768]{2,1,0:T(8,128)S(1)} %get-tuple-element.103), channel_id=1, source_target_pairs={{0,112},{1,113},{2,114},{3,115},{4,116},{5,117},{6,118},{7,119},{8... | collective-permute-start | bytes 442376 | tf_op jit(solution)/shard_map/ppermute | solution.py:19
  95.4 3.9 %collective-permute-start.16 = (f32[3,16,768]{2,1,0:T(8,128)}, f32[3,16,768]{2,1,0:T(8,128)}, u32[]{:S(2)}, u32[]{:S(2)}) collective-permute-start(f32[3,16,768]{2,1,0:T(8,128)} %get-tuple-element.105), channel_id=1, source_target_pairs={{0,112},{1,113},{2,114},{3,115},{4,116},{5,117},{6,118},{7,119},{8... | collective-permute-start | bytes 442376 | tf_op jit(solution)/shard_map/ppermute | solution.py:19
  99.3 3.1 %collective-permute-done.12 = f32[3,16,768]{2,1,0:T(8,128)} collective-permute-done((f32[3,16,768]{2,1,0:T(8,128)S(1)}, f32[3,16,768]{2,1,0:T(8,128)}, u32[]{:S(2)}, u32[]{:S(2)}) %collective-permute-start.12) | collective-permute-done | bytes 147488 | tf_op jit(solution)/shard_map/ppermute | solution.py:19
  102.3 4.1 %collective-permute-done.13 = f32[3,16,768]{2,1,0:T(8,128)} collective-permute-done((f32[3,16,768]{2,1,0:T(8,128)S(1)}, f32[3,16,768]{2,1,0:T(8,128)}, u32[]{:S(2)}, u32[]{:S(2)}) %collective-permute-start.13) | collective-permute-done | bytes 147488 | tf_op jit(solution)/shard_map/ppermute | solution.py:19
  106.5 17.2 %all-gather.3.cloned.1.call-done = bf16[3,512,768]{2,1,0:T(8,128)(2,1)} async-done(((bf16[3,64,768]{2,1,0:T(8,128)(2,1)}), bf16[3,512,768]{2,1,0:T(8,128)(2,1)}) %all-gather.3.cloned.1.call-update) | async-done | bytes 2359312 | tf_op jit(solution)/shard_map/all_gather | solution.py:133
  131.4 2.9 %collective-permute-start.20 = (f32[3,32,768]{2,1,0:T(8,128)S(1)}, f32[3,32,768]{2,1,0:T(8,128)}, u32[]{:S(2)}, u32[]{:S(2)}) collective-permute-start(f32[3,32,768]{2,1,0:T(8,128)S(1)} %pad_maximum_fusion.9), channel_id=1, source_target_pairs={{0,112},{1,113},{2,114},{3,115},{4,116},{5,117},{6,118},{7,119},{8... | collective-permute-start | bytes 884744 | tf_op jit(solution)/shard_map/ppermute | solution.py:19
  134.3 2.6 %collective-permute-done.14 = f32[3,32,768]{2,1,0:T(8,128)S(1)} collective-permute-done((f32[3,32,768]{2,1,0:T(8,128)S(1)}, f32[3,32,768]{2,1,0:T(8,128)S(1)}, u32[]{:S(2)}, u32[]{:S(2)}) %collective-permute-start.14) | collective-permute-done | bytes 294944 | tf_op jit(solution)/shard_map/ppermute | solution.py:19
  137.0 2.0 fusion.18
  144.6 2.3 %collective-permute-start.24 = (f32[3,32,768]{2,1,0:T(8,128)S(1)}, f32[3,32,768]{2,1,0:T(8,128)}, u32[]{:S(2)}, u32[]{:S(2)}) collective-permute-start(f32[3,32,768]{2,1,0:T(8,128)S(1)} %get-tuple-element.62), channel_id=1, source_target_pairs={{0,112},{1,113},{2,114},{3,115},{4,116},{5,117},{6,118},{7,119},{8... | collective-permute-start | bytes 884744 | tf_op jit(solution)/shard_map/ppermute | solution.py:19
  146.9 2.7 %collective-permute-done.18 = f32[3,32,768]{2,1,0:T(8,128)S(1)} collective-permute-done((f32[3,32,768]{2,1,0:T(8,128)}, f32[3,32,768]{2,1,0:T(8,128)S(1)}, u32[]{:S(2)}, u32[]{:S(2)}) %collective-permute-start.18) | collective-permute-done | bytes 294944 | tf_op jit(solution)/shard_map/ppermute | solution.py:19
  151.3 1.9 fusion.12
  157.0 3.2 %collective-permute-done.22 = f32[3,32,768]{2,1,0:T(8,128)S(1)} collective-permute-done((f32[3,32,768]{2,1,0:T(8,128)}, f32[3,32,768]{2,1,0:T(8,128)S(1)}, u32[]{:S(2)}, u32[]{:S(2)}) %collective-permute-start.22) | collective-permute-done | bytes 294944 | tf_op jit(solution)/shard_map/ppermute | solution.py:19
  165.5 4.7 %collective-permute-done.26 = f32[3,32,768]{2,1,0:T(8,128)S(1)} collective-permute-done((f32[3,32,768]{2,1,0:T(8,128)S(1)}, f32[3,32,768]{2,1,0:T(8,128)S(1)}, u32[]{:S(2)}, u32[]{:S(2)}) %collective-permute-start.26) | collective-permute-done | bytes 294944 | tf_op jit(solution)/shard_map/ppermute | solution.py:19
  175.6 13.2 %collective-permute-done.28 = bf16[3,8,64,768]{3,2,1,0:T(8,128)(2,1)} collective-permute-done((bf16[3,8,64,768]{3,2,1,0:T(8,128)(2,1)}, bf16[3,8,64,768]{3,2,1,0:T(8,128)(2,1)}, u32[]{:S(2)}, u32[]{:S(2)}) %collective-permute-start.28) | collective-permute-done | bytes 2359328 | tf_op jit(solution)/shard_map/ppermute | solution.py:19
  188.7 2.5 %fusion.56 = f32[3,512,128]{1,2,0:T(8,128)S(1)} fusion(bf16[3,512,768]{2,1,0:T(8,128)(2,1)} %bitcast.41, bf16[3,128,768]{2,1,0:T(8,128)(2,1)S(1)} %bitcast.280), kind=kOutput, calls=%fused_computation.125 | convolution fusion | flops 301989888 | bytes 3735552 | tf_op jit(solution)/shard_map/knr,kmr->knm/dot_general | solution.py:81
  197.9 2.6 %collective-permute-done.31 = f32[3,2,32,128]{3,2,1,0:T(8,128)S(1)} collective-permute-done((f32[3,2,32,128]{3,2,1,0:T(8,128)S(1)}, f32[3,2,32,128]{3,2,1,0:T(8,128)S(1)}, u32[]{:S(2)}, u32[]{:S(2)}) %collective-permute-start.31) | collective-permute-done | bytes 98336 | tf_op jit(solution)/shard_map/ppermute | solution.py:19
  200.5 2.0 collective-permute-done.32
  202.6 2.8 %collective-permute-start.33 = (f32[3,32,128]{2,1,0:T(8,128)S(1)}, f32[3,32,128]{2,1,0:T(8,128)S(1)}, u32[]{:S(2)}, u32[]{:S(2)}) collective-permute-start(f32[3,32,128]{2,1,0:T(8,128)S(1)} %slice_bitcast_fusion.2), channel_id=1, source_target_pairs={{0,2},{1,3},{2,0},{3,1},{4,6},{5,7},{6,4},{7,5},{8,10},{9,11},{10,... | collective-permute-start | bytes 147464 | tf_op jit(solution)/shard_map/ppermute | solution.py:19
  206.3 2.0 collective-permute-done.33
  (121 shorter events, 60.7 us)
Async XLA Ops:
  7.2 116.5 %all-gather.3.cloned.1.call-start = ((), (), s32[]{:S(2)}) async-start(), calls=%async_computation | async-start | bytes 2654208 | tf_op jit(solution)/shard_map/all_gather | solution.py:133
  9.2 17.0 %collective-permute-start = (bf16[3,64,768]{2,1,0:T(8,128)(2,1)S(1)}, bf16[3,64,768]{2,1,0:T(8,128)(2,1)S(1)}, u32[]{:S(2)}, u32[]{:S(2)}) collective-permute-start(bf16[3,64,768]{2,1,0:T(8,128)(2,1)S(1)} %multiply_bitcast_fusion), channel_id=1, source_target_pairs={{0,0},{1,1},{2,2},{3,3},{4,4},{5,5},{6,6},{7,7},{8,132},{9,133},{1... | collective-permute-start | bytes 884744 | tf_op jit(solution)/shard_map/ppermute | solution.py:19
  12.6 17.4 %collective-permute-start.1 = (bf16[3,64,768]{2,1,0:T(8,128)(2,1)S(1)}, bf16[3,64,768]{2,1,0:T(8,128)(2,1)S(1)}, u32[]{:S(2)}, u32[]{:S(2)}) collective-permute-start(bf16[3,64,768]{2,1,0:T(8,128)(2,1)S(1)} %multiply_bitcast_fusion), channel_id=1, source_target_pairs={{0,2},{1,3},{2,0},{3,1},{4,6},{5,7},{6,4},{7,5},{8,134},{9,135},{1... | collective-permute-start | bytes 884744 | tf_op jit(solution)/shard_map/ppermute | solution.py:19
  17.0 15.3 %collective-permute-start.2 = (bf16[3,64,768]{2,1,0:T(8,128)(2,1)S(1)}, bf16[3,64,768]{2,1,0:T(8,128)(2,1)S(1)}, u32[]{:S(2)}, u32[]{:S(2)}) collective-permute-start(bf16[3,64,768]{2,1,0:T(8,128)(2,1)S(1)} %multiply_bitcast_fusion), channel_id=1, source_target_pairs={{0,0},{1,17},{2,34},{3,51},{4,68},{5,85},{6,102},{7,119},{8,8},{9,... | collective-permute-start | bytes 884744 | tf_op jit(solution)/shard_map/ppermute | solution.py:19
  33.2 18.9 %collective-permute-start.3 = (bf16[3,2,64,768]{3,2,1,0:T(8,128)(2,1)}, bf16[3,2,64,768]{3,2,1,0:T(8,128)(2,1)S(1)}, u32[]{:S(2)}, u32[]{:S(2)}) collective-permute-start(bf16[3,2,64,768]{3,2,1,0:T(8,128)(2,1)} %pad_maximum_fusion.4), channel_id=1, source_target_pairs={{0,4},{1,5},{2,6},{3,7},{4,8},{5,9},{6,10},{7,11},{8,12},{9,13},{1... | collective-permute-start | bytes 1769480 | tf_op jit(solution)/shard_map/ppermute | solution.py:19
  33.2 18.9 %collective-permute-start.4 = (bf16[3,2,64,768]{3,2,1,0:T(8,128)(2,1)}, bf16[3,2,64,768]{3,2,1,0:T(8,128)(2,1)S(1)}, u32[]{:S(2)}, u32[]{:S(2)}) collective-permute-start(bf16[3,2,64,768]{3,2,1,0:T(8,128)(2,1)} %pad_maximum_fusion.4), channel_id=1, source_target_pairs={{0,12},{1,13},{2,14},{3,15},{4,0},{5,1},{6,2},{7,3},{8,4},{9,5},{1... | collective-permute-start | bytes 1769480 | tf_op jit(solution)/shard_map/ppermute | solution.py:19
  36.1 16.0 %collective-permute-start.6 = (bf16[384,768]{1,0:T(8,128)(2,1)}, bf16[384,768]{1,0:T(8,128)(2,1)S(1)}, u32[]{:S(2)}, u32[]{:S(2)}) collective-permute-start(bf16[384,768]{1,0:T(8,128)(2,1)} %split.9), channel_id=1, source_target_pairs={{0,128},{1,129},{2,130},{3,131},{4,132},{5,133},{6,134},{7,135},{8... | collective-permute-start | bytes 1769480 | tf_op jit(solution)/shard_map/ppermute | solution.py:19
  36.1 16.0 %collective-permute-start.5 = (bf16[3,64,768]{2,1,0:T(8,128)(2,1)S(1)}, bf16[3,64,768]{2,1,0:T(8,128)(2,1)}, u32[]{:S(2)}, u32[]{:S(2)}) collective-permute-start(bf16[3,64,768]{2,1,0:T(8,128)(2,1)S(1)} %collective-permute-done.2), channel_id=1, source_target_pairs={{0,0},{1,1},{2,2},{3,3},{4,4},{5,5},{6,6},{7,7},{8,128},{9,129},{1... | collective-permute-start | bytes 884744 | tf_op jit(solution)/shard_map/ppermute | solution.py:19
  39.1 24.2 %collective-permute-start.9 = (bf16[256,768]{1,0:T(8,128)(2,1)}, bf16[256,768]{1,0:T(8,128)(2,1)S(1)}, u32[]{:S(2)}, u32[]{:S(2)}) collective-permute-start(bf16[256,768]{1,0:T(8,128)(2,1)} %split.10), channel_id=1, source_target_pairs={{0,128},{1,129},{2,130},{3,131},{4,132},{5,133},{6,134},{7,135},{8... | collective-permute-start | bytes 1179656 | tf_op jit(solution)/shard_map/ppermute | solution.py:19
  52.9 10.4 %collective-permute-start.7 = (bf16[3,1,64,768]{3,2,1,0:T(8,128)(2,1)}, bf16[3,1,64,768]{3,2,1,0:T(8,128)(2,1)S(1)}, u32[]{:S(2)}, u32[]{:S(2)}) collective-permute-start(bf16[3,1,64,768]{3,2,1,0:T(8,128)(2,1)} %slice.114), channel_id=1, source_target_pairs={{0,4},{1,5},{2,6},{3,7},{4,8},{5,9},{6,10},{7,11},{8,12},{9,13},{1... | collective-permute-start | bytes 884744 | tf_op jit(solution)/shard_map/ppermute | solution.py:19
  53.7 10.4 %collective-permute-start.8 = (bf16[3,1,64,768]{3,2,1,0:T(8,128)(2,1)}, bf16[3,1,64,768]{3,2,1,0:T(8,128)(2,1)S(1)}, u32[]{:S(2)}, u32[]{:S(2)}) collective-permute-start(bf16[3,1,64,768]{3,2,1,0:T(8,128)(2,1)} %slice.115), channel_id=1, source_target_pairs={{0,12},{1,13},{2,14},{3,15},{4,0},{5,1},{6,2},{7,3},{8,4},{9,5},{1... | collective-permute-start | bytes 884744 | tf_op jit(solution)/shard_map/ppermute | solution.py:19
  67.3 15.7 %collective-permute-start.10 = (bf16[2,3,2,2,64,768]{5,4,3,2,1,0:T(8,128)(2,1)}, bf16[2,3,2,2,64,768]{5,4,3,2,1,0:T(8,128)(2,1)S(1)}, u32[]{:S(2)}, u32[]{:S(2)}) collective-permute-start(bf16[2,3,2,2,64,768]{5,4,3,2,1,0:T(8,128)(2,1)} %pad_maximum_fusion), channel_id=1, source_target_pairs={{0,1},{1,0},{2,3},{3,2},{4,5},{5,4},{6,7},{7,6},{8,9},{9,8},{10,11... | collective-permute-start | bytes 7077896 | tf_op jit(solution)/shard_map/ppermute | solution.py:19
  76.1 6.9 %collective-permute-start.11 = (bf16[128,768]{1,0:T(8,128)(2,1)S(1)}, bf16[128,768]{1,0:T(8,128)(2,1)S(1)}, u32[]{:S(2)}, u32[]{:S(2)}) collective-permute-start(bf16[128,768]{1,0:T(8,128)(2,1)S(1)} %split.11), channel_id=1, source_target_pairs={{0,128},{1,129},{2,130},{3,131},{4,132},{5,133},{6,134},{7,135},{8... | collective-permute-start | bytes 589832 | tf_op jit(solution)/shard_map/ppermute | solution.py:19
  89.2 13.2 %collective-permute-start.12 = (f32[3,16,768]{2,1,0:T(8,128)S(1)}, f32[3,16,768]{2,1,0:T(8,128)}, u32[]{:S(2)}, u32[]{:S(2)}) collective-permute-start(f32[3,16,768]{2,1,0:T(8,128)S(1)} %get-tuple-element.103), channel_id=1, source_target_pairs={{0,112},{1,113},{2,114},{3,115},{4,116},{5,117},{6,118},{7,119},{8... | collective-permute-start | bytes 442376 | tf_op jit(solution)/shard_map/ppermute | solution.py:19
  93.1 13.4 %collective-permute-start.13 = (f32[3,16,768]{2,1,0:T(8,128)S(1)}, f32[3,16,768]{2,1,0:T(8,128)}, u32[]{:S(2)}, u32[]{:S(2)}) collective-permute-start(f32[3,16,768]{2,1,0:T(8,128)S(1)} %get-tuple-element.102), channel_id=1, source_target_pairs={{0,16},{1,17},{2,18},{3,19},{4,20},{5,21},{6,22},{7,23},{8,24},{9,... | collective-permute-start | bytes 442376 | tf_op jit(solution)/shard_map/ppermute | solution.py:19
  95.4 33.6 %collective-permute-start.16 = (f32[3,16,768]{2,1,0:T(8,128)}, f32[3,16,768]{2,1,0:T(8,128)}, u32[]{:S(2)}, u32[]{:S(2)}) collective-permute-start(f32[3,16,768]{2,1,0:T(8,128)} %get-tuple-element.105), channel_id=1, source_target_pairs={{0,112},{1,113},{2,114},{3,115},{4,116},{5,117},{6,118},{7,119},{8... | collective-permute-start | bytes 442376 | tf_op jit(solution)/shard_map/ppermute | solution.py:19
  99.3 29.7 %collective-permute-start.17 = (f32[3,16,768]{2,1,0:T(8,128)}, f32[3,16,768]{2,1,0:T(8,128)}, u32[]{:S(2)}, u32[]{:S(2)}) collective-permute-start(f32[3,16,768]{2,1,0:T(8,128)} %get-tuple-element.104), channel_id=1, source_target_pairs={{0,16},{1,17},{2,18},{3,19},{4,20},{5,21},{6,22},{7,23},{8,24},{9,... | collective-permute-start | bytes 442376 | tf_op jit(solution)/shard_map/ppermute | solution.py:19
  124.7 9.7 %collective-permute-start.15 = (f32[3,32,768]{2,1,0:T(8,128)S(1)}, f32[3,32,768]{2,1,0:T(8,128)S(1)}, u32[]{:S(2)}, u32[]{:S(2)}) collective-permute-start(f32[3,32,768]{2,1,0:T(8,128)S(1)} %pad_maximum_fusion.8), channel_id=1, source_target_pairs={{0,16},{1,17},{2,18},{3,19},{4,20},{5,21},{6,22},{7,23},{8,24},{9,... | collective-permute-start | bytes 884744 | tf_op jit(solution)/shard_map/ppermute | solution.py:19
  127.3 9.7 %collective-permute-start.14 = (f32[3,32,768]{2,1,0:T(8,128)S(1)}, f32[3,32,768]{2,1,0:T(8,128)S(1)}, u32[]{:S(2)}, u32[]{:S(2)}) collective-permute-start(f32[3,32,768]{2,1,0:T(8,128)S(1)} %pad_maximum_fusion.7), channel_id=1, source_target_pairs={{0,112},{1,113},{2,114},{3,115},{4,116},{5,117},{6,118},{7,119},{8... | collective-permute-start | bytes 884744 | tf_op jit(solution)/shard_map/ppermute | solution.py:19
  130.0 12.7 %collective-permute-start.21 = (f32[3,32,768]{2,1,0:T(8,128)S(1)}, f32[3,32,768]{2,1,0:T(8,128)S(1)}, u32[]{:S(2)}, u32[]{:S(2)}) collective-permute-start(f32[3,32,768]{2,1,0:T(8,128)S(1)} %pad_maximum_fusion.10), channel_id=1, source_target_pairs={{0,16},{1,17},{2,18},{3,19},{4,20},{5,21},{6,22},{7,23},{8,24},{9,... | collective-permute-start | bytes 884744 | tf_op jit(solution)/shard_map/ppermute | solution.py:19
  131.4 12.0 %collective-permute-start.20 = (f32[3,32,768]{2,1,0:T(8,128)S(1)}, f32[3,32,768]{2,1,0:T(8,128)}, u32[]{:S(2)}, u32[]{:S(2)}) collective-permute-start(f32[3,32,768]{2,1,0:T(8,128)S(1)} %pad_maximum_fusion.9), channel_id=1, source_target_pairs={{0,112},{1,113},{2,114},{3,115},{4,116},{5,117},{6,118},{7,119},{8... | collective-permute-start | bytes 884744 | tf_op jit(solution)/shard_map/ppermute | solution.py:19
  139.0 10.6 %collective-permute-start.18 = (f32[3,32,768]{2,1,0:T(8,128)}, f32[3,32,768]{2,1,0:T(8,128)S(1)}, u32[]{:S(2)}, u32[]{:S(2)}) collective-permute-start(f32[3,32,768]{2,1,0:T(8,128)} %get-tuple-element.64), channel_id=1, source_target_pairs={{0,112},{1,113},{2,114},{3,115},{4,116},{5,117},{6,118},{7,119},{8... | collective-permute-start | bytes 884744 | tf_op jit(solution)/shard_map/ppermute | solution.py:19
  140.5 10.9 %collective-permute-start.19 = (f32[3,32,768]{2,1,0:T(8,128)}, f32[3,32,768]{2,1,0:T(8,128)}, u32[]{:S(2)}, u32[]{:S(2)}) collective-permute-start(f32[3,32,768]{2,1,0:T(8,128)} %get-tuple-element.63), channel_id=1, source_target_pairs={{0,16},{1,17},{2,18},{3,19},{4,20},{5,21},{6,22},{7,23},{8,24},{9,... | collective-permute-start | bytes 884744 | tf_op jit(solution)/shard_map/ppermute | solution.py:19
  141.0 47.7 %collective-permute-start.28 = (bf16[3,8,64,768]{3,2,1,0:T(8,128)(2,1)}, bf16[3,8,64,768]{3,2,1,0:T(8,128)(2,1)}, u32[]{:S(2)}, u32[]{:S(2)}) collective-permute-start(bf16[3,8,64,768]{3,2,1,0:T(8,128)(2,1)} %bitcast.287), channel_id=1, source_target_pairs={{0,128},{1,129},{2,130},{3,131},{4,132},{5,133},{6,134},{7,135},{8... | collective-permute-start | bytes 7077896 | tf_op jit(solution)/shard_map/ppermute | solution.py:19
  144.6 11.4 %collective-permute-start.24 = (f32[3,32,768]{2,1,0:T(8,128)S(1)}, f32[3,32,768]{2,1,0:T(8,128)}, u32[]{:S(2)}, u32[]{:S(2)}) collective-permute-start(f32[3,32,768]{2,1,0:T(8,128)S(1)} %get-tuple-element.62), channel_id=1, source_target_pairs={{0,112},{1,113},{2,114},{3,115},{4,116},{5,117},{6,118},{7,119},{8... | collective-permute-start | bytes 884744 | tf_op jit(solution)/shard_map/ppermute | solution.py:19
  146.9 10.1 %collective-permute-start.25 = (f32[3,32,768]{2,1,0:T(8,128)S(1)}, f32[3,32,768]{2,1,0:T(8,128)}, u32[]{:S(2)}, u32[]{:S(2)}) collective-permute-start(f32[3,32,768]{2,1,0:T(8,128)S(1)} %get-tuple-element.61), channel_id=1, source_target_pairs={{0,16},{1,17},{2,18},{3,19},{4,20},{5,21},{6,22},{7,23},{8,24},{9,... | collective-permute-start | bytes 884744 | tf_op jit(solution)/shard_map/ppermute | solution.py:19
  153.3 6.9 %collective-permute-start.22 = (f32[3,32,768]{2,1,0:T(8,128)}, f32[3,32,768]{2,1,0:T(8,128)S(1)}, u32[]{:S(2)}, u32[]{:S(2)}) collective-permute-start(f32[3,32,768]{2,1,0:T(8,128)} %get-tuple-element.60), channel_id=1, source_target_pairs={{0,112},{1,113},{2,114},{3,115},{4,116},{5,117},{6,118},{7,119},{8... | collective-permute-start | bytes 884744 | tf_op jit(solution)/shard_map/ppermute | solution.py:19
  153.8 8.0 %collective-permute-start.23 = (f32[3,32,768]{2,1,0:T(8,128)S(1)}, f32[3,32,768]{2,1,0:T(8,128)}, u32[]{:S(2)}, u32[]{:S(2)}) collective-permute-start(f32[3,32,768]{2,1,0:T(8,128)S(1)} %get-tuple-element.59), channel_id=1, source_target_pairs={{0,16},{1,17},{2,18},{3,19},{4,20},{5,21},{6,22},{7,23},{8,24},{9,... | collective-permute-start | bytes 884744 | tf_op jit(solution)/shard_map/ppermute | solution.py:19
  163.4 6.8 %collective-permute-start.26 = (f32[3,32,768]{2,1,0:T(8,128)S(1)}, f32[3,32,768]{2,1,0:T(8,128)S(1)}, u32[]{:S(2)}, u32[]{:S(2)}) collective-permute-start(f32[3,32,768]{2,1,0:T(8,128)S(1)} %get-tuple-element.57), channel_id=1, source_target_pairs={{0,112},{1,113},{2,114},{3,115},{4,116},{5,117},{6,118},{7,119},{8... | collective-permute-start | bytes 884744 | tf_op jit(solution)/shard_map/ppermute | solution.py:19
  163.9 7.9 %collective-permute-start.27 = (f32[3,32,768]{2,1,0:T(8,128)S(1)}, f32[3,32,768]{2,1,0:T(8,128)S(1)}, u32[]{:S(2)}, u32[]{:S(2)}) collective-permute-start(f32[3,32,768]{2,1,0:T(8,128)S(1)} %get-tuple-element.58), channel_id=1, source_target_pairs={{0,16},{1,17},{2,18},{3,19},{4,20},{5,21},{6,22},{7,23},{8,24},{9,... | collective-permute-start | bytes 884744 | tf_op jit(solution)/shard_map/ppermute | solution.py:19
  193.9 6.5 %collective-permute-start.31 = (f32[3,2,32,128]{3,2,1,0:T(8,128)S(1)}, f32[3,2,32,128]{3,2,1,0:T(8,128)S(1)}, u32[]{:S(2)}, u32[]{:S(2)}) collective-permute-start(f32[3,2,32,128]{3,2,1,0:T(8,128)S(1)} %get-tuple-element.86), channel_id=1, source_target_pairs={{0,8},{1,9},{2,10},{3,11},{4,12},{5,13},{6,14},{7,15},{8,0},{9,1},... | collective-permute-start | bytes 294920 | tf_op jit(solution)/shard_map/ppermute | solution.py:19
  195.4 7.0 %collective-permute-start.32 = (f32[3,2,32,128]{3,2,1,0:T(8,128)S(1)}, f32[3,2,32,128]{3,2,1,0:T(8,128)S(1)}, u32[]{:S(2)}, u32[]{:S(2)}) collective-permute-start(f32[3,2,32,128]{3,2,1,0:T(8,128)S(1)} %get-tuple-element.85), channel_id=1, source_target_pairs={{0,12},{1,13},{2,14},{3,15},{4,8},{5,9},{6,10},{7,11},{8,4},{9,5},... | collective-permute-start | bytes 294920 | tf_op jit(solution)/shard_map/ppermute | solution.py:19
  (12 other events, 74.1 us)
Sparse Core Ops, SparseCore 0:
  74.8 48.8 all-gather.2

commit v10 on v9

--- a/solution.py
+++ b/solution.py
@@ -52,6 +52,10 @@
     return x // 2, z, yl * 2 + place // 4, place // 2 % 2, place % 2
 
 
+def turned_place(*place):
+    return facing_place(*skewed(*place))
+
+
 def over_y(yl, z, x, yh, c):
     return yl, z, x, 1 - yh, c
 
@@ -97,7 +101,7 @@
     return down, up
 
 
-def sum_over_z(first, second, half, extra):
+def sum_over_z(first, second, half):
     def both_ways(pair):
         return send(pair[0], along_z(-1)), send(pair[1], along_z(1))
 
@@ -106,13 +110,10 @@
 
     one, two = ((block(4)[:, :half], block(4)[:, half:]) for block in (first, second))
     for offset in (3, 2, 1):
-        got = both_ways(one)
-        if offset == 3:
-            *got, extra = together(*got, extra)
-        one = with_own(first, half, offset, *behind(got, *two))
+        one = with_own(first, half, offset, *behind(both_ways(one), *two))
         two = with_own(second, half, offset, *behind(both_ways(two), *one))
     one, two = both_ways(one), both_ways(two)
-    return first(0) + one[0] + one[1], second(0) + two[0] + two[1], extra
+    return first(0) + one[0] + one[1], second(0) + two[0] + two[1]
 
 
 def shards(ancestor_inverse, factor_panel, pattern, diagonal_inverse):
@@ -124,12 +125,11 @@
     keep_cols = row_mask(pattern, col, per).astype(jnp.float32)
     own = factor_panel.transpose(0, 2, 1) * keep_rows[:, None, :]
     near, far = send(own, swap), send(own, swap_far)
-    near, far, turned, ancestor = together(near, far, send(own, skewed), ancestor_inverse)
+    near, far, turned, ancestor = together(near, far, send(own, turned_place), ancestor_inverse)
     beside = [send(piece, across) for piece in jnp.split(ancestor, (rows // 2, rows * 5 // 6))]
     plane = jnp.stack([near, far], axis=1)
     left, right = send(plane, along_x(1)), send(plane, along_x(3))
-    turned = send(turned, facing_place)
-    left, right, _, beside[0] = together(left, right, turned, beside[0])
+    left, right, beside[0] = together(left, right, beside[0])
     facing = [lax.all_gather(turned, "z", axis=1), None]
     opposite = send(left[:, :1], along_x(1)), send(right[:, 1:], along_x(3))
     *opposite, beside[1] = together(*opposite, beside[1])
@@ -141,7 +141,7 @@
         whole = dot_nt(panel[0], ancestor_inverse) + dot_nt(panel[1], beside)
         return whole.reshape(count, 4, cols, rows)
 
-    theirs, beside[2] = together(send(mine, sibling), beside[2])
+    theirs, beside[2], facing[0] = together(send(mine, sibling), beside[2], facing[0])
     beside = jnp.concatenate(beside)
     near, far = product(mine), product(theirs)
     column = jnp.where(own_rows, x % 2, 1 - x % 2)
@@ -155,7 +155,7 @@
         return jnp.where(place % 2 == core, *picked).reshape(count, wide, rows)
 
     chunks = [lambda offset, first=first: block(first, offset) for first in (0, wide)]
-    *reduced, facing[0] = sum_over_z(*chunks, wide // 2, facing[0])
+    reduced = sum_over_z(*chunks, wide // 2)
     facing[1] = send(facing[0], across)
     reduced = jnp.concatenate(reduced, axis=1)
     offdiag = -(reduced * keep_cols[:, None, :])

time: 217 us -> 193 us (0.89)
  starting transfers between devices: 65.9 us -> 55.3 us
  waiting for transfers between devices: 94.2 us -> 84.7 us
  other arithmetic: 20.3 us -> 16 us
    all_gather x1, waiting for transfers between devices: 17.2 us -> 1.77 us  [shards(): facing = [lax.all_gather(turned, 'z', axis=1), None]]
    ppermute x34 -> x33, starting transfers between devices: 65.8 us -> 55.3 us  [send(): return lax.ppermute(value, AXES, pairs(move))]
    ppermute x34 -> x33, waiting for transfers between devices: 76.9 us -> 82.9 us  [send(): return lax.ppermute(value, AXES, pairs(move))]
  transfers between devices with their start and end apart: 35 -> 34, of which waited for: 23 -> 26; matrix products, arithmetic and copies ran while one was open for 12% -> 12% of each run, Pallas kernels for 0% -> 0%
where the time goes in v10:
time: 193 us
  waiting for transfers between devices  84.7 us (44%)
  starting transfers between devices  55.3 us (29%)
  other arithmetic  16 us (8%)
  between operations  14.5 us (8%)
  local copies, waits for them, and re-layouts  11.7 us (6%)
  matrix products  10.7 us (6%)
    ppermute x33, waiting for transfers between devices, send(): return lax.ppermute(value, AXES, pairs(move))  82.9 us
    ppermute x33, starting transfers between devices, send(): return lax.ppermute(value, AXES, pairs(move))  55.3 us
    dot_general x4, matrix products, dot_nt(): return lax.dot_general(a, b, NT, preferred_element_type=jnp.float32)  7.22 us
    unnamed x25, local copies, waits for them, and re-layouts  5.95 us
    add x3, other arithmetic, with_own(): return (below + down, above + up)  4.16 us
  transfers between devices with their start and end apart: 34, of which 26 were waited for; matrix products, arithmetic and copies ran while one was open for 12% of the time, Pallas kernels for 0%

profile of v10, /device:TPU:6, one launch (start us, length us, event | category | flops | bytes accessed | tf_op | source)
XLA Modules:
  0.0 192.7 jit_solution(12422539953057695917)
XLA Ops:
  9.2 3.4 %collective-permute-start = (bf16[3,64,768]{2,1,0:T(8,128)(2,1)S(1)}, bf16[3,64,768]{2,1,0:T(8,128)(2,1)S(1)}, u32[]{:S(2)}, u32[]{:S(2)}) collective-permute-start(bf16[3,64,768]{2,1,0:T(8,128)(2,1)S(1)} %multiply_bitcast_fusion), channel_id=1, source_target_pairs={{0,0},{1,1},{2,2},{3,3},{4,4},{5,5},{6,6},{7,7},{8,132},{9,133},{1... | collective-permute-start | bytes 884744 | tf_op jit(solution)/shard_map/ppermute | solution.py:19
  12.6 4.5 %collective-permute-start.1 = (bf16[3,64,768]{2,1,0:T(8,128)(2,1)S(1)}, bf16[3,64,768]{2,1,0:T(8,128)(2,1)S(1)}, u32[]{:S(2)}, u32[]{:S(2)}) collective-permute-start(bf16[3,64,768]{2,1,0:T(8,128)(2,1)S(1)} %multiply_bitcast_fusion), channel_id=1, source_target_pairs={{0,2},{1,3},{2,0},{3,1},{4,6},{5,7},{6,4},{7,5},{8,134},{9,135},{1... | collective-permute-start | bytes 884744 | tf_op jit(solution)/shard_map/ppermute | solution.py:19
  17.0 9.1 %collective-permute-start.2 = (bf16[3,64,768]{2,1,0:T(8,128)(2,1)S(1)}, bf16[3,64,768]{2,1,0:T(8,128)(2,1)}, u32[]{:S(2)}, u32[]{:S(2)}) collective-permute-start(bf16[3,64,768]{2,1,0:T(8,128)(2,1)S(1)} %multiply_bitcast_fusion), channel_id=1, source_target_pairs={{0,0},{1,16},{2,32},{3,48},{4,64},{5,80},{6,96},{7,112},{8,128},{9... | collective-permute-start | bytes 884744 | tf_op jit(solution)/shard_map/ppermute | solution.py:19
  26.2 10.2 %collective-permute-done.1 = bf16[3,64,768]{2,1,0:T(8,128)(2,1)S(1)} collective-permute-done((bf16[3,64,768]{2,1,0:T(8,128)(2,1)S(1)}, bf16[3,64,768]{2,1,0:T(8,128)(2,1)S(1)}, u32[]{:S(2)}, u32[]{:S(2)}) %collective-permute-start.1) | collective-permute-done | bytes 294944 | tf_op jit(solution)/shard_map/ppermute | solution.py:19
  36.3 2.1 %collective-permute-done.2 = bf16[3,64,768]{2,1,0:T(8,128)(2,1)} collective-permute-done((bf16[3,64,768]{2,1,0:T(8,128)(2,1)S(1)}, bf16[3,64,768]{2,1,0:T(8,128)(2,1)}, u32[]{:S(2)}, u32[]{:S(2)}) %collective-permute-start.2) | collective-permute-done | bytes 294944 | tf_op jit(solution)/shard_map/ppermute | solution.py:19
  39.3 2.0 %collective-permute-start.4 = (bf16[3,2,64,768]{3,2,1,0:T(8,128)(2,1)}, bf16[3,2,64,768]{3,2,1,0:T(8,128)(2,1)S(1)}, u32[]{:S(2)}, u32[]{:S(2)}) collective-permute-start(bf16[3,2,64,768]{3,2,1,0:T(8,128)(2,1)} %pad_maximum_fusion.4), channel_id=1, source_target_pairs={{0,12},{1,13},{2,14},{3,15},{4,0},{5,1},{6,2},{7,3},{8,4},{9,5},{1... | collective-permute-start | bytes 1769480 | tf_op jit(solution)/shard_map/ppermute | solution.py:19
  42.9 2.0 %collective-permute-start.8 = (bf16[256,768]{1,0:T(8,128)(2,1)}, bf16[256,768]{1,0:T(8,128)(2,1)}, u32[]{:S(2)}, u32[]{:S(2)}) collective-permute-start(bf16[256,768]{1,0:T(8,128)(2,1)} %split.10), channel_id=1, source_target_pairs={{0,128},{1,129},{2,130},{3,131},{4,132},{5,133},{6,134},{7,135},{8... | collective-permute-start | bytes 1179656 | tf_op jit(solution)/shard_map/ppermute | solution.py:19
  45.0 10.5 %collective-permute-done.3 = bf16[3,2,64,768]{3,2,1,0:T(8,128)(2,1)S(1)} collective-permute-done((bf16[3,2,64,768]{3,2,1,0:T(8,128)(2,1)}, bf16[3,2,64,768]{3,2,1,0:T(8,128)(2,1)S(1)}, u32[]{:S(2)}, u32[]{:S(2)}) %collective-permute-start.3) | collective-permute-done | bytes 589856 | tf_op jit(solution)/shard_map/ppermute | solution.py:19
  56.6 1.9 collective-permute-done.5
  62.0 4.2 %collective-permute-done.8 = bf16[256,768]{1,0:T(8,128)(2,1)} collective-permute-done((bf16[256,768]{1,0:T(8,128)(2,1)}, bf16[256,768]{1,0:T(8,128)(2,1)}, u32[]{:S(2)}, u32[]{:S(2)}) %collective-permute-start.8) | collective-permute-done | bytes 393248 | tf_op jit(solution)/shard_map/ppermute | solution.py:19
  67.1 3.6 %collective-permute-done.7 = bf16[3,1,64,768]{3,2,1,0:T(8,128)(2,1)} collective-permute-done((bf16[3,1,64,768]{3,2,1,0:T(8,128)(2,1)}, bf16[3,1,64,768]{3,2,1,0:T(8,128)(2,1)}, u32[]{:S(2)}, u32[]{:S(2)}) %collective-permute-start.7) | collective-permute-done | bytes 294944 | tf_op jit(solution)/shard_map/ppermute | solution.py:19
  77.8 3.9 %fusion.53 = f32[768,768]{1,0:T(8,128)} fusion(bf16[768,768]{1,0:T(8,128)(2,1)} %bitcast.288, bf16[768,768]{1,0:T(8,128)(2,1)S(1)} %copy-done.5), kind=kOutput, calls=%fused_computation.122 | convolution fusion | flops 905969664 | bytes 4718592 | tf_op jit(solution)/shard_map/dot_general | solution.py:73
  91.5 3.2 %collective-permute-start.11 = (f32[3,16,768]{2,1,0:T(8,128)S(1)}, f32[3,16,768]{2,1,0:T(8,128)S(1)}, u32[]{:S(2)}, u32[]{:S(2)}) collective-permute-start(f32[3,16,768]{2,1,0:T(8,128)S(1)} %get-tuple-element.99), channel_id=1, source_target_pairs={{0,112},{1,113},{2,114},{3,115},{4,116},{5,117},{6,118},{7,119},{8... | collective-permute-start | bytes 442376 | tf_op jit(solution)/shard_map/ppermute | solution.py:19
  94.7 3.3 %collective-permute-start.15 = (f32[3,16,768]{2,1,0:T(8,128)S(1)}, f32[3,16,768]{2,1,0:T(8,128)S(1)}, u32[]{:S(2)}, u32[]{:S(2)}) collective-permute-start(f32[3,16,768]{2,1,0:T(8,128)S(1)} %get-tuple-element.101), channel_id=1, source_target_pairs={{0,112},{1,113},{2,114},{3,115},{4,116},{5,117},{6,118},{7,119},{8... | collective-permute-start | bytes 442376 | tf_op jit(solution)/shard_map/ppermute | solution.py:19
  98.5 3.4 %collective-permute-done.12 = f32[3,16,768]{2,1,0:T(8,128)S(1)} collective-permute-done((f32[3,16,768]{2,1,0:T(8,128)S(1)}, f32[3,16,768]{2,1,0:T(8,128)S(1)}, u32[]{:S(2)}, u32[]{:S(2)}) %collective-permute-start.12) | collective-permute-done | bytes 147488 | tf_op jit(solution)/shard_map/ppermute | solution.py:19
  102.1 3.3 %collective-permute-start.13 = (f32[3,32,768]{2,1,0:T(8,128)S(1)}, f32[3,32,768]{2,1,0:T(8,128)S(1)}, u32[]{:S(2)}, u32[]{:S(2)}) collective-permute-start(f32[3,32,768]{2,1,0:T(8,128)S(1)} %pad_maximum_fusion.7), channel_id=1, source_target_pairs={{0,112},{1,113},{2,114},{3,115},{4,116},{5,117},{6,118},{7,119},{8... | collective-permute-start | bytes 884744 | tf_op jit(solution)/shard_map/ppermute | solution.py:19
  105.7 3.3 %collective-permute-start.19 = (f32[3,32,768]{2,1,0:T(8,128)S(1)}, f32[3,32,768]{2,1,0:T(8,128)}, u32[]{:S(2)}, u32[]{:S(2)}) collective-permute-start(f32[3,32,768]{2,1,0:T(8,128)S(1)} %pad_maximum_fusion.9), channel_id=1, source_target_pairs={{0,112},{1,113},{2,114},{3,115},{4,116},{5,117},{6,118},{7,119},{8... | collective-permute-start | bytes 884744 | tf_op jit(solution)/shard_map/ppermute | solution.py:19
  109.0 4.3 %collective-permute-done.14 = f32[3,32,768]{2,1,0:T(8,128)S(1)} collective-permute-done((f32[3,32,768]{2,1,0:T(8,128)S(1)}, f32[3,32,768]{2,1,0:T(8,128)S(1)}, u32[]{:S(2)}, u32[]{:S(2)}) %collective-permute-start.14) | collective-permute-done | bytes 294944 | tf_op jit(solution)/shard_map/ppermute | solution.py:19
  114.2 3.4 %collective-permute-start.17 = (f32[3,32,768]{2,1,0:T(8,128)}, f32[3,32,768]{2,1,0:T(8,128)S(1)}, u32[]{:S(2)}, u32[]{:S(2)}) collective-permute-start(f32[3,32,768]{2,1,0:T(8,128)} %get-tuple-element.60), channel_id=1, source_target_pairs={{0,112},{1,113},{2,114},{3,115},{4,116},{5,117},{6,118},{7,119},{8... | collective-permute-start | bytes 884744 | tf_op jit(solution)/shard_map/ppermute | solution.py:19
  120.4 3.9 %collective-permute-start.23 = (f32[3,32,768]{2,1,0:T(8,128)S(1)}, f32[3,32,768]{2,1,0:T(8,128)}, u32[]{:S(2)}, u32[]{:S(2)}) collective-permute-start(f32[3,32,768]{2,1,0:T(8,128)S(1)} %get-tuple-element.58), channel_id=1, source_target_pairs={{0,112},{1,113},{2,114},{3,115},{4,116},{5,117},{6,118},{7,119},{8... | collective-permute-start | bytes 884744 | tf_op jit(solution)/shard_map/ppermute | solution.py:19
  125.6 3.0 %collective-permute-done.18 = f32[3,32,768]{2,1,0:T(8,128)} collective-permute-done((f32[3,32,768]{2,1,0:T(8,128)}, f32[3,32,768]{2,1,0:T(8,128)}, u32[]{:S(2)}, u32[]{:S(2)}) %collective-permute-start.18) | collective-permute-done | bytes 294944 | tf_op jit(solution)/shard_map/ppermute | solution.py:19
  128.6 1.9 %fusion.12 = (f32[3,32,768]{2,1,0:T(8,128)S(1)}, f32[3,32,768]{2,1,0:T(8,128)}) fusion(f32[3,32,768]{2,1,0:T(8,128)} %collective-permute-done.18, f32[3,4,64,768]{3,2,1,0:T(8,128)} %bitcast.276, s32[]{:T(128)S(6)} %select_n.508, f32[3,4,64,768]{3,2,1,0:T(8,128)S(1)} %bitcast.270, pred[]{:T(512)S(6)} %eq.108, f32[3,32,768]{2,1,0:T(8,128)S(1)} %collective-permute-done.17, ...), kind=kLoop, calls=%fused_computation.43 | loop fusion | flops 294912 | bytes 2359306 | tf_op jit(solution)/shard_map/add | solution.py:98
  132.6 2.3 %collective-permute-done.24 = f32[3,32,768]{2,1,0:T(8,128)} collective-permute-done((f32[3,32,768]{2,1,0:T(8,128)S(1)}, f32[3,32,768]{2,1,0:T(8,128)}, u32[]{:S(2)}, u32[]{:S(2)}) %collective-permute-start.24) | collective-permute-done | bytes 294944 | tf_op jit(solution)/shard_map/ppermute | solution.py:19
  134.9 2.6 %collective-permute-done.21 = f32[3,32,768]{2,1,0:T(8,128)S(1)} collective-permute-done((f32[3,32,768]{2,1,0:T(8,128)}, f32[3,32,768]{2,1,0:T(8,128)S(1)}, u32[]{:S(2)}, u32[]{:S(2)}) %collective-permute-start.21) | collective-permute-done | bytes 294944 | tf_op jit(solution)/shard_map/ppermute | solution.py:19
  141.0 1.9 collective-permute-start.26
  142.9 4.7 %collective-permute-done.25 = f32[3,32,768]{2,1,0:T(8,128)S(1)} collective-permute-done((f32[3,32,768]{2,1,0:T(8,128)S(1)}, f32[3,32,768]{2,1,0:T(8,128)S(1)}, u32[]{:S(2)}, u32[]{:S(2)}) %collective-permute-start.25) | collective-permute-done | bytes 294944 | tf_op jit(solution)/shard_map/ppermute | solution.py:19
  152.8 12.9 %collective-permute-done.27 = bf16[3,8,64,768]{3,2,1,0:T(8,128)(2,1)} collective-permute-done((bf16[3,8,64,768]{3,2,1,0:T(8,128)(2,1)}, bf16[3,8,64,768]{3,2,1,0:T(8,128)(2,1)}, u32[]{:S(2)}, u32[]{:S(2)}) %collective-permute-start.27) | collective-permute-done | bytes 2359328 | tf_op jit(solution)/shard_map/ppermute | solution.py:19
  165.8 2.6 %fusion.56 = f32[3,512,128]{1,2,0:T(8,128)S(1)} fusion(bf16[3,512,768]{2,1,0:T(8,128)(2,1)} %bitcast.41, bf16[3,128,768]{2,1,0:T(8,128)(2,1)S(1)} %bitcast.280), kind=kOutput, calls=%fused_computation.125 | convolution fusion | flops 301989888 | bytes 3735552 | tf_op jit(solution)/shard_map/knr,kmr->knm/dot_general | solution.py:85
  172.7 2.2 %collective-permute-start.29 = (f32[3,2,32,128]{3,2,1,0:T(8,128)S(1)}, f32[3,2,32,128]{3,2,1,0:T(8,128)S(1)}, u32[]{:S(2)}, u32[]{:S(2)}) collective-permute-start(f32[3,2,32,128]{3,2,1,0:T(8,128)S(1)} %fusion.39), channel_id=1, source_target_pairs={{0,4},{1,5},{2,6},{3,7},{4,0},{5,1},{6,2},{7,3},{8,12},{9,13},{10,... | collective-permute-start | bytes 294920 | tf_op jit(solution)/shard_map/ppermute | solution.py:19
  174.9 3.3 %collective-permute-done.30 = f32[3,2,32,128]{3,2,1,0:T(8,128)S(1)} collective-permute-done((f32[3,2,32,128]{3,2,1,0:T(8,128)S(1)}, f32[3,2,32,128]{3,2,1,0:T(8,128)S(1)}, u32[]{:S(2)}, u32[]{:S(2)}) %collective-permute-start.30) | collective-permute-done | bytes 98336 | tf_op jit(solution)/shard_map/ppermute | solution.py:19
  179.5 2.5 %collective-permute-start.32 = (f32[3,32,128]{2,1,0:T(8,128)S(1)}, f32[3,32,128]{2,1,0:T(8,128)S(1)}, u32[]{:S(2)}, u32[]{:S(2)}) collective-permute-start(f32[3,32,128]{2,1,0:T(8,128)S(1)} %slice_bitcast_fusion.2), channel_id=1, source_target_pairs={{0,2},{1,3},{2,0},{3,1},{4,6},{5,7},{6,4},{7,5},{8,10},{9,11},{10,... | collective-permute-start | bytes 147464 | tf_op jit(solution)/shard_map/ppermute | solution.py:19
  182.8 2.4 %collective-permute-done.32 = f32[3,32,128]{2,1,0:T(8,128)S(1)} collective-permute-done((f32[3,32,128]{2,1,0:T(8,128)S(1)}, f32[3,32,128]{2,1,0:T(8,128)S(1)}, u32[]{:S(2)}, u32[]{:S(2)}) %collective-permute-start.32) | collective-permute-done | bytes 49184 | tf_op jit(solution)/shard_map/ppermute | solution.py:19
  (119 shorter events, 50.7 us)
Async XLA Ops:
  7.2 78.3 %all-gather.3.cloned.1.call-start = ((), (), s32[]{:S(2)}) async-start(), calls=%async_computation | async-start | bytes 2654208 | tf_op jit(solution)/shard_map/all_gather | solution.py:133
  9.2 17.0 %collective-permute-start = (bf16[3,64,768]{2,1,0:T(8,128)(2,1)S(1)}, bf16[3,64,768]{2,1,0:T(8,128)(2,1)S(1)}, u32[]{:S(2)}, u32[]{:S(2)}) collective-permute-start(bf16[3,64,768]{2,1,0:T(8,128)(2,1)S(1)} %multiply_bitcast_fusion), channel_id=1, source_target_pairs={{0,0},{1,1},{2,2},{3,3},{4,4},{5,5},{6,6},{7,7},{8,132},{9,133},{1... | collective-permute-start | bytes 884744 | tf_op jit(solution)/shard_map/ppermute | solution.py:19
  12.6 23.8 %collective-permute-start.1 = (bf16[3,64,768]{2,1,0:T(8,128)(2,1)S(1)}, bf16[3,64,768]{2,1,0:T(8,128)(2,1)S(1)}, u32[]{:S(2)}, u32[]{:S(2)}) collective-permute-start(bf16[3,64,768]{2,1,0:T(8,128)(2,1)S(1)} %multiply_bitcast_fusion), channel_id=1, source_target_pairs={{0,2},{1,3},{2,0},{3,1},{4,6},{5,7},{6,4},{7,5},{8,134},{9,135},{1... | collective-permute-start | bytes 884744 | tf_op jit(solution)/shard_map/ppermute | solution.py:19
  17.0 21.3 %collective-permute-start.2 = (bf16[3,64,768]{2,1,0:T(8,128)(2,1)S(1)}, bf16[3,64,768]{2,1,0:T(8,128)(2,1)}, u32[]{:S(2)}, u32[]{:S(2)}) collective-permute-start(bf16[3,64,768]{2,1,0:T(8,128)(2,1)S(1)} %multiply_bitcast_fusion), channel_id=1, source_target_pairs={{0,0},{1,16},{2,32},{3,48},{4,64},{5,80},{6,96},{7,112},{8,128},{9... | collective-permute-start | bytes 884744 | tf_op jit(solution)/shard_map/ppermute | solution.py:19
  39.3 16.2 %collective-permute-start.3 = (bf16[3,2,64,768]{3,2,1,0:T(8,128)(2,1)}, bf16[3,2,64,768]{3,2,1,0:T(8,128)(2,1)S(1)}, u32[]{:S(2)}, u32[]{:S(2)}) collective-permute-start(bf16[3,2,64,768]{3,2,1,0:T(8,128)(2,1)} %pad_maximum_fusion.4), channel_id=1, source_target_pairs={{0,4},{1,5},{2,6},{3,7},{4,8},{5,9},{6,10},{7,11},{8,12},{9,13},{1... | collective-permute-start | bytes 1769480 | tf_op jit(solution)/shard_map/ppermute | solution.py:19
  39.3 17.4 %collective-permute-start.4 = (bf16[3,2,64,768]{3,2,1,0:T(8,128)(2,1)}, bf16[3,2,64,768]{3,2,1,0:T(8,128)(2,1)S(1)}, u32[]{:S(2)}, u32[]{:S(2)}) collective-permute-start(bf16[3,2,64,768]{3,2,1,0:T(8,128)(2,1)} %pad_maximum_fusion.4), channel_id=1, source_target_pairs={{0,12},{1,13},{2,14},{3,15},{4,0},{5,1},{6,2},{7,3},{8,4},{9,5},{1... | collective-permute-start | bytes 1769480 | tf_op jit(solution)/shard_map/ppermute | solution.py:19
  42.1 16.4 %collective-permute-start.5 = (bf16[384,768]{1,0:T(8,128)(2,1)}, bf16[384,768]{1,0:T(8,128)(2,1)S(1)}, u32[]{:S(2)}, u32[]{:S(2)}) collective-permute-start(bf16[384,768]{1,0:T(8,128)(2,1)} %split.9), channel_id=1, source_target_pairs={{0,128},{1,129},{2,130},{3,131},{4,132},{5,133},{6,134},{7,135},{8... | collective-permute-start | bytes 1769480 | tf_op jit(solution)/shard_map/ppermute | solution.py:19
  42.9 23.3 %collective-permute-start.8 = (bf16[256,768]{1,0:T(8,128)(2,1)}, bf16[256,768]{1,0:T(8,128)(2,1)}, u32[]{:S(2)}, u32[]{:S(2)}) collective-permute-start(bf16[256,768]{1,0:T(8,128)(2,1)} %split.10), channel_id=1, source_target_pairs={{0,128},{1,129},{2,130},{3,131},{4,132},{5,133},{6,134},{7,135},{8... | collective-permute-start | bytes 1179656 | tf_op jit(solution)/shard_map/ppermute | solution.py:19
  59.3 7.8 %collective-permute-start.6 = (bf16[3,1,64,768]{3,2,1,0:T(8,128)(2,1)}, bf16[3,1,64,768]{3,2,1,0:T(8,128)(2,1)}, u32[]{:S(2)}, u32[]{:S(2)}) collective-permute-start(bf16[3,1,64,768]{3,2,1,0:T(8,128)(2,1)} %slice.114), channel_id=1, source_target_pairs={{0,4},{1,5},{2,6},{3,7},{4,8},{5,9},{6,10},{7,11},{8,12},{9,13},{1... | collective-permute-start | bytes 884744 | tf_op jit(solution)/shard_map/ppermute | solution.py:19
  61.2 9.5 %collective-permute-start.7 = (bf16[3,1,64,768]{3,2,1,0:T(8,128)(2,1)}, bf16[3,1,64,768]{3,2,1,0:T(8,128)(2,1)}, u32[]{:S(2)}, u32[]{:S(2)}) collective-permute-start(bf16[3,1,64,768]{3,2,1,0:T(8,128)(2,1)} %slice.115), channel_id=1, source_target_pairs={{0,12},{1,13},{2,14},{3,15},{4,0},{5,1},{6,2},{7,3},{8,4},{9,5},{1... | collective-permute-start | bytes 884744 | tf_op jit(solution)/shard_map/ppermute | solution.py:19
  76.2 7.5 %collective-permute-start.9 = (bf16[2,3,2,2,64,768]{5,4,3,2,1,0:T(8,128)(2,1)}, bf16[2,3,2,2,64,768]{5,4,3,2,1,0:T(8,128)(2,1)S(1)}, u32[]{:S(2)}, u32[]{:S(2)}) collective-permute-start(bf16[2,3,2,2,64,768]{5,4,3,2,1,0:T(8,128)(2,1)} %pad_maximum_fusion), channel_id=1, source_target_pairs={{0,1},{1,0},{2,3},{3,2},{4,5},{5,4},{6,7},{7,6},{8,9},{9,8},{10,11... | collective-permute-start | bytes 7077896 | tf_op jit(solution)/shard_map/ppermute | solution.py:19
  76.2 7.5 %collective-permute-start.10 = (bf16[128,768]{1,0:T(8,128)(2,1)S(1)}, bf16[128,768]{1,0:T(8,128)(2,1)}, u32[]{:S(2)}, u32[]{:S(2)}) collective-permute-start(bf16[128,768]{1,0:T(8,128)(2,1)S(1)} %split.11), channel_id=1, source_target_pairs={{0,128},{1,129},{2,130},{3,131},{4,132},{5,133},{6,134},{7,135},{8... | collective-permute-start | bytes 589832 | tf_op jit(solution)/shard_map/ppermute | solution.py:19
  91.5 7.0 %collective-permute-start.11 = (f32[3,16,768]{2,1,0:T(8,128)S(1)}, f32[3,16,768]{2,1,0:T(8,128)S(1)}, u32[]{:S(2)}, u32[]{:S(2)}) collective-permute-start(f32[3,16,768]{2,1,0:T(8,128)S(1)} %get-tuple-element.99), channel_id=1, source_target_pairs={{0,112},{1,113},{2,114},{3,115},{4,116},{5,117},{6,118},{7,119},{8... | collective-permute-start | bytes 442376 | tf_op jit(solution)/shard_map/ppermute | solution.py:19
  94.7 7.2 %collective-permute-start.12 = (f32[3,16,768]{2,1,0:T(8,128)S(1)}, f32[3,16,768]{2,1,0:T(8,128)S(1)}, u32[]{:S(2)}, u32[]{:S(2)}) collective-permute-start(f32[3,16,768]{2,1,0:T(8,128)S(1)} %get-tuple-element.98), channel_id=1, source_target_pairs={{0,16},{1,17},{2,18},{3,19},{4,20},{5,21},{6,22},{7,23},{8,24},{9,... | collective-permute-start | bytes 442376 | tf_op jit(solution)/shard_map/ppermute | solution.py:19
  94.7 10.7 %collective-permute-start.15 = (f32[3,16,768]{2,1,0:T(8,128)S(1)}, f32[3,16,768]{2,1,0:T(8,128)S(1)}, u32[]{:S(2)}, u32[]{:S(2)}) collective-permute-start(f32[3,16,768]{2,1,0:T(8,128)S(1)} %get-tuple-element.101), channel_id=1, source_target_pairs={{0,112},{1,113},{2,114},{3,115},{4,116},{5,117},{6,118},{7,119},{8... | collective-permute-start | bytes 442376 | tf_op jit(solution)/shard_map/ppermute | solution.py:19
  98.0 7.4 %collective-permute-start.16 = (f32[3,16,768]{2,1,0:T(8,128)S(1)}, f32[3,16,768]{2,1,0:T(8,128)S(1)}, u32[]{:S(2)}, u32[]{:S(2)}) collective-permute-start(f32[3,16,768]{2,1,0:T(8,128)S(1)} %get-tuple-element.100), channel_id=1, source_target_pairs={{0,16},{1,17},{2,18},{3,19},{4,20},{5,21},{6,22},{7,23},{8,24},{9,... | collective-permute-start | bytes 442376 | tf_op jit(solution)/shard_map/ppermute | solution.py:19
  102.0 11.2 %collective-permute-start.14 = (f32[3,32,768]{2,1,0:T(8,128)S(1)}, f32[3,32,768]{2,1,0:T(8,128)S(1)}, u32[]{:S(2)}, u32[]{:S(2)}) collective-permute-start(f32[3,32,768]{2,1,0:T(8,128)S(1)} %pad_maximum_fusion.8), channel_id=1, source_target_pairs={{0,16},{1,17},{2,18},{3,19},{4,20},{5,21},{6,22},{7,23},{8,24},{9,... | collective-permute-start | bytes 884744 | tf_op jit(solution)/shard_map/ppermute | solution.py:19
  102.1 11.1 %collective-permute-start.13 = (f32[3,32,768]{2,1,0:T(8,128)S(1)}, f32[3,32,768]{2,1,0:T(8,128)S(1)}, u32[]{:S(2)}, u32[]{:S(2)}) collective-permute-start(f32[3,32,768]{2,1,0:T(8,128)S(1)} %pad_maximum_fusion.7), channel_id=1, source_target_pairs={{0,112},{1,113},{2,114},{3,115},{4,116},{5,117},{6,118},{7,119},{8... | collective-permute-start | bytes 884744 | tf_op jit(solution)/shard_map/ppermute | solution.py:19
  105.5 12.9 %collective-permute-start.20 = (f32[3,32,768]{2,1,0:T(8,128)S(1)}, f32[3,32,768]{2,1,0:T(8,128)S(1)}, u32[]{:S(2)}, u32[]{:S(2)}) collective-permute-start(f32[3,32,768]{2,1,0:T(8,128)S(1)} %pad_maximum_fusion.10), channel_id=1, source_target_pairs={{0,16},{1,17},{2,18},{3,19},{4,20},{5,21},{6,22},{7,23},{8,24},{9,... | collective-permute-start | bytes 884744 | tf_op jit(solution)/shard_map/ppermute | solution.py:19
  105.7 13.6 %collective-permute-start.19 = (f32[3,32,768]{2,1,0:T(8,128)S(1)}, f32[3,32,768]{2,1,0:T(8,128)}, u32[]{:S(2)}, u32[]{:S(2)}) collective-permute-start(f32[3,32,768]{2,1,0:T(8,128)S(1)} %pad_maximum_fusion.9), channel_id=1, source_target_pairs={{0,112},{1,113},{2,114},{3,115},{4,116},{5,117},{6,118},{7,119},{8... | collective-permute-start | bytes 884744 | tf_op jit(solution)/shard_map/ppermute | solution.py:19
  114.2 11.4 %collective-permute-start.17 = (f32[3,32,768]{2,1,0:T(8,128)}, f32[3,32,768]{2,1,0:T(8,128)S(1)}, u32[]{:S(2)}, u32[]{:S(2)}) collective-permute-start(f32[3,32,768]{2,1,0:T(8,128)} %get-tuple-element.60), channel_id=1, source_target_pairs={{0,112},{1,113},{2,114},{3,115},{4,116},{5,117},{6,118},{7,119},{8... | collective-permute-start | bytes 884744 | tf_op jit(solution)/shard_map/ppermute | solution.py:19
  117.6 11.1 %collective-permute-start.18 = (f32[3,32,768]{2,1,0:T(8,128)}, f32[3,32,768]{2,1,0:T(8,128)}, u32[]{:S(2)}, u32[]{:S(2)}) collective-permute-start(f32[3,32,768]{2,1,0:T(8,128)} %get-tuple-element.59), channel_id=1, source_target_pairs={{0,16},{1,17},{2,18},{3,19},{4,20},{5,21},{6,22},{7,23},{8,24},{9,... | collective-permute-start | bytes 884744 | tf_op jit(solution)/shard_map/ppermute | solution.py:19
  117.6 48.2 %collective-permute-start.27 = (bf16[3,8,64,768]{3,2,1,0:T(8,128)(2,1)}, bf16[3,8,64,768]{3,2,1,0:T(8,128)(2,1)}, u32[]{:S(2)}, u32[]{:S(2)}) collective-permute-start(bf16[3,8,64,768]{3,2,1,0:T(8,128)(2,1)} %bitcast.287), channel_id=1, source_target_pairs={{0,128},{1,129},{2,130},{3,131},{4,132},{5,133},{6,134},{7,135},{8... | collective-permute-start | bytes 7077896 | tf_op jit(solution)/shard_map/ppermute | solution.py:19
  120.4 12.2 %collective-permute-start.23 = (f32[3,32,768]{2,1,0:T(8,128)S(1)}, f32[3,32,768]{2,1,0:T(8,128)}, u32[]{:S(2)}, u32[]{:S(2)}) collective-permute-start(f32[3,32,768]{2,1,0:T(8,128)S(1)} %get-tuple-element.58), channel_id=1, source_target_pairs={{0,112},{1,113},{2,114},{3,115},{4,116},{5,117},{6,118},{7,119},{8... | collective-permute-start | bytes 884744 | tf_op jit(solution)/shard_map/ppermute | solution.py:19
  124.3 10.6 %collective-permute-start.24 = (f32[3,32,768]{2,1,0:T(8,128)S(1)}, f32[3,32,768]{2,1,0:T(8,128)}, u32[]{:S(2)}, u32[]{:S(2)}) collective-permute-start(f32[3,32,768]{2,1,0:T(8,128)S(1)} %get-tuple-element.57), channel_id=1, source_target_pairs={{0,16},{1,17},{2,18},{3,19},{4,20},{5,21},{6,22},{7,23},{8,24},{9,... | collective-permute-start | bytes 884744 | tf_op jit(solution)/shard_map/ppermute | solution.py:19
  130.6 6.9 %collective-permute-start.21 = (f32[3,32,768]{2,1,0:T(8,128)}, f32[3,32,768]{2,1,0:T(8,128)S(1)}, u32[]{:S(2)}, u32[]{:S(2)}) collective-permute-start(f32[3,32,768]{2,1,0:T(8,128)} %get-tuple-element.56), channel_id=1, source_target_pairs={{0,112},{1,113},{2,114},{3,115},{4,116},{5,117},{6,118},{7,119},{8... | collective-permute-start | bytes 884744 | tf_op jit(solution)/shard_map/ppermute | solution.py:19
  131.2 8.0 %collective-permute-start.22 = (f32[3,32,768]{2,1,0:T(8,128)S(1)}, f32[3,32,768]{2,1,0:T(8,128)}, u32[]{:S(2)}, u32[]{:S(2)}) collective-permute-start(f32[3,32,768]{2,1,0:T(8,128)S(1)} %get-tuple-element.55), channel_id=1, source_target_pairs={{0,16},{1,17},{2,18},{3,19},{4,20},{5,21},{6,22},{7,23},{8,24},{9,... | collective-permute-start | bytes 884744 | tf_op jit(solution)/shard_map/ppermute | solution.py:19
  140.8 6.8 %collective-permute-start.25 = (f32[3,32,768]{2,1,0:T(8,128)S(1)}, f32[3,32,768]{2,1,0:T(8,128)S(1)}, u32[]{:S(2)}, u32[]{:S(2)}) collective-permute-start(f32[3,32,768]{2,1,0:T(8,128)S(1)} %get-tuple-element.53), channel_id=1, source_target_pairs={{0,112},{1,113},{2,114},{3,115},{4,116},{5,117},{6,118},{7,119},{8... | collective-permute-start | bytes 884744 | tf_op jit(solution)/shard_map/ppermute | solution.py:19
  141.0 8.1 %collective-permute-start.26 = (f32[3,32,768]{2,1,0:T(8,128)S(1)}, f32[3,32,768]{2,1,0:T(8,128)S(1)}, u32[]{:S(2)}, u32[]{:S(2)}) collective-permute-start(f32[3,32,768]{2,1,0:T(8,128)S(1)} %get-tuple-element.54), channel_id=1, source_target_pairs={{0,16},{1,17},{2,18},{3,19},{4,20},{5,21},{6,22},{7,23},{8,24},{9,... | collective-permute-start | bytes 884744 | tf_op jit(solution)/shard_map/ppermute | solution.py:19
  171.0 7.3 %collective-permute-start.30 = (f32[3,2,32,128]{3,2,1,0:T(8,128)S(1)}, f32[3,2,32,128]{3,2,1,0:T(8,128)S(1)}, u32[]{:S(2)}, u32[]{:S(2)}) collective-permute-start(f32[3,2,32,128]{3,2,1,0:T(8,128)S(1)} %get-tuple-element.82), channel_id=1, source_target_pairs={{0,8},{1,9},{2,10},{3,11},{4,12},{5,13},{6,14},{7,15},{8,0},{9,1},... | collective-permute-start | bytes 294920 | tf_op jit(solution)/shard_map/ppermute | solution.py:19
  171.1 8.2 %collective-permute-start.31 = (f32[3,2,32,128]{3,2,1,0:T(8,128)S(1)}, f32[3,2,32,128]{3,2,1,0:T(8,128)S(1)}, u32[]{:S(2)}, u32[]{:S(2)}) collective-permute-start(f32[3,2,32,128]{3,2,1,0:T(8,128)S(1)} %get-tuple-element.81), channel_id=1, source_target_pairs={{0,12},{1,13},{2,14},{3,15},{4,8},{5,9},{6,10},{7,11},{8,4},{9,5},... | collective-permute-start | bytes 294920 | tf_op jit(solution)/shard_map/ppermute | solution.py:19
  172.7 6.7 %collective-permute-start.29 = (f32[3,2,32,128]{3,2,1,0:T(8,128)S(1)}, f32[3,2,32,128]{3,2,1,0:T(8,128)S(1)}, u32[]{:S(2)}, u32[]{:S(2)}) collective-permute-start(f32[3,2,32,128]{3,2,1,0:T(8,128)S(1)} %fusion.39), channel_id=1, source_target_pairs={{0,4},{1,5},{2,6},{3,7},{4,0},{5,1},{6,2},{7,3},{8,12},{9,13},{10,... | collective-permute-start | bytes 294920 | tf_op jit(solution)/shard_map/ppermute | solution.py:19
  (11 other events, 96.8 us)
Sparse Core Ops, SparseCore 0:
  42.3 43.1 all-gather.2

commit v11 on v10

--- a/solution.py
+++ b/solution.py
@@ -101,7 +101,7 @@
     return down, up
 
 
-def sum_over_z(first, second, half):
+def sum_over_z(first, second, half, beside):
     def both_ways(pair):
         return send(pair[0], along_z(-1)), send(pair[1], along_z(1))
 
@@ -112,8 +112,9 @@
     for offset in (3, 2, 1):
         one = with_own(first, half, offset, *behind(both_ways(one), *two))
         two = with_own(second, half, offset, *behind(both_ways(two), *one))
+    *two, beside = together(*two, beside)
     one, two = both_ways(one), both_ways(two)
-    return first(0) + one[0] + one[1], second(0) + two[0] + two[1]
+    return first(0) + one[0] + one[1], second(0) + two[0] + two[1], beside
 
 
 def shards(ancestor_inverse, factor_panel, pattern, diagonal_inverse):
@@ -126,7 +127,7 @@
     own = factor_panel.transpose(0, 2, 1) * keep_rows[:, None, :]
     near, far = send(own, swap), send(own, swap_far)
     near, far, turned, ancestor = together(near, far, send(own, turned_place), ancestor_inverse)
-    beside = [send(piece, across) for piece in jnp.split(ancestor, (rows // 2, rows * 5 // 6))]
+    beside = [send(piece, across) for piece in jnp.split(ancestor, (rows * 2 // 3,))]
     plane = jnp.stack([near, far], axis=1)
     left, right = send(plane, along_x(1)), send(plane, along_x(3))
     left, right, beside[0] = together(left, right, beside[0])
@@ -141,7 +142,7 @@
         whole = dot_nt(panel[0], ancestor_inverse) + dot_nt(panel[1], beside)
         return whole.reshape(count, 4, cols, rows)
 
-    theirs, beside[2], facing[0] = together(send(mine, sibling), beside[2], facing[0])
+    theirs, facing[0] = together(send(mine, sibling), facing[0])
     beside = jnp.concatenate(beside)
     near, far = product(mine), product(theirs)
     column = jnp.where(own_rows, x % 2, 1 - x % 2)
@@ -155,8 +156,7 @@
         return jnp.where(place % 2 == core, *picked).reshape(count, wide, rows)
 
     chunks = [lambda offset, first=first: block(first, offset) for first in (0, wide)]
-    reduced = sum_over_z(*chunks, wide // 2)
-    facing[1] = send(facing[0], across)
+    *reduced, facing[1] = sum_over_z(*chunks, wide // 2, send(facing[0], across))
     reduced = jnp.concatenate(reduced, axis=1)
     offdiag = -(reduced * keep_cols[:, None, :])
     high = lax.reduce_precision(reduced, 8, 7)

time: 193 us -> 188 us (0.974)
  waiting for transfers between devices: 84.7 us -> 82 us
  local copies, waits for them, and re-layouts: 11.7 us -> 9.01 us
    ppermute x33 -> x32, waiting for transfers between devices: 82.9 us -> 75.1 us  [send(): return lax.ppermute(value, AXES, pairs(move))]
    all_gather x1, waiting for transfers between devices: 1.77 us -> 6.8 us  [shards(): facing = [lax.all_gather(turned, 'z', axis=1), None]]
    unnamed x25 -> x18, local copies, waits for them, and re-layouts: 5.95 us -> 1.73 us
    dot_general x4, matrix products: 7.22 us -> 4.47 us  [dot_nt(): return lax.dot_general(a, b, NT, preferred_element_type=jnp.float32)]
    ppermute x33 -> x32, starting transfers between devices: 55.3 us -> 56.5 us  [send(): return lax.ppermute(value, AXES, pairs(move))]
  transfers between devices with their start and end apart: 34 -> 33, of which waited for: 26 -> 27; matrix products, arithmetic and copies ran while one was open for 12% -> 10% of each run, Pallas kernels for 0% -> 0%
where the time goes in v11:
time: 188 us; the launch traced here: 187 us
  waiting for transfers between devices  82 us (44%)
  starting transfers between devices  56.6 us (30%)
  other arithmetic  15.6 us (8%)
  between operations  14.4 us (8%)
  matrix products  9.57 us (5%)
  local copies, waits for them, and re-layouts  9.01 us (5%)
    ppermute x32, waiting for transfers between devices, send(): return lax.ppermute(value, AXES, pairs(move))  75.1 us
    ppermute x32, starting transfers between devices, send(): return lax.ppermute(value, AXES, pairs(move))  56.5 us
    all_gather x1, waiting for transfers between devices, shards(): facing = [lax.all_gather(turned, 'z', axis=1), None]  6.8 us
    dot_general x2, matrix products, dot_each(): return jnp.einsum('knr,kmr->knm', a, b, preferred_element_type=jnp.float32)  5.09 us
    dot_general x4, matrix products, dot_nt(): return lax.dot_general(a, b, NT, preferred_element_type=jnp.float32)  4.47 us
    add x3, other arithmetic, with_own(): return (below + down, above + up)  4.13 us
  transfers between devices with their start and end apart: 33, of which 27 were waited for; matrix products, arithmetic and copies ran while one was open for 10% of the time, Pallas kernels for 0%

profile of v11, /device:TPU:6, one launch (start us, length us, event | category | flops | bytes accessed | tf_op | source)
XLA Modules:
  0.0 187.1 jit_solution(16814895584751576506)
XLA Ops:
  9.1 3.4 %collective-permute-start = (bf16[3,64,768]{2,1,0:T(8,128)(2,1)S(1)}, bf16[3,64,768]{2,1,0:T(8,128)(2,1)S(1)}, u32[]{:S(2)}, u32[]{:S(2)}) collective-permute-start(bf16[3,64,768]{2,1,0:T(8,128)(2,1)S(1)} %multiply_bitcast_fusion), channel_id=1, source_target_pairs={{0,0},{1,1},{2,2},{3,3},{4,4},{5,5},{6,6},{7,7},{8,132},{9,133},{1... | collective-permute-start | bytes 884744 | tf_op jit(solution)/shard_map/ppermute | solution.py:19
  12.5 4.5 %collective-permute-start.1 = (bf16[3,64,768]{2,1,0:T(8,128)(2,1)S(1)}, bf16[3,64,768]{2,1,0:T(8,128)(2,1)S(1)}, u32[]{:S(2)}, u32[]{:S(2)}) collective-permute-start(bf16[3,64,768]{2,1,0:T(8,128)(2,1)S(1)} %multiply_bitcast_fusion), channel_id=1, source_target_pairs={{0,2},{1,3},{2,0},{3,1},{4,6},{5,7},{6,4},{7,5},{8,134},{9,135},{1... | collective-permute-start | bytes 884744 | tf_op jit(solution)/shard_map/ppermute | solution.py:19
  17.0 9.1 %collective-permute-start.2 = (bf16[3,64,768]{2,1,0:T(8,128)(2,1)S(1)}, bf16[3,64,768]{2,1,0:T(8,128)(2,1)}, u32[]{:S(2)}, u32[]{:S(2)}) collective-permute-start(bf16[3,64,768]{2,1,0:T(8,128)(2,1)S(1)} %multiply_bitcast_fusion), channel_id=1, source_target_pairs={{0,0},{1,16},{2,32},{3,48},{4,64},{5,80},{6,96},{7,112},{8,128},{9... | collective-permute-start | bytes 884744 | tf_op jit(solution)/shard_map/ppermute | solution.py:19
  26.1 10.2 %collective-permute-done.1 = bf16[3,64,768]{2,1,0:T(8,128)(2,1)S(1)} collective-permute-done((bf16[3,64,768]{2,1,0:T(8,128)(2,1)S(1)}, bf16[3,64,768]{2,1,0:T(8,128)(2,1)S(1)}, u32[]{:S(2)}, u32[]{:S(2)}) %collective-permute-start.1) | collective-permute-done | bytes 294944 | tf_op jit(solution)/shard_map/ppermute | solution.py:19
  36.3 2.1 %collective-permute-done.2 = bf16[3,64,768]{2,1,0:T(8,128)(2,1)} collective-permute-done((bf16[3,64,768]{2,1,0:T(8,128)(2,1)S(1)}, bf16[3,64,768]{2,1,0:T(8,128)(2,1)}, u32[]{:S(2)}, u32[]{:S(2)}) %collective-permute-start.2) | collective-permute-done | bytes 294944 | tf_op jit(solution)/shard_map/ppermute | solution.py:19
  40.5 2.0 %collective-permute-start.4 = (bf16[3,2,64,768]{3,2,1,0:T(8,128)(2,1)}, bf16[3,2,64,768]{3,2,1,0:T(8,128)(2,1)S(1)}, u32[]{:S(2)}, u32[]{:S(2)}) collective-permute-start(bf16[3,2,64,768]{3,2,1,0:T(8,128)(2,1)} %pad_maximum_fusion.4), channel_id=1, source_target_pairs={{0,12},{1,13},{2,14},{3,15},{4,0},{5,1},{6,2},{7,3},{8,4},{9,5},{1... | collective-permute-start | bytes 1769480 | tf_op jit(solution)/shard_map/ppermute | solution.py:19
  46.4 10.3 %collective-permute-done.3 = bf16[3,2,64,768]{3,2,1,0:T(8,128)(2,1)S(1)} collective-permute-done((bf16[3,2,64,768]{3,2,1,0:T(8,128)(2,1)}, bf16[3,2,64,768]{3,2,1,0:T(8,128)(2,1)S(1)}, u32[]{:S(2)}, u32[]{:S(2)}) %collective-permute-start.3) | collective-permute-done | bytes 589856 | tf_op jit(solution)/shard_map/ppermute | solution.py:19
  57.9 2.2 %collective-permute-done.5 = bf16[512,768]{1,0:T(8,128)(2,1)S(1)} collective-permute-done((bf16[512,768]{1,0:T(8,128)(2,1)S(1)}, bf16[512,768]{1,0:T(8,128)(2,1)S(1)}, u32[]{:S(2)}, u32[]{:S(2)}) %collective-permute-start.5) | collective-permute-done | bytes 786464 | tf_op jit(solution)/shard_map/ppermute | solution.py:19
  62.9 5.4 %collective-permute-done.8 = bf16[256,768]{1,0:T(8,128)(2,1)} collective-permute-done((bf16[256,768]{1,0:T(8,128)(2,1)}, bf16[256,768]{1,0:T(8,128)(2,1)}, u32[]{:S(2)}, u32[]{:S(2)}) %collective-permute-start.8) | collective-permute-done | bytes 393248 | tf_op jit(solution)/shard_map/ppermute | solution.py:19
  68.8 2.3 %collective-permute-done.7 = bf16[3,1,64,768]{3,2,1,0:T(8,128)(2,1)S(1)} collective-permute-done((bf16[3,1,64,768]{3,2,1,0:T(8,128)(2,1)}, bf16[3,1,64,768]{3,2,1,0:T(8,128)(2,1)S(1)}, u32[]{:S(2)}, u32[]{:S(2)}) %collective-permute-start.7) | collective-permute-done | bytes 294944 | tf_op jit(solution)/shard_map/ppermute | solution.py:19
  79.2 6.8 %all-gather.3.cloned.1.call-done = bf16[3,512,768]{2,1,0:T(8,128)(2,1)} async-done(((bf16[3,64,768]{2,1,0:T(8,128)(2,1)}), bf16[3,512,768]{2,1,0:T(8,128)(2,1)}) %all-gather.3.cloned.1.call-update) | async-done | bytes 2359312 | tf_op jit(solution)/shard_map/all_gather | solution.py:134
  90.6 2.3 %collective-permute-start.10 = (f32[3,16,768]{2,1,0:T(8,128)S(1)}, f32[3,16,768]{2,1,0:T(8,128)S(1)}, u32[]{:S(2)}, u32[]{:S(2)}) collective-permute-start(f32[3,16,768]{2,1,0:T(8,128)S(1)} %get-tuple-element.103), channel_id=1, source_target_pairs={{0,112},{1,113},{2,114},{3,115},{4,116},{5,117},{6,118},{7,119},{8... | collective-permute-start | bytes 442376 | tf_op jit(solution)/shard_map/ppermute | solution.py:19
  92.9 3.3 %collective-permute-start.14 = (f32[3,16,768]{2,1,0:T(8,128)S(1)}, f32[3,16,768]{2,1,0:T(8,128)S(1)}, u32[]{:S(2)}, u32[]{:S(2)}) collective-permute-start(f32[3,16,768]{2,1,0:T(8,128)S(1)} %get-tuple-element.105), channel_id=1, source_target_pairs={{0,112},{1,113},{2,114},{3,115},{4,116},{5,117},{6,118},{7,119},{8... | collective-permute-start | bytes 442376 | tf_op jit(solution)/shard_map/ppermute | solution.py:19
  97.7 2.8 %collective-permute-done.11 = f32[3,16,768]{2,1,0:T(8,128)S(1)} collective-permute-done((f32[3,16,768]{2,1,0:T(8,128)S(1)}, f32[3,16,768]{2,1,0:T(8,128)S(1)}, u32[]{:S(2)}, u32[]{:S(2)}) %collective-permute-start.11) | collective-permute-done | bytes 147488 | tf_op jit(solution)/shard_map/ppermute | solution.py:19
  100.8 3.3 %collective-permute-start.12 = (f32[3,32,768]{2,1,0:T(8,128)S(1)}, f32[3,32,768]{2,1,0:T(8,128)S(1)}, u32[]{:S(2)}, u32[]{:S(2)}) collective-permute-start(f32[3,32,768]{2,1,0:T(8,128)S(1)} %pad_maximum_fusion.7), channel_id=1, source_target_pairs={{0,112},{1,113},{2,114},{3,115},{4,116},{5,117},{6,118},{7,119},{8... | collective-permute-start | bytes 884744 | tf_op jit(solution)/shard_map/ppermute | solution.py:19
  104.4 3.3 %collective-permute-start.18 = (f32[3,32,768]{2,1,0:T(8,128)S(1)}, f32[3,32,768]{2,1,0:T(8,128)}, u32[]{:S(2)}, u32[]{:S(2)}) collective-permute-start(f32[3,32,768]{2,1,0:T(8,128)S(1)} %pad_maximum_fusion.9), channel_id=1, source_target_pairs={{0,112},{1,113},{2,114},{3,115},{4,116},{5,117},{6,118},{7,119},{8... | collective-permute-start | bytes 884744 | tf_op jit(solution)/shard_map/ppermute | solution.py:19
  107.7 2.6 %collective-permute-done.13 = f32[3,32,768]{2,1,0:T(8,128)S(1)} collective-permute-done((f32[3,32,768]{2,1,0:T(8,128)S(1)}, f32[3,32,768]{2,1,0:T(8,128)S(1)}, u32[]{:S(2)}, u32[]{:S(2)}) %collective-permute-start.13) | collective-permute-done | bytes 294944 | tf_op jit(solution)/shard_map/ppermute | solution.py:19
  111.3 3.2 %collective-permute-start.16 = (f32[3,32,768]{2,1,0:T(8,128)}, f32[3,32,768]{2,1,0:T(8,128)S(1)}, u32[]{:S(2)}, u32[]{:S(2)}) collective-permute-start(f32[3,32,768]{2,1,0:T(8,128)} %get-tuple-element.64), channel_id=1, source_target_pairs={{0,112},{1,113},{2,114},{3,115},{4,116},{5,117},{6,118},{7,119},{8... | collective-permute-start | bytes 884744 | tf_op jit(solution)/shard_map/ppermute | solution.py:19
  114.5 2.1 %collective-permute-done.19 = f32[3,32,768]{2,1,0:T(8,128)S(1)} collective-permute-done((f32[3,32,768]{2,1,0:T(8,128)S(1)}, f32[3,32,768]{2,1,0:T(8,128)S(1)}, u32[]{:S(2)}, u32[]{:S(2)}) %collective-permute-start.19) | collective-permute-done | bytes 294944 | tf_op jit(solution)/shard_map/ppermute | solution.py:19
  117.9 3.4 %collective-permute-start.22 = (f32[3,32,768]{2,1,0:T(8,128)S(1)}, f32[3,32,768]{2,1,0:T(8,128)}, u32[]{:S(2)}, u32[]{:S(2)}) collective-permute-start(f32[3,32,768]{2,1,0:T(8,128)S(1)} %get-tuple-element.62), channel_id=1, source_target_pairs={{0,112},{1,113},{2,114},{3,115},{4,116},{5,117},{6,118},{7,119},{8... | collective-permute-start | bytes 884744 | tf_op jit(solution)/shard_map/ppermute | solution.py:19
  125.3 2.9 %collective-permute-start.20 = (f32[3,32,768]{2,1,0:T(8,128)}, f32[3,32,768]{2,1,0:T(8,128)S(1)}, u32[]{:S(2)}, u32[]{:S(2)}) collective-permute-start(f32[3,32,768]{2,1,0:T(8,128)} %get-tuple-element.60), channel_id=1, source_target_pairs={{0,112},{1,113},{2,114},{3,115},{4,116},{5,117},{6,118},{7,119},{8... | collective-permute-start | bytes 884744 | tf_op jit(solution)/shard_map/ppermute | solution.py:19
  129.4 3.3 %collective-permute-done.20 = f32[3,32,768]{2,1,0:T(8,128)S(1)} collective-permute-done((f32[3,32,768]{2,1,0:T(8,128)}, f32[3,32,768]{2,1,0:T(8,128)S(1)}, u32[]{:S(2)}, u32[]{:S(2)}) %collective-permute-start.20) | collective-permute-done | bytes 294944 | tf_op jit(solution)/shard_map/ppermute | solution.py:19
  132.7 3.5 %collective-permute-done.21 = f32[3,32,768]{2,1,0:T(8,128)} collective-permute-done((f32[3,32,768]{2,1,0:T(8,128)S(1)}, f32[3,32,768]{2,1,0:T(8,128)}, u32[]{:S(2)}, u32[]{:S(2)}) %collective-permute-start.21) | collective-permute-done | bytes 294944 | tf_op jit(solution)/shard_map/ppermute | solution.py:19
  137.7 7.3 %collective-permute-done.24 = bf16[3,8,64,768]{3,2,1,0:T(8,128)(2,1)} collective-permute-done((bf16[3,8,64,768]{3,2,1,0:T(8,128)(2,1)}, bf16[3,8,64,768]{3,2,1,0:T(8,128)(2,1)}, u32[]{:S(2)}, u32[]{:S(2)}) %collective-permute-start.24) | collective-permute-done | bytes 2359328 | tf_op jit(solution)/shard_map/ppermute | solution.py:19
  145.0 3.0 %collective-permute-start.25 = (f32[3,32,768]{2,1,0:T(8,128)S(1)}, f32[3,32,768]{2,1,0:T(8,128)S(1)}, u32[]{:S(2)}, u32[]{:S(2)}) collective-permute-start(f32[3,32,768]{2,1,0:T(8,128)S(1)} %get-tuple-element.53), channel_id=1, source_target_pairs={{0,112},{1,113},{2,114},{3,115},{4,116},{5,117},{6,118},{7,119},{8... | collective-permute-start | bytes 884744 | tf_op jit(solution)/shard_map/ppermute | solution.py:19
  148.0 4.2 %collective-permute-done.25 = f32[3,32,768]{2,1,0:T(8,128)S(1)} collective-permute-done((f32[3,32,768]{2,1,0:T(8,128)S(1)}, f32[3,32,768]{2,1,0:T(8,128)S(1)}, u32[]{:S(2)}, u32[]{:S(2)}) %collective-permute-start.25) | collective-permute-done | bytes 294944 | tf_op jit(solution)/shard_map/ppermute | solution.py:19
  152.2 3.7 %collective-permute-done.26 = f32[3,32,768]{2,1,0:T(8,128)S(1)} collective-permute-done((f32[3,32,768]{2,1,0:T(8,128)S(1)}, f32[3,32,768]{2,1,0:T(8,128)S(1)}, u32[]{:S(2)}, u32[]{:S(2)}) %collective-permute-start.26) | collective-permute-done | bytes 294944 | tf_op jit(solution)/shard_map/ppermute | solution.py:19
  157.2 2.5 %fusion.55 = f32[3,512,128]{1,2,0:T(8,128)S(1)} fusion(bf16[3,512,768]{2,1,0:T(8,128)(2,1)} %bitcast.37, bf16[3,128,768]{2,1,0:T(8,128)(2,1)S(1)} %bitcast.279), kind=kOutput, calls=%fused_computation.123 | convolution fusion | flops 301989888 | bytes 3735552 | tf_op jit(solution)/shard_map/knr,kmr->knm/dot_general | solution.py:85
  159.8 2.6 %fusion.56 = f32[3,512,128]{1,2,0:T(8,128)S(1)} fusion(bf16[3,512,768]{2,1,0:T(8,128)(2,1)} %bitcast.41, bf16[3,128,768]{2,1,0:T(8,128)(2,1)S(1)} %bitcast.280), kind=kOutput, calls=%fused_computation.124 | convolution fusion | flops 301989888 | bytes 3735552 | tf_op jit(solution)/shard_map/knr,kmr->knm/dot_general | solution.py:85
  166.8 2.1 %collective-permute-start.30 = (f32[3,2,32,128]{3,2,1,0:T(8,128)S(1)}, f32[3,2,32,128]{3,2,1,0:T(8,128)S(1)}, u32[]{:S(2)}, u32[]{:S(2)}) collective-permute-start(f32[3,2,32,128]{3,2,1,0:T(8,128)S(1)} %get-tuple-element.85), channel_id=1, source_target_pairs={{0,12},{1,13},{2,14},{3,15},{4,8},{5,9},{6,10},{7,11},{8,4},{9,5},... | collective-permute-start | bytes 294920 | tf_op jit(solution)/shard_map/ppermute | solution.py:19
  169.2 2.3 %collective-permute-done.29 = f32[3,2,32,128]{3,2,1,0:T(8,128)S(1)} collective-permute-done((f32[3,2,32,128]{3,2,1,0:T(8,128)S(1)}, f32[3,2,32,128]{3,2,1,0:T(8,128)S(1)}, u32[]{:S(2)}, u32[]{:S(2)}) %collective-permute-start.29) | collective-permute-done | bytes 98336 | tf_op jit(solution)/shard_map/ppermute | solution.py:19
  173.9 3.1 %collective-permute-start.31 = (f32[3,32,128]{2,1,0:T(8,128)S(1)}, f32[3,32,128]{2,1,0:T(8,128)S(1)}, u32[]{:S(2)}, u32[]{:S(2)}) collective-permute-start(f32[3,32,128]{2,1,0:T(8,128)S(1)} %slice_bitcast_fusion.2), channel_id=1, source_target_pairs={{0,2},{1,3},{2,0},{3,1},{4,6},{5,7},{6,4},{7,5},{8,10},{9,11},{10,... | collective-permute-start | bytes 147464 | tf_op jit(solution)/shard_map/ppermute | solution.py:19
  (109 shorter events, 47.7 us)
Async XLA Ops:
  7.2 78.8 %all-gather.3.cloned.1.call-start = ((), (), s32[]{:S(2)}) async-start(), calls=%async_computation | async-start | bytes 2654208 | tf_op jit(solution)/shard_map/all_gather | solution.py:134
  9.1 17.0 %collective-permute-start = (bf16[3,64,768]{2,1,0:T(8,128)(2,1)S(1)}, bf16[3,64,768]{2,1,0:T(8,128)(2,1)S(1)}, u32[]{:S(2)}, u32[]{:S(2)}) collective-permute-start(bf16[3,64,768]{2,1,0:T(8,128)(2,1)S(1)} %multiply_bitcast_fusion), channel_id=1, source_target_pairs={{0,0},{1,1},{2,2},{3,3},{4,4},{5,5},{6,6},{7,7},{8,132},{9,133},{1... | collective-permute-start | bytes 884744 | tf_op jit(solution)/shard_map/ppermute | solution.py:19
  12.5 23.8 %collective-permute-start.1 = (bf16[3,64,768]{2,1,0:T(8,128)(2,1)S(1)}, bf16[3,64,768]{2,1,0:T(8,128)(2,1)S(1)}, u32[]{:S(2)}, u32[]{:S(2)}) collective-permute-start(bf16[3,64,768]{2,1,0:T(8,128)(2,1)S(1)} %multiply_bitcast_fusion), channel_id=1, source_target_pairs={{0,2},{1,3},{2,0},{3,1},{4,6},{5,7},{6,4},{7,5},{8,134},{9,135},{1... | collective-permute-start | bytes 884744 | tf_op jit(solution)/shard_map/ppermute | solution.py:19
  17.0 21.3 %collective-permute-start.2 = (bf16[3,64,768]{2,1,0:T(8,128)(2,1)S(1)}, bf16[3,64,768]{2,1,0:T(8,128)(2,1)}, u32[]{:S(2)}, u32[]{:S(2)}) collective-permute-start(bf16[3,64,768]{2,1,0:T(8,128)(2,1)S(1)} %multiply_bitcast_fusion), channel_id=1, source_target_pairs={{0,0},{1,16},{2,32},{3,48},{4,64},{5,80},{6,96},{7,112},{8,128},{9... | collective-permute-start | bytes 884744 | tf_op jit(solution)/shard_map/ppermute | solution.py:19
  39.5 20.5 %collective-permute-start.5 = (bf16[512,768]{1,0:T(8,128)(2,1)S(1)}, bf16[512,768]{1,0:T(8,128)(2,1)S(1)}, u32[]{:S(2)}, u32[]{:S(2)}) collective-permute-start(bf16[512,768]{1,0:T(8,128)(2,1)S(1)} %split.6), channel_id=1, source_target_pairs={{0,128},{1,129},{2,130},{3,131},{4,132},{5,133},{6,134},{7,135},{8... | collective-permute-start | bytes 2359304 | tf_op jit(solution)/shard_map/ppermute | solution.py:19
  40.5 16.2 %collective-permute-start.3 = (bf16[3,2,64,768]{3,2,1,0:T(8,128)(2,1)}, bf16[3,2,64,768]{3,2,1,0:T(8,128)(2,1)S(1)}, u32[]{:S(2)}, u32[]{:S(2)}) collective-permute-start(bf16[3,2,64,768]{3,2,1,0:T(8,128)(2,1)} %pad_maximum_fusion.4), channel_id=1, source_target_pairs={{0,4},{1,5},{2,6},{3,7},{4,8},{5,9},{6,10},{7,11},{8,12},{9,13},{1... | collective-permute-start | bytes 1769480 | tf_op jit(solution)/shard_map/ppermute | solution.py:19
  40.5 17.4 %collective-permute-start.4 = (bf16[3,2,64,768]{3,2,1,0:T(8,128)(2,1)}, bf16[3,2,64,768]{3,2,1,0:T(8,128)(2,1)S(1)}, u32[]{:S(2)}, u32[]{:S(2)}) collective-permute-start(bf16[3,2,64,768]{3,2,1,0:T(8,128)(2,1)} %pad_maximum_fusion.4), channel_id=1, source_target_pairs={{0,12},{1,13},{2,14},{3,15},{4,0},{5,1},{6,2},{7,3},{8,4},{9,5},{1... | collective-permute-start | bytes 1769480 | tf_op jit(solution)/shard_map/ppermute | solution.py:19
  44.3 24.0 %collective-permute-start.8 = (bf16[256,768]{1,0:T(8,128)(2,1)}, bf16[256,768]{1,0:T(8,128)(2,1)}, u32[]{:S(2)}, u32[]{:S(2)}) collective-permute-start(bf16[256,768]{1,0:T(8,128)(2,1)} %split.7), channel_id=1, source_target_pairs={{0,128},{1,129},{2,130},{3,131},{4,132},{5,133},{6,134},{7,135},{8... | collective-permute-start | bytes 1179656 | tf_op jit(solution)/shard_map/ppermute | solution.py:19
  60.1 8.7 %collective-permute-start.6 = (bf16[3,1,64,768]{3,2,1,0:T(8,128)(2,1)S(1)}, bf16[3,1,64,768]{3,2,1,0:T(8,128)(2,1)S(1)}, u32[]{:S(2)}, u32[]{:S(2)}) collective-permute-start(bf16[3,1,64,768]{3,2,1,0:T(8,128)(2,1)S(1)} %slice.114), channel_id=1, source_target_pairs={{0,4},{1,5},{2,6},{3,7},{4,8},{5,9},{6,10},{7,11},{8,12},{9,13},{1... | collective-permute-start | bytes 884744 | tf_op jit(solution)/shard_map/ppermute | solution.py:19
  61.0 10.1 %collective-permute-start.7 = (bf16[3,1,64,768]{3,2,1,0:T(8,128)(2,1)}, bf16[3,1,64,768]{3,2,1,0:T(8,128)(2,1)S(1)}, u32[]{:S(2)}, u32[]{:S(2)}) collective-permute-start(bf16[3,1,64,768]{3,2,1,0:T(8,128)(2,1)} %slice.115), channel_id=1, source_target_pairs={{0,12},{1,13},{2,14},{3,15},{4,0},{5,1},{6,2},{7,3},{8,4},{9,5},{1... | collective-permute-start | bytes 884744 | tf_op jit(solution)/shard_map/ppermute | solution.py:19
  74.3 4.9 %collective-permute-start.9 = (bf16[2,3,2,2,64,768]{5,4,3,2,1,0:T(8,128)(2,1)}, bf16[2,3,2,2,64,768]{5,4,3,2,1,0:T(8,128)(2,1)}, u32[]{:S(2)}, u32[]{:S(2)}) collective-permute-start(bf16[2,3,2,2,64,768]{5,4,3,2,1,0:T(8,128)(2,1)} %pad_maximum_fusion), channel_id=1, source_target_pairs={{0,1},{1,0},{2,3},{3,2},{4,5},{5,4},{6,7},{7,6},{8,9},{9,8},{10,11... | collective-permute-start | bytes 7077896 | tf_op jit(solution)/shard_map/ppermute | solution.py:19
  90.6 7.1 %collective-permute-start.10 = (f32[3,16,768]{2,1,0:T(8,128)S(1)}, f32[3,16,768]{2,1,0:T(8,128)S(1)}, u32[]{:S(2)}, u32[]{:S(2)}) collective-permute-start(f32[3,16,768]{2,1,0:T(8,128)S(1)} %get-tuple-element.103), channel_id=1, source_target_pairs={{0,112},{1,113},{2,114},{3,115},{4,116},{5,117},{6,118},{7,119},{8... | collective-permute-start | bytes 442376 | tf_op jit(solution)/shard_map/ppermute | solution.py:19
  92.9 7.7 %collective-permute-start.11 = (f32[3,16,768]{2,1,0:T(8,128)S(1)}, f32[3,16,768]{2,1,0:T(8,128)S(1)}, u32[]{:S(2)}, u32[]{:S(2)}) collective-permute-start(f32[3,16,768]{2,1,0:T(8,128)S(1)} %get-tuple-element.102), channel_id=1, source_target_pairs={{0,16},{1,17},{2,18},{3,19},{4,20},{5,21},{6,22},{7,23},{8,24},{9,... | collective-permute-start | bytes 442376 | tf_op jit(solution)/shard_map/ppermute | solution.py:19
  92.9 11.2 %collective-permute-start.14 = (f32[3,16,768]{2,1,0:T(8,128)S(1)}, f32[3,16,768]{2,1,0:T(8,128)S(1)}, u32[]{:S(2)}, u32[]{:S(2)}) collective-permute-start(f32[3,16,768]{2,1,0:T(8,128)S(1)} %get-tuple-element.105), channel_id=1, source_target_pairs={{0,112},{1,113},{2,114},{3,115},{4,116},{5,117},{6,118},{7,119},{8... | collective-permute-start | bytes 442376 | tf_op jit(solution)/shard_map/ppermute | solution.py:19
  96.2 8.0 %collective-permute-start.15 = (f32[3,16,768]{2,1,0:T(8,128)S(1)}, f32[3,16,768]{2,1,0:T(8,128)S(1)}, u32[]{:S(2)}, u32[]{:S(2)}) collective-permute-start(f32[3,16,768]{2,1,0:T(8,128)S(1)} %get-tuple-element.104), channel_id=1, source_target_pairs={{0,16},{1,17},{2,18},{3,19},{4,20},{5,21},{6,22},{7,23},{8,24},{9,... | collective-permute-start | bytes 442376 | tf_op jit(solution)/shard_map/ppermute | solution.py:19
  96.2 48.8 %collective-permute-start.24 = (bf16[3,8,64,768]{3,2,1,0:T(8,128)(2,1)}, bf16[3,8,64,768]{3,2,1,0:T(8,128)(2,1)}, u32[]{:S(2)}, u32[]{:S(2)}) collective-permute-start(bf16[3,8,64,768]{3,2,1,0:T(8,128)(2,1)} %bitcast.16), channel_id=1, source_target_pairs={{0,128},{1,129},{2,130},{3,131},{4,132},{5,133},{6,134},{7,135},{8... | collective-permute-start | bytes 7077896 | tf_op jit(solution)/shard_map/ppermute | solution.py:19
  100.6 9.7 %collective-permute-start.13 = (f32[3,32,768]{2,1,0:T(8,128)S(1)}, f32[3,32,768]{2,1,0:T(8,128)S(1)}, u32[]{:S(2)}, u32[]{:S(2)}) collective-permute-start(f32[3,32,768]{2,1,0:T(8,128)S(1)} %pad_maximum_fusion.8), channel_id=1, source_target_pairs={{0,16},{1,17},{2,18},{3,19},{4,20},{5,21},{6,22},{7,23},{8,24},{9,... | collective-permute-start | bytes 884744 | tf_op jit(solution)/shard_map/ppermute | solution.py:19
  100.8 9.5 %collective-permute-start.12 = (f32[3,32,768]{2,1,0:T(8,128)S(1)}, f32[3,32,768]{2,1,0:T(8,128)S(1)}, u32[]{:S(2)}, u32[]{:S(2)}) collective-permute-start(f32[3,32,768]{2,1,0:T(8,128)S(1)} %pad_maximum_fusion.7), channel_id=1, source_target_pairs={{0,112},{1,113},{2,114},{3,115},{4,116},{5,117},{6,118},{7,119},{8... | collective-permute-start | bytes 884744 | tf_op jit(solution)/shard_map/ppermute | solution.py:19
  104.3 12.3 %collective-permute-start.19 = (f32[3,32,768]{2,1,0:T(8,128)S(1)}, f32[3,32,768]{2,1,0:T(8,128)S(1)}, u32[]{:S(2)}, u32[]{:S(2)}) collective-permute-start(f32[3,32,768]{2,1,0:T(8,128)S(1)} %pad_maximum_fusion.10), channel_id=1, source_target_pairs={{0,16},{1,17},{2,18},{3,19},{4,20},{5,21},{6,22},{7,23},{8,24},{9,... | collective-permute-start | bytes 884744 | tf_op jit(solution)/shard_map/ppermute | solution.py:19
  104.4 12.2 %collective-permute-start.18 = (f32[3,32,768]{2,1,0:T(8,128)S(1)}, f32[3,32,768]{2,1,0:T(8,128)}, u32[]{:S(2)}, u32[]{:S(2)}) collective-permute-start(f32[3,32,768]{2,1,0:T(8,128)S(1)} %pad_maximum_fusion.9), channel_id=1, source_target_pairs={{0,112},{1,113},{2,114},{3,115},{4,116},{5,117},{6,118},{7,119},{8... | collective-permute-start | bytes 884744 | tf_op jit(solution)/shard_map/ppermute | solution.py:19
  111.3 11.3 %collective-permute-start.16 = (f32[3,32,768]{2,1,0:T(8,128)}, f32[3,32,768]{2,1,0:T(8,128)S(1)}, u32[]{:S(2)}, u32[]{:S(2)}) collective-permute-start(f32[3,32,768]{2,1,0:T(8,128)} %get-tuple-element.64), channel_id=1, source_target_pairs={{0,112},{1,113},{2,114},{3,115},{4,116},{5,117},{6,118},{7,119},{8... | collective-permute-start | bytes 884744 | tf_op jit(solution)/shard_map/ppermute | solution.py:19
  114.5 8.8 %collective-permute-start.17 = (f32[3,32,768]{2,1,0:T(8,128)}, f32[3,32,768]{2,1,0:T(8,128)}, u32[]{:S(2)}, u32[]{:S(2)}) collective-permute-start(f32[3,32,768]{2,1,0:T(8,128)} %get-tuple-element.63), channel_id=1, source_target_pairs={{0,16},{1,17},{2,18},{3,19},{4,20},{5,21},{6,22},{7,23},{8,24},{9,... | collective-permute-start | bytes 884744 | tf_op jit(solution)/shard_map/ppermute | solution.py:19
  117.9 10.3 %collective-permute-start.22 = (f32[3,32,768]{2,1,0:T(8,128)S(1)}, f32[3,32,768]{2,1,0:T(8,128)}, u32[]{:S(2)}, u32[]{:S(2)}) collective-permute-start(f32[3,32,768]{2,1,0:T(8,128)S(1)} %get-tuple-element.62), channel_id=1, source_target_pairs={{0,112},{1,113},{2,114},{3,115},{4,116},{5,117},{6,118},{7,119},{8... | collective-permute-start | bytes 884744 | tf_op jit(solution)/shard_map/ppermute | solution.py:19
  121.3 8.1 %collective-permute-start.23 = (f32[3,32,768]{2,1,0:T(8,128)S(1)}, f32[3,32,768]{2,1,0:T(8,128)}, u32[]{:S(2)}, u32[]{:S(2)}) collective-permute-start(f32[3,32,768]{2,1,0:T(8,128)S(1)} %get-tuple-element.61), channel_id=1, source_target_pairs={{0,16},{1,17},{2,18},{3,19},{4,20},{5,21},{6,22},{7,23},{8,24},{9,... | collective-permute-start | bytes 884744 | tf_op jit(solution)/shard_map/ppermute | solution.py:19
  125.3 7.4 %collective-permute-start.20 = (f32[3,32,768]{2,1,0:T(8,128)}, f32[3,32,768]{2,1,0:T(8,128)S(1)}, u32[]{:S(2)}, u32[]{:S(2)}) collective-permute-start(f32[3,32,768]{2,1,0:T(8,128)} %get-tuple-element.60), channel_id=1, source_target_pairs={{0,112},{1,113},{2,114},{3,115},{4,116},{5,117},{6,118},{7,119},{8... | collective-permute-start | bytes 884744 | tf_op jit(solution)/shard_map/ppermute | solution.py:19
  128.1 8.0 %collective-permute-start.21 = (f32[3,32,768]{2,1,0:T(8,128)S(1)}, f32[3,32,768]{2,1,0:T(8,128)}, u32[]{:S(2)}, u32[]{:S(2)}) collective-permute-start(f32[3,32,768]{2,1,0:T(8,128)S(1)} %get-tuple-element.59), channel_id=1, source_target_pairs={{0,16},{1,17},{2,18},{3,19},{4,20},{5,21},{6,22},{7,23},{8,24},{9,... | collective-permute-start | bytes 884744 | tf_op jit(solution)/shard_map/ppermute | solution.py:19
  145.0 7.2 %collective-permute-start.25 = (f32[3,32,768]{2,1,0:T(8,128)S(1)}, f32[3,32,768]{2,1,0:T(8,128)S(1)}, u32[]{:S(2)}, u32[]{:S(2)}) collective-permute-start(f32[3,32,768]{2,1,0:T(8,128)S(1)} %get-tuple-element.53), channel_id=1, source_target_pairs={{0,112},{1,113},{2,114},{3,115},{4,116},{5,117},{6,118},{7,119},{8... | collective-permute-start | bytes 884744 | tf_op jit(solution)/shard_map/ppermute | solution.py:19
  148.0 7.9 %collective-permute-start.26 = (f32[3,32,768]{2,1,0:T(8,128)S(1)}, f32[3,32,768]{2,1,0:T(8,128)S(1)}, u32[]{:S(2)}, u32[]{:S(2)}) collective-permute-start(f32[3,32,768]{2,1,0:T(8,128)S(1)} %get-tuple-element.54), channel_id=1, source_target_pairs={{0,16},{1,17},{2,18},{3,19},{4,20},{5,21},{6,22},{7,23},{8,24},{9,... | collective-permute-start | bytes 884744 | tf_op jit(solution)/shard_map/ppermute | solution.py:19
  165.0 6.5 %collective-permute-start.29 = (f32[3,2,32,128]{3,2,1,0:T(8,128)S(1)}, f32[3,2,32,128]{3,2,1,0:T(8,128)S(1)}, u32[]{:S(2)}, u32[]{:S(2)}) collective-permute-start(f32[3,2,32,128]{3,2,1,0:T(8,128)S(1)} %get-tuple-element.86), channel_id=1, source_target_pairs={{0,8},{1,9},{2,10},{3,11},{4,12},{5,13},{6,14},{7,15},{8,0},{9,1},... | collective-permute-start | bytes 294920 | tf_op jit(solution)/shard_map/ppermute | solution.py:19
  166.8 6.7 %collective-permute-start.30 = (f32[3,2,32,128]{3,2,1,0:T(8,128)S(1)}, f32[3,2,32,128]{3,2,1,0:T(8,128)S(1)}, u32[]{:S(2)}, u32[]{:S(2)}) collective-permute-start(f32[3,2,32,128]{3,2,1,0:T(8,128)S(1)} %get-tuple-element.85), channel_id=1, source_target_pairs={{0,12},{1,13},{2,14},{3,15},{4,8},{5,9},{6,10},{7,11},{8,4},{9,5},... | collective-permute-start | bytes 294920 | tf_op jit(solution)/shard_map/ppermute | solution.py:19
  169.0 4.7 %collective-permute-start.28 = (f32[3,2,32,128]{3,2,1,0:T(8,128)S(1)}, f32[3,2,32,128]{3,2,1,0:T(8,128)S(1)}, u32[]{:S(2)}, u32[]{:S(2)}) collective-permute-start(f32[3,2,32,128]{3,2,1,0:T(8,128)S(1)} %fusion.39), channel_id=1, source_target_pairs={{0,4},{1,5},{2,6},{3,7},{4,0},{5,1},{6,2},{7,3},{8,12},{9,13},{10,... | collective-permute-start | bytes 294920 | tf_op jit(solution)/shard_map/ppermute | solution.py:19
  173.9 5.7 %collective-permute-start.31 = (f32[3,32,128]{2,1,0:T(8,128)S(1)}, f32[3,32,128]{2,1,0:T(8,128)S(1)}, u32[]{:S(2)}, u32[]{:S(2)}) collective-permute-start(f32[3,32,128]{2,1,0:T(8,128)S(1)} %slice_bitcast_fusion.2), channel_id=1, source_target_pairs={{0,2},{1,3},{2,0},{3,1},{4,6},{5,7},{6,4},{7,5},{8,10},{9,11},{10,... | collective-permute-start | bytes 147464 | tf_op jit(solution)/shard_map/ppermute | solution.py:19
  (7 other events, 49.0 us)
Sparse Core Ops, SparseCore 0:
  42.7 43.2 all-gather.2

commit v12 on v11

--- a/solution.py
+++ b/solution.py
@@ -112,8 +112,8 @@
     for offset in (3, 2, 1):
         one = with_own(first, half, offset, *behind(both_ways(one), *two))
         two = with_own(second, half, offset, *behind(both_ways(two), *one))
+    one, two = both_ways(one), both_ways(two)
     *two, beside = together(*two, beside)
-    one, two = both_ways(one), both_ways(two)
     return first(0) + one[0] + one[1], second(0) + two[0] + two[1], beside
 
 

time: 188 us -> 179 us (0.952)
  waiting for transfers between devices: 82 us -> 74 us
    ppermute x32, waiting for transfers between devices: 75.1 us -> 67.2 us  [send(): return lax.ppermute(value, AXES, pairs(move))]
  transfers between devices with their start and end apart: 33 -> 33, of which waited for: 27 -> 25; matrix products, arithmetic and copies ran while one was open for 10% -> 10% of each run, Pallas kernels for 0% -> 0%
where the time goes in v12:
time: 179 us; the launch traced here: 178 us
  waiting for transfers between devices  74 us (41%)
  starting transfers between devices  55.5 us (31%)
  other arithmetic  15.6 us (9%)
  between operations  14.4 us (8%)
  matrix products  9.59 us (5%)
  local copies, waits for them, and re-layouts  9.01 us (5%)
    ppermute x32, waiting for transfers between devices, send(): return lax.ppermute(value, AXES, pairs(move))  67.2 us
    ppermute x32, starting transfers between devices, send(): return lax.ppermute(value, AXES, pairs(move))  55.4 us
    all_gather x1, waiting for transfers between devices, shards(): facing = [lax.all_gather(turned, 'z', axis=1), None]  6.8 us
    dot_general x2, matrix products, dot_each(): return jnp.einsum('knr,kmr->knm', a, b, preferred_element_type=jnp.float32)  5.11 us
    dot_general x4, matrix products, dot_nt(): return lax.dot_general(a, b, NT, preferred_element_type=jnp.float32)  4.47 us
    add x3, other arithmetic, with_own(): return (below + down, above + up)  4.13 us
  transfers between devices with their start and end apart: 33, of which 25 were waited for; matrix products, arithmetic and copies ran while one was open for 10% of the time, Pallas kernels for 0%

profile of v12, /device:TPU:6, one launch (start us, length us, event | category | flops | bytes accessed | tf_op | source)
XLA Modules:
  0.0 178.1 jit_solution(1828962750494028591)
XLA Ops:
  9.1 3.4 %collective-permute-start = (bf16[3,64,768]{2,1,0:T(8,128)(2,1)S(1)}, bf16[3,64,768]{2,1,0:T(8,128)(2,1)S(1)}, u32[]{:S(2)}, u32[]{:S(2)}) collective-permute-start(bf16[3,64,768]{2,1,0:T(8,128)(2,1)S(1)} %multiply_bitcast_fusion), channel_id=1, source_target_pairs={{0,0},{1,1},{2,2},{3,3},{4,4},{5,5},{6,6},{7,7},{8,132},{9,133},{1... | collective-permute-start | bytes 884744 | tf_op jit(solution)/shard_map/ppermute | solution.py:19
  12.5 4.5 %collective-permute-start.1 = (bf16[3,64,768]{2,1,0:T(8,128)(2,1)S(1)}, bf16[3,64,768]{2,1,0:T(8,128)(2,1)S(1)}, u32[]{:S(2)}, u32[]{:S(2)}) collective-permute-start(bf16[3,64,768]{2,1,0:T(8,128)(2,1)S(1)} %multiply_bitcast_fusion), channel_id=1, source_target_pairs={{0,2},{1,3},{2,0},{3,1},{4,6},{5,7},{6,4},{7,5},{8,134},{9,135},{1... | collective-permute-start | bytes 884744 | tf_op jit(solution)/shard_map/ppermute | solution.py:19
  17.0 9.1 %collective-permute-start.2 = (bf16[3,64,768]{2,1,0:T(8,128)(2,1)S(1)}, bf16[3,64,768]{2,1,0:T(8,128)(2,1)}, u32[]{:S(2)}, u32[]{:S(2)}) collective-permute-start(bf16[3,64,768]{2,1,0:T(8,128)(2,1)S(1)} %multiply_bitcast_fusion), channel_id=1, source_target_pairs={{0,0},{1,16},{2,32},{3,48},{4,64},{5,80},{6,96},{7,112},{8,128},{9... | collective-permute-start | bytes 884744 | tf_op jit(solution)/shard_map/ppermute | solution.py:19
  26.1 10.2 %collective-permute-done.1 = bf16[3,64,768]{2,1,0:T(8,128)(2,1)S(1)} collective-permute-done((bf16[3,64,768]{2,1,0:T(8,128)(2,1)S(1)}, bf16[3,64,768]{2,1,0:T(8,128)(2,1)S(1)}, u32[]{:S(2)}, u32[]{:S(2)}) %collective-permute-start.1) | collective-permute-done | bytes 294944 | tf_op jit(solution)/shard_map/ppermute | solution.py:19
  36.3 2.1 %collective-permute-done.2 = bf16[3,64,768]{2,1,0:T(8,128)(2,1)} collective-permute-done((bf16[3,64,768]{2,1,0:T(8,128)(2,1)S(1)}, bf16[3,64,768]{2,1,0:T(8,128)(2,1)}, u32[]{:S(2)}, u32[]{:S(2)}) %collective-permute-start.2) | collective-permute-done | bytes 294944 | tf_op jit(solution)/shard_map/ppermute | solution.py:19
  40.5 2.0 %collective-permute-start.4 = (bf16[3,2,64,768]{3,2,1,0:T(8,128)(2,1)}, bf16[3,2,64,768]{3,2,1,0:T(8,128)(2,1)S(1)}, u32[]{:S(2)}, u32[]{:S(2)}) collective-permute-start(bf16[3,2,64,768]{3,2,1,0:T(8,128)(2,1)} %pad_maximum_fusion.4), channel_id=1, source_target_pairs={{0,12},{1,13},{2,14},{3,15},{4,0},{5,1},{6,2},{7,3},{8,4},{9,5},{1... | collective-permute-start | bytes 1769480 | tf_op jit(solution)/shard_map/ppermute | solution.py:19
  44.3 2.0 %collective-permute-start.8 = (bf16[256,768]{1,0:T(8,128)(2,1)}, bf16[256,768]{1,0:T(8,128)(2,1)}, u32[]{:S(2)}, u32[]{:S(2)}) collective-permute-start(bf16[256,768]{1,0:T(8,128)(2,1)} %split.7), channel_id=1, source_target_pairs={{0,128},{1,129},{2,130},{3,131},{4,132},{5,133},{6,134},{7,135},{8... | collective-permute-start | bytes 1179656 | tf_op jit(solution)/shard_map/ppermute | solution.py:19
  46.4 10.3 %collective-permute-done.3 = bf16[3,2,64,768]{3,2,1,0:T(8,128)(2,1)S(1)} collective-permute-done((bf16[3,2,64,768]{3,2,1,0:T(8,128)(2,1)}, bf16[3,2,64,768]{3,2,1,0:T(8,128)(2,1)S(1)}, u32[]{:S(2)}, u32[]{:S(2)}) %collective-permute-start.3) | collective-permute-done | bytes 589856 | tf_op jit(solution)/shard_map/ppermute | solution.py:19
  57.9 2.2 %collective-permute-done.5 = bf16[512,768]{1,0:T(8,128)(2,1)S(1)} collective-permute-done((bf16[512,768]{1,0:T(8,128)(2,1)S(1)}, bf16[512,768]{1,0:T(8,128)(2,1)S(1)}, u32[]{:S(2)}, u32[]{:S(2)}) %collective-permute-start.5) | collective-permute-done | bytes 786464 | tf_op jit(solution)/shard_map/ppermute | solution.py:19
  62.9 5.4 %collective-permute-done.8 = bf16[256,768]{1,0:T(8,128)(2,1)} collective-permute-done((bf16[256,768]{1,0:T(8,128)(2,1)}, bf16[256,768]{1,0:T(8,128)(2,1)}, u32[]{:S(2)}, u32[]{:S(2)}) %collective-permute-start.8) | collective-permute-done | bytes 393248 | tf_op jit(solution)/shard_map/ppermute | solution.py:19
  68.8 2.3 %collective-permute-done.7 = bf16[3,1,64,768]{3,2,1,0:T(8,128)(2,1)S(1)} collective-permute-done((bf16[3,1,64,768]{3,2,1,0:T(8,128)(2,1)}, bf16[3,1,64,768]{3,2,1,0:T(8,128)(2,1)S(1)}, u32[]{:S(2)}, u32[]{:S(2)}) %collective-permute-start.7) | collective-permute-done | bytes 294944 | tf_op jit(solution)/shard_map/ppermute | solution.py:19
  79.2 6.8 %all-gather.3.cloned.1.call-done = bf16[3,512,768]{2,1,0:T(8,128)(2,1)} async-done(((bf16[3,64,768]{2,1,0:T(8,128)(2,1)}), bf16[3,512,768]{2,1,0:T(8,128)(2,1)}) %all-gather.3.cloned.1.call-update) | async-done | bytes 2359312 | tf_op jit(solution)/shard_map/all_gather | solution.py:134
  90.6 2.3 %collective-permute-start.10 = (f32[3,16,768]{2,1,0:T(8,128)S(1)}, f32[3,16,768]{2,1,0:T(8,128)S(1)}, u32[]{:S(2)}, u32[]{:S(2)}) collective-permute-start(f32[3,16,768]{2,1,0:T(8,128)S(1)} %get-tuple-element.103), channel_id=1, source_target_pairs={{0,112},{1,113},{2,114},{3,115},{4,116},{5,117},{6,118},{7,119},{8... | collective-permute-start | bytes 442376 | tf_op jit(solution)/shard_map/ppermute | solution.py:19
  92.9 3.3 %collective-permute-start.14 = (f32[3,16,768]{2,1,0:T(8,128)S(1)}, f32[3,16,768]{2,1,0:T(8,128)S(1)}, u32[]{:S(2)}, u32[]{:S(2)}) collective-permute-start(f32[3,16,768]{2,1,0:T(8,128)S(1)} %get-tuple-element.105), channel_id=1, source_target_pairs={{0,112},{1,113},{2,114},{3,115},{4,116},{5,117},{6,118},{7,119},{8... | collective-permute-start | bytes 442376 | tf_op jit(solution)/shard_map/ppermute | solution.py:19
  97.7 2.8 %collective-permute-done.11 = f32[3,16,768]{2,1,0:T(8,128)S(1)} collective-permute-done((f32[3,16,768]{2,1,0:T(8,128)S(1)}, f32[3,16,768]{2,1,0:T(8,128)S(1)}, u32[]{:S(2)}, u32[]{:S(2)}) %collective-permute-start.11) | collective-permute-done | bytes 147488 | tf_op jit(solution)/shard_map/ppermute | solution.py:19
  100.8 3.3 %collective-permute-start.12 = (f32[3,32,768]{2,1,0:T(8,128)S(1)}, f32[3,32,768]{2,1,0:T(8,128)S(1)}, u32[]{:S(2)}, u32[]{:S(2)}) collective-permute-start(f32[3,32,768]{2,1,0:T(8,128)S(1)} %pad_maximum_fusion.7), channel_id=1, source_target_pairs={{0,112},{1,113},{2,114},{3,115},{4,116},{5,117},{6,118},{7,119},{8... | collective-permute-start | bytes 884744 | tf_op jit(solution)/shard_map/ppermute | solution.py:19
  104.4 3.3 %collective-permute-start.18 = (f32[3,32,768]{2,1,0:T(8,128)S(1)}, f32[3,32,768]{2,1,0:T(8,128)}, u32[]{:S(2)}, u32[]{:S(2)}) collective-permute-start(f32[3,32,768]{2,1,0:T(8,128)S(1)} %pad_maximum_fusion.9), channel_id=1, source_target_pairs={{0,112},{1,113},{2,114},{3,115},{4,116},{5,117},{6,118},{7,119},{8... | collective-permute-start | bytes 884744 | tf_op jit(solution)/shard_map/ppermute | solution.py:19
  107.7 2.6 %collective-permute-done.13 = f32[3,32,768]{2,1,0:T(8,128)S(1)} collective-permute-done((f32[3,32,768]{2,1,0:T(8,128)S(1)}, f32[3,32,768]{2,1,0:T(8,128)S(1)}, u32[]{:S(2)}, u32[]{:S(2)}) %collective-permute-start.13) | collective-permute-done | bytes 294944 | tf_op jit(solution)/shard_map/ppermute | solution.py:19
  111.3 3.2 %collective-permute-start.16 = (f32[3,32,768]{2,1,0:T(8,128)}, f32[3,32,768]{2,1,0:T(8,128)S(1)}, u32[]{:S(2)}, u32[]{:S(2)}) collective-permute-start(f32[3,32,768]{2,1,0:T(8,128)} %get-tuple-element.64), channel_id=1, source_target_pairs={{0,112},{1,113},{2,114},{3,115},{4,116},{5,117},{6,118},{7,119},{8... | collective-permute-start | bytes 884744 | tf_op jit(solution)/shard_map/ppermute | solution.py:19
  114.5 2.1 %collective-permute-done.19 = f32[3,32,768]{2,1,0:T(8,128)S(1)} collective-permute-done((f32[3,32,768]{2,1,0:T(8,128)S(1)}, f32[3,32,768]{2,1,0:T(8,128)S(1)}, u32[]{:S(2)}, u32[]{:S(2)}) %collective-permute-start.19) | collective-permute-done | bytes 294944 | tf_op jit(solution)/shard_map/ppermute | solution.py:19
  117.9 3.4 %collective-permute-start.22 = (f32[3,32,768]{2,1,0:T(8,128)S(1)}, f32[3,32,768]{2,1,0:T(8,128)}, u32[]{:S(2)}, u32[]{:S(2)}) collective-permute-start(f32[3,32,768]{2,1,0:T(8,128)S(1)} %get-tuple-element.62), channel_id=1, source_target_pairs={{0,112},{1,113},{2,114},{3,115},{4,116},{5,117},{6,118},{7,119},{8... | collective-permute-start | bytes 884744 | tf_op jit(solution)/shard_map/ppermute | solution.py:19
  125.3 2.9 %collective-permute-start.20 = (f32[3,32,768]{2,1,0:T(8,128)}, f32[3,32,768]{2,1,0:T(8,128)S(1)}, u32[]{:S(2)}, u32[]{:S(2)}) collective-permute-start(f32[3,32,768]{2,1,0:T(8,128)} %get-tuple-element.60), channel_id=1, source_target_pairs={{0,112},{1,113},{2,114},{3,115},{4,116},{5,117},{6,118},{7,119},{8... | collective-permute-start | bytes 884744 | tf_op jit(solution)/shard_map/ppermute | solution.py:19
  129.4 4.3 %collective-permute-done.20 = f32[3,32,768]{2,1,0:T(8,128)S(1)} collective-permute-done((f32[3,32,768]{2,1,0:T(8,128)}, f32[3,32,768]{2,1,0:T(8,128)S(1)}, u32[]{:S(2)}, u32[]{:S(2)}) %collective-permute-start.20) | collective-permute-done | bytes 294944 | tf_op jit(solution)/shard_map/ppermute | solution.py:19
  133.7 3.6 %collective-permute-done.21 = f32[3,32,768]{2,1,0:T(8,128)} collective-permute-done((f32[3,32,768]{2,1,0:T(8,128)S(1)}, f32[3,32,768]{2,1,0:T(8,128)}, u32[]{:S(2)}, u32[]{:S(2)}) %collective-permute-start.21) | collective-permute-done | bytes 294944 | tf_op jit(solution)/shard_map/ppermute | solution.py:19
  138.9 2.0 %collective-permute-start.25 = (f32[3,32,768]{2,1,0:T(8,128)S(1)}, f32[3,32,768]{2,1,0:T(8,128)S(1)}, u32[]{:S(2)}, u32[]{:S(2)}) collective-permute-start(f32[3,32,768]{2,1,0:T(8,128)S(1)} %get-tuple-element.58), channel_id=1, source_target_pairs={{0,16},{1,17},{2,18},{3,19},{4,20},{5,21},{6,22},{7,23},{8,24},{9,... | collective-permute-start | bytes 884744 | tf_op jit(solution)/shard_map/ppermute | solution.py:19
  140.9 4.7 %collective-permute-done.24 = f32[3,32,768]{2,1,0:T(8,128)S(1)} collective-permute-done((f32[3,32,768]{2,1,0:T(8,128)S(1)}, f32[3,32,768]{2,1,0:T(8,128)S(1)}, u32[]{:S(2)}, u32[]{:S(2)}) %collective-permute-start.24) | collective-permute-done | bytes 294944 | tf_op jit(solution)/shard_map/ppermute | solution.py:19
  148.3 2.6 %fusion.55 = f32[3,512,128]{1,2,0:T(8,128)S(1)} fusion(bf16[3,512,768]{2,1,0:T(8,128)(2,1)} %bitcast.37, bf16[3,128,768]{2,1,0:T(8,128)(2,1)S(1)} %bitcast.279), kind=kOutput, calls=%fused_computation.123 | convolution fusion | flops 301989888 | bytes 3735552 | tf_op jit(solution)/shard_map/knr,kmr->knm/dot_general | solution.py:85
  151.0 2.6 %fusion.56 = f32[3,512,128]{1,2,0:T(8,128)S(1)} fusion(bf16[3,512,768]{2,1,0:T(8,128)(2,1)} %bitcast.41, bf16[3,128,768]{2,1,0:T(8,128)(2,1)S(1)} %bitcast.280), kind=kOutput, calls=%fused_computation.124 | convolution fusion | flops 301989888 | bytes 3735552 | tf_op jit(solution)/shard_map/knr,kmr->knm/dot_general | solution.py:85
  157.7 2.1 %collective-permute-start.30 = (f32[3,2,32,128]{3,2,1,0:T(8,128)S(1)}, f32[3,2,32,128]{3,2,1,0:T(8,128)S(1)}, u32[]{:S(2)}, u32[]{:S(2)}) collective-permute-start(f32[3,2,32,128]{3,2,1,0:T(8,128)S(1)} %get-tuple-element.85), channel_id=1, source_target_pairs={{0,12},{1,13},{2,14},{3,15},{4,8},{5,9},{6,10},{7,11},{8,4},{9,5},... | collective-permute-start | bytes 294920 | tf_op jit(solution)/shard_map/ppermute | solution.py:19
  160.2 2.6 %collective-permute-done.29 = f32[3,2,32,128]{3,2,1,0:T(8,128)S(1)} collective-permute-done((f32[3,2,32,128]{3,2,1,0:T(8,128)S(1)}, f32[3,2,32,128]{3,2,1,0:T(8,128)S(1)}, u32[]{:S(2)}, u32[]{:S(2)}) %collective-permute-start.29) | collective-permute-done | bytes 98336 | tf_op jit(solution)/shard_map/ppermute | solution.py:19
  162.7 2.0 %collective-permute-done.30 = f32[3,2,32,128]{3,2,1,0:T(8,128)S(1)} collective-permute-done((f32[3,2,32,128]{3,2,1,0:T(8,128)S(1)}, f32[3,2,32,128]{3,2,1,0:T(8,128)S(1)}, u32[]{:S(2)}, u32[]{:S(2)}) %collective-permute-start.30) | collective-permute-done | bytes 98336 | tf_op jit(solution)/shard_map/ppermute | solution.py:19
  164.8 3.1 %collective-permute-start.31 = (f32[3,32,128]{2,1,0:T(8,128)S(1)}, f32[3,32,128]{2,1,0:T(8,128)S(1)}, u32[]{:S(2)}, u32[]{:S(2)}) collective-permute-start(f32[3,32,128]{2,1,0:T(8,128)S(1)} %slice_bitcast_fusion.2), channel_id=1, source_target_pairs={{0,2},{1,3},{2,0},{3,1},{4,6},{5,7},{6,4},{7,5},{8,10},{9,11},{10,... | collective-permute-start | bytes 147464 | tf_op jit(solution)/shard_map/ppermute | solution.py:19
  (109 shorter events, 44.9 us)
Async XLA Ops:
  7.2 78.8 %all-gather.3.cloned.1.call-start = ((), (), s32[]{:S(2)}) async-start(), calls=%async_computation | async-start | bytes 2654208 | tf_op jit(solution)/shard_map/all_gather | solution.py:134
  9.1 17.0 %collective-permute-start = (bf16[3,64,768]{2,1,0:T(8,128)(2,1)S(1)}, bf16[3,64,768]{2,1,0:T(8,128)(2,1)S(1)}, u32[]{:S(2)}, u32[]{:S(2)}) collective-permute-start(bf16[3,64,768]{2,1,0:T(8,128)(2,1)S(1)} %multiply_bitcast_fusion), channel_id=1, source_target_pairs={{0,0},{1,1},{2,2},{3,3},{4,4},{5,5},{6,6},{7,7},{8,132},{9,133},{1... | collective-permute-start | bytes 884744 | tf_op jit(solution)/shard_map/ppermute | solution.py:19
  12.5 23.8 %collective-permute-start.1 = (bf16[3,64,768]{2,1,0:T(8,128)(2,1)S(1)}, bf16[3,64,768]{2,1,0:T(8,128)(2,1)S(1)}, u32[]{:S(2)}, u32[]{:S(2)}) collective-permute-start(bf16[3,64,768]{2,1,0:T(8,128)(2,1)S(1)} %multiply_bitcast_fusion), channel_id=1, source_target_pairs={{0,2},{1,3},{2,0},{3,1},{4,6},{5,7},{6,4},{7,5},{8,134},{9,135},{1... | collective-permute-start | bytes 884744 | tf_op jit(solution)/shard_map/ppermute | solution.py:19
  17.0 21.3 %collective-permute-start.2 = (bf16[3,64,768]{2,1,0:T(8,128)(2,1)S(1)}, bf16[3,64,768]{2,1,0:T(8,128)(2,1)}, u32[]{:S(2)}, u32[]{:S(2)}) collective-permute-start(bf16[3,64,768]{2,1,0:T(8,128)(2,1)S(1)} %multiply_bitcast_fusion), channel_id=1, source_target_pairs={{0,0},{1,16},{2,32},{3,48},{4,64},{5,80},{6,96},{7,112},{8,128},{9... | collective-permute-start | bytes 884744 | tf_op jit(solution)/shard_map/ppermute | solution.py:19
  39.5 20.5 %collective-permute-start.5 = (bf16[512,768]{1,0:T(8,128)(2,1)S(1)}, bf16[512,768]{1,0:T(8,128)(2,1)S(1)}, u32[]{:S(2)}, u32[]{:S(2)}) collective-permute-start(bf16[512,768]{1,0:T(8,128)(2,1)S(1)} %split.6), channel_id=1, source_target_pairs={{0,128},{1,129},{2,130},{3,131},{4,132},{5,133},{6,134},{7,135},{8... | collective-permute-start | bytes 2359304 | tf_op jit(solution)/shard_map/ppermute | solution.py:19
  40.5 16.2 %collective-permute-start.3 = (bf16[3,2,64,768]{3,2,1,0:T(8,128)(2,1)}, bf16[3,2,64,768]{3,2,1,0:T(8,128)(2,1)S(1)}, u32[]{:S(2)}, u32[]{:S(2)}) collective-permute-start(bf16[3,2,64,768]{3,2,1,0:T(8,128)(2,1)} %pad_maximum_fusion.4), channel_id=1, source_target_pairs={{0,4},{1,5},{2,6},{3,7},{4,8},{5,9},{6,10},{7,11},{8,12},{9,13},{1... | collective-permute-start | bytes 1769480 | tf_op jit(solution)/shard_map/ppermute | solution.py:19
  40.5 17.4 %collective-permute-start.4 = (bf16[3,2,64,768]{3,2,1,0:T(8,128)(2,1)}, bf16[3,2,64,768]{3,2,1,0:T(8,128)(2,1)S(1)}, u32[]{:S(2)}, u32[]{:S(2)}) collective-permute-start(bf16[3,2,64,768]{3,2,1,0:T(8,128)(2,1)} %pad_maximum_fusion.4), channel_id=1, source_target_pairs={{0,12},{1,13},{2,14},{3,15},{4,0},{5,1},{6,2},{7,3},{8,4},{9,5},{1... | collective-permute-start | bytes 1769480 | tf_op jit(solution)/shard_map/ppermute | solution.py:19
  44.3 24.0 %collective-permute-start.8 = (bf16[256,768]{1,0:T(8,128)(2,1)}, bf16[256,768]{1,0:T(8,128)(2,1)}, u32[]{:S(2)}, u32[]{:S(2)}) collective-permute-start(bf16[256,768]{1,0:T(8,128)(2,1)} %split.7), channel_id=1, source_target_pairs={{0,128},{1,129},{2,130},{3,131},{4,132},{5,133},{6,134},{7,135},{8... | collective-permute-start | bytes 1179656 | tf_op jit(solution)/shard_map/ppermute | solution.py:19
  60.1 8.7 %collective-permute-start.6 = (bf16[3,1,64,768]{3,2,1,0:T(8,128)(2,1)S(1)}, bf16[3,1,64,768]{3,2,1,0:T(8,128)(2,1)S(1)}, u32[]{:S(2)}, u32[]{:S(2)}) collective-permute-start(bf16[3,1,64,768]{3,2,1,0:T(8,128)(2,1)S(1)} %slice.114), channel_id=1, source_target_pairs={{0,4},{1,5},{2,6},{3,7},{4,8},{5,9},{6,10},{7,11},{8,12},{9,13},{1... | collective-permute-start | bytes 884744 | tf_op jit(solution)/shard_map/ppermute | solution.py:19
  61.0 10.1 %collective-permute-start.7 = (bf16[3,1,64,768]{3,2,1,0:T(8,128)(2,1)}, bf16[3,1,64,768]{3,2,1,0:T(8,128)(2,1)S(1)}, u32[]{:S(2)}, u32[]{:S(2)}) collective-permute-start(bf16[3,1,64,768]{3,2,1,0:T(8,128)(2,1)} %slice.115), channel_id=1, source_target_pairs={{0,12},{1,13},{2,14},{3,15},{4,0},{5,1},{6,2},{7,3},{8,4},{9,5},{1... | collective-permute-start | bytes 884744 | tf_op jit(solution)/shard_map/ppermute | solution.py:19
  74.3 4.9 %collective-permute-start.9 = (bf16[2,3,2,2,64,768]{5,4,3,2,1,0:T(8,128)(2,1)}, bf16[2,3,2,2,64,768]{5,4,3,2,1,0:T(8,128)(2,1)}, u32[]{:S(2)}, u32[]{:S(2)}) collective-permute-start(bf16[2,3,2,2,64,768]{5,4,3,2,1,0:T(8,128)(2,1)} %pad_maximum_fusion), channel_id=1, source_target_pairs={{0,1},{1,0},{2,3},{3,2},{4,5},{5,4},{6,7},{7,6},{8,9},{9,8},{10,11... | collective-permute-start | bytes 7077896 | tf_op jit(solution)/shard_map/ppermute | solution.py:19
  90.6 7.1 %collective-permute-start.10 = (f32[3,16,768]{2,1,0:T(8,128)S(1)}, f32[3,16,768]{2,1,0:T(8,128)S(1)}, u32[]{:S(2)}, u32[]{:S(2)}) collective-permute-start(f32[3,16,768]{2,1,0:T(8,128)S(1)} %get-tuple-element.103), channel_id=1, source_target_pairs={{0,112},{1,113},{2,114},{3,115},{4,116},{5,117},{6,118},{7,119},{8... | collective-permute-start | bytes 442376 | tf_op jit(solution)/shard_map/ppermute | solution.py:19
  92.9 7.7 %collective-permute-start.11 = (f32[3,16,768]{2,1,0:T(8,128)S(1)}, f32[3,16,768]{2,1,0:T(8,128)S(1)}, u32[]{:S(2)}, u32[]{:S(2)}) collective-permute-start(f32[3,16,768]{2,1,0:T(8,128)S(1)} %get-tuple-element.102), channel_id=1, source_target_pairs={{0,16},{1,17},{2,18},{3,19},{4,20},{5,21},{6,22},{7,23},{8,24},{9,... | collective-permute-start | bytes 442376 | tf_op jit(solution)/shard_map/ppermute | solution.py:19
  92.9 11.2 %collective-permute-start.14 = (f32[3,16,768]{2,1,0:T(8,128)S(1)}, f32[3,16,768]{2,1,0:T(8,128)S(1)}, u32[]{:S(2)}, u32[]{:S(2)}) collective-permute-start(f32[3,16,768]{2,1,0:T(8,128)S(1)} %get-tuple-element.105), channel_id=1, source_target_pairs={{0,112},{1,113},{2,114},{3,115},{4,116},{5,117},{6,118},{7,119},{8... | collective-permute-start | bytes 442376 | tf_op jit(solution)/shard_map/ppermute | solution.py:19
  96.2 8.0 %collective-permute-start.15 = (f32[3,16,768]{2,1,0:T(8,128)S(1)}, f32[3,16,768]{2,1,0:T(8,128)S(1)}, u32[]{:S(2)}, u32[]{:S(2)}) collective-permute-start(f32[3,16,768]{2,1,0:T(8,128)S(1)} %get-tuple-element.104), channel_id=1, source_target_pairs={{0,16},{1,17},{2,18},{3,19},{4,20},{5,21},{6,22},{7,23},{8,24},{9,... | collective-permute-start | bytes 442376 | tf_op jit(solution)/shard_map/ppermute | solution.py:19
  96.2 50.9 %collective-permute-start.26 = (bf16[3,8,64,768]{3,2,1,0:T(8,128)(2,1)}, bf16[3,8,64,768]{3,2,1,0:T(8,128)(2,1)}, u32[]{:S(2)}, u32[]{:S(2)}) collective-permute-start(bf16[3,8,64,768]{3,2,1,0:T(8,128)(2,1)} %bitcast.16), channel_id=1, source_target_pairs={{0,128},{1,129},{2,130},{3,131},{4,132},{5,133},{6,134},{7,135},{8... | collective-permute-start | bytes 7077896 | tf_op jit(solution)/shard_map/ppermute | solution.py:19
  100.6 9.7 %collective-permute-start.13 = (f32[3,32,768]{2,1,0:T(8,128)S(1)}, f32[3,32,768]{2,1,0:T(8,128)S(1)}, u32[]{:S(2)}, u32[]{:S(2)}) collective-permute-start(f32[3,32,768]{2,1,0:T(8,128)S(1)} %pad_maximum_fusion.8), channel_id=1, source_target_pairs={{0,16},{1,17},{2,18},{3,19},{4,20},{5,21},{6,22},{7,23},{8,24},{9,... | collective-permute-start | bytes 884744 | tf_op jit(solution)/shard_map/ppermute | solution.py:19
  100.8 9.5 %collective-permute-start.12 = (f32[3,32,768]{2,1,0:T(8,128)S(1)}, f32[3,32,768]{2,1,0:T(8,128)S(1)}, u32[]{:S(2)}, u32[]{:S(2)}) collective-permute-start(f32[3,32,768]{2,1,0:T(8,128)S(1)} %pad_maximum_fusion.7), channel_id=1, source_target_pairs={{0,112},{1,113},{2,114},{3,115},{4,116},{5,117},{6,118},{7,119},{8... | collective-permute-start | bytes 884744 | tf_op jit(solution)/shard_map/ppermute | solution.py:19
  104.3 12.3 %collective-permute-start.19 = (f32[3,32,768]{2,1,0:T(8,128)S(1)}, f32[3,32,768]{2,1,0:T(8,128)S(1)}, u32[]{:S(2)}, u32[]{:S(2)}) collective-permute-start(f32[3,32,768]{2,1,0:T(8,128)S(1)} %pad_maximum_fusion.10), channel_id=1, source_target_pairs={{0,16},{1,17},{2,18},{3,19},{4,20},{5,21},{6,22},{7,23},{8,24},{9,... | collective-permute-start | bytes 884744 | tf_op jit(solution)/shard_map/ppermute | solution.py:19
  104.4 12.2 %collective-permute-start.18 = (f32[3,32,768]{2,1,0:T(8,128)S(1)}, f32[3,32,768]{2,1,0:T(8,128)}, u32[]{:S(2)}, u32[]{:S(2)}) collective-permute-start(f32[3,32,768]{2,1,0:T(8,128)S(1)} %pad_maximum_fusion.9), channel_id=1, source_target_pairs={{0,112},{1,113},{2,114},{3,115},{4,116},{5,117},{6,118},{7,119},{8... | collective-permute-start | bytes 884744 | tf_op jit(solution)/shard_map/ppermute | solution.py:19
  111.3 11.3 %collective-permute-start.16 = (f32[3,32,768]{2,1,0:T(8,128)}, f32[3,32,768]{2,1,0:T(8,128)S(1)}, u32[]{:S(2)}, u32[]{:S(2)}) collective-permute-start(f32[3,32,768]{2,1,0:T(8,128)} %get-tuple-element.64), channel_id=1, source_target_pairs={{0,112},{1,113},{2,114},{3,115},{4,116},{5,117},{6,118},{7,119},{8... | collective-permute-start | bytes 884744 | tf_op jit(solution)/shard_map/ppermute | solution.py:19
  114.5 8.8 %collective-permute-start.17 = (f32[3,32,768]{2,1,0:T(8,128)}, f32[3,32,768]{2,1,0:T(8,128)}, u32[]{:S(2)}, u32[]{:S(2)}) collective-permute-start(f32[3,32,768]{2,1,0:T(8,128)} %get-tuple-element.63), channel_id=1, source_target_pairs={{0,16},{1,17},{2,18},{3,19},{4,20},{5,21},{6,22},{7,23},{8,24},{9,... | collective-permute-start | bytes 884744 | tf_op jit(solution)/shard_map/ppermute | solution.py:19
  117.9 10.3 %collective-permute-start.22 = (f32[3,32,768]{2,1,0:T(8,128)S(1)}, f32[3,32,768]{2,1,0:T(8,128)}, u32[]{:S(2)}, u32[]{:S(2)}) collective-permute-start(f32[3,32,768]{2,1,0:T(8,128)S(1)} %get-tuple-element.62), channel_id=1, source_target_pairs={{0,112},{1,113},{2,114},{3,115},{4,116},{5,117},{6,118},{7,119},{8... | collective-permute-start | bytes 884744 | tf_op jit(solution)/shard_map/ppermute | solution.py:19
  121.3 8.1 %collective-permute-start.23 = (f32[3,32,768]{2,1,0:T(8,128)S(1)}, f32[3,32,768]{2,1,0:T(8,128)}, u32[]{:S(2)}, u32[]{:S(2)}) collective-permute-start(f32[3,32,768]{2,1,0:T(8,128)S(1)} %get-tuple-element.61), channel_id=1, source_target_pairs={{0,16},{1,17},{2,18},{3,19},{4,20},{5,21},{6,22},{7,23},{8,24},{9,... | collective-permute-start | bytes 884744 | tf_op jit(solution)/shard_map/ppermute | solution.py:19
  125.3 8.4 %collective-permute-start.20 = (f32[3,32,768]{2,1,0:T(8,128)}, f32[3,32,768]{2,1,0:T(8,128)S(1)}, u32[]{:S(2)}, u32[]{:S(2)}) collective-permute-start(f32[3,32,768]{2,1,0:T(8,128)} %get-tuple-element.60), channel_id=1, source_target_pairs={{0,112},{1,113},{2,114},{3,115},{4,116},{5,117},{6,118},{7,119},{8... | collective-permute-start | bytes 884744 | tf_op jit(solution)/shard_map/ppermute | solution.py:19
  128.1 9.1 %collective-permute-start.21 = (f32[3,32,768]{2,1,0:T(8,128)S(1)}, f32[3,32,768]{2,1,0:T(8,128)}, u32[]{:S(2)}, u32[]{:S(2)}) collective-permute-start(f32[3,32,768]{2,1,0:T(8,128)S(1)} %get-tuple-element.59), channel_id=1, source_target_pairs={{0,16},{1,17},{2,18},{3,19},{4,20},{5,21},{6,22},{7,23},{8,24},{9,... | collective-permute-start | bytes 884744 | tf_op jit(solution)/shard_map/ppermute | solution.py:19
  138.8 6.8 %collective-permute-start.24 = (f32[3,32,768]{2,1,0:T(8,128)S(1)}, f32[3,32,768]{2,1,0:T(8,128)S(1)}, u32[]{:S(2)}, u32[]{:S(2)}) collective-permute-start(f32[3,32,768]{2,1,0:T(8,128)S(1)} %get-tuple-element.57), channel_id=1, source_target_pairs={{0,112},{1,113},{2,114},{3,115},{4,116},{5,117},{6,118},{7,119},{8... | collective-permute-start | bytes 884744 | tf_op jit(solution)/shard_map/ppermute | solution.py:19
  138.9 8.2 %collective-permute-start.25 = (f32[3,32,768]{2,1,0:T(8,128)S(1)}, f32[3,32,768]{2,1,0:T(8,128)S(1)}, u32[]{:S(2)}, u32[]{:S(2)}) collective-permute-start(f32[3,32,768]{2,1,0:T(8,128)S(1)} %get-tuple-element.58), channel_id=1, source_target_pairs={{0,16},{1,17},{2,18},{3,19},{4,20},{5,21},{6,22},{7,23},{8,24},{9,... | collective-permute-start | bytes 884744 | tf_op jit(solution)/shard_map/ppermute | solution.py:19
  156.2 6.5 %collective-permute-start.29 = (f32[3,2,32,128]{3,2,1,0:T(8,128)S(1)}, f32[3,2,32,128]{3,2,1,0:T(8,128)S(1)}, u32[]{:S(2)}, u32[]{:S(2)}) collective-permute-start(f32[3,2,32,128]{3,2,1,0:T(8,128)S(1)} %get-tuple-element.86), channel_id=1, source_target_pairs={{0,8},{1,9},{2,10},{3,11},{4,12},{5,13},{6,14},{7,15},{8,0},{9,1},... | collective-permute-start | bytes 294920 | tf_op jit(solution)/shard_map/ppermute | solution.py:19
  157.7 7.0 %collective-permute-start.30 = (f32[3,2,32,128]{3,2,1,0:T(8,128)S(1)}, f32[3,2,32,128]{3,2,1,0:T(8,128)S(1)}, u32[]{:S(2)}, u32[]{:S(2)}) collective-permute-start(f32[3,2,32,128]{3,2,1,0:T(8,128)S(1)} %get-tuple-element.85), channel_id=1, source_target_pairs={{0,12},{1,13},{2,14},{3,15},{4,8},{5,9},{6,10},{7,11},{8,4},{9,5},... | collective-permute-start | bytes 294920 | tf_op jit(solution)/shard_map/ppermute | solution.py:19
  160.0 4.7 %collective-permute-start.28 = (f32[3,2,32,128]{3,2,1,0:T(8,128)S(1)}, f32[3,2,32,128]{3,2,1,0:T(8,128)S(1)}, u32[]{:S(2)}, u32[]{:S(2)}) collective-permute-start(f32[3,2,32,128]{3,2,1,0:T(8,128)S(1)} %fusion.39), channel_id=1, source_target_pairs={{0,4},{1,5},{2,6},{3,7},{4,0},{5,1},{6,2},{7,3},{8,12},{9,13},{10,... | collective-permute-start | bytes 294920 | tf_op jit(solution)/shard_map/ppermute | solution.py:19
  164.8 5.7 %collective-permute-start.31 = (f32[3,32,128]{2,1,0:T(8,128)S(1)}, f32[3,32,128]{2,1,0:T(8,128)S(1)}, u32[]{:S(2)}, u32[]{:S(2)}) collective-permute-start(f32[3,32,128]{2,1,0:T(8,128)S(1)} %slice_bitcast_fusion.2), channel_id=1, source_target_pairs={{0,2},{1,3},{2,0},{3,1},{4,6},{5,7},{6,4},{7,5},{8,10},{9,11},{10,... | collective-permute-start | bytes 147464 | tf_op jit(solution)/shard_map/ppermute | solution.py:19
  (7 other events, 49.0 us)
Sparse Core Ops, SparseCore 0:
  42.7 43.2 all-gather.2

commit v13 on v12

--- a/solution.py
+++ b/solution.py
@@ -126,10 +126,11 @@
     keep_cols = row_mask(pattern, col, per).astype(jnp.float32)
     own = factor_panel.transpose(0, 2, 1) * keep_rows[:, None, :]
     near, far = send(own, swap), send(own, swap_far)
-    near, far, turned, ancestor = together(near, far, send(own, turned_place), ancestor_inverse)
-    beside = [send(piece, across) for piece in jnp.split(ancestor, (rows * 2 // 3,))]
+    pieces = jnp.split(ancestor_inverse, (rows // 2,))
+    near, far, turned, *pieces = together(near, far, send(own, turned_place), *pieces)
     plane = jnp.stack([near, far], axis=1)
     left, right = send(plane, along_x(1)), send(plane, along_x(3))
+    beside = [send(piece, across) for piece in pieces]
     left, right, beside[0] = together(left, right, beside[0])
     facing = [lax.all_gather(turned, "z", axis=1), None]
     opposite = send(left[:, :1], along_x(1)), send(right[:, 1:], along_x(3))

time: 179 us -> 177 us (0.989)
  waiting for transfers between devices: 74 us -> 72.2 us
  transfers between devices with their start and end apart: 33 -> 33, of which waited for: 25 -> 24; matrix products, arithmetic and copies ran while one was open for 10% -> 11% of each run, Pallas kernels for 0% -> 0%
where the time goes in v13:
time: 177 us; the launch traced here: 176 us
  waiting for transfers between devices  72.2 us (41%)
  starting transfers between devices  55.7 us (31%)
  other arithmetic  14.8 us (8%)
  between operations  14.4 us (8%)
  matrix products  9.59 us (5%)
  local copies, waits for them, and re-layouts  9.31 us (5%)
    ppermute x32, waiting for transfers between devices, send(): return lax.ppermute(value, AXES, pairs(move))  65.7 us
    ppermute x32, starting transfers between devices, send(): return lax.ppermute(value, AXES, pairs(move))  55.7 us
    all_gather x1, waiting for transfers between devices, shards(): facing = [lax.all_gather(turned, 'z', axis=1), None]  6.47 us
    dot_general x2, matrix products, dot_each(): return jnp.einsum('knr,kmr->knm', a, b, preferred_element_type=jnp.float32)  5.11 us
    dot_general x4, matrix products, dot_nt(): return lax.dot_general(a, b, NT, preferred_element_type=jnp.float32)  4.48 us
    add x3, other arithmetic, with_own(): return (below + down, above + up)  4.15 us
  transfers between devices with their start and end apart: 33, of which 24 were waited for; matrix products, arithmetic and copies ran while one was open for 11% of the time, Pallas kernels for 0%

profile of v13, /device:TPU:6, one launch (start us, length us, event | category | flops | bytes accessed | tf_op | source)
XLA Modules:
  0.0 176.0 jit_solution(9741004539084105376)
XLA Ops:
  9.1 3.4 %collective-permute-start = (bf16[3,64,768]{2,1,0:T(8,128)(2,1)S(1)}, bf16[3,64,768]{2,1,0:T(8,128)(2,1)S(1)}, u32[]{:S(2)}, u32[]{:S(2)}) collective-permute-start(bf16[3,64,768]{2,1,0:T(8,128)(2,1)S(1)} %multiply_bitcast_fusion), channel_id=1, source_target_pairs={{0,0},{1,1},{2,2},{3,3},{4,4},{5,5},{6,6},{7,7},{8,132},{9,133},{1... | collective-permute-start | bytes 884744 | tf_op jit(solution)/shard_map/ppermute | solution.py:19
  12.5 4.5 %collective-permute-start.1 = (bf16[3,64,768]{2,1,0:T(8,128)(2,1)S(1)}, bf16[3,64,768]{2,1,0:T(8,128)(2,1)S(1)}, u32[]{:S(2)}, u32[]{:S(2)}) collective-permute-start(bf16[3,64,768]{2,1,0:T(8,128)(2,1)S(1)} %multiply_bitcast_fusion), channel_id=1, source_target_pairs={{0,2},{1,3},{2,0},{3,1},{4,6},{5,7},{6,4},{7,5},{8,134},{9,135},{1... | collective-permute-start | bytes 884744 | tf_op jit(solution)/shard_map/ppermute | solution.py:19
  17.0 9.1 %collective-permute-start.2 = (bf16[3,64,768]{2,1,0:T(8,128)(2,1)S(1)}, bf16[3,64,768]{2,1,0:T(8,128)(2,1)S(1)}, u32[]{:S(2)}, u32[]{:S(2)}) collective-permute-start(bf16[3,64,768]{2,1,0:T(8,128)(2,1)S(1)} %multiply_bitcast_fusion), channel_id=1, source_target_pairs={{0,0},{1,16},{2,32},{3,48},{4,64},{5,80},{6,96},{7,112},{8,128},{9... | collective-permute-start | bytes 884744 | tf_op jit(solution)/shard_map/ppermute | solution.py:19
  26.1 2.3 %fusion.46 = (bf16[384,768]{1,0:T(8,128)(2,1)}, bf16[384,768]{1,0:T(8,128)(2,1)}) fusion(bf16[768,768]{1,0:T(8,128)(2,1)} %param.4), kind=kLoop, calls=%fused_computation.114 | loop fusion | bytes 2359296 | tf_op jit(solution)/shard_map/split | solution.py:129
  28.5 7.8 %collective-permute-done.1 = bf16[3,64,768]{2,1,0:T(8,128)(2,1)S(1)} collective-permute-done((bf16[3,64,768]{2,1,0:T(8,128)(2,1)S(1)}, bf16[3,64,768]{2,1,0:T(8,128)(2,1)S(1)}, u32[]{:S(2)}, u32[]{:S(2)}) %collective-permute-start.1) | collective-permute-done | bytes 294944 | tf_op jit(solution)/shard_map/ppermute | solution.py:19
  36.3 1.9 %collective-permute-done.2 = bf16[3,64,768]{2,1,0:T(8,128)(2,1)S(1)} collective-permute-done((bf16[3,64,768]{2,1,0:T(8,128)(2,1)S(1)}, bf16[3,64,768]{2,1,0:T(8,128)(2,1)S(1)}, u32[]{:S(2)}, u32[]{:S(2)}) %collective-permute-start.2) | collective-permute-done | bytes 294944 | tf_op jit(solution)/shard_map/ppermute | solution.py:19
  38.4 2.0 %collective-permute-start.4 = (bf16[3,2,64,768]{3,2,1,0:T(8,128)(2,1)S(1)}, bf16[3,2,64,768]{3,2,1,0:T(8,128)(2,1)S(1)}, u32[]{:S(2)}, u32[]{:S(2)}) collective-permute-start(bf16[3,2,64,768]{3,2,1,0:T(8,128)(2,1)S(1)} %pad_maximum_fusion.4), channel_id=1, source_target_pairs={{0,12},{1,13},{2,14},{3,15},{4,0},{5,1},{6,2},{7,3},{8,4},{9,5},{1... | collective-permute-start | bytes 1769480 | tf_op jit(solution)/shard_map/ppermute | solution.py:19
  40.4 2.1 %collective-permute-start.8 = (bf16[384,768]{1,0:T(8,128)(2,1)}, bf16[384,768]{1,0:T(8,128)(2,1)S(1)}, u32[]{:S(2)}, u32[]{:S(2)}) collective-permute-start(bf16[384,768]{1,0:T(8,128)(2,1)} %get-tuple-element.35), channel_id=1, source_target_pairs={{0,128},{1,129},{2,130},{3,131},{4,132},{5,133},{6,134},{7,135},{8... | collective-permute-start | bytes 1769480 | tf_op jit(solution)/shard_map/ppermute | solution.py:19
  42.6 11.8 %collective-permute-done.3 = bf16[3,2,64,768]{3,2,1,0:T(8,128)(2,1)S(1)} collective-permute-done((bf16[3,2,64,768]{3,2,1,0:T(8,128)(2,1)S(1)}, bf16[3,2,64,768]{3,2,1,0:T(8,128)(2,1)S(1)}, u32[]{:S(2)}, u32[]{:S(2)}) %collective-permute-start.3) | collective-permute-done | bytes 589856 | tf_op jit(solution)/shard_map/ppermute | solution.py:19
  60.4 8.3 %collective-permute-done.8 = bf16[384,768]{1,0:T(8,128)(2,1)S(1)} collective-permute-done((bf16[384,768]{1,0:T(8,128)(2,1)}, bf16[384,768]{1,0:T(8,128)(2,1)S(1)}, u32[]{:S(2)}, u32[]{:S(2)}) %collective-permute-start.8) | collective-permute-done | bytes 589856 | tf_op jit(solution)/shard_map/ppermute | solution.py:19
  77.3 6.5 %all-gather.3.cloned.1.call-done = bf16[3,512,768]{2,1,0:T(8,128)(2,1)} async-done(((bf16[3,64,768]{2,1,0:T(8,128)(2,1)}), bf16[3,512,768]{2,1,0:T(8,128)(2,1)}) %all-gather.3.cloned.1.call-update) | async-done | bytes 2359312 | tf_op jit(solution)/shard_map/all_gather | solution.py:135
  88.4 2.4 %collective-permute-start.10 = (f32[3,16,768]{2,1,0:T(8,128)S(1)}, f32[3,16,768]{2,1,0:T(8,128)S(1)}, u32[]{:S(2)}, u32[]{:S(2)}) collective-permute-start(f32[3,16,768]{2,1,0:T(8,128)S(1)} %get-tuple-element.107), channel_id=1, source_target_pairs={{0,112},{1,113},{2,114},{3,115},{4,116},{5,117},{6,118},{7,119},{8... | collective-permute-start | bytes 442376 | tf_op jit(solution)/shard_map/ppermute | solution.py:19
  90.8 3.3 %collective-permute-start.14 = (f32[3,16,768]{2,1,0:T(8,128)S(1)}, f32[3,16,768]{2,1,0:T(8,128)S(1)}, u32[]{:S(2)}, u32[]{:S(2)}) collective-permute-start(f32[3,16,768]{2,1,0:T(8,128)S(1)} %get-tuple-element.109), channel_id=1, source_target_pairs={{0,112},{1,113},{2,114},{3,115},{4,116},{5,117},{6,118},{7,119},{8... | collective-permute-start | bytes 442376 | tf_op jit(solution)/shard_map/ppermute | solution.py:19
  95.6 2.6 %collective-permute-done.11 = f32[3,16,768]{2,1,0:T(8,128)S(1)} collective-permute-done((f32[3,16,768]{2,1,0:T(8,128)S(1)}, f32[3,16,768]{2,1,0:T(8,128)S(1)}, u32[]{:S(2)}, u32[]{:S(2)}) %collective-permute-start.11) | collective-permute-done | bytes 147488 | tf_op jit(solution)/shard_map/ppermute | solution.py:19
  98.5 3.3 %collective-permute-start.12 = (f32[3,32,768]{2,1,0:T(8,128)S(1)}, f32[3,32,768]{2,1,0:T(8,128)S(1)}, u32[]{:S(2)}, u32[]{:S(2)}) collective-permute-start(f32[3,32,768]{2,1,0:T(8,128)S(1)} %pad_maximum_fusion.7), channel_id=1, source_target_pairs={{0,112},{1,113},{2,114},{3,115},{4,116},{5,117},{6,118},{7,119},{8... | collective-permute-start | bytes 884744 | tf_op jit(solution)/shard_map/ppermute | solution.py:19
  102.4 3.3 %collective-permute-start.18 = (f32[3,32,768]{2,1,0:T(8,128)S(1)}, f32[3,32,768]{2,1,0:T(8,128)}, u32[]{:S(2)}, u32[]{:S(2)}) collective-permute-start(f32[3,32,768]{2,1,0:T(8,128)S(1)} %pad_maximum_fusion.9), channel_id=1, source_target_pairs={{0,112},{1,113},{2,114},{3,115},{4,116},{5,117},{6,118},{7,119},{8... | collective-permute-start | bytes 884744 | tf_op jit(solution)/shard_map/ppermute | solution.py:19
  105.7 2.6 %collective-permute-done.13 = f32[3,32,768]{2,1,0:T(8,128)S(1)} collective-permute-done((f32[3,32,768]{2,1,0:T(8,128)S(1)}, f32[3,32,768]{2,1,0:T(8,128)S(1)}, u32[]{:S(2)}, u32[]{:S(2)}) %collective-permute-start.13) | collective-permute-done | bytes 294944 | tf_op jit(solution)/shard_map/ppermute | solution.py:19
  109.2 3.2 %collective-permute-start.16 = (f32[3,32,768]{2,1,0:T(8,128)}, f32[3,32,768]{2,1,0:T(8,128)S(1)}, u32[]{:S(2)}, u32[]{:S(2)}) collective-permute-start(f32[3,32,768]{2,1,0:T(8,128)} %get-tuple-element.66), channel_id=1, source_target_pairs={{0,112},{1,113},{2,114},{3,115},{4,116},{5,117},{6,118},{7,119},{8... | collective-permute-start | bytes 884744 | tf_op jit(solution)/shard_map/ppermute | solution.py:19
  112.4 2.1 %collective-permute-done.19 = f32[3,32,768]{2,1,0:T(8,128)S(1)} collective-permute-done((f32[3,32,768]{2,1,0:T(8,128)S(1)}, f32[3,32,768]{2,1,0:T(8,128)S(1)}, u32[]{:S(2)}, u32[]{:S(2)}) %collective-permute-start.19) | collective-permute-done | bytes 294944 | tf_op jit(solution)/shard_map/ppermute | solution.py:19
  115.8 3.4 %collective-permute-start.22 = (f32[3,32,768]{2,1,0:T(8,128)S(1)}, f32[3,32,768]{2,1,0:T(8,128)}, u32[]{:S(2)}, u32[]{:S(2)}) collective-permute-start(f32[3,32,768]{2,1,0:T(8,128)S(1)} %get-tuple-element.64), channel_id=1, source_target_pairs={{0,112},{1,113},{2,114},{3,115},{4,116},{5,117},{6,118},{7,119},{8... | collective-permute-start | bytes 884744 | tf_op jit(solution)/shard_map/ppermute | solution.py:19
  121.2 1.9 %fusion.12 = (f32[3,32,768]{2,1,0:T(8,128)S(1)}, f32[3,32,768]{2,1,0:T(8,128)}) fusion(f32[3,32,768]{2,1,0:T(8,128)} %collective-permute-done.17, f32[3,4,64,768]{3,2,1,0:T(8,128)} %bitcast.276, s32[]{:T(128)S(6)} %select_n.508, f32[3,4,64,768]{3,2,1,0:T(8,128)S(1)} %bitcast.270, pred[]{:T(512)S(6)} %eq.108, f32[3,32,768]{2,1,0:T(8,128)S(1)} %collective-permute-done.16, ...), kind=kLoop, calls=%fused_computation.43 | loop fusion | flops 294912 | bytes 2359306 | tf_op jit(solution)/shard_map/add | solution.py:98
  123.2 2.9 %collective-permute-start.20 = (f32[3,32,768]{2,1,0:T(8,128)}, f32[3,32,768]{2,1,0:T(8,128)S(1)}, u32[]{:S(2)}, u32[]{:S(2)}) collective-permute-start(f32[3,32,768]{2,1,0:T(8,128)} %get-tuple-element.62), channel_id=1, source_target_pairs={{0,112},{1,113},{2,114},{3,115},{4,116},{5,117},{6,118},{7,119},{8... | collective-permute-start | bytes 884744 | tf_op jit(solution)/shard_map/ppermute | solution.py:19
  127.3 4.2 %collective-permute-done.20 = f32[3,32,768]{2,1,0:T(8,128)S(1)} collective-permute-done((f32[3,32,768]{2,1,0:T(8,128)}, f32[3,32,768]{2,1,0:T(8,128)S(1)}, u32[]{:S(2)}, u32[]{:S(2)}) %collective-permute-start.20) | collective-permute-done | bytes 294944 | tf_op jit(solution)/shard_map/ppermute | solution.py:19
  131.5 3.6 %collective-permute-done.21 = f32[3,32,768]{2,1,0:T(8,128)} collective-permute-done((f32[3,32,768]{2,1,0:T(8,128)S(1)}, f32[3,32,768]{2,1,0:T(8,128)}, u32[]{:S(2)}, u32[]{:S(2)}) %collective-permute-start.21) | collective-permute-done | bytes 294944 | tf_op jit(solution)/shard_map/ppermute | solution.py:19
  136.8 2.0 %collective-permute-start.25 = (f32[3,32,768]{2,1,0:T(8,128)S(1)}, f32[3,32,768]{2,1,0:T(8,128)S(1)}, u32[]{:S(2)}, u32[]{:S(2)}) collective-permute-start(f32[3,32,768]{2,1,0:T(8,128)S(1)} %get-tuple-element.60), channel_id=1, source_target_pairs={{0,16},{1,17},{2,18},{3,19},{4,20},{5,21},{6,22},{7,23},{8,24},{9,... | collective-permute-start | bytes 884744 | tf_op jit(solution)/shard_map/ppermute | solution.py:19
  138.8 4.7 %collective-permute-done.24 = f32[3,32,768]{2,1,0:T(8,128)S(1)} collective-permute-done((f32[3,32,768]{2,1,0:T(8,128)S(1)}, f32[3,32,768]{2,1,0:T(8,128)S(1)}, u32[]{:S(2)}, u32[]{:S(2)}) %collective-permute-start.24) | collective-permute-done | bytes 294944 | tf_op jit(solution)/shard_map/ppermute | solution.py:19
  146.2 2.6 %fusion.56 = f32[3,512,128]{1,2,0:T(8,128)S(1)} fusion(bf16[3,512,768]{2,1,0:T(8,128)(2,1)} %bitcast.37, bf16[3,128,768]{2,1,0:T(8,128)(2,1)S(1)} %bitcast.279), kind=kOutput, calls=%fused_computation.124 | convolution fusion | flops 301989888 | bytes 3735552 | tf_op jit(solution)/shard_map/knr,kmr->knm/dot_general | solution.py:85
  148.8 2.6 %fusion.57 = f32[3,512,128]{1,2,0:T(8,128)S(1)} fusion(bf16[3,512,768]{2,1,0:T(8,128)(2,1)} %bitcast.41, bf16[3,128,768]{2,1,0:T(8,128)(2,1)S(1)} %bitcast.280), kind=kOutput, calls=%fused_computation.125 | convolution fusion | flops 301989888 | bytes 3735552 | tf_op jit(solution)/shard_map/knr,kmr->knm/dot_general | solution.py:85
  155.6 2.1 %collective-permute-start.30 = (f32[3,2,32,128]{3,2,1,0:T(8,128)S(1)}, f32[3,2,32,128]{3,2,1,0:T(8,128)S(1)}, u32[]{:S(2)}, u32[]{:S(2)}) collective-permute-start(f32[3,2,32,128]{3,2,1,0:T(8,128)S(1)} %get-tuple-element.89), channel_id=1, source_target_pairs={{0,12},{1,13},{2,14},{3,15},{4,8},{5,9},{6,10},{7,11},{8,4},{9,5},... | collective-permute-start | bytes 294920 | tf_op jit(solution)/shard_map/ppermute | solution.py:19
  158.0 2.5 %collective-permute-done.29 = f32[3,2,32,128]{3,2,1,0:T(8,128)S(1)} collective-permute-done((f32[3,2,32,128]{3,2,1,0:T(8,128)S(1)}, f32[3,2,32,128]{3,2,1,0:T(8,128)S(1)}, u32[]{:S(2)}, u32[]{:S(2)}) %collective-permute-start.29) | collective-permute-done | bytes 98336 | tf_op jit(solution)/shard_map/ppermute | solution.py:19
  160.6 2.0 %collective-permute-done.30 = f32[3,2,32,128]{3,2,1,0:T(8,128)S(1)} collective-permute-done((f32[3,2,32,128]{3,2,1,0:T(8,128)S(1)}, f32[3,2,32,128]{3,2,1,0:T(8,128)S(1)}, u32[]{:S(2)}, u32[]{:S(2)}) %collective-permute-start.30) | collective-permute-done | bytes 98336 | tf_op jit(solution)/shard_map/ppermute | solution.py:19
  162.7 3.1 %collective-permute-start.31 = (f32[3,32,128]{2,1,0:T(8,128)S(1)}, f32[3,32,128]{2,1,0:T(8,128)S(1)}, u32[]{:S(2)}, u32[]{:S(2)}) collective-permute-start(f32[3,32,128]{2,1,0:T(8,128)S(1)} %slice_bitcast_fusion.2), channel_id=1, source_target_pairs={{0,2},{1,3},{2,0},{3,1},{4,6},{5,7},{6,4},{7,5},{8,10},{9,11},{10,... | collective-permute-start | bytes 147464 | tf_op jit(solution)/shard_map/ppermute | solution.py:19
  (112 shorter events, 41.4 us)
Async XLA Ops:
  7.2 76.6 %all-gather.3.cloned.1.call-start = ((), (), s32[]{:S(2)}) async-start(), calls=%async_computation | async-start | bytes 2654208 | tf_op jit(solution)/shard_map/all_gather | solution.py:135
  9.1 19.3 %collective-permute-start = (bf16[3,64,768]{2,1,0:T(8,128)(2,1)S(1)}, bf16[3,64,768]{2,1,0:T(8,128)(2,1)S(1)}, u32[]{:S(2)}, u32[]{:S(2)}) collective-permute-start(bf16[3,64,768]{2,1,0:T(8,128)(2,1)S(1)} %multiply_bitcast_fusion), channel_id=1, source_target_pairs={{0,0},{1,1},{2,2},{3,3},{4,4},{5,5},{6,6},{7,7},{8,132},{9,133},{1... | collective-permute-start | bytes 884744 | tf_op jit(solution)/shard_map/ppermute | solution.py:19
  12.5 23.8 %collective-permute-start.1 = (bf16[3,64,768]{2,1,0:T(8,128)(2,1)S(1)}, bf16[3,64,768]{2,1,0:T(8,128)(2,1)S(1)}, u32[]{:S(2)}, u32[]{:S(2)}) collective-permute-start(bf16[3,64,768]{2,1,0:T(8,128)(2,1)S(1)} %multiply_bitcast_fusion), channel_id=1, source_target_pairs={{0,2},{1,3},{2,0},{3,1},{4,6},{5,7},{6,4},{7,5},{8,134},{9,135},{1... | collective-permute-start | bytes 884744 | tf_op jit(solution)/shard_map/ppermute | solution.py:19
  17.0 21.2 %collective-permute-start.2 = (bf16[3,64,768]{2,1,0:T(8,128)(2,1)S(1)}, bf16[3,64,768]{2,1,0:T(8,128)(2,1)S(1)}, u32[]{:S(2)}, u32[]{:S(2)}) collective-permute-start(bf16[3,64,768]{2,1,0:T(8,128)(2,1)S(1)} %multiply_bitcast_fusion), channel_id=1, source_target_pairs={{0,0},{1,16},{2,32},{3,48},{4,64},{5,80},{6,96},{7,112},{8,128},{9... | collective-permute-start | bytes 884744 | tf_op jit(solution)/shard_map/ppermute | solution.py:19
  38.3 16.0 %collective-permute-start.3 = (bf16[3,2,64,768]{3,2,1,0:T(8,128)(2,1)S(1)}, bf16[3,2,64,768]{3,2,1,0:T(8,128)(2,1)S(1)}, u32[]{:S(2)}, u32[]{:S(2)}) collective-permute-start(bf16[3,2,64,768]{3,2,1,0:T(8,128)(2,1)S(1)} %pad_maximum_fusion.4), channel_id=1, source_target_pairs={{0,4},{1,5},{2,6},{3,7},{4,8},{5,9},{6,10},{7,11},{8,12},{9,13},{1... | collective-permute-start | bytes 1769480 | tf_op jit(solution)/shard_map/ppermute | solution.py:19
  38.4 17.2 %collective-permute-start.4 = (bf16[3,2,64,768]{3,2,1,0:T(8,128)(2,1)S(1)}, bf16[3,2,64,768]{3,2,1,0:T(8,128)(2,1)S(1)}, u32[]{:S(2)}, u32[]{:S(2)}) collective-permute-start(bf16[3,2,64,768]{3,2,1,0:T(8,128)(2,1)S(1)} %pad_maximum_fusion.4), channel_id=1, source_target_pairs={{0,12},{1,13},{2,14},{3,15},{4,0},{5,1},{6,2},{7,3},{8,4},{9,5},{1... | collective-permute-start | bytes 1769480 | tf_op jit(solution)/shard_map/ppermute | solution.py:19
  40.4 16.4 %collective-permute-start.5 = (bf16[384,768]{1,0:T(8,128)(2,1)}, bf16[384,768]{1,0:T(8,128)(2,1)S(1)}, u32[]{:S(2)}, u32[]{:S(2)}) collective-permute-start(bf16[384,768]{1,0:T(8,128)(2,1)} %get-tuple-element.32), channel_id=1, source_target_pairs={{0,128},{1,129},{2,130},{3,131},{4,132},{5,133},{6,134},{7,135},{8... | collective-permute-start | bytes 1769480 | tf_op jit(solution)/shard_map/ppermute | solution.py:19
  40.4 28.2 %collective-permute-start.8 = (bf16[384,768]{1,0:T(8,128)(2,1)}, bf16[384,768]{1,0:T(8,128)(2,1)S(1)}, u32[]{:S(2)}, u32[]{:S(2)}) collective-permute-start(bf16[384,768]{1,0:T(8,128)(2,1)} %get-tuple-element.35), channel_id=1, source_target_pairs={{0,128},{1,129},{2,130},{3,131},{4,132},{5,133},{6,134},{7,135},{8... | collective-permute-start | bytes 1769480 | tf_op jit(solution)/shard_map/ppermute | solution.py:19
  57.6 11.1 %collective-permute-start.6 = (bf16[3,1,64,768]{3,2,1,0:T(8,128)(2,1)}, bf16[3,1,64,768]{3,2,1,0:T(8,128)(2,1)S(1)}, u32[]{:S(2)}, u32[]{:S(2)}) collective-permute-start(bf16[3,1,64,768]{3,2,1,0:T(8,128)(2,1)} %slice.114), channel_id=1, source_target_pairs={{0,4},{1,5},{2,6},{3,7},{4,8},{5,9},{6,10},{7,11},{8,12},{9,13},{1... | collective-permute-start | bytes 884744 | tf_op jit(solution)/shard_map/ppermute | solution.py:19
  59.6 9.3 %collective-permute-start.7 = (bf16[3,1,64,768]{3,2,1,0:T(8,128)(2,1)}, bf16[3,1,64,768]{3,2,1,0:T(8,128)(2,1)S(1)}, u32[]{:S(2)}, u32[]{:S(2)}) collective-permute-start(bf16[3,1,64,768]{3,2,1,0:T(8,128)(2,1)} %slice.115), channel_id=1, source_target_pairs={{0,12},{1,13},{2,14},{3,15},{4,0},{5,1},{6,2},{7,3},{8,4},{9,5},{1... | collective-permute-start | bytes 884744 | tf_op jit(solution)/shard_map/ppermute | solution.py:19
  72.5 4.9 %collective-permute-start.9 = (bf16[2,3,2,2,64,768]{5,4,3,2,1,0:T(8,128)(2,1)}, bf16[2,3,2,2,64,768]{5,4,3,2,1,0:T(8,128)(2,1)}, u32[]{:S(2)}, u32[]{:S(2)}) collective-permute-start(bf16[2,3,2,2,64,768]{5,4,3,2,1,0:T(8,128)(2,1)} %pad_maximum_fusion), channel_id=1, source_target_pairs={{0,1},{1,0},{2,3},{3,2},{4,5},{5,4},{6,7},{7,6},{8,9},{9,8},{10,11... | collective-permute-start | bytes 7077896 | tf_op jit(solution)/shard_map/ppermute | solution.py:19
  88.4 7.2 %collective-permute-start.10 = (f32[3,16,768]{2,1,0:T(8,128)S(1)}, f32[3,16,768]{2,1,0:T(8,128)S(1)}, u32[]{:S(2)}, u32[]{:S(2)}) collective-permute-start(f32[3,16,768]{2,1,0:T(8,128)S(1)} %get-tuple-element.107), channel_id=1, source_target_pairs={{0,112},{1,113},{2,114},{3,115},{4,116},{5,117},{6,118},{7,119},{8... | collective-permute-start | bytes 442376 | tf_op jit(solution)/shard_map/ppermute | solution.py:19
  90.8 7.5 %collective-permute-start.11 = (f32[3,16,768]{2,1,0:T(8,128)S(1)}, f32[3,16,768]{2,1,0:T(8,128)S(1)}, u32[]{:S(2)}, u32[]{:S(2)}) collective-permute-start(f32[3,16,768]{2,1,0:T(8,128)S(1)} %get-tuple-element.106), channel_id=1, source_target_pairs={{0,16},{1,17},{2,18},{3,19},{4,20},{5,21},{6,22},{7,23},{8,24},{9,... | collective-permute-start | bytes 442376 | tf_op jit(solution)/shard_map/ppermute | solution.py:19
  90.8 11.0 %collective-permute-start.14 = (f32[3,16,768]{2,1,0:T(8,128)S(1)}, f32[3,16,768]{2,1,0:T(8,128)S(1)}, u32[]{:S(2)}, u32[]{:S(2)}) collective-permute-start(f32[3,16,768]{2,1,0:T(8,128)S(1)} %get-tuple-element.109), channel_id=1, source_target_pairs={{0,112},{1,113},{2,114},{3,115},{4,116},{5,117},{6,118},{7,119},{8... | collective-permute-start | bytes 442376 | tf_op jit(solution)/shard_map/ppermute | solution.py:19
  94.1 8.0 %collective-permute-start.15 = (f32[3,16,768]{2,1,0:T(8,128)S(1)}, f32[3,16,768]{2,1,0:T(8,128)S(1)}, u32[]{:S(2)}, u32[]{:S(2)}) collective-permute-start(f32[3,16,768]{2,1,0:T(8,128)S(1)} %get-tuple-element.108), channel_id=1, source_target_pairs={{0,16},{1,17},{2,18},{3,19},{4,20},{5,21},{6,22},{7,23},{8,24},{9,... | collective-permute-start | bytes 442376 | tf_op jit(solution)/shard_map/ppermute | solution.py:19
  94.2 50.8 %collective-permute-start.26 = (bf16[3,8,64,768]{3,2,1,0:T(8,128)(2,1)}, bf16[3,8,64,768]{3,2,1,0:T(8,128)(2,1)}, u32[]{:S(2)}, u32[]{:S(2)}) collective-permute-start(bf16[3,8,64,768]{3,2,1,0:T(8,128)(2,1)} %bitcast.16), channel_id=1, source_target_pairs={{0,128},{1,129},{2,130},{3,131},{4,132},{5,133},{6,134},{7,135},{8... | collective-permute-start | bytes 7077896 | tf_op jit(solution)/shard_map/ppermute | solution.py:19
  98.4 9.9 %collective-permute-start.13 = (f32[3,32,768]{2,1,0:T(8,128)S(1)}, f32[3,32,768]{2,1,0:T(8,128)S(1)}, u32[]{:S(2)}, u32[]{:S(2)}) collective-permute-start(f32[3,32,768]{2,1,0:T(8,128)S(1)} %pad_maximum_fusion.8), channel_id=1, source_target_pairs={{0,16},{1,17},{2,18},{3,19},{4,20},{5,21},{6,22},{7,23},{8,24},{9,... | collective-permute-start | bytes 884744 | tf_op jit(solution)/shard_map/ppermute | solution.py:19
  98.5 9.7 %collective-permute-start.12 = (f32[3,32,768]{2,1,0:T(8,128)S(1)}, f32[3,32,768]{2,1,0:T(8,128)S(1)}, u32[]{:S(2)}, u32[]{:S(2)}) collective-permute-start(f32[3,32,768]{2,1,0:T(8,128)S(1)} %pad_maximum_fusion.7), channel_id=1, source_target_pairs={{0,112},{1,113},{2,114},{3,115},{4,116},{5,117},{6,118},{7,119},{8... | collective-permute-start | bytes 884744 | tf_op jit(solution)/shard_map/ppermute | solution.py:19
  102.2 12.3 %collective-permute-start.19 = (f32[3,32,768]{2,1,0:T(8,128)S(1)}, f32[3,32,768]{2,1,0:T(8,128)S(1)}, u32[]{:S(2)}, u32[]{:S(2)}) collective-permute-start(f32[3,32,768]{2,1,0:T(8,128)S(1)} %pad_maximum_fusion.10), channel_id=1, source_target_pairs={{0,16},{1,17},{2,18},{3,19},{4,20},{5,21},{6,22},{7,23},{8,24},{9,... | collective-permute-start | bytes 884744 | tf_op jit(solution)/shard_map/ppermute | solution.py:19
  102.4 12.2 %collective-permute-start.18 = (f32[3,32,768]{2,1,0:T(8,128)S(1)}, f32[3,32,768]{2,1,0:T(8,128)}, u32[]{:S(2)}, u32[]{:S(2)}) collective-permute-start(f32[3,32,768]{2,1,0:T(8,128)S(1)} %pad_maximum_fusion.9), channel_id=1, source_target_pairs={{0,112},{1,113},{2,114},{3,115},{4,116},{5,117},{6,118},{7,119},{8... | collective-permute-start | bytes 884744 | tf_op jit(solution)/shard_map/ppermute | solution.py:19
  109.2 11.3 %collective-permute-start.16 = (f32[3,32,768]{2,1,0:T(8,128)}, f32[3,32,768]{2,1,0:T(8,128)S(1)}, u32[]{:S(2)}, u32[]{:S(2)}) collective-permute-start(f32[3,32,768]{2,1,0:T(8,128)} %get-tuple-element.66), channel_id=1, source_target_pairs={{0,112},{1,113},{2,114},{3,115},{4,116},{5,117},{6,118},{7,119},{8... | collective-permute-start | bytes 884744 | tf_op jit(solution)/shard_map/ppermute | solution.py:19
  112.4 8.8 %collective-permute-start.17 = (f32[3,32,768]{2,1,0:T(8,128)}, f32[3,32,768]{2,1,0:T(8,128)}, u32[]{:S(2)}, u32[]{:S(2)}) collective-permute-start(f32[3,32,768]{2,1,0:T(8,128)} %get-tuple-element.65), channel_id=1, source_target_pairs={{0,16},{1,17},{2,18},{3,19},{4,20},{5,21},{6,22},{7,23},{8,24},{9,... | collective-permute-start | bytes 884744 | tf_op jit(solution)/shard_map/ppermute | solution.py:19
  115.8 10.3 %collective-permute-start.22 = (f32[3,32,768]{2,1,0:T(8,128)S(1)}, f32[3,32,768]{2,1,0:T(8,128)}, u32[]{:S(2)}, u32[]{:S(2)}) collective-permute-start(f32[3,32,768]{2,1,0:T(8,128)S(1)} %get-tuple-element.64), channel_id=1, source_target_pairs={{0,112},{1,113},{2,114},{3,115},{4,116},{5,117},{6,118},{7,119},{8... | collective-permute-start | bytes 884744 | tf_op jit(solution)/shard_map/ppermute | solution.py:19
  119.2 8.1 %collective-permute-start.23 = (f32[3,32,768]{2,1,0:T(8,128)S(1)}, f32[3,32,768]{2,1,0:T(8,128)}, u32[]{:S(2)}, u32[]{:S(2)}) collective-permute-start(f32[3,32,768]{2,1,0:T(8,128)S(1)} %get-tuple-element.63), channel_id=1, source_target_pairs={{0,16},{1,17},{2,18},{3,19},{4,20},{5,21},{6,22},{7,23},{8,24},{9,... | collective-permute-start | bytes 884744 | tf_op jit(solution)/shard_map/ppermute | solution.py:19
  123.2 8.4 %collective-permute-start.20 = (f32[3,32,768]{2,1,0:T(8,128)}, f32[3,32,768]{2,1,0:T(8,128)S(1)}, u32[]{:S(2)}, u32[]{:S(2)}) collective-permute-start(f32[3,32,768]{2,1,0:T(8,128)} %get-tuple-element.62), channel_id=1, source_target_pairs={{0,112},{1,113},{2,114},{3,115},{4,116},{5,117},{6,118},{7,119},{8... | collective-permute-start | bytes 884744 | tf_op jit(solution)/shard_map/ppermute | solution.py:19
  126.0 9.0 %collective-permute-start.21 = (f32[3,32,768]{2,1,0:T(8,128)S(1)}, f32[3,32,768]{2,1,0:T(8,128)}, u32[]{:S(2)}, u32[]{:S(2)}) collective-permute-start(f32[3,32,768]{2,1,0:T(8,128)S(1)} %get-tuple-element.61), channel_id=1, source_target_pairs={{0,16},{1,17},{2,18},{3,19},{4,20},{5,21},{6,22},{7,23},{8,24},{9,... | collective-permute-start | bytes 884744 | tf_op jit(solution)/shard_map/ppermute | solution.py:19
  136.7 6.8 %collective-permute-start.24 = (f32[3,32,768]{2,1,0:T(8,128)S(1)}, f32[3,32,768]{2,1,0:T(8,128)S(1)}, u32[]{:S(2)}, u32[]{:S(2)}) collective-permute-start(f32[3,32,768]{2,1,0:T(8,128)S(1)} %get-tuple-element.59), channel_id=1, source_target_pairs={{0,112},{1,113},{2,114},{3,115},{4,116},{5,117},{6,118},{7,119},{8... | collective-permute-start | bytes 884744 | tf_op jit(solution)/shard_map/ppermute | solution.py:19
  136.8 8.2 %collective-permute-start.25 = (f32[3,32,768]{2,1,0:T(8,128)S(1)}, f32[3,32,768]{2,1,0:T(8,128)S(1)}, u32[]{:S(2)}, u32[]{:S(2)}) collective-permute-start(f32[3,32,768]{2,1,0:T(8,128)S(1)} %get-tuple-element.60), channel_id=1, source_target_pairs={{0,16},{1,17},{2,18},{3,19},{4,20},{5,21},{6,22},{7,23},{8,24},{9,... | collective-permute-start | bytes 884744 | tf_op jit(solution)/shard_map/ppermute | solution.py:19
  154.1 6.5 %collective-permute-start.29 = (f32[3,2,32,128]{3,2,1,0:T(8,128)S(1)}, f32[3,2,32,128]{3,2,1,0:T(8,128)S(1)}, u32[]{:S(2)}, u32[]{:S(2)}) collective-permute-start(f32[3,2,32,128]{3,2,1,0:T(8,128)S(1)} %get-tuple-element.90), channel_id=1, source_target_pairs={{0,8},{1,9},{2,10},{3,11},{4,12},{5,13},{6,14},{7,15},{8,0},{9,1},... | collective-permute-start | bytes 294920 | tf_op jit(solution)/shard_map/ppermute | solution.py:19
  155.6 7.0 %collective-permute-start.30 = (f32[3,2,32,128]{3,2,1,0:T(8,128)S(1)}, f32[3,2,32,128]{3,2,1,0:T(8,128)S(1)}, u32[]{:S(2)}, u32[]{:S(2)}) collective-permute-start(f32[3,2,32,128]{3,2,1,0:T(8,128)S(1)} %get-tuple-element.89), channel_id=1, source_target_pairs={{0,12},{1,13},{2,14},{3,15},{4,8},{5,9},{6,10},{7,11},{8,4},{9,5},... | collective-permute-start | bytes 294920 | tf_op jit(solution)/shard_map/ppermute | solution.py:19
  157.9 4.7 %collective-permute-start.28 = (f32[3,2,32,128]{3,2,1,0:T(8,128)S(1)}, f32[3,2,32,128]{3,2,1,0:T(8,128)S(1)}, u32[]{:S(2)}, u32[]{:S(2)}) collective-permute-start(f32[3,2,32,128]{3,2,1,0:T(8,128)S(1)} %fusion.39), channel_id=1, source_target_pairs={{0,4},{1,5},{2,6},{3,7},{4,0},{5,1},{6,2},{7,3},{8,12},{9,13},{10,... | collective-permute-start | bytes 294920 | tf_op jit(solution)/shard_map/ppermute | solution.py:19
  162.7 5.7 %collective-permute-start.31 = (f32[3,32,128]{2,1,0:T(8,128)S(1)}, f32[3,32,128]{2,1,0:T(8,128)S(1)}, u32[]{:S(2)}, u32[]{:S(2)}) collective-permute-start(f32[3,32,128]{2,1,0:T(8,128)S(1)} %slice_bitcast_fusion.2), channel_id=1, source_target_pairs={{0,2},{1,3},{2,0},{3,1},{4,6},{5,7},{6,4},{7,5},{8,10},{9,11},{10,... | collective-permute-start | bytes 147464 | tf_op jit(solution)/shard_map/ppermute | solution.py:19
  (9 other events, 53.2 us)
Sparse Core Ops, SparseCore 0:
  40.6 43.2 all-gather.2

commit v14 on v13

--- a/solution.py
+++ b/solution.py
@@ -60,8 +60,8 @@
     return yl, z, x, 1 - yh, c
 
 
-def flip_x(bits):
-    return lambda yl, z, x, yh, c: (yl, z, x ^ bits, yh, c)
+def flip_plane(bits, bit):
+    return lambda yl, z, x, yh, c: (yl, z, x ^ bits, yh ^ bit, c)
 
 
 def row_mask(pattern, block, per):
@@ -171,9 +171,10 @@
     tiles = tiles[:, :, :, 0] + send(tiles[:, :, :, 1], sibling)
     kept, given = ordered((x // 2) == yl, tiles[..., :cols], tiles[..., cols:])
     kept, given = (jnp.concatenate([t[:, :, :, :wide], t[:, :, :, wide:]], axis=4) for t in (kept, given))
-    packed = kept[:, 0] + send(kept[:, 1], flip_x(1))
-    packed += send(given[:, 0], flip_x(2)) + send(given[:, 1], flip_x(3))
-    packed = packed[:, 0] + send(packed[:, 1], over_y)
+    packed = kept[:, 0, 0]
+    for bits in range(1, 8):
+        side = given if bits & 4 else kept
+        packed += send(side[:, bits >> 1 & 1, bits & 1], flip_plane(bits >> 1, bits & 1))
     diagonal = jnp.concatenate([packed[..., :cols], packed[..., cols:]], axis=1)
     diagonal += diagonal_inverse
     return offdiag.transpose(0, 2, 1), diagonal

time: 177 us -> 183 us (1.034)
  starting transfers between devices: 55.7 us -> 63.2 us
  waiting for transfers between devices: 72.2 us -> 69.9 us
    ppermute x32 -> x35, starting transfers between devices: 55.7 us -> 63.2 us  [send(): return lax.ppermute(value, AXES, pairs(move))]
    ppermute x32 -> x35, waiting for transfers between devices: 65.7 us -> 63.4 us  [send(): return lax.ppermute(value, AXES, pairs(move))]
  transfers between devices with their start and end apart: 33 -> 36, of which waited for: 24 -> 23; matrix products, arithmetic and copies ran while one was open for 11% -> 10% of each run, Pallas kernels for 0% -> 0%
where the time goes in v14:
time: 183 us; the launch traced here: 181 us
  waiting for transfers between devices  69.9 us (38%)
  starting transfers between devices  63.2 us (35%)
  other arithmetic  14.8 us (8%)
  between operations  14.4 us (8%)
  matrix products  9.59 us (5%)
  local copies, waits for them, and re-layouts  9.32 us (5%)
    ppermute x35, waiting for transfers between devices, send(): return lax.ppermute(value, AXES, pairs(move))  63.4 us
    ppermute x35, starting transfers between devices, send(): return lax.ppermute(value, AXES, pairs(move))  63.2 us
    all_gather x1, waiting for transfers between devices, shards(): facing = [lax.all_gather(turned, 'z', axis=1), None]  6.48 us
    dot_general x2, matrix products, dot_each(): return jnp.einsum('knr,kmr->knm', a, b, preferred_element_type=jnp.float32)  5.11 us
    dot_general x4, matrix products, dot_nt(): return lax.dot_general(a, b, NT, preferred_element_type=jnp.float32)  4.48 us
    add x3, other arithmetic, with_own(): return (below + down, above + up)  4.17 us
  transfers between devices with their start and end apart: 36, of which 23 were waited for; matrix products, arithmetic and copies ran while one was open for 10% of the time, Pallas kernels for 0%

profile of v14, /device:TPU:6, one launch (start us, length us, event | category | flops | bytes accessed | tf_op | source)
XLA Modules:
  0.0 181.3 jit_solution(14839340228144937643)
XLA Ops:
  9.1 3.4 %collective-permute-start = (bf16[3,64,768]{2,1,0:T(8,128)(2,1)S(1)}, bf16[3,64,768]{2,1,0:T(8,128)(2,1)S(1)}, u32[]{:S(2)}, u32[]{:S(2)}) collective-permute-start(bf16[3,64,768]{2,1,0:T(8,128)(2,1)S(1)} %multiply_bitcast_fusion), channel_id=1, source_target_pairs={{0,0},{1,1},{2,2},{3,3},{4,4},{5,5},{6,6},{7,7},{8,132},{9,133},{1... | collective-permute-start | bytes 884744 | tf_op jit(solution)/shard_map/ppermute | solution.py:19
  12.5 4.5 %collective-permute-start.1 = (bf16[3,64,768]{2,1,0:T(8,128)(2,1)S(1)}, bf16[3,64,768]{2,1,0:T(8,128)(2,1)S(1)}, u32[]{:S(2)}, u32[]{:S(2)}) collective-permute-start(bf16[3,64,768]{2,1,0:T(8,128)(2,1)S(1)} %multiply_bitcast_fusion), channel_id=1, source_target_pairs={{0,2},{1,3},{2,0},{3,1},{4,6},{5,7},{6,4},{7,5},{8,134},{9,135},{1... | collective-permute-start | bytes 884744 | tf_op jit(solution)/shard_map/ppermute | solution.py:19
  17.0 9.1 %collective-permute-start.2 = (bf16[3,64,768]{2,1,0:T(8,128)(2,1)S(1)}, bf16[3,64,768]{2,1,0:T(8,128)(2,1)S(1)}, u32[]{:S(2)}, u32[]{:S(2)}) collective-permute-start(bf16[3,64,768]{2,1,0:T(8,128)(2,1)S(1)} %multiply_bitcast_fusion), channel_id=1, source_target_pairs={{0,0},{1,16},{2,32},{3,48},{4,64},{5,80},{6,96},{7,112},{8,128},{9... | collective-permute-start | bytes 884744 | tf_op jit(solution)/shard_map/ppermute | solution.py:19
  26.1 2.3 %fusion.58 = (bf16[384,768]{1,0:T(8,128)(2,1)}, bf16[384,768]{1,0:T(8,128)(2,1)}) fusion(bf16[768,768]{1,0:T(8,128)(2,1)} %param.4), kind=kLoop, calls=%fused_computation.132 | loop fusion | bytes 2359296 | tf_op jit(solution)/shard_map/split | solution.py:129
  28.5 7.8 %collective-permute-done.1 = bf16[3,64,768]{2,1,0:T(8,128)(2,1)S(1)} collective-permute-done((bf16[3,64,768]{2,1,0:T(8,128)(2,1)S(1)}, bf16[3,64,768]{2,1,0:T(8,128)(2,1)S(1)}, u32[]{:S(2)}, u32[]{:S(2)}) %collective-permute-start.1) | collective-permute-done | bytes 294944 | tf_op jit(solution)/shard_map/ppermute | solution.py:19
  36.3 1.9 %collective-permute-done.2 = bf16[3,64,768]{2,1,0:T(8,128)(2,1)S(1)} collective-permute-done((bf16[3,64,768]{2,1,0:T(8,128)(2,1)S(1)}, bf16[3,64,768]{2,1,0:T(8,128)(2,1)S(1)}, u32[]{:S(2)}, u32[]{:S(2)}) %collective-permute-start.2) | collective-permute-done | bytes 294944 | tf_op jit(solution)/shard_map/ppermute | solution.py:19
  38.4 2.0 %collective-permute-start.4 = (bf16[3,2,64,768]{3,2,1,0:T(8,128)(2,1)S(1)}, bf16[3,2,64,768]{3,2,1,0:T(8,128)(2,1)S(1)}, u32[]{:S(2)}, u32[]{:S(2)}) collective-permute-start(bf16[3,2,64,768]{3,2,1,0:T(8,128)(2,1)S(1)} %pad_maximum_fusion.4), channel_id=1, source_target_pairs={{0,12},{1,13},{2,14},{3,15},{4,0},{5,1},{6,2},{7,3},{8,4},{9,5},{1... | collective-permute-start | bytes 1769480 | tf_op jit(solution)/shard_map/ppermute | solution.py:19
  40.4 2.1 %collective-permute-start.8 = (bf16[384,768]{1,0:T(8,128)(2,1)}, bf16[384,768]{1,0:T(8,128)(2,1)S(1)}, u32[]{:S(2)}, u32[]{:S(2)}) collective-permute-start(bf16[384,768]{1,0:T(8,128)(2,1)} %get-tuple-element.35), channel_id=1, source_target_pairs={{0,128},{1,129},{2,130},{3,131},{4,132},{5,133},{6,134},{7,135},{8... | collective-permute-start | bytes 1769480 | tf_op jit(solution)/shard_map/ppermute | solution.py:19
  42.6 11.8 %collective-permute-done.3 = bf16[3,2,64,768]{3,2,1,0:T(8,128)(2,1)S(1)} collective-permute-done((bf16[3,2,64,768]{3,2,1,0:T(8,128)(2,1)S(1)}, bf16[3,2,64,768]{3,2,1,0:T(8,128)(2,1)S(1)}, u32[]{:S(2)}, u32[]{:S(2)}) %collective-permute-start.3) | collective-permute-done | bytes 589856 | tf_op jit(solution)/shard_map/ppermute | solution.py:19
  60.3 8.3 %collective-permute-done.8 = bf16[384,768]{1,0:T(8,128)(2,1)S(1)} collective-permute-done((bf16[384,768]{1,0:T(8,128)(2,1)}, bf16[384,768]{1,0:T(8,128)(2,1)S(1)}, u32[]{:S(2)}, u32[]{:S(2)}) %collective-permute-start.8) | collective-permute-done | bytes 589856 | tf_op jit(solution)/shard_map/ppermute | solution.py:19
  77.3 6.5 %all-gather.3.cloned.1.call-done = bf16[3,512,768]{2,1,0:T(8,128)(2,1)} async-done(((bf16[3,64,768]{2,1,0:T(8,128)(2,1)}), bf16[3,512,768]{2,1,0:T(8,128)(2,1)}) %all-gather.3.cloned.1.call-update) | async-done | bytes 2359312 | tf_op jit(solution)/shard_map/all_gather | solution.py:135
  88.4 2.4 %collective-permute-start.10 = (f32[3,16,768]{2,1,0:T(8,128)S(1)}, f32[3,16,768]{2,1,0:T(8,128)S(1)}, u32[]{:S(2)}, u32[]{:S(2)}) collective-permute-start(f32[3,16,768]{2,1,0:T(8,128)S(1)} %get-tuple-element.112), channel_id=1, source_target_pairs={{0,112},{1,113},{2,114},{3,115},{4,116},{5,117},{6,118},{7,119},{8... | collective-permute-start | bytes 442376 | tf_op jit(solution)/shard_map/ppermute | solution.py:19
  90.8 3.3 %collective-permute-start.14 = (f32[3,16,768]{2,1,0:T(8,128)S(1)}, f32[3,16,768]{2,1,0:T(8,128)S(1)}, u32[]{:S(2)}, u32[]{:S(2)}) collective-permute-start(f32[3,16,768]{2,1,0:T(8,128)S(1)} %get-tuple-element.114), channel_id=1, source_target_pairs={{0,112},{1,113},{2,114},{3,115},{4,116},{5,117},{6,118},{7,119},{8... | collective-permute-start | bytes 442376 | tf_op jit(solution)/shard_map/ppermute | solution.py:19
  95.6 2.6 %collective-permute-done.11 = f32[3,16,768]{2,1,0:T(8,128)S(1)} collective-permute-done((f32[3,16,768]{2,1,0:T(8,128)S(1)}, f32[3,16,768]{2,1,0:T(8,128)S(1)}, u32[]{:S(2)}, u32[]{:S(2)}) %collective-permute-start.11) | collective-permute-done | bytes 147488 | tf_op jit(solution)/shard_map/ppermute | solution.py:19
  98.5 3.3 %collective-permute-start.12 = (f32[3,32,768]{2,1,0:T(8,128)S(1)}, f32[3,32,768]{2,1,0:T(8,128)S(1)}, u32[]{:S(2)}, u32[]{:S(2)}) collective-permute-start(f32[3,32,768]{2,1,0:T(8,128)S(1)} %pad_maximum_fusion.7), channel_id=1, source_target_pairs={{0,112},{1,113},{2,114},{3,115},{4,116},{5,117},{6,118},{7,119},{8... | collective-permute-start | bytes 884744 | tf_op jit(solution)/shard_map/ppermute | solution.py:19
  102.4 3.3 %collective-permute-start.18 = (f32[3,32,768]{2,1,0:T(8,128)S(1)}, f32[3,32,768]{2,1,0:T(8,128)}, u32[]{:S(2)}, u32[]{:S(2)}) collective-permute-start(f32[3,32,768]{2,1,0:T(8,128)S(1)} %pad_maximum_fusion.9), channel_id=1, source_target_pairs={{0,112},{1,113},{2,114},{3,115},{4,116},{5,117},{6,118},{7,119},{8... | collective-permute-start | bytes 884744 | tf_op jit(solution)/shard_map/ppermute | solution.py:19
  105.7 2.6 %collective-permute-done.13 = f32[3,32,768]{2,1,0:T(8,128)S(1)} collective-permute-done((f32[3,32,768]{2,1,0:T(8,128)S(1)}, f32[3,32,768]{2,1,0:T(8,128)S(1)}, u32[]{:S(2)}, u32[]{:S(2)}) %collective-permute-start.13) | collective-permute-done | bytes 294944 | tf_op jit(solution)/shard_map/ppermute | solution.py:19
  109.2 3.2 %collective-permute-start.16 = (f32[3,32,768]{2,1,0:T(8,128)}, f32[3,32,768]{2,1,0:T(8,128)S(1)}, u32[]{:S(2)}, u32[]{:S(2)}) collective-permute-start(f32[3,32,768]{2,1,0:T(8,128)} %get-tuple-element.66), channel_id=1, source_target_pairs={{0,112},{1,113},{2,114},{3,115},{4,116},{5,117},{6,118},{7,119},{8... | collective-permute-start | bytes 884744 | tf_op jit(solution)/shard_map/ppermute | solution.py:19
  112.4 2.1 %collective-permute-done.19 = f32[3,32,768]{2,1,0:T(8,128)S(1)} collective-permute-done((f32[3,32,768]{2,1,0:T(8,128)S(1)}, f32[3,32,768]{2,1,0:T(8,128)S(1)}, u32[]{:S(2)}, u32[]{:S(2)}) %collective-permute-start.19) | collective-permute-done | bytes 294944 | tf_op jit(solution)/shard_map/ppermute | solution.py:19
  115.7 3.4 %collective-permute-start.22 = (f32[3,32,768]{2,1,0:T(8,128)S(1)}, f32[3,32,768]{2,1,0:T(8,128)}, u32[]{:S(2)}, u32[]{:S(2)}) collective-permute-start(f32[3,32,768]{2,1,0:T(8,128)S(1)} %get-tuple-element.64), channel_id=1, source_target_pairs={{0,112},{1,113},{2,114},{3,115},{4,116},{5,117},{6,118},{7,119},{8... | collective-permute-start | bytes 884744 | tf_op jit(solution)/shard_map/ppermute | solution.py:19
  121.2 1.9 %fusion.12 = (f32[3,32,768]{2,1,0:T(8,128)S(1)}, f32[3,32,768]{2,1,0:T(8,128)}) fusion(f32[3,32,768]{2,1,0:T(8,128)} %collective-permute-done.17, f32[3,4,64,768]{3,2,1,0:T(8,128)} %bitcast.290, s32[]{:T(128)S(6)} %select_n.508, f32[3,4,64,768]{3,2,1,0:T(8,128)S(1)} %bitcast.284, pred[]{:T(512)S(6)} %eq.108, f32[3,32,768]{2,1,0:T(8,128)S(1)} %collective-permute-done.16, ...), kind=kLoop, calls=%fused_computation.43 | loop fusion | flops 294912 | bytes 2359306 | tf_op jit(solution)/shard_map/add | solution.py:98
  123.2 2.9 %collective-permute-start.20 = (f32[3,32,768]{2,1,0:T(8,128)}, f32[3,32,768]{2,1,0:T(8,128)S(1)}, u32[]{:S(2)}, u32[]{:S(2)}) collective-permute-start(f32[3,32,768]{2,1,0:T(8,128)} %get-tuple-element.62), channel_id=1, source_target_pairs={{0,112},{1,113},{2,114},{3,115},{4,116},{5,117},{6,118},{7,119},{8... | collective-permute-start | bytes 884744 | tf_op jit(solution)/shard_map/ppermute | solution.py:19
  127.3 4.2 %collective-permute-done.20 = f32[3,32,768]{2,1,0:T(8,128)S(1)} collective-permute-done((f32[3,32,768]{2,1,0:T(8,128)}, f32[3,32,768]{2,1,0:T(8,128)S(1)}, u32[]{:S(2)}, u32[]{:S(2)}) %collective-permute-start.20) | collective-permute-done | bytes 294944 | tf_op jit(solution)/shard_map/ppermute | solution.py:19
  131.5 3.6 %collective-permute-done.21 = f32[3,32,768]{2,1,0:T(8,128)} collective-permute-done((f32[3,32,768]{2,1,0:T(8,128)S(1)}, f32[3,32,768]{2,1,0:T(8,128)}, u32[]{:S(2)}, u32[]{:S(2)}) %collective-permute-start.21) | collective-permute-done | bytes 294944 | tf_op jit(solution)/shard_map/ppermute | solution.py:19
  136.7 2.0 %collective-permute-start.25 = (f32[3,32,768]{2,1,0:T(8,128)S(1)}, f32[3,32,768]{2,1,0:T(8,128)S(1)}, u32[]{:S(2)}, u32[]{:S(2)}) collective-permute-start(f32[3,32,768]{2,1,0:T(8,128)S(1)} %get-tuple-element.60), channel_id=1, source_target_pairs={{0,16},{1,17},{2,18},{3,19},{4,20},{5,21},{6,22},{7,23},{8,24},{9,... | collective-permute-start | bytes 884744 | tf_op jit(solution)/shard_map/ppermute | solution.py:19
  138.7 4.7 %collective-permute-done.24 = f32[3,32,768]{2,1,0:T(8,128)S(1)} collective-permute-done((f32[3,32,768]{2,1,0:T(8,128)S(1)}, f32[3,32,768]{2,1,0:T(8,128)S(1)}, u32[]{:S(2)}, u32[]{:S(2)}) %collective-permute-start.24) | collective-permute-done | bytes 294944 | tf_op jit(solution)/shard_map/ppermute | solution.py:19
  146.2 2.6 %fusion.69 = f32[3,512,128]{1,2,0:T(8,128)S(1)} fusion(bf16[3,512,768]{2,1,0:T(8,128)(2,1)} %bitcast.37, bf16[3,128,768]{2,1,0:T(8,128)(2,1)S(1)} %bitcast.293), kind=kOutput, calls=%fused_computation.143 | convolution fusion | flops 301989888 | bytes 3735552 | tf_op jit(solution)/shard_map/knr,kmr->knm/dot_general | solution.py:85
  148.8 2.6 %fusion.70 = f32[3,512,128]{1,2,0:T(8,128)S(1)} fusion(bf16[3,512,768]{2,1,0:T(8,128)(2,1)} %bitcast.41, bf16[3,128,768]{2,1,0:T(8,128)(2,1)S(1)} %bitcast.294), kind=kOutput, calls=%fused_computation.144 | convolution fusion | flops 301989888 | bytes 3735552 | tf_op jit(solution)/shard_map/knr,kmr->knm/dot_general | solution.py:85
  154.1 3.1 %collective-permute-start.28 = (f32[3,32,128]{2,1,0:T(8,128)S(1)}, f32[3,32,128]{2,1,0:T(8,128)S(1)}, u32[]{:S(2)}, u32[]{:S(2)}) collective-permute-start(f32[3,32,128]{2,1,0:T(8,128)S(1)} %get-tuple-element.89), channel_id=1, source_target_pairs={{0,2},{1,3},{2,0},{3,1},{4,6},{5,7},{6,4},{7,5},{8,10},{9,11},{10,... | collective-permute-start | bytes 147464 | tf_op jit(solution)/shard_map/ppermute | solution.py:19
  160.8 4.5 %collective-permute-start.32 = (f32[3,32,128]{2,1,0:T(8,128)S(1)}, f32[3,32,128]{2,1,0:T(8,128)S(1)}, u32[]{:S(2)}, u32[]{:S(2)}) collective-permute-start(f32[3,32,128]{2,1,0:T(8,128)S(1)} %get-tuple-element.98), channel_id=1, source_target_pairs={{0,10},{1,11},{2,8},{3,9},{4,14},{5,15},{6,12},{7,13},{8,2},{9,3},... | collective-permute-start | bytes 147464 | tf_op jit(solution)/shard_map/ppermute | solution.py:19
  165.9 2.6 %collective-permute-start.34 = (f32[3,32,128]{2,1,0:T(8,128)S(1)}, f32[3,32,128]{2,1,0:T(8,128)S(1)}, u32[]{:S(2)}, u32[]{:S(2)}) collective-permute-start(f32[3,32,128]{2,1,0:T(8,128)S(1)} %get-tuple-element.99), channel_id=1, source_target_pairs={{0,14},{1,15},{2,12},{3,13},{4,10},{5,11},{6,8},{7,9},{8,6},{9,7},... | collective-permute-start | bytes 147464 | tf_op jit(solution)/shard_map/ppermute | solution.py:19
  170.7 3.0 %collective-permute-done.34 = f32[3,32,128]{2,1,0:T(8,128)S(1)} collective-permute-done((f32[3,32,128]{2,1,0:T(8,128)S(1)}, f32[3,32,128]{2,1,0:T(8,128)S(1)}, u32[]{:S(2)}, u32[]{:S(2)}) %collective-permute-start.34) | collective-permute-done | bytes 49184 | tf_op jit(solution)/shard_map/ppermute | solution.py:19
  (116 shorter events, 43.3 us)
Async XLA Ops:
  7.2 76.6 %all-gather.3.cloned.1.call-start = ((), (), s32[]{:S(2)}) async-start(), calls=%async_computation | async-start | bytes 2654208 | tf_op jit(solution)/shard_map/all_gather | solution.py:135
  9.1 19.3 %collective-permute-start = (bf16[3,64,768]{2,1,0:T(8,128)(2,1)S(1)}, bf16[3,64,768]{2,1,0:T(8,128)(2,1)S(1)}, u32[]{:S(2)}, u32[]{:S(2)}) collective-permute-start(bf16[3,64,768]{2,1,0:T(8,128)(2,1)S(1)} %multiply_bitcast_fusion), channel_id=1, source_target_pairs={{0,0},{1,1},{2,2},{3,3},{4,4},{5,5},{6,6},{7,7},{8,132},{9,133},{1... | collective-permute-start | bytes 884744 | tf_op jit(solution)/shard_map/ppermute | solution.py:19
  12.5 23.8 %collective-permute-start.1 = (bf16[3,64,768]{2,1,0:T(8,128)(2,1)S(1)}, bf16[3,64,768]{2,1,0:T(8,128)(2,1)S(1)}, u32[]{:S(2)}, u32[]{:S(2)}) collective-permute-start(bf16[3,64,768]{2,1,0:T(8,128)(2,1)S(1)} %multiply_bitcast_fusion), channel_id=1, source_target_pairs={{0,2},{1,3},{2,0},{3,1},{4,6},{5,7},{6,4},{7,5},{8,134},{9,135},{1... | collective-permute-start | bytes 884744 | tf_op jit(solution)/shard_map/ppermute | solution.py:19
  17.0 21.2 %collective-permute-start.2 = (bf16[3,64,768]{2,1,0:T(8,128)(2,1)S(1)}, bf16[3,64,768]{2,1,0:T(8,128)(2,1)S(1)}, u32[]{:S(2)}, u32[]{:S(2)}) collective-permute-start(bf16[3,64,768]{2,1,0:T(8,128)(2,1)S(1)} %multiply_bitcast_fusion), channel_id=1, source_target_pairs={{0,0},{1,16},{2,32},{3,48},{4,64},{5,80},{6,96},{7,112},{8,128},{9... | collective-permute-start | bytes 884744 | tf_op jit(solution)/shard_map/ppermute | solution.py:19
  38.3 16.0 %collective-permute-start.3 = (bf16[3,2,64,768]{3,2,1,0:T(8,128)(2,1)S(1)}, bf16[3,2,64,768]{3,2,1,0:T(8,128)(2,1)S(1)}, u32[]{:S(2)}, u32[]{:S(2)}) collective-permute-start(bf16[3,2,64,768]{3,2,1,0:T(8,128)(2,1)S(1)} %pad_maximum_fusion.4), channel_id=1, source_target_pairs={{0,4},{1,5},{2,6},{3,7},{4,8},{5,9},{6,10},{7,11},{8,12},{9,13},{1... | collective-permute-start | bytes 1769480 | tf_op jit(solution)/shard_map/ppermute | solution.py:19
  38.4 17.2 %collective-permute-start.4 = (bf16[3,2,64,768]{3,2,1,0:T(8,128)(2,1)S(1)}, bf16[3,2,64,768]{3,2,1,0:T(8,128)(2,1)S(1)}, u32[]{:S(2)}, u32[]{:S(2)}) collective-permute-start(bf16[3,2,64,768]{3,2,1,0:T(8,128)(2,1)S(1)} %pad_maximum_fusion.4), channel_id=1, source_target_pairs={{0,12},{1,13},{2,14},{3,15},{4,0},{5,1},{6,2},{7,3},{8,4},{9,5},{1... | collective-permute-start | bytes 1769480 | tf_op jit(solution)/shard_map/ppermute | solution.py:19
  40.4 16.4 %collective-permute-start.5 = (bf16[384,768]{1,0:T(8,128)(2,1)}, bf16[384,768]{1,0:T(8,128)(2,1)S(1)}, u32[]{:S(2)}, u32[]{:S(2)}) collective-permute-start(bf16[384,768]{1,0:T(8,128)(2,1)} %get-tuple-element.32), channel_id=1, source_target_pairs={{0,128},{1,129},{2,130},{3,131},{4,132},{5,133},{6,134},{7,135},{8... | collective-permute-start | bytes 1769480 | tf_op jit(solution)/shard_map/ppermute | solution.py:19
  40.4 28.2 %collective-permute-start.8 = (bf16[384,768]{1,0:T(8,128)(2,1)}, bf16[384,768]{1,0:T(8,128)(2,1)S(1)}, u32[]{:S(2)}, u32[]{:S(2)}) collective-permute-start(bf16[384,768]{1,0:T(8,128)(2,1)} %get-tuple-element.35), channel_id=1, source_target_pairs={{0,128},{1,129},{2,130},{3,131},{4,132},{5,133},{6,134},{7,135},{8... | collective-permute-start | bytes 1769480 | tf_op jit(solution)/shard_map/ppermute | solution.py:19
  57.6 11.1 %collective-permute-start.6 = (bf16[3,1,64,768]{3,2,1,0:T(8,128)(2,1)}, bf16[3,1,64,768]{3,2,1,0:T(8,128)(2,1)S(1)}, u32[]{:S(2)}, u32[]{:S(2)}) collective-permute-start(bf16[3,1,64,768]{3,2,1,0:T(8,128)(2,1)} %slice.120), channel_id=1, source_target_pairs={{0,4},{1,5},{2,6},{3,7},{4,8},{5,9},{6,10},{7,11},{8,12},{9,13},{1... | collective-permute-start | bytes 884744 | tf_op jit(solution)/shard_map/ppermute | solution.py:19
  59.6 9.3 %collective-permute-start.7 = (bf16[3,1,64,768]{3,2,1,0:T(8,128)(2,1)}, bf16[3,1,64,768]{3,2,1,0:T(8,128)(2,1)S(1)}, u32[]{:S(2)}, u32[]{:S(2)}) collective-permute-start(bf16[3,1,64,768]{3,2,1,0:T(8,128)(2,1)} %slice.121), channel_id=1, source_target_pairs={{0,12},{1,13},{2,14},{3,15},{4,0},{5,1},{6,2},{7,3},{8,4},{9,5},{1... | collective-permute-start | bytes 884744 | tf_op jit(solution)/shard_map/ppermute | solution.py:19
  88.4 7.2 %collective-permute-start.10 = (f32[3,16,768]{2,1,0:T(8,128)S(1)}, f32[3,16,768]{2,1,0:T(8,128)S(1)}, u32[]{:S(2)}, u32[]{:S(2)}) collective-permute-start(f32[3,16,768]{2,1,0:T(8,128)S(1)} %get-tuple-element.112), channel_id=1, source_target_pairs={{0,112},{1,113},{2,114},{3,115},{4,116},{5,117},{6,118},{7,119},{8... | collective-permute-start | bytes 442376 | tf_op jit(solution)/shard_map/ppermute | solution.py:19
  90.8 7.5 %collective-permute-start.11 = (f32[3,16,768]{2,1,0:T(8,128)S(1)}, f32[3,16,768]{2,1,0:T(8,128)S(1)}, u32[]{:S(2)}, u32[]{:S(2)}) collective-permute-start(f32[3,16,768]{2,1,0:T(8,128)S(1)} %get-tuple-element.111), channel_id=1, source_target_pairs={{0,16},{1,17},{2,18},{3,19},{4,20},{5,21},{6,22},{7,23},{8,24},{9,... | collective-permute-start | bytes 442376 | tf_op jit(solution)/shard_map/ppermute | solution.py:19
  90.8 11.0 %collective-permute-start.14 = (f32[3,16,768]{2,1,0:T(8,128)S(1)}, f32[3,16,768]{2,1,0:T(8,128)S(1)}, u32[]{:S(2)}, u32[]{:S(2)}) collective-permute-start(f32[3,16,768]{2,1,0:T(8,128)S(1)} %get-tuple-element.114), channel_id=1, source_target_pairs={{0,112},{1,113},{2,114},{3,115},{4,116},{5,117},{6,118},{7,119},{8... | collective-permute-start | bytes 442376 | tf_op jit(solution)/shard_map/ppermute | solution.py:19
  94.1 8.0 %collective-permute-start.15 = (f32[3,16,768]{2,1,0:T(8,128)S(1)}, f32[3,16,768]{2,1,0:T(8,128)S(1)}, u32[]{:S(2)}, u32[]{:S(2)}) collective-permute-start(f32[3,16,768]{2,1,0:T(8,128)S(1)} %get-tuple-element.113), channel_id=1, source_target_pairs={{0,16},{1,17},{2,18},{3,19},{4,20},{5,21},{6,22},{7,23},{8,24},{9,... | collective-permute-start | bytes 442376 | tf_op jit(solution)/shard_map/ppermute | solution.py:19
  94.2 50.8 %collective-permute-start.26 = (bf16[3,8,64,768]{3,2,1,0:T(8,128)(2,1)}, bf16[3,8,64,768]{3,2,1,0:T(8,128)(2,1)}, u32[]{:S(2)}, u32[]{:S(2)}) collective-permute-start(bf16[3,8,64,768]{3,2,1,0:T(8,128)(2,1)} %bitcast.16), channel_id=1, source_target_pairs={{0,128},{1,129},{2,130},{3,131},{4,132},{5,133},{6,134},{7,135},{8... | collective-permute-start | bytes 7077896 | tf_op jit(solution)/shard_map/ppermute | solution.py:19
  98.4 9.9 %collective-permute-start.13 = (f32[3,32,768]{2,1,0:T(8,128)S(1)}, f32[3,32,768]{2,1,0:T(8,128)S(1)}, u32[]{:S(2)}, u32[]{:S(2)}) collective-permute-start(f32[3,32,768]{2,1,0:T(8,128)S(1)} %pad_maximum_fusion.8), channel_id=1, source_target_pairs={{0,16},{1,17},{2,18},{3,19},{4,20},{5,21},{6,22},{7,23},{8,24},{9,... | collective-permute-start | bytes 884744 | tf_op jit(solution)/shard_map/ppermute | solution.py:19
  98.5 9.7 %collective-permute-start.12 = (f32[3,32,768]{2,1,0:T(8,128)S(1)}, f32[3,32,768]{2,1,0:T(8,128)S(1)}, u32[]{:S(2)}, u32[]{:S(2)}) collective-permute-start(f32[3,32,768]{2,1,0:T(8,128)S(1)} %pad_maximum_fusion.7), channel_id=1, source_target_pairs={{0,112},{1,113},{2,114},{3,115},{4,116},{5,117},{6,118},{7,119},{8... | collective-permute-start | bytes 884744 | tf_op jit(solution)/shard_map/ppermute | solution.py:19
  102.2 12.3 %collective-permute-start.19 = (f32[3,32,768]{2,1,0:T(8,128)S(1)}, f32[3,32,768]{2,1,0:T(8,128)S(1)}, u32[]{:S(2)}, u32[]{:S(2)}) collective-permute-start(f32[3,32,768]{2,1,0:T(8,128)S(1)} %pad_maximum_fusion.10), channel_id=1, source_target_pairs={{0,16},{1,17},{2,18},{3,19},{4,20},{5,21},{6,22},{7,23},{8,24},{9,... | collective-permute-start | bytes 884744 | tf_op jit(solution)/shard_map/ppermute | solution.py:19
  102.4 12.1 %collective-permute-start.18 = (f32[3,32,768]{2,1,0:T(8,128)S(1)}, f32[3,32,768]{2,1,0:T(8,128)}, u32[]{:S(2)}, u32[]{:S(2)}) collective-permute-start(f32[3,32,768]{2,1,0:T(8,128)S(1)} %pad_maximum_fusion.9), channel_id=1, source_target_pairs={{0,112},{1,113},{2,114},{3,115},{4,116},{5,117},{6,118},{7,119},{8... | collective-permute-start | bytes 884744 | tf_op jit(solution)/shard_map/ppermute | solution.py:19
  109.2 11.3 %collective-permute-start.16 = (f32[3,32,768]{2,1,0:T(8,128)}, f32[3,32,768]{2,1,0:T(8,128)S(1)}, u32[]{:S(2)}, u32[]{:S(2)}) collective-permute-start(f32[3,32,768]{2,1,0:T(8,128)} %get-tuple-element.66), channel_id=1, source_target_pairs={{0,112},{1,113},{2,114},{3,115},{4,116},{5,117},{6,118},{7,119},{8... | collective-permute-start | bytes 884744 | tf_op jit(solution)/shard_map/ppermute | solution.py:19
  112.4 8.8 %collective-permute-start.17 = (f32[3,32,768]{2,1,0:T(8,128)}, f32[3,32,768]{2,1,0:T(8,128)}, u32[]{:S(2)}, u32[]{:S(2)}) collective-permute-start(f32[3,32,768]{2,1,0:T(8,128)} %get-tuple-element.65), channel_id=1, source_target_pairs={{0,16},{1,17},{2,18},{3,19},{4,20},{5,21},{6,22},{7,23},{8,24},{9,... | collective-permute-start | bytes 884744 | tf_op jit(solution)/shard_map/ppermute | solution.py:19
  115.7 10.3 %collective-permute-start.22 = (f32[3,32,768]{2,1,0:T(8,128)S(1)}, f32[3,32,768]{2,1,0:T(8,128)}, u32[]{:S(2)}, u32[]{:S(2)}) collective-permute-start(f32[3,32,768]{2,1,0:T(8,128)S(1)} %get-tuple-element.64), channel_id=1, source_target_pairs={{0,112},{1,113},{2,114},{3,115},{4,116},{5,117},{6,118},{7,119},{8... | collective-permute-start | bytes 884744 | tf_op jit(solution)/shard_map/ppermute | solution.py:19
  119.2 8.1 %collective-permute-start.23 = (f32[3,32,768]{2,1,0:T(8,128)S(1)}, f32[3,32,768]{2,1,0:T(8,128)}, u32[]{:S(2)}, u32[]{:S(2)}) collective-permute-start(f32[3,32,768]{2,1,0:T(8,128)S(1)} %get-tuple-element.63), channel_id=1, source_target_pairs={{0,16},{1,17},{2,18},{3,19},{4,20},{5,21},{6,22},{7,23},{8,24},{9,... | collective-permute-start | bytes 884744 | tf_op jit(solution)/shard_map/ppermute | solution.py:19
  123.2 8.3 %collective-permute-start.20 = (f32[3,32,768]{2,1,0:T(8,128)}, f32[3,32,768]{2,1,0:T(8,128)S(1)}, u32[]{:S(2)}, u32[]{:S(2)}) collective-permute-start(f32[3,32,768]{2,1,0:T(8,128)} %get-tuple-element.62), channel_id=1, source_target_pairs={{0,112},{1,113},{2,114},{3,115},{4,116},{5,117},{6,118},{7,119},{8... | collective-permute-start | bytes 884744 | tf_op jit(solution)/shard_map/ppermute | solution.py:19
  126.0 9.0 %collective-permute-start.21 = (f32[3,32,768]{2,1,0:T(8,128)S(1)}, f32[3,32,768]{2,1,0:T(8,128)}, u32[]{:S(2)}, u32[]{:S(2)}) collective-permute-start(f32[3,32,768]{2,1,0:T(8,128)S(1)} %get-tuple-element.61), channel_id=1, source_target_pairs={{0,16},{1,17},{2,18},{3,19},{4,20},{5,21},{6,22},{7,23},{8,24},{9,... | collective-permute-start | bytes 884744 | tf_op jit(solution)/shard_map/ppermute | solution.py:19
  136.7 8.2 %collective-permute-start.25 = (f32[3,32,768]{2,1,0:T(8,128)S(1)}, f32[3,32,768]{2,1,0:T(8,128)S(1)}, u32[]{:S(2)}, u32[]{:S(2)}) collective-permute-start(f32[3,32,768]{2,1,0:T(8,128)S(1)} %get-tuple-element.60), channel_id=1, source_target_pairs={{0,16},{1,17},{2,18},{3,19},{4,20},{5,21},{6,22},{7,23},{8,24},{9,... | collective-permute-start | bytes 884744 | tf_op jit(solution)/shard_map/ppermute | solution.py:19
  154.1 11.3 %collective-permute-start.28 = (f32[3,32,128]{2,1,0:T(8,128)S(1)}, f32[3,32,128]{2,1,0:T(8,128)S(1)}, u32[]{:S(2)}, u32[]{:S(2)}) collective-permute-start(f32[3,32,128]{2,1,0:T(8,128)S(1)} %get-tuple-element.89), channel_id=1, source_target_pairs={{0,2},{1,3},{2,0},{3,1},{4,6},{5,7},{6,4},{7,5},{8,10},{9,11},{10,... | collective-permute-start | bytes 147464 | tf_op jit(solution)/shard_map/ppermute | solution.py:19
  157.1 8.8 %collective-permute-start.29 = (f32[3,32,128]{2,1,0:T(8,128)S(1)}, f32[3,32,128]{2,1,0:T(8,128)S(1)}, u32[]{:S(2)}, u32[]{:S(2)}) collective-permute-start(f32[3,32,128]{2,1,0:T(8,128)S(1)} %get-tuple-element.91), channel_id=1, source_target_pairs={{0,4},{1,5},{2,6},{3,7},{4,0},{5,1},{6,2},{7,3},{8,12},{9,13},{10,... | collective-permute-start | bytes 147464 | tf_op jit(solution)/shard_map/ppermute | solution.py:19
  158.0 11.4 %collective-permute-start.30 = (f32[3,32,128]{2,1,0:T(8,128)S(1)}, f32[3,32,128]{2,1,0:T(8,128)S(1)}, u32[]{:S(2)}, u32[]{:S(2)}) collective-permute-start(f32[3,32,128]{2,1,0:T(8,128)S(1)} %get-tuple-element.90), channel_id=1, source_target_pairs={{0,6},{1,7},{2,4},{3,5},{4,2},{5,3},{6,0},{7,1},{8,14},{9,15},{10,... | collective-permute-start | bytes 147464 | tf_op jit(solution)/shard_map/ppermute | solution.py:19
  159.3 10.1 %collective-permute-start.31 = (f32[3,32,128]{2,1,0:T(8,128)S(1)}, f32[3,32,128]{2,1,0:T(8,128)S(1)}, u32[]{:S(2)}, u32[]{:S(2)}) collective-permute-start(f32[3,32,128]{2,1,0:T(8,128)S(1)} %get-tuple-element.97), channel_id=1, source_target_pairs={{0,8},{1,9},{2,10},{3,11},{4,12},{5,13},{6,14},{7,15},{8,0},{9,1},... | collective-permute-start | bytes 147464 | tf_op jit(solution)/shard_map/ppermute | solution.py:19
  160.8 8.6 %collective-permute-start.32 = (f32[3,32,128]{2,1,0:T(8,128)S(1)}, f32[3,32,128]{2,1,0:T(8,128)S(1)}, u32[]{:S(2)}, u32[]{:S(2)}) collective-permute-start(f32[3,32,128]{2,1,0:T(8,128)S(1)} %get-tuple-element.98), channel_id=1, source_target_pairs={{0,10},{1,11},{2,8},{3,9},{4,14},{5,15},{6,12},{7,13},{8,2},{9,3},... | collective-permute-start | bytes 147464 | tf_op jit(solution)/shard_map/ppermute | solution.py:19
  165.9 7.7 %collective-permute-start.34 = (f32[3,32,128]{2,1,0:T(8,128)S(1)}, f32[3,32,128]{2,1,0:T(8,128)S(1)}, u32[]{:S(2)}, u32[]{:S(2)}) collective-permute-start(f32[3,32,128]{2,1,0:T(8,128)S(1)} %get-tuple-element.99), channel_id=1, source_target_pairs={{0,14},{1,15},{2,12},{3,13},{4,10},{5,11},{6,8},{7,9},{8,6},{9,7},... | collective-permute-start | bytes 147464 | tf_op jit(solution)/shard_map/ppermute | solution.py:19
  (12 other events, 74.3 us)
Sparse Core Ops, SparseCore 0:
  40.6 43.2 all-gather.2

commit v15 on v13

--- a/solution.py
+++ b/solution.py
@@ -126,12 +126,13 @@
     keep_cols = row_mask(pattern, col, per).astype(jnp.float32)
     own = factor_panel.transpose(0, 2, 1) * keep_rows[:, None, :]
     near, far = send(own, swap), send(own, swap_far)
-    pieces = jnp.split(ancestor_inverse, (rows // 2,))
+    pieces = jnp.split(ancestor_inverse, (rows * 7 // 12,))
     near, far, turned, *pieces = together(near, far, send(own, turned_place), *pieces)
     plane = jnp.stack([near, far], axis=1)
     left, right = send(plane, along_x(1)), send(plane, along_x(3))
-    beside = [send(piece, across) for piece in pieces]
-    left, right, beside[0] = together(left, right, beside[0])
+    beside = [send(pieces[0], across), None]
+    left, right, beside[0], last = together(left, right, beside[0], pieces[1])
+    beside[1] = send(last, across)
     facing = [lax.all_gather(turned, "z", axis=1), None]
     opposite = send(left[:, :1], along_x(1)), send(right[:, 1:], along_x(3))
     *opposite, beside[1] = together(*opposite, beside[1])
@@ -139,11 +140,12 @@
     mine = pair_rows(x, own_rows, plane, left, right, opposite)
 
     def product(panel):
-        panel = panel.reshape(2, count * 4 * cols, rows)
+        panel = [side.reshape(count * 4 * cols, rows) for side in panel]
         whole = dot_nt(panel[0], ancestor_inverse) + dot_nt(panel[1], beside)
         return whole.reshape(count, 4, cols, rows)
 
-    theirs, facing[0] = together(send(mine, sibling), facing[0])
+    theirs = list(send(mine, sibling))
+    theirs[1], facing[0] = together(theirs[1], facing[0])
     beside = jnp.concatenate(beside)
     near, far = product(mine), product(theirs)
     column = jnp.where(own_rows, x % 2, 1 - x % 2)

time: 177 us -> 181 us (1.023)
  starting transfers between devices: 55.7 us -> 51.4 us
  local copies, waits for them, and re-layouts: 9.31 us -> 13.1 us
  waiting for transfers between devices: 72.2 us -> 74.6 us
  matrix products: 9.59 us -> 11.4 us
    ppermute x32, waiting for transfers between devices: 65.7 us -> 73.4 us  [send(): return lax.ppermute(value, AXES, pairs(move))]
    all_gather x1, waiting for transfers between devices: 6.47 us -> 1.16 us  [shards(): facing = [lax.all_gather(turned, 'z', axis=1), None]]
    ppermute x32, starting transfers between devices: 55.7 us -> 51.4 us  [send(): return lax.ppermute(value, AXES, pairs(move))]
    another operation x0 -> x1, local copies, waits for them, and re-layouts: none -> 2.87 us  [shards(): theirs = list(send(mine, sibling))]
    slice x1 -> x0, local copies, waits for them, and re-layouts: 1.87 us -> none  [product(): whole = dot_nt(panel[0], ancestor_inverse) + dot_nt(panel[1], beside)]
  transfers between devices with their start and end apart: 33 -> 33, of which waited for: 24 -> 28; matrix products, arithmetic and copies ran while one was open for 11% -> 13% of each run, Pallas kernels for 0% -> 0%
where the time goes in v15:
time: 181 us; the launch traced here: 180 us
  waiting for transfers between devices  74.6 us (41%)
  starting transfers between devices  51.4 us (28%)
  other arithmetic  14.7 us (8%)
  between operations  14.4 us (8%)
  local copies, waits for them, and re-layouts  13.1 us (7%)
  matrix products  11.4 us (6%)
    ppermute x32, waiting for transfers between devices, send(): return lax.ppermute(value, AXES, pairs(move))  73.4 us
    ppermute x32, starting transfers between devices, send(): return lax.ppermute(value, AXES, pairs(move))  51.4 us
    dot_general x4, matrix products, dot_nt(): return lax.dot_general(a, b, NT, preferred_element_type=jnp.float32)  6.26 us
    dot_general x2, matrix products, dot_each(): return jnp.einsum('knr,kmr->knm', a, b, preferred_element_type=jnp.float32)  5.11 us
    add x3, other arithmetic, with_own(): return (below + down, above + up)  4.14 us
  transfers between devices with their start and end apart: 33, of which 28 were waited for; matrix products, arithmetic and copies ran while one was open for 13% of the time, Pallas kernels for 0%

profile of v15, /device:TPU:6, one launch (start us, length us, event | category | flops | bytes accessed | tf_op | source)
XLA Modules:
  0.0 179.6 jit_solution(9388180620346892545)
XLA Ops:
  9.2 3.4 %collective-permute-start = (bf16[3,64,768]{2,1,0:T(8,128)(2,1)S(1)}, bf16[3,64,768]{2,1,0:T(8,128)(2,1)S(1)}, u32[]{:S(2)}, u32[]{:S(2)}) collective-permute-start(bf16[3,64,768]{2,1,0:T(8,128)(2,1)S(1)} %multiply_bitcast_fusion), channel_id=1, source_target_pairs={{0,0},{1,1},{2,2},{3,3},{4,4},{5,5},{6,6},{7,7},{8,132},{9,133},{1... | collective-permute-start | bytes 884744 | tf_op jit(solution)/shard_map/ppermute | solution.py:19
  12.6 4.5 %collective-permute-start.1 = (bf16[3,64,768]{2,1,0:T(8,128)(2,1)S(1)}, bf16[3,64,768]{2,1,0:T(8,128)(2,1)S(1)}, u32[]{:S(2)}, u32[]{:S(2)}) collective-permute-start(bf16[3,64,768]{2,1,0:T(8,128)(2,1)S(1)} %multiply_bitcast_fusion), channel_id=1, source_target_pairs={{0,2},{1,3},{2,0},{3,1},{4,6},{5,7},{6,4},{7,5},{8,134},{9,135},{1... | collective-permute-start | bytes 884744 | tf_op jit(solution)/shard_map/ppermute | solution.py:19
  17.0 9.1 %collective-permute-start.2 = (bf16[3,64,768]{2,1,0:T(8,128)(2,1)S(1)}, bf16[3,64,768]{2,1,0:T(8,128)(2,1)S(1)}, u32[]{:S(2)}, u32[]{:S(2)}) collective-permute-start(bf16[3,64,768]{2,1,0:T(8,128)(2,1)S(1)} %multiply_bitcast_fusion), channel_id=1, source_target_pairs={{0,0},{1,16},{2,32},{3,48},{4,64},{5,80},{6,96},{7,112},{8,128},{9... | collective-permute-start | bytes 884744 | tf_op jit(solution)/shard_map/ppermute | solution.py:19
  26.2 2.0 %split.6 = bf16[448,768]{1,0:T(8,128)(2,1)} slice(bf16[768,768]{1,0:T(8,128)(2,1)} %param.4), slice={[0:448], [0:768]} | slice | bytes 1376256 | tf_op jit(solution)/shard_map/split | solution.py:129
  29.0 7.4 %collective-permute-done.1 = bf16[3,64,768]{2,1,0:T(8,128)(2,1)S(1)} collective-permute-done((bf16[3,64,768]{2,1,0:T(8,128)(2,1)S(1)}, bf16[3,64,768]{2,1,0:T(8,128)(2,1)S(1)}, u32[]{:S(2)}, u32[]{:S(2)}) %collective-permute-start.1) | collective-permute-done | bytes 294944 | tf_op jit(solution)/shard_map/ppermute | solution.py:19
  39.2 2.0 %collective-permute-start.4 = (bf16[3,2,64,768]{3,2,1,0:T(8,128)(2,1)S(1)}, bf16[3,2,64,768]{3,2,1,0:T(8,128)(2,1)S(1)}, u32[]{:S(2)}, u32[]{:S(2)}) collective-permute-start(bf16[3,2,64,768]{3,2,1,0:T(8,128)(2,1)S(1)} %pad_maximum_fusion.4), channel_id=1, source_target_pairs={{0,12},{1,13},{2,14},{3,15},{4,0},{5,1},{6,2},{7,3},{8,4},{9,5},{1... | collective-permute-start | bytes 1769480 | tf_op jit(solution)/shard_map/ppermute | solution.py:19
  41.2 13.9 %collective-permute-done.3 = bf16[3,2,64,768]{3,2,1,0:T(8,128)(2,1)S(1)} collective-permute-done((bf16[3,2,64,768]{3,2,1,0:T(8,128)(2,1)S(1)}, bf16[3,2,64,768]{3,2,1,0:T(8,128)(2,1)S(1)}, u32[]{:S(2)}, u32[]{:S(2)}) %collective-permute-start.3) | collective-permute-done | bytes 589856 | tf_op jit(solution)/shard_map/ppermute | solution.py:19
  61.0 5.8 %collective-permute-done.6 = bf16[3,1,64,768]{3,2,1,0:T(8,128)(2,1)} collective-permute-done((bf16[3,1,64,768]{3,2,1,0:T(8,128)(2,1)}, bf16[3,1,64,768]{3,2,1,0:T(8,128)(2,1)}, u32[]{:S(2)}, u32[]{:S(2)}) %collective-permute-start.6) | collective-permute-done | bytes 294944 | tf_op jit(solution)/shard_map/ppermute | solution.py:19
  66.8 2.1 %collective-permute-done.7 = bf16[3,1,64,768]{3,2,1,0:T(8,128)(2,1)} collective-permute-done((bf16[3,1,64,768]{3,2,1,0:T(8,128)(2,1)}, bf16[3,1,64,768]{3,2,1,0:T(8,128)(2,1)}, u32[]{:S(2)}, u32[]{:S(2)}) %collective-permute-start.7) | collective-permute-done | bytes 294944 | tf_op jit(solution)/shard_map/ppermute | solution.py:19
  80.0 2.9 %fusion.45 = (bf16[1,3,2,2,64,768]{5,4,3,2,1,0:T(8,128)(2,1)S(1)}, bf16[3,2,2,64,768]{4,3,2,1,0:T(8,128)(2,1)}) fusion(bf16[2,3,2,2,64,768]{5,4,3,2,1,0:T(8,128)(2,1)} %collective-permute-done.9), kind=kLoop, calls=%fused_computation.114 | loop fusion | bytes 4718592 | tf_op jit(solution)/shard_map/unstack | solution.py:147
  84.0 2.8 %fusion.54 = f32[768,768]{1,0:T(8,128)S(1)} fusion(bf16[768,768]{1,0:T(8,128)(2,1)} %bitcast.294, bf16[768,768]{1,0:T(8,128)(2,1)} %copy-done.3), kind=kOutput, calls=%fused_computation.123 | convolution fusion | flops 905969664 | bytes 4718592 | tf_op jit(solution)/shard_map/dot_general | solution.py:73
  88.4 2.4 %collective-permute-start.10 = (f32[3,16,768]{2,1,0:T(8,128)S(1)}, f32[3,16,768]{2,1,0:T(8,128)S(1)}, u32[]{:S(2)}, u32[]{:S(2)}) collective-permute-start(f32[3,16,768]{2,1,0:T(8,128)S(1)} %get-tuple-element.107), channel_id=1, source_target_pairs={{0,112},{1,113},{2,114},{3,115},{4,116},{5,117},{6,118},{7,119},{8... | collective-permute-start | bytes 442376 | tf_op jit(solution)/shard_map/ppermute | solution.py:19
  90.8 3.3 %collective-permute-start.14 = (f32[3,16,768]{2,1,0:T(8,128)S(1)}, f32[3,16,768]{2,1,0:T(8,128)S(1)}, u32[]{:S(2)}, u32[]{:S(2)}) collective-permute-start(f32[3,16,768]{2,1,0:T(8,128)S(1)} %get-tuple-element.109), channel_id=1, source_target_pairs={{0,112},{1,113},{2,114},{3,115},{4,116},{5,117},{6,118},{7,119},{8... | collective-permute-start | bytes 442376 | tf_op jit(solution)/shard_map/ppermute | solution.py:19
  95.6 2.1 %collective-permute-done.11 = f32[3,16,768]{2,1,0:T(8,128)S(1)} collective-permute-done((f32[3,16,768]{2,1,0:T(8,128)S(1)}, f32[3,16,768]{2,1,0:T(8,128)S(1)}, u32[]{:S(2)}, u32[]{:S(2)}) %collective-permute-start.11) | collective-permute-done | bytes 147488 | tf_op jit(solution)/shard_map/ppermute | solution.py:19
  102.9 4.9 %collective-permute-done.12 = f32[3,32,768]{2,1,0:T(8,128)S(1)} collective-permute-done((f32[3,32,768]{2,1,0:T(8,128)S(1)}, f32[3,32,768]{2,1,0:T(8,128)S(1)}, u32[]{:S(2)}, u32[]{:S(2)}) %collective-permute-start.12) | collective-permute-done | bytes 294944 | tf_op jit(solution)/shard_map/ppermute | solution.py:19
  107.8 2.5 %collective-permute-done.13 = f32[3,32,768]{2,1,0:T(8,128)S(1)} collective-permute-done((f32[3,32,768]{2,1,0:T(8,128)S(1)}, f32[3,32,768]{2,1,0:T(8,128)S(1)}, u32[]{:S(2)}, u32[]{:S(2)}) %collective-permute-start.13) | collective-permute-done | bytes 294944 | tf_op jit(solution)/shard_map/ppermute | solution.py:19
  111.3 2.0 %collective-permute-start.17 = (f32[3,32,768]{2,1,0:T(8,128)}, f32[3,32,768]{2,1,0:T(8,128)}, u32[]{:S(2)}, u32[]{:S(2)}) collective-permute-start(f32[3,32,768]{2,1,0:T(8,128)} %get-tuple-element.67), channel_id=1, source_target_pairs={{0,16},{1,17},{2,18},{3,19},{4,20},{5,21},{6,22},{7,23},{8,24},{9,... | collective-permute-start | bytes 884744 | tf_op jit(solution)/shard_map/ppermute | solution.py:19
  114.1 2.6 %collective-permute-done.19 = f32[3,32,768]{2,1,0:T(8,128)} collective-permute-done((f32[3,32,768]{2,1,0:T(8,128)S(1)}, f32[3,32,768]{2,1,0:T(8,128)}, u32[]{:S(2)}, u32[]{:S(2)}) %collective-permute-start.19) | collective-permute-done | bytes 294944 | tf_op jit(solution)/shard_map/ppermute | solution.py:19
  118.1 2.0 %collective-permute-start.23 = (f32[3,32,768]{2,1,0:T(8,128)S(1)}, f32[3,32,768]{2,1,0:T(8,128)}, u32[]{:S(2)}, u32[]{:S(2)}) collective-permute-start(f32[3,32,768]{2,1,0:T(8,128)S(1)} %get-tuple-element.65), channel_id=1, source_target_pairs={{0,16},{1,17},{2,18},{3,19},{4,20},{5,21},{6,22},{7,23},{8,24},{9,... | collective-permute-start | bytes 884744 | tf_op jit(solution)/shard_map/ppermute | solution.py:19
  121.1 2.0 %collective-permute-done.17 = f32[3,32,768]{2,1,0:T(8,128)} collective-permute-done((f32[3,32,768]{2,1,0:T(8,128)}, f32[3,32,768]{2,1,0:T(8,128)}, u32[]{:S(2)}, u32[]{:S(2)}) %collective-permute-start.17) | collective-permute-done | bytes 294944 | tf_op jit(solution)/shard_map/ppermute | solution.py:19
  123.1 1.9 %fusion.12 = (f32[3,32,768]{2,1,0:T(8,128)}, f32[3,32,768]{2,1,0:T(8,128)S(1)}) fusion(f32[3,32,768]{2,1,0:T(8,128)} %collective-permute-done.17, f32[3,4,64,768]{3,2,1,0:T(8,128)} %bitcast.278, s32[]{:T(128)S(6)} %select_n.508, f32[3,4,64,768]{3,2,1,0:T(8,128)S(1)} %bitcast.272, pred[]{:T(512)S(6)} %eq.108, f32[3,32,768]{2,1,0:T(8,128)S(1)} %collective-permute-done.16, ...), kind=kLoop, calls=%fused_computation.44 | loop fusion | flops 294912 | bytes 2359306 | tf_op jit(solution)/shard_map/add | solution.py:98
  125.5 2.7 %collective-permute-start.20 = (f32[3,32,768]{2,1,0:T(8,128)S(1)}, f32[3,32,768]{2,1,0:T(8,128)}, u32[]{:S(2)}, u32[]{:S(2)}) collective-permute-start(f32[3,32,768]{2,1,0:T(8,128)S(1)} %get-tuple-element.64), channel_id=1, source_target_pairs={{0,112},{1,113},{2,114},{3,115},{4,116},{5,117},{6,118},{7,119},{8... | collective-permute-start | bytes 884744 | tf_op jit(solution)/shard_map/ppermute | solution.py:19
  129.4 3.8 %collective-permute-done.21 = f32[3,32,768]{2,1,0:T(8,128)S(1)} collective-permute-done((f32[3,32,768]{2,1,0:T(8,128)}, f32[3,32,768]{2,1,0:T(8,128)S(1)}, u32[]{:S(2)}, u32[]{:S(2)}) %collective-permute-start.21) | collective-permute-done | bytes 294944 | tf_op jit(solution)/shard_map/ppermute | solution.py:19
  134.9 3.9 %collective-permute-start.24 = (f32[3,32,768]{2,1,0:T(8,128)S(1)}, f32[3,32,768]{2,1,0:T(8,128)S(1)}, u32[]{:S(2)}, u32[]{:S(2)}) collective-permute-start(f32[3,32,768]{2,1,0:T(8,128)S(1)} %get-tuple-element.61), channel_id=1, source_target_pairs={{0,112},{1,113},{2,114},{3,115},{4,116},{5,117},{6,118},{7,119},{8... | collective-permute-start | bytes 884744 | tf_op jit(solution)/shard_map/ppermute | solution.py:19
  138.8 4.2 %collective-permute-done.24 = f32[3,32,768]{2,1,0:T(8,128)S(1)} collective-permute-done((f32[3,32,768]{2,1,0:T(8,128)S(1)}, f32[3,32,768]{2,1,0:T(8,128)S(1)}, u32[]{:S(2)}, u32[]{:S(2)}) %collective-permute-start.24) | collective-permute-done | bytes 294944 | tf_op jit(solution)/shard_map/ppermute | solution.py:19
  143.1 3.7 %collective-permute-done.25 = f32[3,32,768]{2,1,0:T(8,128)S(1)} collective-permute-done((f32[3,32,768]{2,1,0:T(8,128)S(1)}, f32[3,32,768]{2,1,0:T(8,128)S(1)}, u32[]{:S(2)}, u32[]{:S(2)}) %collective-permute-start.25) | collective-permute-done | bytes 294944 | tf_op jit(solution)/shard_map/ppermute | solution.py:19
  148.0 2.6 %fusion.56 = f32[3,512,128]{1,2,0:T(8,128)S(1)} fusion(bf16[3,512,768]{2,1,0:T(8,128)(2,1)} %bitcast.42, bf16[3,128,768]{2,1,0:T(8,128)(2,1)S(1)} %bitcast.281), kind=kOutput, calls=%fused_computation.125 | convolution fusion | flops 301989888 | bytes 3735552 | tf_op jit(solution)/shard_map/knr,kmr->knm/dot_general | solution.py:85
  150.6 2.6 %fusion.55 = f32[3,512,128]{1,2,0:T(8,128)S(1)} fusion(bf16[3,512,768]{2,1,0:T(8,128)(2,1)} %bitcast.38, bf16[3,128,768]{2,1,0:T(8,128)(2,1)S(1)} %bitcast.282), kind=kOutput, calls=%fused_computation.124 | convolution fusion | flops 301989888 | bytes 3735552 | tf_op jit(solution)/shard_map/knr,kmr->knm/dot_general | solution.py:85
  155.9 2.1 %collective-permute-start.28 = (f32[3,2,32,128]{3,2,1,0:T(8,128)S(1)}, f32[3,2,32,128]{3,2,1,0:T(8,128)S(1)}, u32[]{:S(2)}, u32[]{:S(2)}) collective-permute-start(f32[3,2,32,128]{3,2,1,0:T(8,128)S(1)} %fusion.39), channel_id=1, source_target_pairs={{0,4},{1,5},{2,6},{3,7},{4,0},{5,1},{6,2},{7,3},{8,12},{9,13},{10,... | collective-permute-start | bytes 294920 | tf_op jit(solution)/shard_map/ppermute | solution.py:19
  158.4 2.5 %collective-permute-start.30 = (f32[3,2,32,128]{3,2,1,0:T(8,128)S(1)}, f32[3,2,32,128]{3,2,1,0:T(8,128)S(1)}, u32[]{:S(2)}, u32[]{:S(2)}) collective-permute-start(f32[3,2,32,128]{3,2,1,0:T(8,128)S(1)} %get-tuple-element.89), channel_id=1, source_target_pairs={{0,12},{1,13},{2,14},{3,15},{4,8},{5,9},{6,10},{7,11},{8,4},{9,5},... | collective-permute-start | bytes 294920 | tf_op jit(solution)/shard_map/ppermute | solution.py:19
  161.6 2.8 %collective-permute-done.29 = f32[3,2,32,128]{3,2,1,0:T(8,128)S(1)} collective-permute-done((f32[3,2,32,128]{3,2,1,0:T(8,128)S(1)}, f32[3,2,32,128]{3,2,1,0:T(8,128)S(1)}, u32[]{:S(2)}, u32[]{:S(2)}) %collective-permute-start.29) | collective-permute-done | bytes 98336 | tf_op jit(solution)/shard_map/ppermute | solution.py:19
  168.9 3.1 %collective-permute-done.31 = f32[3,32,128]{2,1,0:T(8,128)S(1)} collective-permute-done((f32[3,32,128]{2,1,0:T(8,128)S(1)}, f32[3,32,128]{2,1,0:T(8,128)S(1)}, u32[]{:S(2)}, u32[]{:S(2)}) %collective-permute-start.31) | collective-permute-done | bytes 49184 | tf_op jit(solution)/shard_map/ppermute | solution.py:19
  (113 shorter events, 49.4 us)
Async XLA Ops:
  7.2 76.9 %all-gather.3.cloned.1.call-start = ((), (), s32[]{:S(2)}) async-start(), calls=%async_computation | async-start | bytes 2654208 | tf_op jit(solution)/shard_map/all_gather | solution.py:136
  9.2 19.8 %collective-permute-start = (bf16[3,64,768]{2,1,0:T(8,128)(2,1)S(1)}, bf16[3,64,768]{2,1,0:T(8,128)(2,1)S(1)}, u32[]{:S(2)}, u32[]{:S(2)}) collective-permute-start(bf16[3,64,768]{2,1,0:T(8,128)(2,1)S(1)} %multiply_bitcast_fusion), channel_id=1, source_target_pairs={{0,0},{1,1},{2,2},{3,3},{4,4},{5,5},{6,6},{7,7},{8,132},{9,133},{1... | collective-permute-start | bytes 884744 | tf_op jit(solution)/shard_map/ppermute | solution.py:19
  12.6 23.8 %collective-permute-start.1 = (bf16[3,64,768]{2,1,0:T(8,128)(2,1)S(1)}, bf16[3,64,768]{2,1,0:T(8,128)(2,1)S(1)}, u32[]{:S(2)}, u32[]{:S(2)}) collective-permute-start(bf16[3,64,768]{2,1,0:T(8,128)(2,1)S(1)} %multiply_bitcast_fusion), channel_id=1, source_target_pairs={{0,2},{1,3},{2,0},{3,1},{4,6},{5,7},{6,4},{7,5},{8,134},{9,135},{1... | collective-permute-start | bytes 884744 | tf_op jit(solution)/shard_map/ppermute | solution.py:19
  17.0 21.2 %collective-permute-start.2 = (bf16[3,64,768]{2,1,0:T(8,128)(2,1)S(1)}, bf16[3,64,768]{2,1,0:T(8,128)(2,1)S(1)}, u32[]{:S(2)}, u32[]{:S(2)}) collective-permute-start(bf16[3,64,768]{2,1,0:T(8,128)(2,1)S(1)} %multiply_bitcast_fusion), channel_id=1, source_target_pairs={{0,0},{1,16},{2,32},{3,48},{4,64},{5,80},{6,96},{7,112},{8,128},{9... | collective-permute-start | bytes 884744 | tf_op jit(solution)/shard_map/ppermute | solution.py:19
  38.3 18.4 %collective-permute-start.5 = (bf16[448,768]{1,0:T(8,128)(2,1)}, bf16[448,768]{1,0:T(8,128)(2,1)}, u32[]{:S(2)}, u32[]{:S(2)}) collective-permute-start(bf16[448,768]{1,0:T(8,128)(2,1)} %split.6), channel_id=1, source_target_pairs={{0,128},{1,129},{2,130},{3,131},{4,132},{5,133},{6,134},{7,135},{8... | collective-permute-start | bytes 2064392 | tf_op jit(solution)/shard_map/ppermute | solution.py:19
  39.1 16.0 %collective-permute-start.3 = (bf16[3,2,64,768]{3,2,1,0:T(8,128)(2,1)S(1)}, bf16[3,2,64,768]{3,2,1,0:T(8,128)(2,1)S(1)}, u32[]{:S(2)}, u32[]{:S(2)}) collective-permute-start(bf16[3,2,64,768]{3,2,1,0:T(8,128)(2,1)S(1)} %pad_maximum_fusion.4), channel_id=1, source_target_pairs={{0,4},{1,5},{2,6},{3,7},{4,8},{5,9},{6,10},{7,11},{8,12},{9,13},{1... | collective-permute-start | bytes 1769480 | tf_op jit(solution)/shard_map/ppermute | solution.py:19
  39.2 17.2 %collective-permute-start.4 = (bf16[3,2,64,768]{3,2,1,0:T(8,128)(2,1)S(1)}, bf16[3,2,64,768]{3,2,1,0:T(8,128)(2,1)S(1)}, u32[]{:S(2)}, u32[]{:S(2)}) collective-permute-start(bf16[3,2,64,768]{3,2,1,0:T(8,128)(2,1)S(1)} %pad_maximum_fusion.4), channel_id=1, source_target_pairs={{0,12},{1,13},{2,14},{3,15},{4,0},{5,1},{6,2},{7,3},{8,4},{9,5},{1... | collective-permute-start | bytes 1769480 | tf_op jit(solution)/shard_map/ppermute | solution.py:19
  56.7 13.2 %collective-permute-start.8 = (bf16[320,768]{1,0:T(8,128)(2,1)}, bf16[320,768]{1,0:T(8,128)(2,1)S(1)}, u32[]{:S(2)}, u32[]{:S(2)}) collective-permute-start(bf16[320,768]{1,0:T(8,128)(2,1)} %split.7), channel_id=1, source_target_pairs={{0,128},{1,129},{2,130},{3,131},{4,132},{5,133},{6,134},{7,135},{8... | collective-permute-start | bytes 1474568 | tf_op jit(solution)/shard_map/ppermute | solution.py:19
  58.2 8.6 %collective-permute-start.6 = (bf16[3,1,64,768]{3,2,1,0:T(8,128)(2,1)}, bf16[3,1,64,768]{3,2,1,0:T(8,128)(2,1)}, u32[]{:S(2)}, u32[]{:S(2)}) collective-permute-start(bf16[3,1,64,768]{3,2,1,0:T(8,128)(2,1)} %slice.102), channel_id=1, source_target_pairs={{0,4},{1,5},{2,6},{3,7},{4,8},{5,9},{6,10},{7,11},{8,12},{9,13},{1... | collective-permute-start | bytes 884744 | tf_op jit(solution)/shard_map/ppermute | solution.py:19
  59.1 9.7 %collective-permute-start.7 = (bf16[3,1,64,768]{3,2,1,0:T(8,128)(2,1)}, bf16[3,1,64,768]{3,2,1,0:T(8,128)(2,1)}, u32[]{:S(2)}, u32[]{:S(2)}) collective-permute-start(bf16[3,1,64,768]{3,2,1,0:T(8,128)(2,1)} %slice.103), channel_id=1, source_target_pairs={{0,12},{1,13},{2,14},{3,15},{4,0},{5,1},{6,2},{7,3},{8,4},{9,5},{1... | collective-permute-start | bytes 884744 | tf_op jit(solution)/shard_map/ppermute | solution.py:19
  75.1 4.9 %collective-permute-start.9 = (bf16[2,3,2,2,64,768]{5,4,3,2,1,0:T(8,128)(2,1)}, bf16[2,3,2,2,64,768]{5,4,3,2,1,0:T(8,128)(2,1)}, u32[]{:S(2)}, u32[]{:S(2)}) collective-permute-start(bf16[2,3,2,2,64,768]{5,4,3,2,1,0:T(8,128)(2,1)} %pad_maximum_fusion), channel_id=1, source_target_pairs={{0,1},{1,0},{2,3},{3,2},{4,5},{5,4},{6,7},{7,6},{8,9},{9,8},{10,11... | collective-permute-start | bytes 7077896 | tf_op jit(solution)/shard_map/ppermute | solution.py:19
  88.4 7.2 %collective-permute-start.10 = (f32[3,16,768]{2,1,0:T(8,128)S(1)}, f32[3,16,768]{2,1,0:T(8,128)S(1)}, u32[]{:S(2)}, u32[]{:S(2)}) collective-permute-start(f32[3,16,768]{2,1,0:T(8,128)S(1)} %get-tuple-element.107), channel_id=1, source_target_pairs={{0,112},{1,113},{2,114},{3,115},{4,116},{5,117},{6,118},{7,119},{8... | collective-permute-start | bytes 442376 | tf_op jit(solution)/shard_map/ppermute | solution.py:19
  90.8 6.9 %collective-permute-start.11 = (f32[3,16,768]{2,1,0:T(8,128)S(1)}, f32[3,16,768]{2,1,0:T(8,128)S(1)}, u32[]{:S(2)}, u32[]{:S(2)}) collective-permute-start(f32[3,16,768]{2,1,0:T(8,128)S(1)} %get-tuple-element.106), channel_id=1, source_target_pairs={{0,16},{1,17},{2,18},{3,19},{4,20},{5,21},{6,22},{7,23},{8,24},{9,... | collective-permute-start | bytes 442376 | tf_op jit(solution)/shard_map/ppermute | solution.py:19
  90.8 9.2 %collective-permute-start.14 = (f32[3,16,768]{2,1,0:T(8,128)S(1)}, f32[3,16,768]{2,1,0:T(8,128)S(1)}, u32[]{:S(2)}, u32[]{:S(2)}) collective-permute-start(f32[3,16,768]{2,1,0:T(8,128)S(1)} %get-tuple-element.109), channel_id=1, source_target_pairs={{0,112},{1,113},{2,114},{3,115},{4,116},{5,117},{6,118},{7,119},{8... | collective-permute-start | bytes 442376 | tf_op jit(solution)/shard_map/ppermute | solution.py:19
  94.2 6.4 %collective-permute-start.15 = (f32[3,16,768]{2,1,0:T(8,128)S(1)}, f32[3,16,768]{2,1,0:T(8,128)S(1)}, u32[]{:S(2)}, u32[]{:S(2)}) collective-permute-start(f32[3,16,768]{2,1,0:T(8,128)S(1)} %get-tuple-element.108), channel_id=1, source_target_pairs={{0,16},{1,17},{2,18},{3,19},{4,20},{5,21},{6,22},{7,23},{8,24},{9,... | collective-permute-start | bytes 442376 | tf_op jit(solution)/shard_map/ppermute | solution.py:19
  94.2 52.6 %collective-permute-start.26 = (bf16[3,8,64,768]{3,2,1,0:T(8,128)(2,1)}, bf16[3,8,64,768]{3,2,1,0:T(8,128)(2,1)}, u32[]{:S(2)}, u32[]{:S(2)}) collective-permute-start(bf16[3,8,64,768]{3,2,1,0:T(8,128)(2,1)} %bitcast.18), channel_id=1, source_target_pairs={{0,128},{1,129},{2,130},{3,131},{4,132},{5,133},{6,134},{7,135},{8... | collective-permute-start | bytes 7077896 | tf_op jit(solution)/shard_map/ppermute | solution.py:19
  97.8 10.0 %collective-permute-start.12 = (f32[3,32,768]{2,1,0:T(8,128)S(1)}, f32[3,32,768]{2,1,0:T(8,128)S(1)}, u32[]{:S(2)}, u32[]{:S(2)}) collective-permute-start(f32[3,32,768]{2,1,0:T(8,128)S(1)} %pad_maximum_fusion.7), channel_id=1, source_target_pairs={{0,112},{1,113},{2,114},{3,115},{4,116},{5,117},{6,118},{7,119},{8... | collective-permute-start | bytes 884744 | tf_op jit(solution)/shard_map/ppermute | solution.py:19
  99.1 11.2 %collective-permute-start.13 = (f32[3,32,768]{2,1,0:T(8,128)S(1)}, f32[3,32,768]{2,1,0:T(8,128)S(1)}, u32[]{:S(2)}, u32[]{:S(2)}) collective-permute-start(f32[3,32,768]{2,1,0:T(8,128)S(1)} %pad_maximum_fusion.8), channel_id=1, source_target_pairs={{0,16},{1,17},{2,18},{3,19},{4,20},{5,21},{6,22},{7,23},{8,24},{9,... | collective-permute-start | bytes 884744 | tf_op jit(solution)/shard_map/ppermute | solution.py:19
  100.6 13.5 %collective-permute-start.18 = (f32[3,32,768]{2,1,0:T(8,128)S(1)}, f32[3,32,768]{2,1,0:T(8,128)S(1)}, u32[]{:S(2)}, u32[]{:S(2)}) collective-permute-start(f32[3,32,768]{2,1,0:T(8,128)S(1)} %pad_maximum_fusion.9), channel_id=1, source_target_pairs={{0,112},{1,113},{2,114},{3,115},{4,116},{5,117},{6,118},{7,119},{8... | collective-permute-start | bytes 884744 | tf_op jit(solution)/shard_map/ppermute | solution.py:19
  102.6 14.1 %collective-permute-start.19 = (f32[3,32,768]{2,1,0:T(8,128)S(1)}, f32[3,32,768]{2,1,0:T(8,128)}, u32[]{:S(2)}, u32[]{:S(2)}) collective-permute-start(f32[3,32,768]{2,1,0:T(8,128)S(1)} %pad_maximum_fusion.10), channel_id=1, source_target_pairs={{0,16},{1,17},{2,18},{3,19},{4,20},{5,21},{6,22},{7,23},{8,24},{9,... | collective-permute-start | bytes 884744 | tf_op jit(solution)/shard_map/ppermute | solution.py:19
  111.3 9.8 %collective-permute-start.16 = (f32[3,32,768]{2,1,0:T(8,128)}, f32[3,32,768]{2,1,0:T(8,128)S(1)}, u32[]{:S(2)}, u32[]{:S(2)}) collective-permute-start(f32[3,32,768]{2,1,0:T(8,128)} %get-tuple-element.68), channel_id=1, source_target_pairs={{0,112},{1,113},{2,114},{3,115},{4,116},{5,117},{6,118},{7,119},{8... | collective-permute-start | bytes 884744 | tf_op jit(solution)/shard_map/ppermute | solution.py:19
  111.3 11.8 %collective-permute-start.17 = (f32[3,32,768]{2,1,0:T(8,128)}, f32[3,32,768]{2,1,0:T(8,128)}, u32[]{:S(2)}, u32[]{:S(2)}) collective-permute-start(f32[3,32,768]{2,1,0:T(8,128)} %get-tuple-element.67), channel_id=1, source_target_pairs={{0,16},{1,17},{2,18},{3,19},{4,20},{5,21},{6,22},{7,23},{8,24},{9,... | collective-permute-start | bytes 884744 | tf_op jit(solution)/shard_map/ppermute | solution.py:19
  118.0 10.3 %collective-permute-start.22 = (f32[3,32,768]{2,1,0:T(8,128)S(1)}, f32[3,32,768]{2,1,0:T(8,128)}, u32[]{:S(2)}, u32[]{:S(2)}) collective-permute-start(f32[3,32,768]{2,1,0:T(8,128)S(1)} %get-tuple-element.66), channel_id=1, source_target_pairs={{0,112},{1,113},{2,114},{3,115},{4,116},{5,117},{6,118},{7,119},{8... | collective-permute-start | bytes 884744 | tf_op jit(solution)/shard_map/ppermute | solution.py:19
  118.1 11.3 %collective-permute-start.23 = (f32[3,32,768]{2,1,0:T(8,128)S(1)}, f32[3,32,768]{2,1,0:T(8,128)}, u32[]{:S(2)}, u32[]{:S(2)}) collective-permute-start(f32[3,32,768]{2,1,0:T(8,128)S(1)} %get-tuple-element.65), channel_id=1, source_target_pairs={{0,16},{1,17},{2,18},{3,19},{4,20},{5,21},{6,22},{7,23},{8,24},{9,... | collective-permute-start | bytes 884744 | tf_op jit(solution)/shard_map/ppermute | solution.py:19
  125.0 8.1 %collective-permute-start.21 = (f32[3,32,768]{2,1,0:T(8,128)}, f32[3,32,768]{2,1,0:T(8,128)S(1)}, u32[]{:S(2)}, u32[]{:S(2)}) collective-permute-start(f32[3,32,768]{2,1,0:T(8,128)} %get-tuple-element.63), channel_id=1, source_target_pairs={{0,16},{1,17},{2,18},{3,19},{4,20},{5,21},{6,22},{7,23},{8,24},{9,... | collective-permute-start | bytes 884744 | tf_op jit(solution)/shard_map/ppermute | solution.py:19
  125.5 7.8 %collective-permute-start.20 = (f32[3,32,768]{2,1,0:T(8,128)S(1)}, f32[3,32,768]{2,1,0:T(8,128)}, u32[]{:S(2)}, u32[]{:S(2)}) collective-permute-start(f32[3,32,768]{2,1,0:T(8,128)S(1)} %get-tuple-element.64), channel_id=1, source_target_pairs={{0,112},{1,113},{2,114},{3,115},{4,116},{5,117},{6,118},{7,119},{8... | collective-permute-start | bytes 884744 | tf_op jit(solution)/shard_map/ppermute | solution.py:19
  134.9 8.1 %collective-permute-start.24 = (f32[3,32,768]{2,1,0:T(8,128)S(1)}, f32[3,32,768]{2,1,0:T(8,128)S(1)}, u32[]{:S(2)}, u32[]{:S(2)}) collective-permute-start(f32[3,32,768]{2,1,0:T(8,128)S(1)} %get-tuple-element.61), channel_id=1, source_target_pairs={{0,112},{1,113},{2,114},{3,115},{4,116},{5,117},{6,118},{7,119},{8... | collective-permute-start | bytes 884744 | tf_op jit(solution)/shard_map/ppermute | solution.py:19
  138.8 7.9 %collective-permute-start.25 = (f32[3,32,768]{2,1,0:T(8,128)S(1)}, f32[3,32,768]{2,1,0:T(8,128)S(1)}, u32[]{:S(2)}, u32[]{:S(2)}) collective-permute-start(f32[3,32,768]{2,1,0:T(8,128)S(1)} %get-tuple-element.62), channel_id=1, source_target_pairs={{0,16},{1,17},{2,18},{3,19},{4,20},{5,21},{6,22},{7,23},{8,24},{9,... | collective-permute-start | bytes 884744 | tf_op jit(solution)/shard_map/ppermute | solution.py:19
  155.9 5.7 %collective-permute-start.28 = (f32[3,2,32,128]{3,2,1,0:T(8,128)S(1)}, f32[3,2,32,128]{3,2,1,0:T(8,128)S(1)}, u32[]{:S(2)}, u32[]{:S(2)}) collective-permute-start(f32[3,2,32,128]{3,2,1,0:T(8,128)S(1)} %fusion.39), channel_id=1, source_target_pairs={{0,4},{1,5},{2,6},{3,7},{4,0},{5,1},{6,2},{7,3},{8,12},{9,13},{10,... | collective-permute-start | bytes 294920 | tf_op jit(solution)/shard_map/ppermute | solution.py:19
  158.2 6.3 %collective-permute-start.29 = (f32[3,2,32,128]{3,2,1,0:T(8,128)S(1)}, f32[3,2,32,128]{3,2,1,0:T(8,128)S(1)}, u32[]{:S(2)}, u32[]{:S(2)}) collective-permute-start(f32[3,2,32,128]{3,2,1,0:T(8,128)S(1)} %get-tuple-element.90), channel_id=1, source_target_pairs={{0,8},{1,9},{2,10},{3,11},{4,12},{5,13},{6,14},{7,15},{8,0},{9,1},... | collective-permute-start | bytes 294920 | tf_op jit(solution)/shard_map/ppermute | solution.py:19
  158.4 7.8 %collective-permute-start.30 = (f32[3,2,32,128]{3,2,1,0:T(8,128)S(1)}, f32[3,2,32,128]{3,2,1,0:T(8,128)S(1)}, u32[]{:S(2)}, u32[]{:S(2)}) collective-permute-start(f32[3,2,32,128]{3,2,1,0:T(8,128)S(1)} %get-tuple-element.89), channel_id=1, source_target_pairs={{0,12},{1,13},{2,14},{3,15},{4,8},{5,9},{6,10},{7,11},{8,4},{9,5},... | collective-permute-start | bytes 294920 | tf_op jit(solution)/shard_map/ppermute | solution.py:19
  166.3 5.7 %collective-permute-start.31 = (f32[3,32,128]{2,1,0:T(8,128)S(1)}, f32[3,32,128]{2,1,0:T(8,128)S(1)}, u32[]{:S(2)}, u32[]{:S(2)}) collective-permute-start(f32[3,32,128]{2,1,0:T(8,128)S(1)} %slice_bitcast_fusion.3), channel_id=1, source_target_pairs={{0,2},{1,3},{2,0},{3,1},{4,6},{5,7},{6,4},{7,5},{8,10},{9,11},{10,... | collective-permute-start | bytes 147464 | tf_op jit(solution)/shard_map/ppermute | solution.py:19
  (9 other events, 65.6 us)
Sparse Core Ops, SparseCore 0:
  41.3 42.6 all-gather.2
